TPU v7x, 32 devices: a whole 2x2x4 slice. The times are simulated.
32 devices in a mesh: ctx: 16 (over z, x, core), head: 2 (over y).
Axes of the slice: x: 2, y: 2, z: 4, core: 2. Of those that a mesh axis runs over, the one named last changes fastest.
Arguments:
- tokens: bfloat16 [4096, 3072], P('ctx', 'head'), may hold values from -48 to 48
- block_order: int32 [32], replicated, may hold values from 0 to 31, each once
- block_mask: int32 [32, 32], replicated, may hold values from 0 to 1, as said below
- w_query: bfloat16 [3072, 3072], P(None, 'head'), may hold values from -0.109375 to 0.109375
- w_key: bfloat16 [3072, 3072], P(None, 'head'), may hold values from -0.109375 to 0.109375
- w_value: bfloat16 [3072, 3072], P(None, 'head'), may hold values from -0.109375 to 0.109375
- w_out: bfloat16 [3072, 3072], P('head'), may hold values from -0.109375 to 0.109375
Outputs:
- mixed: bfloat16 [4096, 3072], P('ctx', 'head')
Inputs may be any that keep to these rules, and one draw needn't show every extreme that they name: `block_order`: a permutation of the block numbers. block_mask[f, f] = 1 for every block f.
All inputs are finite; a program needn't handle non-finite values.
Results may differ from a plain program's by a relative error of at most 0.02.
The roundings to bfloat16 on the way count: a program that leaves them out, or rounds other values in their place, can miss the bound.
Values may be sent and summed in bfloat16 or wider, within the bound.
No kernel may reach another device: no remote copies, remote signals or barrier semaphores. Data moves between devices by JAX's collectives and lax.ppermute only.
A program may use at most 128 MiB of HBM per device.

v0:
```python
import jax
import jax.numpy as jnp
from jax import lax
from jax.sharding import PartitionSpec as P

HEAD_DIM = 128
BLOCK = 128


def per_device(tokens, block_order, block_mask, w_query, w_key, w_value, w_out):
    row_count = tokens.shape[0]
    local_width = w_query.shape[1]
    local_heads = local_width // HEAD_DIM
    block_count = block_order.shape[0]
    portion = lax.all_gather(tokens, "head", axis=1, tiled=True)
    projected = tuple(
        (
            jnp.dot(portion, weight, preferred_element_type=jnp.float32)
            for weight in (w_query, w_key, w_value)
        )
    )
    query_rows, key_rows, value_rows = [
        part_sum.astype(jnp.bfloat16).reshape(row_count, local_heads, HEAD_DIM)
        for part_sum in projected
    ]
    frame_ids = jnp.arange(block_count, dtype=jnp.int32)
    placed = (block_order[None, :] == frame_ids[:, None]).astype(jnp.float32)
    mask_float = block_mask.astype(jnp.float32)
    cycle_live = jnp.dot(
        jnp.dot(placed.T, mask_float, precision=lax.Precision.HIGHEST),
        placed,
        precision=lax.Precision.HIGHEST,
    )
    cycle_index = lax.axis_index("ctx")
    global_rows = cycle_index * row_count + jnp.arange(row_count, dtype=jnp.int32)
    row_blocks = global_rows // BLOCK
    row_pick = (row_blocks[:, None] == frame_ids[None, :]).astype(jnp.float32)
    live_columns = jnp.dot(row_pick, cycle_live, precision=lax.Precision.HIGHEST).T
    inv_root = 1.0 / HEAD_DIM**0.5

    def update(state, key_tile, value_tile, key_keep):
        top_now, total_now, accum = state
        scores = (
            jnp.einsum("qhd,khd->hqk", query_rows, key_tile, preferred_element_type=jnp.float32)
            * inv_root
        )
        allowed = key_keep[None, :, None]
        top_next = jnp.maximum(top_now, jnp.max(jnp.where(allowed, scores, -1e30), axis=-1))
        factor = jnp.exp(top_now - top_next)
        weights = jnp.where(allowed, jnp.exp(scores - top_next[..., None]), 0.0)
        total_next = total_now * factor + jnp.sum(weights, axis=-1)
        accum = accum * factor[..., None] + jnp.einsum(
            "hqk,khd->hqd",
            weights.astype(jnp.bfloat16),
            value_tile,
            preferred_element_type=jnp.float32,
        )
        return (top_next, total_next, accum)

    initial = (
        jnp.full((local_heads, row_count), -1e30, jnp.float32),
        jnp.zeros((local_heads, row_count), jnp.float32),
        jnp.zeros((local_heads, row_count, HEAD_DIM), jnp.float32),
    )
    carry = initial
    key_part = lax.all_gather(key_rows, "ctx", axis=0, tiled=True)
    value_part = lax.all_gather(value_rows, "ctx", axis=0, tiled=True)
    tile_count = key_part.shape[0] // BLOCK
    key_tiles = key_part.reshape(tile_count, BLOCK, local_heads, HEAD_DIM)
    value_tiles = value_part.reshape(tile_count, BLOCK, local_heads, HEAD_DIM)

    def advance(state, inputs):
        key_tile, value_tile, offset = inputs
        key_keep = lax.dynamic_index_in_dim(live_columns, offset, 0, keepdims=False) > 0.5
        state = update(state, key_tile, value_tile, key_keep)
        return (state, None)

    carry, _ = lax.scan(
        advance, carry, (key_tiles, value_tiles, jnp.arange(tile_count, dtype=jnp.int32))
    )
    top_final, total_final, accum_final = carry
    attended = (
        (accum_final / total_final[..., None])
        .transpose(1, 0, 2)
        .reshape(row_count, local_width)
        .astype(jnp.bfloat16)
    )
    partial_out = jnp.dot(attended, w_out, preferred_element_type=jnp.float32)
    return lax.psum_scatter(
        partial_out.astype(jnp.bfloat16), "head", scatter_dimension=1, tiled=True
    )


def solution(mesh):
    in_specs = (
        P("ctx", "head"),
        P(),
        P(),
        P(None, "head"),
        P(None, "head"),
        P(None, "head"),
        P("head", None),
    )
    out_specs = P("ctx", "head")
    return jax.shard_map(
        per_device, mesh=mesh, in_specs=in_specs, out_specs=out_specs, check_vma=False
    )
```

profile of v0, /device:TPU:0, one launch (start us, length us, event | category | flops | bytes accessed | tf_op | source)
XLA Modules:
  0.0 517.9 jit_solution(12459821957731257862)
XLA Ops:
  7.3 31.5 %all-gather.4.cloned.1.call-done = bf16[256,3072]{1,0:T(8,128)(2,1)} async-done(((bf16[256,1536]{1,0:T(8,128)(2,1)}), bf16[256,3072]{1,0:T(8,128)(2,1)}) %all-gather.4.cloned.1.call-update) | async-done | bytes 1572880 | tf_op jit(solution)/shard_map/all_gather | solution.py:15
  38.8 6.8 %convolution_convert_fusion.1 = bf16[256,1536]{1,0:T(8,128)(2,1)S(1)} fusion(bf16[256,3072]{1,0:T(8,128)(2,1)} %all-gather.4.cloned.1.call-done, bf16[3072,1536]{1,0:T(8,128)(2,1)} %param.14), kind=kOutput, calls=%fused_computation.23 | convolution fusion | flops 2416312320 | bytes 11796480 | tf_op jit(solution)/shard_map/dot_general | solution.py:18
  47.3 6.3 %convolution_convert_fusion.3 = bf16[256,1536]{1,0:T(8,128)(2,1)S(1)} fusion(bf16[256,3072]{1,0:T(8,128)(2,1)S(1)} %copy-done.2, bf16[3072,1536]{1,0:T(8,128)(2,1)} %param.13), kind=kOutput, calls=%fused_computation.25 | convolution fusion | flops 2416312320 | bytes 11796480 | tf_op jit(solution)/shard_map/dot_general | solution.py:18
  55.5 7.0 %convolution_convert_fusion.2 = bf16[256,1536]{1,0:T(8,128)(2,1)S(1)} fusion(bf16[256,3072]{1,0:T(8,128)(2,1)} %all-gather.4.cloned.1.call-done, bf16[3072,1536]{1,0:T(8,128)(2,1)} %param.12), kind=kOutput, calls=%fused_computation.24 | convolution fusion | flops 2416312320 | bytes 11796480 | tf_op jit(solution)/shard_map/dot_general | solution.py:18
  63.2 87.7 %all-gather.8.cloned.1.call-done = bf16[4096,12,128]{0,2,1:T(8,128)(2,1)} async-done(((bf16[256,12,128]{0,2,1:T(8,128)(2,1)}), bf16[4096,12,128]{0,2,1:T(8,128)(2,1)}) %all-gather.8.cloned.1.call-update) | async-done | bytes 12582928 | tf_op jit(solution)/shard_map/all_gather | solution.py:67
  150.9 16.7 %copy.15 = bf16[4096,12,128]{2,0,1:T(8,128)(2,1)} copy(bf16[4096,12,128]{0,2,1:T(8,128)(2,1)} %all-gather.8.cloned.1.call-done) | data formatting | bytes 25165824 | tf_op jit(solution)/shard_map/all_gather | solution.py:67
  167.6 87.6 %all-gather.6.cloned.1.call-done = bf16[4096,12,128]{0,2,1:T(8,128)(2,1)} async-done(((bf16[256,12,128]{0,2,1:T(8,128)(2,1)}), bf16[4096,12,128]{0,2,1:T(8,128)(2,1)}) %all-gather.6.cloned.1.call-update) | async-done | bytes 12582928 | tf_op jit(solution)/shard_map/all_gather | solution.py:66
  255.2 16.6 %copy.12 = bf16[4096,12,128]{2,0,1:T(8,128)(2,1)} copy(bf16[4096,12,128]{0,2,1:T(8,128)(2,1)} %all-gather.6.cloned.1.call-done) | data formatting | bytes 25165824 | tf_op jit(solution)/shard_map/all_gather | solution.py:66
  271.9 206.9 %while.15 = (s32[]{:T(128)}, f32[12,256]{1,0:T(8,128)S(1)}, f32[12,256]{1,0:T(8,128)S(1)}, f32[12,256,128]{2,1,0:T(8,128)S(1)}, s32[32]{0:T(128)S(1)}, /*index=5...) while((s32[]{:T(128)}, f32[12,256]{1,0:T(8,128)S(1)}, ...), condition=%wide.region_3.4_spmd.clone, body=%wide.region_0.3_spmd.clone.sunk | while | flops 206060800 | bytes 9636035 | solution.py:78
  276.2 2.2 fusion.37
  282.6 2.2 fusion.37
  289.1 2.2 fusion.37
  295.6 2.2 fusion.37
  302.0 2.2 fusion.37
  306.8 1.4 select_reduce_fusion.2
  308.5 2.2 fusion.37
  315.0 2.2 fusion.37
  319.7 1.4 select_reduce_fusion.2
  321.4 2.2 fusion.37
  327.9 2.2 fusion.37
  332.6 1.4 select_reduce_fusion.2
  334.4 2.2 fusion.37
  340.8 2.2 fusion.37
  345.6 1.4 select_reduce_fusion.2
  347.3 2.2 fusion.37
  353.8 2.2 fusion.37
  360.2 2.2 fusion.37
  366.7 2.2 fusion.37
  373.2 2.2 fusion.37
  379.6 2.2 fusion.37
  386.1 2.2 fusion.37
  392.6 2.2 fusion.37
  399.0 2.2 fusion.37
  405.5 2.2 fusion.37
  412.0 2.2 fusion.37
  418.4 2.2 fusion.37
  424.9 2.2 fusion.37
  431.4 2.2 fusion.37
  437.8 2.2 fusion.37
  444.3 2.2 fusion.37
  450.8 2.2 fusion.37
  457.2 2.2 fusion.37
  463.7 2.2 fusion.37
  470.2 2.2 fusion.37
  474.9 1.4 select_reduce_fusion.2
  476.6 2.2 fusion.37
  479.5 7.4 %convolution_convert_fusion = bf16[256,3072]{1,0:T(8,128)(2,1)} fusion(bf16[256,1536]{0,1:T(8,128)(2,1)S(1)} %bitcast.50, bf16[1536,3072]{1,0:T(8,128)(2,1)} %param.15), kind=kOutput, calls=%fused_computation.22 | convolution fusion | flops 2416705536 | bytes 11796480 | tf_op jit(solution)/shard_map/dot_general | solution.py:88
  487.0 24.4 %reduce-scatter.2.cloned.1.call-done = bf16[256,1536]{1,0:T(8,128)(2,1)} async-done(((bf16[256,3072]{1,0:T(8,128)(2,1)}), bf16[256,1536]{1,0:T(8,128)(2,1)}) %reduce-scatter.2.cloned.1.call-update) | async-done | bytes 786448 | tf_op jit(solution)/shard_map/reduce_scatter | solution.py:89
  (247 shorter events, 72.5 us)
Async XLA Ops:
  6.5 32.3 %all-gather.4.cloned.1.call-start = ((), (), s32[]{:S(2)}) async-start(), calls=%async_computation.1 | async-start | bytes 2359296 | tf_op jit(solution)/shard_map/all_gather | solution.py:15
  7.3 143.7 %all-gather.8.cloned.1.call-start = ((), (), s32[]{:S(2)}) async-start(), calls=%async_computation.3 | async-start | bytes 13369344 | tf_op jit(solution)/shard_map/all_gather | solution.py:67
  45.6 1.7 copy-start.2
  46.8 208.4 %all-gather.6.cloned.1.call-start = ((), (), s32[]{:S(2)}) async-start(), calls=%async_computation.2 | async-start | bytes 13369344 | tf_op jit(solution)/shard_map/all_gather | solution.py:66
  53.6 1.3 copy-start
  53.6 1.3 copy-start.1
  54.8 456.6 %reduce-scatter.2.cloned.1.call-start = ((), (), s32[]{:S(2)}) async-start(), calls=%async_computation.4 | async-start | bytes 2359296 | tf_op jit(solution)/shard_map/reduce_scatter | solution.py:89
Sparse Core Ops, SparseCore 0:
  8.9 29.8 all-gather.3
  46.9 103.9 all-gather.7
  153.1 102.1 all-gather.5
  487.1 24.2 reduce-scatter.1
where the time goes:
time: 522 us; the launch traced here: 518 us
  waiting for transfers between devices  232 us (44%)
  matrix products  141 us (27%)
  loops' own time  64.2 us (12%)
  local copies, waits for them, and re-layouts  56.1 us (11%)
  between operations  13.3 us (3%)
  other arithmetic  10.8 us (2%)
    all_gather x1, waiting for transfers between devices, per_device(): value_part = lax.all_gather(value_rows, 'ctx', axis=0, tiled=True)  87.7 us
    all_gather x1, waiting for transfers between devices, per_device(): key_part = lax.all_gather(key_rows, 'ctx', axis=0, tiled=True)  87.6 us
    dot_general x32, matrix products, update(): jnp.einsum('hqk,khd->hqd', weights.astype(jnp.bfloat16), value_tile, pref...  68.9 us
    another operation x1, loops' own time, per_device(): lax.scan(advance, carry, (key_tiles, value_tiles, jnp.arange(tile_count,...  64.2 us
    dot_general x32, matrix products, update(): jnp.einsum('qhd,khd->hqk', query_rows, key_tile, preferred_element_type=j...  44.4 us
    all_gather x1, waiting for transfers between devices, per_device(): portion = lax.all_gather(tokens, 'head', axis=1, tiled=True)  31.5 us
    reduce_scatter x1, waiting for transfers between devices, per_device(): lax.psum_scatter(partial_out.astype(jnp.bfloat16), 'head', scatter_dimens...  24.4 us
    dot_general x3, matrix products, per_device(): jnp.dot(portion, weight, preferred_element_type=jnp.float32)  20 us
  transfers between devices with their start and end apart: 4, of which 4 were waited for; matrix products, arithmetic and copies ran while one was open for 6% of the time, Pallas kernels for 0%

commit v1 on v0

v1 whole, which is shorter than its diff:
```python
import functools
import math

import jax
import jax.numpy as jnp
from jax import lax
from jax.experimental import pallas as pl
from jax.experimental.pallas import tpu as pltpu
from jax.sharding import PartitionSpec as P

HEAD_DIM = 128
BLOCK = 128
Z, X, C = 4, 2, 2
MIB = 1 << 20
BF16, F32 = jnp.bfloat16, jnp.float32


def place(z, x, c):
    return (z * X + x) * C + c


def hop(dz, dx, dc):
    return [
        (place(z, x, c), place(z ^ dz, x ^ dx, c ^ dc))
        for z in range(Z)
        for x in range(X)
        for c in range(C)
    ]


def params(mib):
    return pltpu.CompilerParams(vmem_limit_bytes=mib * MIB)


def project(where, own, other, weights, width, first):
    rows, half = own.shape
    kinds = len(weights)

    def column(i, s):
        return (s[1] ^ i) * first[1] + first[0]

    def body(s, own_ref, other_ref, *refs):
        mine, theirs = refs[:kinds], refs[kinds : 2 * kinds]
        outs = refs[2 * kinds :]
        step = pl.program_id(0)
        w_mine = jnp.concatenate([r[...] for r in mine], axis=1)
        w_theirs = jnp.concatenate([r[...] for r in theirs], axis=1)
        total = jnp.dot(own_ref[...], w_mine, preferred_element_type=F32)
        total += jnp.dot(other_ref[...], w_theirs, preferred_element_type=F32)
        total = total.astype(BF16)
        for i in range(Z):

            @pl.when(step == i)
            def _(i=i):
                for k in range(kinds):
                    outs[i][k] = total[:, k * width : (k + 1) * width]

    row_spec = pl.BlockSpec((rows, half), lambda i, s: (0, 0))
    mine_spec = pl.BlockSpec((half, width), lambda i, s: (s[0], column(i, s)))
    theirs_spec = pl.BlockSpec((half, width), lambda i, s: (1 - s[0], column(i, s)))
    return pl.pallas_call(
        body,
        grid_spec=pltpu.PrefetchScalarGridSpec(
            num_scalar_prefetch=1,
            grid=(Z,),
            in_specs=[row_spec, row_spec] + [mine_spec] * kinds + [theirs_spec] * kinds,
            out_specs=[pl.BlockSpec((kinds, rows, width), lambda i, s: (0, 0, 0))] * Z,
        ),
        out_shape=[jax.ShapeDtypeStruct((kinds, rows, width), BF16)] * Z,
        compiler_params=params(24),
        cost_estimate=pl.CostEstimate(
            flops=2 * rows * 2 * half * width * kinds * Z,
            bytes_accessed=2 * 2 * half * width * kinds * Z,
            transcendentals=0,
        ),
    )(where, own, other, *weights, *weights)


def attend(queries, parts, bias, head):
    rows = queries[0].shape[1]
    tile = parts[0].shape[2]
    tiles = len(parts) * Z
    key_count = tiles * tile
    scale = math.log2(math.e) / math.sqrt(HEAD_DIM)
    per = rows // BLOCK

    def body(*refs):
        q_refs, kv_refs, bias_ref = refs[:Z], refs[Z : Z + len(parts)], refs[Z + len(parts)]
        outs = refs[Z + len(parts) + 1 : Z + len(parts) + 1 + Z]
        s_ref, q_ref = refs[-2:]
        step = pl.program_id(0)
        for i in range(Z):

            @pl.when(step == i)
            def _(i=i):
                q_ref[...] = q_refs[i][0]

        query = q_ref[...]
        top = jnp.full((rows, 1), -jnp.inf, F32)
        for t in range(tiles):
            key = kv_refs[t // Z][t % Z, 0]
            score = lax.dot_general(
                query, key, (((1,), (1,)), ((), ())), preferred_element_type=F32
            )
            keep = [
                jnp.broadcast_to(
                    bias_ref[pl.ds(step * per + r, 1), t * tile : (t + 1) * tile], (BLOCK, tile)
                )
                for r in range(per)
            ]
            score = score + jnp.concatenate(keep, axis=0)
            s_ref[:, t * tile : (t + 1) * tile] = score
            top = jnp.maximum(top, jnp.max(score, axis=1, keepdims=True))
        shift = top * scale
        total = jnp.zeros((rows, 1), F32)
        accum = jnp.zeros((rows, HEAD_DIM), F32)
        for t in range(tiles):
            weight = jnp.exp2(s_ref[:, t * tile : (t + 1) * tile] * scale - shift)
            total += jnp.sum(weight, axis=1, keepdims=True)
            accum += jnp.dot(
                weight.astype(BF16), kv_refs[t // Z][t % Z, 1], preferred_element_type=F32
            )
        result = (accum / total).astype(BF16)
        for i in range(Z):

            @pl.when(step == i)
            def _(i=i):
                outs[i][...] = result

    return pl.pallas_call(
        body,
        grid=(Z,),
        in_specs=[pl.BlockSpec((1, rows, HEAD_DIM), lambda i: (0, 0, head))] * Z
        + [pl.BlockSpec(p.shape, lambda i: (0, 0, 0, 0)) for p in parts]
        + [pl.BlockSpec(bias.shape, lambda i: (0, 0))],
        out_specs=[pl.BlockSpec((rows, HEAD_DIM), lambda i: (0, 0))] * Z,
        out_shape=[jax.ShapeDtypeStruct((rows, HEAD_DIM), BF16)] * Z,
        scratch_shapes=[pltpu.VMEM((rows, key_count), F32), pltpu.VMEM((rows, HEAD_DIM), BF16)],
        compiler_params=params(32),
        cost_estimate=pl.CostEstimate(
            flops=4 * Z * rows * key_count * HEAD_DIM,
            bytes_accessed=4 * key_count * HEAD_DIM,
            transcendentals=Z * rows * key_count,
        ),
    )(*queries, *parts, bias)


def mix(where, attended, w_out, flip, step_width):
    rows = attended[0].shape[0]
    depth = w_out.shape[0] // Z
    half = w_out.shape[1] // 2
    steps = half // step_width
    count = len(attended)

    def body(s, *refs):
        rows_all = jnp.concatenate([r[...] for r in refs[:count]], axis=1)
        weight = jnp.concatenate([r[...] for r in refs[count : count + Z]], axis=0)
        refs[-1][...] = jnp.dot(rows_all, weight, preferred_element_type=F32).astype(BF16)

    def weight_spec(dz):
        return pl.BlockSpec(
            (depth, step_width),
            lambda i, s: (s[1] ^ dz, (1 - s[0] if flip else s[0]) * steps + i),
        )

    return pl.pallas_call(
        body,
        grid_spec=pltpu.PrefetchScalarGridSpec(
            num_scalar_prefetch=1,
            grid=(steps,),
            in_specs=[pl.BlockSpec(a.shape, lambda i, s: (0, 0)) for a in attended]
            + [weight_spec(dz) for dz in range(Z)],
            out_specs=pl.BlockSpec((rows, step_width), lambda i, s: (0, i)),
        ),
        out_shape=jax.ShapeDtypeStruct((rows, half), BF16),
        compiler_params=params(24),
        cost_estimate=pl.CostEstimate(
            flops=2 * rows * Z * depth * half,
            bytes_accessed=2 * Z * depth * half,
            transcendentals=0,
        ),
    )(where, *attended, *([w_out] * Z))


def split_heads(tokens, block_order, block_mask, w_query, w_key, w_value, w_out):
    rows, half = tokens.shape
    group_heads = w_query.shape[1] // HEAD_DIM // Z
    block_count = block_order.shape[0]
    per = rows // BLOCK
    ctx = lax.axis_index("ctx")
    y = lax.axis_index("head")
    z, x, c = ctx // (X * C), (ctx // C) % X, ctx % C
    where = jnp.stack([y, z]).astype(jnp.int32)

    other = lax.ppermute(tokens, "head", [(0, 1), (1, 0)])

    def blocks(pairs):
        first = jnp.stack([place(z ^ dz, x ^ dx, c ^ dc) for dz, dx, dc in pairs]) * per
        return (first[:, None] + jnp.arange(per)[None, :]).reshape(-1)

    query_blocks = blocks([(dz, 0, 0) for dz in range(Z)])
    key_blocks = blocks([(dz, dx, dc) for dc, dx in ((0, 0), (0, 1), (1, 0), (1, 1)) for dz in range(Z)])
    frames = jnp.arange(block_count, dtype=jnp.int32)
    order_hot = (block_order[:, None] == frames[None, :]).astype(F32)

    def pick(wanted):
        place_hot = (wanted[:, None] == frames[None, :]).astype(F32)
        return jnp.dot(place_hot, order_hot)

    live = jnp.dot(
        jnp.dot(pick(query_blocks), block_mask.astype(F32)), pick(key_blocks).T
    )
    bias = jnp.repeat(jnp.where(live > 0.5, 0.0, -1e30).astype(F32), BLOCK, axis=1)

    def share(pieces):
        return [pieces[0]] + [lax.ppermute(pieces[dz], "ctx", hop(dz, 0, 0)) for dz in range(1, Z)]

    gathered = []
    queries = None
    for j in range(group_heads):
        pieces = share(
            project(where, tokens, other, (w_key, w_value), HEAD_DIM, (j, group_heads))
        )
        part = jnp.stack(pieces)
        across = lax.ppermute(part, "ctx", hop(0, 1, 0))
        gathered.append(
            (
                part,
                across,
                lax.ppermute(part, "ctx", hop(0, 0, 1)),
                lax.ppermute(across, "ctx", hop(0, 0, 1)),
            )
        )
        if j == 0:
            queries = share(
                project(where, tokens, other, (w_query,), HEAD_DIM * group_heads, (0, 1))
            )
    results = [share(attend(queries, gathered[j], bias, j)) for j in range(group_heads)]
    attended = [results[j][dz] for dz in range(Z) for j in range(group_heads)]
    away = mix(where, attended, w_out, True, 512)
    arrived = lax.ppermute(away, "head", [(0, 1), (1, 0)])
    home = mix(where, attended, w_out, False, 512)
    return (home.astype(F32) + arrived.astype(F32)).astype(BF16)


def gather_all(tokens, block_order, block_mask, w_query, w_key, w_value, w_out):
    row_count = tokens.shape[0]
    local_width = w_query.shape[1]
    local_heads = local_width // HEAD_DIM
    block_count = block_order.shape[0]
    portion = lax.all_gather(tokens, "head", axis=1, tiled=True)
    query_rows, key_rows, value_rows = [
        jnp.dot(portion, weight, preferred_element_type=F32)
        .astype(BF16)
        .reshape(row_count, local_heads, HEAD_DIM)
        for weight in (w_query, w_key, w_value)
    ]
    cycle_live = block_mask[block_order][:, block_order]
    row_blocks = (
        lax.axis_index("ctx") * row_count + jnp.arange(row_count, dtype=jnp.int32)
    ) // BLOCK
    live_columns = cycle_live[row_blocks].T
    inv_root = 1.0 / HEAD_DIM**0.5

    def advance(state, inputs):
        key_tile, value_tile, offset = inputs
        keep = lax.dynamic_index_in_dim(live_columns, offset, 0, keepdims=False) > 0
        top_now, total_now, accum = state
        scores = (
            jnp.einsum("qhd,khd->hqk", query_rows, key_tile, preferred_element_type=F32)
            * inv_root
        )
        allowed = keep[None, :, None]
        top_next = jnp.maximum(top_now, jnp.max(jnp.where(allowed, scores, -1e30), axis=-1))
        factor = jnp.exp(top_now - top_next)
        weights = jnp.where(allowed, jnp.exp(scores - top_next[..., None]), 0.0)
        total_next = total_now * factor + jnp.sum(weights, axis=-1)
        accum = accum * factor[..., None] + jnp.einsum(
            "hqk,khd->hqd", weights.astype(BF16), value_tile, preferred_element_type=F32
        )
        return (top_next, total_next, accum), None

    initial = (
        jnp.full((local_heads, row_count), -1e30, F32),
        jnp.zeros((local_heads, row_count), F32),
        jnp.zeros((local_heads, row_count, HEAD_DIM), F32),
    )
    tiles = [
        lax.all_gather(part, "ctx", axis=0, tiled=True).reshape(
            block_count, BLOCK, local_heads, HEAD_DIM
        )
        for part in (key_rows, value_rows)
    ]
    (_, total, accum), _ = lax.scan(
        advance, initial, (*tiles, jnp.arange(block_count, dtype=jnp.int32))
    )
    attended = (
        (accum / total[..., None]).transpose(1, 0, 2).reshape(row_count, local_width).astype(BF16)
    )
    partial_out = jnp.dot(attended, w_out, preferred_element_type=F32)
    return lax.psum_scatter(partial_out.astype(BF16), "head", scatter_dimension=1, tiled=True)


def solution(mesh):
    in_specs = (
        P("ctx", "head"),
        P(),
        P(),
        P(None, "head"),
        P(None, "head"),
        P(None, "head"),
        P("head", None),
    )

    def per_device(tokens, block_order, block_mask, w_query, w_key, w_value, w_out):
        args = (tokens, block_order, block_mask, w_query, w_key, w_value, w_out)
        heads = w_query.shape[1] // HEAD_DIM
        fits = mesh.shape["ctx"] == Z * X * C and mesh.shape["head"] == 2 and heads % Z == 0
        return split_heads(*args) if fits else gather_all(*args)

    return jax.shard_map(
        per_device, mesh=mesh, in_specs=in_specs, out_specs=P("ctx", "head"), check_vma=False
    )
```

time: 522 us -> 173 us (0.33)
  waiting for transfers between devices: 232 us -> 61.9 us
  matrix products: 141 us -> 0.6 us
  loops' own time: 64.2 us -> 0 us
  Pallas kernels: 0 us -> 52.7 us
  local copies, waits for them, and re-layouts: 56.1 us -> 13.6 us
  starting transfers between devices: 0.12 us -> 42.4 us
  between operations: 13.3 us -> 0.3 us
  other arithmetic: 10.8 us -> 1.57 us
    all_gather x3 -> x0, waiting for transfers between devices: 207 us -> none  [the longest x1 87.7 us: per_device(): value_part = lax.all_gather(value_rows, 'ctx', axis=0, tiled=True)]
    dot_general x71 -> x2, matrix products: 141 us -> 0.6 us  [the longest x1 0.3 us: split_heads(): jnp.dot(jnp.dot(pick(query_blocks), block_mask.astype(F32)), pick(key_blo...]
    another operation x1 -> x0, loops' own time: 64.2 us -> none  [per_device(): lax.scan(advance, carry, (key_tiles, value_tiles, jnp.arange(tile_count,...]
    ppermute x0 -> x32, waiting for transfers between devices: none -> 61.9 us  [the longest x21 24.3 us: share(): lax.ppermute(pieces[dz], 'ctx', hop(dz, 0, 0))]
    pallas_call x0 -> x9, Pallas kernels: none -> 52.7 us  [the longest x3 27.9 us: attend(): pl.pallas_call(body, grid=(Z,), in_specs=[pl.BlockSpec((1, rows, HEAD_DIM...]
    ppermute x0 -> x32, starting transfers between devices: none -> 42.4 us  [the longest x21 32.1 us: share(): lax.ppermute(pieces[dz], 'ctx', hop(dz, 0, 0))]
    all_gather x2 -> x0, local copies, waits for them, and re-layouts: 33.4 us -> none  [the longest x1 16.7 us: per_device(): value_part = lax.all_gather(value_rows, 'ctx', axis=0, tiled=True)]
    reduce_scatter x1 -> x0, waiting for transfers between devices: 24.4 us -> none  [per_device(): lax.psum_scatter(partial_out.astype(jnp.bfloat16), 'head', scatter_dimens...]
  transfers between devices with their start and end apart: 4 -> 32, of which waited for: 4 -> 11; matrix products, arithmetic and copies ran while one was open for 6% -> 1% of each run, Pallas kernels for 0% -> 26%
where the time goes in v1:
time: 173 us
  waiting for transfers between devices  61.9 us (36%)
  Pallas kernels  52.7 us (30%)
  starting transfers between devices  42.4 us (25%)
  local copies, waits for them, and re-layouts  13.6 us (8%)
    ppermute x21, starting transfers between devices, share(): lax.ppermute(pieces[dz], 'ctx', hop(dz, 0, 0))  32.1 us
    pallas_call x3, Pallas kernels, attend(): pl.pallas_call(body, grid=(Z,), in_specs=[pl.BlockSpec((1, rows, HEAD_DIM...  27.9 us
    ppermute x21, waiting for transfers between devices, share(): lax.ppermute(pieces[dz], 'ctx', hop(dz, 0, 0))  24.3 us
    pallas_call x4, Pallas kernels, project(): pl.pallas_call(body, grid_spec=pltpu.PrefetchScalarGridSpec(num_scalar_pr...  19.2 us
    ppermute x1, waiting for transfers between devices, split_heads(): other = lax.ppermute(tokens, 'head', [(0, 1), (1, 0)])  17.4 us
    unnamed x38, local copies, waits for them, and re-layouts  13.1 us
    ppermute x1, waiting for transfers between devices, split_heads(): arrived = lax.ppermute(away, 'head', [(0, 1), (1, 0)])  13 us
    ppermute x3, waiting for transfers between devices, split_heads(): across = lax.ppermute(part, 'ctx', hop(0, 1, 0))  7.13 us
  transfers between devices with their start and end apart: 32, of which 11 were waited for; matrix products, arithmetic and copies ran while one was open for 1% of the time, Pallas kernels for 26%

profile of v1, /device:TPU:0, one launch (start us, length us, event | category | flops | bytes accessed | tf_op | source)
XLA Modules:
  0.0 173.0 jit_solution(2550650249902306264)
XLA Ops:
  0.0 3.0 %collective-permute-start = (bf16[256,1536]{1,0:T(8,128)(2,1)}, bf16[256,1536]{1,0:T(8,128)(2,1)S(1)}, u32[]{:S(2)}, u32[]{:S(2)}) collective-permute-start(bf16[256,1536]{1,0:T(8,128)(2,1)} %own_ref.7), channel_id=1, source_target_pairs={{0,1},{1,0},{2,3},{3,2},{4,5},{5,4},{6,7},{7,6},{8,9},{9,8},{10,11... | collective-permute-start | bytes 2359304 | tf_op jit(solution)/shard_map/ppermute | solution.py:195
  3.3 17.4 %collective-permute-done.other_ref = bf16[256,1536]{1,0:T(8,128)(2,1)S(1)} collective-permute-done((bf16[256,1536]{1,0:T(8,128)(2,1)}, bf16[256,1536]{1,0:T(8,128)(2,1)S(1)}, u32[]{:S(2)}, u32[]{:S(2)}) %collective-permute-start) | collective-permute-done | bytes 786464 | tf_op jit(solution)/shard_map/ppermute | solution.py:195
  20.7 3.7 %copy-done = bf16[3072,1536]{1,0:T(8,128)(2,1)S(1)} copy-done((bf16[3072,1536]{1,0:T(8,128)(2,1)S(1)}, bf16[3072,1536]{1,0:T(8,128)(2,1)}, u32[]{:S(2)}) %copy-start) | copy-done | bytes 9437208
  24.4 3.7 %copy-done.1 = bf16[3072,1536]{1,0:T(8,128)(2,1)S(1)} copy-done((bf16[3072,1536]{1,0:T(8,128)(2,1)S(1)}, bf16[3072,1536]{1,0:T(8,128)(2,1)}, u32[]{:S(2)}) %copy-start.1) | copy-done | bytes 9437208
  28.1 1.1 copy-done.3
  29.2 4.3 %shard_map.76 = (bf16[2,256,128]{2,1,0:T(8,128)(2,1)S(1)}, bf16[2,256,128]{2,1,0:T(8,128)(2,1)S(1)}, bf16[2,256,128]{2,1,0:T(8,128)(2,1)S(1)}, bf16[2,256,128]{2,1,0:T(8,128)(2,1)S(1)}) custom-call(s32[2]{0:T(128)S(1)} %pad_add_fusion.s, bf16[256,1536]{1,0:T(8,128)(2,1)S(1)} %copy-done.3, bf16[256,1536]{1,0:T(8,128)(2,1)S(1)} %collective-permute-done.other_ref, ...), custom_call_target="tpu_custom_call" | custom-call | flops 1610612736 | bytes 6291456 | tf_op jit(solution)/shard_map/pallas_call | solution.py:61
  33.5 1.9 %collective-permute-start.10 = (bf16[2,256,128]{2,1,0:T(8,128)(2,1)S(1)}, bf16[2,256,128]{2,1,0:T(8,128)(2,1)S(1)}, u32[]{:S(2)}, u32[]{:S(2)}) collective-permute-start(bf16[2,256,128]{2,1,0:T(8,128)(2,1)S(1)} %get-tuple-element.43), channel_id=1, source_target_pairs={{0,8},{2,10},{4,12},{6,14},{8,0},{10,2},{12,4},{14,6},{16,24},{18,... | collective-permute-start | bytes 393224 | tf_op jit(solution)/shard_map/ppermute | solution.py:216
  35.4 2.6 %collective-permute-start.11 = (bf16[2,256,128]{2,1,0:T(8,128)(2,1)S(1)}, bf16[2,256,128]{2,1,0:T(8,128)(2,1)S(1)}, u32[]{:S(2)}, u32[]{:S(2)}) collective-permute-start(bf16[2,256,128]{2,1,0:T(8,128)(2,1)S(1)} %get-tuple-element.44), channel_id=1, source_target_pairs={{0,16},{2,18},{4,20},{6,22},{8,24},{10,26},{12,28},{14,30},{16,0},... | collective-permute-start | bytes 393224 | tf_op jit(solution)/shard_map/ppermute | solution.py:216
  38.0 4.3 %shard_map.74 = (bf16[2,256,128]{2,1,0:T(8,128)(2,1)S(1)}, bf16[2,256,128]{2,1,0:T(8,128)(2,1)S(1)}, bf16[2,256,128]{2,1,0:T(8,128)(2,1)S(1)}, bf16[2,256,128]{2,1,0:T(8,128)(2,1)S(1)}) custom-call(s32[2]{0:T(128)S(1)} %pad_add_fusion.s, bf16[256,1536]{1,0:T(8,128)(2,1)S(1)} %copy-done.3, bf16[256,1536]{1,0:T(8,128)(2,1)S(1)} %collective-permute-done.other_ref, ...), custom_call_target="tpu_custom_call" | custom-call | flops 1610612736 | bytes 6291456 | tf_op jit(solution)/shard_map/pallas_call | solution.py:61
  42.2 1.0 collective-permute-start.4
  43.2 3.5 %collective-permute-start.5 = (bf16[2,256,128]{2,1,0:T(8,128)(2,1)S(1)}, bf16[2,256,128]{2,1,0:T(8,128)(2,1)S(1)}, u32[]{:S(2)}, u32[]{:S(2)}) collective-permute-start(bf16[2,256,128]{2,1,0:T(8,128)(2,1)S(1)} %get-tuple-element.39), channel_id=1, source_target_pairs={{0,16},{2,18},{4,20},{6,22},{8,24},{10,26},{12,28},{14,30},{16,0},... | collective-permute-start | bytes 393224 | tf_op jit(solution)/shard_map/ppermute | solution.py:216
  46.8 3.7 %copy-done.2 = bf16[3072,1536]{1,0:T(8,128)(2,1)S(1)} copy-done((bf16[3072,1536]{1,0:T(8,128)(2,1)S(1)}, bf16[3072,1536]{1,0:T(8,128)(2,1)}, u32[]{:S(2)}) %copy-start.2) | copy-done | bytes 9437208
  50.5 6.3 %shard_map.73 = (bf16[1,256,384]{2,1,0:T(8,128)(2,1)S(1)}, bf16[1,256,384]{2,1,0:T(8,128)(2,1)}, bf16[1,256,384]{2,1,0:T(8,128)(2,1)S(1)}, bf16[1,256,384]{2,1,0:T(8,128)(2,1)S(1)}) custom-call(s32[2]{0:T(128)S(1)} %pad_add_fusion.s, bf16[256,1536]{1,0:T(8,128)(2,1)S(1)} %copy-done.3, bf16[256,1536]{1,0:T(8,128)(2,1)S(1)} %collective-permute-done.other_ref, ...), custom_call_target="tpu_custom_call" | custom-call | flops 2415919104 | bytes 9437184 | tf_op jit(solution)/shard_map/pallas_call | solution.py:61
  56.8 0.4 collective-permute-start.6
  57.2 4.3 %shard_map.78 = (bf16[2,256,128]{2,1,0:T(8,128)(2,1)S(1)}, bf16[2,256,128]{2,1,0:T(8,128)(2,1)S(1)}, bf16[2,256,128]{2,1,0:T(8,128)(2,1)S(1)}, bf16[2,256,128]{2,1,0:T(8,128)(2,1)S(1)}) custom-call(s32[2]{0:T(128)S(1)} %pad_add_fusion.s, bf16[256,1536]{1,0:T(8,128)(2,1)S(1)} %copy-done.3, bf16[256,1536]{1,0:T(8,128)(2,1)S(1)} %collective-permute-done.other_ref, ...), custom_call_target="tpu_custom_call" | custom-call | flops 1610612736 | bytes 6291456 | tf_op jit(solution)/shard_map/pallas_call | solution.py:61
  61.6 0.5 collective-permute-start.16
  62.1 3.7 %collective-permute-start.17 = (bf16[2,256,128]{2,1,0:T(8,128)(2,1)S(1)}, bf16[2,256,128]{2,1,0:T(8,128)(2,1)S(1)}, u32[]{:S(2)}, u32[]{:S(2)}) collective-permute-start(bf16[2,256,128]{2,1,0:T(8,128)(2,1)S(1)} %get-tuple-element.49), channel_id=1, source_target_pairs={{0,16},{2,18},{4,20},{6,22},{8,24},{10,26},{12,28},{14,30},{16,0},... | collective-permute-start | bytes 393224 | tf_op jit(solution)/shard_map/ppermute | solution.py:216
  66.1 0.4 collective-permute-start.1
  66.6 3.6 %collective-permute-done.16 = bf16[2,256,128]{2,1,0:T(8,128)(2,1)S(1)} collective-permute-done((bf16[2,256,128]{2,1,0:T(8,128)(2,1)S(1)}, bf16[2,256,128]{2,1,0:T(8,128)(2,1)S(1)}, u32[]{:S(2)}, u32[]{:S(2)}) %collective-permute-start.16) | collective-permute-done | bytes 131104 | tf_op jit(solution)/shard_map/ppermute | solution.py:216
  70.1 1.9 %collective-permute-start.7 = (bf16[4,2,256,128]{3,2,1,0:T(8,128)(2,1)S(1)}, bf16[4,2,256,128]{3,2,1,0:T(8,128)(2,1)}, u32[]{:S(2)}, u32[]{:S(2)}) collective-permute-start(bf16[4,2,256,128]{3,2,1,0:T(8,128)(2,1)S(1)} %pad_maximum_fusion.refs_4_), channel_id=1, source_target_pairs={{0,4},{2,6},{4,0},{6,2},{8,12},{10,14},{12,8},{14,10},{16,20},{18,... | collective-permute-start | bytes 1572872 | tf_op jit(solution)/shard_map/ppermute | solution.py:225
  72.3 1.5 collective-permute-start.13
  73.7 0.7 collective-permute-done.18
  74.6 1.6 collective-permute-start.19
  76.4 2.0 %collective-permute-start.2 = (bf16[1,256,384]{2,1,0:T(8,128)(2,1)}, bf16[1,256,384]{2,1,0:T(8,128)(2,1)}, u32[]{:S(2)}, u32[]{:S(2)}) collective-permute-start(bf16[1,256,384]{2,1,0:T(8,128)(2,1)} %copy-done.7), channel_id=1, source_target_pairs={{0,16},{2,18},{4,20},{6,22},{8,24},{10,26},{12,28},{14,30},{16,0},... | collective-permute-start | bytes 589832 | tf_op jit(solution)/shard_map/ppermute | solution.py:216
  78.7 8.3 %collective-permute-done.2.refs_2_ = bf16[1,256,384]{2,1,0:T(8,128)(2,1)} collective-permute-done((bf16[1,256,384]{2,1,0:T(8,128)(2,1)}, bf16[1,256,384]{2,1,0:T(8,128)(2,1)}, u32[]{:S(2)}, u32[]{:S(2)}) %collective-permute-start.2) | collective-permute-done | bytes 196640 | tf_op jit(solution)/shard_map/ppermute | solution.py:216
  87.0 1.6 collective-permute-start.3
  89.0 6.5 %collective-permute-done.3.refs_3_ = bf16[1,256,384]{2,1,0:T(8,128)(2,1)} collective-permute-done((bf16[1,256,384]{2,1,0:T(8,128)(2,1)}, bf16[1,256,384]{2,1,0:T(8,128)(2,1)}, u32[]{:S(2)}, u32[]{:S(2)}) %collective-permute-start.3) | collective-permute-done | bytes 196640 | tf_op jit(solution)/shard_map/ppermute | solution.py:216
  95.5 0.5 collective-permute-start.20
  96.5 7.0 %collective-permute-done.19.refs_5_ = bf16[4,2,256,128]{3,2,1,0:T(8,128)(2,1)S(1)} collective-permute-done((bf16[4,2,256,128]{3,2,1,0:T(8,128)(2,1)S(1)}, bf16[4,2,256,128]{3,2,1,0:T(8,128)(2,1)S(1)}, u32[]{:S(2)}, u32[]{:S(2)}) %collective-permute-start.19) | collective-permute-done | bytes 524320 | tf_op jit(solution)/shard_map/ppermute | solution.py:225
  103.6 0.9 copy-done.5
  104.5 9.5 %shard_map.75 = (bf16[256,128]{1,0:T(8,128)(2,1)S(1)}, bf16[256,128]{1,0:T(8,128)(2,1)S(1)}, bf16[256,128]{1,0:T(8,128)(2,1)S(1)}, bf16[256,128]{1,0:T(8,128)(2,1)S(1)}) custom-call(bf16[1,256,384]{2,1,0:T(8,128)(2,1)S(1)} %copy-done.5, bf16[1,256,384]{2,1,0:T(8,128)(2,1)S(1)} %collective-permute-done.1.refs_1_, ...), custom_call_target="tpu_custom_call" | custom-call | flops 2147483648 | bytes 2097152 | tf_op jit(solution)/shard_map/pallas_call | solution.py:130
  114.0 1.9 %collective-permute-start.22 = (bf16[256,128]{1,0:T(8,128)(2,1)S(1)}, bf16[256,128]{1,0:T(8,128)(2,1)S(1)}, u32[]{:S(2)}, u32[]{:S(2)}) collective-permute-start(bf16[256,128]{1,0:T(8,128)(2,1)S(1)} %get-tuple-element.52), channel_id=1, source_target_pairs={{0,8},{2,10},{4,12},{6,14},{8,0},{10,2},{12,4},{14,6},{16,24},{18,... | collective-permute-start | bytes 196616 | tf_op jit(solution)/shard_map/ppermute | solution.py:216
  115.9 2.1 %collective-permute-start.25 = (bf16[256,128]{1,0:T(8,128)(2,1)S(1)}, bf16[256,128]{1,0:T(8,128)(2,1)S(1)}, u32[]{:S(2)}, u32[]{:S(2)}) collective-permute-start(bf16[256,128]{1,0:T(8,128)(2,1)S(1)} %get-tuple-element.55), channel_id=1, source_target_pairs={{0,16},{2,18},{4,20},{6,22},{8,24},{10,26},{12,28},{14,30},{16,0},... | collective-permute-start | bytes 196616 | tf_op jit(solution)/shard_map/ppermute | solution.py:216
  117.9 1.5 collective-permute-start.28
  119.4 9.2 %shard_map.77 = (bf16[256,128]{1,0:T(8,128)(2,1)S(1)}, bf16[256,128]{1,0:T(8,128)(2,1)S(1)}, bf16[256,128]{1,0:T(8,128)(2,1)S(1)}, bf16[256,128]{1,0:T(8,128)(2,1)S(1)}) custom-call(bf16[1,256,384]{2,1,0:T(8,128)(2,1)S(1)} %copy-done.5, bf16[1,256,384]{2,1,0:T(8,128)(2,1)S(1)} %collective-permute-done.1.refs_1_, ...), custom_call_target="tpu_custom_call" | custom-call | flops 2147483648 | bytes 2097152 | tf_op jit(solution)/shard_map/pallas_call | solution.py:130
  128.6 0.7 collective-permute-start.23
  129.3 2.3 %collective-permute-start.26 = (bf16[256,128]{1,0:T(8,128)(2,1)S(1)}, bf16[256,128]{1,0:T(8,128)(2,1)S(1)}, u32[]{:S(2)}, u32[]{:S(2)}) collective-permute-start(bf16[256,128]{1,0:T(8,128)(2,1)S(1)} %get-tuple-element.56), channel_id=1, source_target_pairs={{0,16},{2,18},{4,20},{6,22},{8,24},{10,26},{12,28},{14,30},{16,0},... | collective-permute-start | bytes 196616 | tf_op jit(solution)/shard_map/ppermute | solution.py:216
  131.6 9.2 %shard_map.79 = (bf16[256,128]{1,0:T(8,128)(2,1)S(1)}, bf16[256,128]{1,0:T(8,128)(2,1)S(1)}, bf16[256,128]{1,0:T(8,128)(2,1)S(1)}, bf16[256,128]{1,0:T(8,128)(2,1)S(1)}) custom-call(bf16[1,256,384]{2,1,0:T(8,128)(2,1)S(1)} %copy-done.5, bf16[1,256,384]{2,1,0:T(8,128)(2,1)S(1)} %collective-permute-done.1.refs_1_, ...), custom_call_target="tpu_custom_call" | custom-call | flops 2147483648 | bytes 2097152 | tf_op jit(solution)/shard_map/pallas_call | solution.py:130
  140.8 1.5 collective-permute-start.29
  142.3 2.9 %collective-permute-start.27 = (bf16[256,128]{1,0:T(8,128)(2,1)S(1)}, bf16[256,128]{1,0:T(8,128)(2,1)S(1)}, u32[]{:S(2)}, u32[]{:S(2)}) collective-permute-start(bf16[256,128]{1,0:T(8,128)(2,1)S(1)} %get-tuple-element.57), channel_id=1, source_target_pairs={{0,16},{2,18},{4,20},{6,22},{8,24},{10,26},{12,28},{14,30},{16,0},... | collective-permute-start | bytes 196616 | tf_op jit(solution)/shard_map/ppermute | solution.py:216
  145.3 1.4 collective-permute-start.30
  146.7 1.0 collective-permute-done.29.refs_10_
  147.7 4.0 %collective-permute-done.27.refs_8_ = bf16[256,128]{1,0:T(8,128)(2,1)S(1)} collective-permute-done((bf16[256,128]{1,0:T(8,128)(2,1)S(1)}, bf16[256,128]{1,0:T(8,128)(2,1)S(1)}, u32[]{:S(2)}, u32[]{:S(2)}) %collective-permute-start.27) | collective-permute-done | bytes 65568 | tf_op jit(solution)/shard_map/ppermute | solution.py:216
  151.7 2.8 %shard_map.81 = bf16[256,1536]{1,0:T(8,128)(2,1)S(1)} custom-call(s32[2]{0:T(128)S(1)} %pad_add_fusion.s, bf16[256,128]{1,0:T(8,128)(2,1)S(1)} %get-tuple-element.41.refs_0_, bf16[256,128]{1,0:T(8,128)(2,1)S(1)} %get-tuple-element.46.refs_1_, bf16[256,128]{1,0:T(8,128)(2,1)S(1)} %get-tuple-element.51.refs_2_, ...), custom_call_target="tpu_custom_call" | custom-call | flops 1207959552 | bytes 4718592 | tf_op jit(solution)/shard_map/pallas_call | solution.py:166
  154.5 1.6 collective-permute-start.31
  156.1 2.8 %shard_map.80 = bf16[256,1536]{1,0:T(8,128)(2,1)S(1)} custom-call(s32[2]{0:T(128)S(1)} %pad_add_fusion.s, bf16[256,128]{1,0:T(8,128)(2,1)S(1)} %get-tuple-element.41.refs_0_, bf16[256,128]{1,0:T(8,128)(2,1)S(1)} %get-tuple-element.46.refs_1_, bf16[256,128]{1,0:T(8,128)(2,1)S(1)} %get-tuple-element.51.refs_2_, ...), custom_call_target="tpu_custom_call" | custom-call | flops 1207959552 | bytes 4718592 | tf_op jit(solution)/shard_map/pallas_call | solution.py:166
  158.9 13.0 %collective-permute-done.31 = bf16[256,1536]{1,0:T(8,128)(2,1)S(1)} collective-permute-done((bf16[256,1536]{1,0:T(8,128)(2,1)S(1)}, bf16[256,1536]{1,0:T(8,128)(2,1)S(1)}, u32[]{:S(2)}, u32[]{:S(2)}) %collective-permute-start.31) | collective-permute-done | bytes 786464 | tf_op jit(solution)/shard_map/ppermute | solution.py:241
  172.0 1.1 add_convert_fusion
  (82 shorter events, 2.7 us)
Async XLA Ops:
  0.0 20.7 %collective-permute-start = (bf16[256,1536]{1,0:T(8,128)(2,1)}, bf16[256,1536]{1,0:T(8,128)(2,1)S(1)}, u32[]{:S(2)}, u32[]{:S(2)}) collective-permute-start(bf16[256,1536]{1,0:T(8,128)(2,1)} %own_ref.7), channel_id=1, source_target_pairs={{0,1},{1,0},{2,3},{3,2},{4,5},{5,4},{6,7},{7,6},{8,9},{9,8},{10,11... | collective-permute-start | bytes 2359304 | tf_op jit(solution)/shard_map/ppermute | solution.py:195
  20.7 3.7 %copy-start = (bf16[3072,1536]{1,0:T(8,128)(2,1)S(1)}, bf16[3072,1536]{1,0:T(8,128)(2,1)}, u32[]{:S(2)}) copy-start(bf16[3072,1536]{1,0:T(8,128)(2,1)} %refs_2_.5) | copy-start | bytes 28311556
  24.4 3.7 %copy-start.1 = (bf16[3072,1536]{1,0:T(8,128)(2,1)S(1)}, bf16[3072,1536]{1,0:T(8,128)(2,1)}, u32[]{:S(2)}) copy-start(bf16[3072,1536]{1,0:T(8,128)(2,1)} %refs_3_.5) | copy-start | bytes 28311556
  33.5 23.3 %collective-permute-start.10 = (bf16[2,256,128]{2,1,0:T(8,128)(2,1)S(1)}, bf16[2,256,128]{2,1,0:T(8,128)(2,1)S(1)}, u32[]{:S(2)}, u32[]{:S(2)}) collective-permute-start(bf16[2,256,128]{2,1,0:T(8,128)(2,1)S(1)} %get-tuple-element.43), channel_id=1, source_target_pairs={{0,8},{2,10},{4,12},{6,14},{8,0},{10,2},{12,4},{14,6},{16,24},{18,... | collective-permute-start | bytes 393224 | tf_op jit(solution)/shard_map/ppermute | solution.py:216
  35.4 30.7 %collective-permute-start.11 = (bf16[2,256,128]{2,1,0:T(8,128)(2,1)S(1)}, bf16[2,256,128]{2,1,0:T(8,128)(2,1)S(1)}, u32[]{:S(2)}, u32[]{:S(2)}) collective-permute-start(bf16[2,256,128]{2,1,0:T(8,128)(2,1)S(1)} %get-tuple-element.44), channel_id=1, source_target_pairs={{0,16},{2,18},{4,20},{6,22},{8,24},{10,26},{12,28},{14,30},{16,0},... | collective-permute-start | bytes 393224 | tf_op jit(solution)/shard_map/ppermute | solution.py:216
  37.9 28.6 %collective-permute-start.12 = (bf16[2,256,128]{2,1,0:T(8,128)(2,1)S(1)}, bf16[2,256,128]{2,1,0:T(8,128)(2,1)S(1)}, u32[]{:S(2)}, u32[]{:S(2)}) collective-permute-start(bf16[2,256,128]{2,1,0:T(8,128)(2,1)S(1)} %get-tuple-element.45), channel_id=1, source_target_pairs={{0,24},{2,26},{4,28},{6,30},{8,16},{10,18},{12,20},{14,22},{16,8},... | collective-permute-start | bytes 393224 | tf_op jit(solution)/shard_map/ppermute | solution.py:216
  38.0 19.2 %slice-start.6 = ((s8[9437184]{0:T(1024)(128)(4,1)}), s8[4194304]{0:T(1024)(128)(4,1)S(1)}, s32[]{:S(2)}) async-start(s8[9437184]{0:T(1024)(128)(4,1)} %bitcast.37), calls=%async_computation.6 | async-start | bytes 8388608
  38.0 19.2 %slice-start.7 = ((s8[9437184]{0:T(1024)(128)(4,1)}), s8[4194304]{0:T(1024)(128)(4,1)S(1)}, s32[]{:S(2)}) async-start(s8[9437184]{0:T(1024)(128)(4,1)} %bitcast.37), calls=%async_computation.7 | async-start | bytes 8388608
  42.2 19.3 %collective-permute-start.4 = (bf16[2,256,128]{2,1,0:T(8,128)(2,1)S(1)}, bf16[2,256,128]{2,1,0:T(8,128)(2,1)S(1)}, u32[]{:S(2)}, u32[]{:S(2)}) collective-permute-start(bf16[2,256,128]{2,1,0:T(8,128)(2,1)S(1)} %get-tuple-element.38), channel_id=1, source_target_pairs={{0,8},{2,10},{4,12},{6,14},{8,0},{10,2},{12,4},{14,6},{16,24},{18,... | collective-permute-start | bytes 393224 | tf_op jit(solution)/shard_map/ppermute | solution.py:216
  43.2 14.0 %slice-start.3 = ((s8[9437184]{0:T(1024)(128)(4,1)}), s8[4194304]{0:T(1024)(128)(4,1)S(1)}, s32[]{:S(2)}) async-start(s8[9437184]{0:T(1024)(128)(4,1)} %bitcast.35), calls=%async_computation.3 | async-start | bytes 8388608
  43.2 14.0 %slice-start.4 = ((s8[9437184]{0:T(1024)(128)(4,1)}), s8[4194304]{0:T(1024)(128)(4,1)S(1)}, s32[]{:S(2)}) async-start(s8[9437184]{0:T(1024)(128)(4,1)} %bitcast.35), calls=%async_computation.4 | async-start | bytes 8388608
  43.2 14.0 %slice-start.5 = ((s8[9437184]{0:T(1024)(128)(4,1)}), s8[1048576]{0:T(1024)(128)(4,1)S(1)}, s32[]{:S(2)}) async-start(s8[9437184]{0:T(1024)(128)(4,1)} %bitcast.35), calls=%async_computation.5 | async-start | bytes 2097152
  43.2 14.0 %slice-start.8 = ((s8[9437184]{0:T(1024)(128)(4,1)}), s8[1048576]{0:T(1024)(128)(4,1)S(1)}, s32[]{:S(2)}) async-start(s8[9437184]{0:T(1024)(128)(4,1)} %bitcast.37), calls=%async_computation.8 | async-start | bytes 2097152
  43.2 18.8 %collective-permute-start.5 = (bf16[2,256,128]{2,1,0:T(8,128)(2,1)S(1)}, bf16[2,256,128]{2,1,0:T(8,128)(2,1)S(1)}, u32[]{:S(2)}, u32[]{:S(2)}) collective-permute-start(bf16[2,256,128]{2,1,0:T(8,128)(2,1)S(1)} %get-tuple-element.39), channel_id=1, source_target_pairs={{0,16},{2,18},{4,20},{6,22},{8,24},{10,26},{12,28},{14,30},{16,0},... | collective-permute-start | bytes 393224 | tf_op jit(solution)/shard_map/ppermute | solution.py:216
  56.8 4.7 %copy-start.4 = (bf16[1,256,384]{2,1,0:T(8,128)(2,1)}, bf16[1,256,384]{2,1,0:T(8,128)(2,1)S(1)}, u32[]{:S(2)}) copy-start(bf16[1,256,384]{2,1,0:T(8,128)(2,1)S(1)} %get-tuple-element.33.refs_0_) | copy-start | bytes 589828
  56.8 4.7 %copy-start.6 = (bf16[1,256,384]{2,1,0:T(8,128)(2,1)}, bf16[1,256,384]{2,1,0:T(8,128)(2,1)S(1)}, u32[]{:S(2)}) copy-start(bf16[1,256,384]{2,1,0:T(8,128)(2,1)S(1)} %get-tuple-element.36) | copy-start | bytes 589828
  56.8 4.8 %copy-start.7 = (bf16[1,256,384]{2,1,0:T(8,128)(2,1)}, bf16[1,256,384]{2,1,0:T(8,128)(2,1)S(1)}, u32[]{:S(2)}) copy-start(bf16[1,256,384]{2,1,0:T(8,128)(2,1)S(1)} %get-tuple-element.35) | copy-start | bytes 589828
  56.8 21.6 %copy-start.8 = (s32[32,32]{1,0:T(8,128)S(1)}, s32[32,32]{1,0:T(8,128)}, u32[]{:S(2)}) copy-start(s32[32,32]{1,0:T(8,128)} %param.9) | copy-start | bytes 12292
  56.8 21.6 %copy-start.9 = (s32[32]{0:T(128)S(1)}, s32[32]{0:T(128)}, u32[]{:S(2)}) copy-start(s32[32]{0:T(128)} %param.8) | copy-start | bytes 388
  56.8 8.9 %collective-permute-start.6 = (bf16[2,256,128]{2,1,0:T(8,128)(2,1)S(1)}, bf16[2,256,128]{2,1,0:T(8,128)(2,1)S(1)}, u32[]{:S(2)}, u32[]{:S(2)}) collective-permute-start(bf16[2,256,128]{2,1,0:T(8,128)(2,1)S(1)} %get-tuple-element.40), channel_id=1, source_target_pairs={{0,24},{2,26},{4,28},{6,30},{8,16},{10,18},{12,20},{14,22},{16,8},... | collective-permute-start | bytes 393224 | tf_op jit(solution)/shard_map/ppermute | solution.py:216
  61.6 8.6 %collective-permute-start.16 = (bf16[2,256,128]{2,1,0:T(8,128)(2,1)S(1)}, bf16[2,256,128]{2,1,0:T(8,128)(2,1)S(1)}, u32[]{:S(2)}, u32[]{:S(2)}) collective-permute-start(bf16[2,256,128]{2,1,0:T(8,128)(2,1)S(1)} %get-tuple-element.48), channel_id=1, source_target_pairs={{0,8},{2,10},{4,12},{6,14},{8,0},{10,2},{12,4},{14,6},{16,24},{18,... | collective-permute-start | bytes 393224 | tf_op jit(solution)/shard_map/ppermute | solution.py:216
  62.1 10.2 %collective-permute-start.17 = (bf16[2,256,128]{2,1,0:T(8,128)(2,1)S(1)}, bf16[2,256,128]{2,1,0:T(8,128)(2,1)S(1)}, u32[]{:S(2)}, u32[]{:S(2)}) collective-permute-start(bf16[2,256,128]{2,1,0:T(8,128)(2,1)S(1)} %get-tuple-element.49), channel_id=1, source_target_pairs={{0,16},{2,18},{4,20},{6,22},{8,24},{10,26},{12,28},{14,30},{16,0},... | collective-permute-start | bytes 393224 | tf_op jit(solution)/shard_map/ppermute | solution.py:216
  65.7 8.8 %collective-permute-start.18 = (bf16[2,256,128]{2,1,0:T(8,128)(2,1)S(1)}, bf16[2,256,128]{2,1,0:T(8,128)(2,1)S(1)}, u32[]{:S(2)}, u32[]{:S(2)}) collective-permute-start(bf16[2,256,128]{2,1,0:T(8,128)(2,1)S(1)} %get-tuple-element.50), channel_id=1, source_target_pairs={{0,24},{2,26},{4,28},{6,30},{8,16},{10,18},{12,20},{14,22},{16,8},... | collective-permute-start | bytes 393224 | tf_op jit(solution)/shard_map/ppermute | solution.py:216
  66.1 10.3 %collective-permute-start.1 = (bf16[1,256,384]{2,1,0:T(8,128)(2,1)}, bf16[1,256,384]{2,1,0:T(8,128)(2,1)S(1)}, u32[]{:S(2)}, u32[]{:S(2)}) collective-permute-start(bf16[1,256,384]{2,1,0:T(8,128)(2,1)} %get-tuple-element.34), channel_id=1, source_target_pairs={{0,8},{2,10},{4,12},{6,14},{8,0},{10,2},{12,4},{14,6},{16,24},{18,... | collective-permute-start | bytes 589832 | tf_op jit(solution)/shard_map/ppermute | solution.py:216
  66.5 29.0 %collective-permute-start.8 = (bf16[4,2,256,128]{3,2,1,0:T(8,128)(2,1)S(1)}, bf16[4,2,256,128]{3,2,1,0:T(8,128)(2,1)S(1)}, u32[]{:S(2)}, u32[]{:S(2)}) collective-permute-start(bf16[4,2,256,128]{3,2,1,0:T(8,128)(2,1)S(1)} %pad_maximum_fusion.refs_4_), channel_id=1, source_target_pairs={{0,2},{2,0},{4,6},{6,4},{8,10},{10,8},{12,14},{14,12},{16,18},{18,... | collective-permute-start | bytes 1572872 | tf_op jit(solution)/shard_map/ppermute | solution.py:230
  70.1 25.9 %collective-permute-start.7 = (bf16[4,2,256,128]{3,2,1,0:T(8,128)(2,1)S(1)}, bf16[4,2,256,128]{3,2,1,0:T(8,128)(2,1)}, u32[]{:S(2)}, u32[]{:S(2)}) collective-permute-start(bf16[4,2,256,128]{3,2,1,0:T(8,128)(2,1)S(1)} %pad_maximum_fusion.refs_4_), channel_id=1, source_target_pairs={{0,4},{2,6},{4,0},{6,2},{8,12},{10,14},{12,8},{14,10},{16,20},{18,... | collective-permute-start | bytes 1572872 | tf_op jit(solution)/shard_map/ppermute | solution.py:225
  72.3 24.0 %collective-permute-start.13 = (bf16[4,2,256,128]{3,2,1,0:T(8,128)(2,1)S(1)}, bf16[4,2,256,128]{3,2,1,0:T(8,128)(2,1)S(1)}, u32[]{:S(2)}, u32[]{:S(2)}) collective-permute-start(bf16[4,2,256,128]{3,2,1,0:T(8,128)(2,1)S(1)} %pad_maximum_fusion.1.refs_4_), channel_id=1, source_target_pairs={{0,4},{2,6},{4,0},{6,2},{8,12},{10,14},{12,8},{14,10},{16,20},{18,... | collective-permute-start | bytes 1572872 | tf_op jit(solution)/shard_map/ppermute | solution.py:225
  74.6 28.9 %collective-permute-start.19 = (bf16[4,2,256,128]{3,2,1,0:T(8,128)(2,1)S(1)}, bf16[4,2,256,128]{3,2,1,0:T(8,128)(2,1)S(1)}, u32[]{:S(2)}, u32[]{:S(2)}) collective-permute-start(bf16[4,2,256,128]{3,2,1,0:T(8,128)(2,1)S(1)} %pad_maximum_fusion.2.refs_4_), channel_id=1, source_target_pairs={{0,4},{2,6},{4,0},{6,2},{8,12},{10,14},{12,8},{14,10},{16,20},{18,... | collective-permute-start | bytes 1572872 | tf_op jit(solution)/shard_map/ppermute | solution.py:225
  76.4 10.6 %collective-permute-start.2 = (bf16[1,256,384]{2,1,0:T(8,128)(2,1)}, bf16[1,256,384]{2,1,0:T(8,128)(2,1)}, u32[]{:S(2)}, u32[]{:S(2)}) collective-permute-start(bf16[1,256,384]{2,1,0:T(8,128)(2,1)} %copy-done.7), channel_id=1, source_target_pairs={{0,16},{2,18},{4,20},{6,22},{8,24},{10,26},{12,28},{14,30},{16,0},... | collective-permute-start | bytes 589832 | tf_op jit(solution)/shard_map/ppermute | solution.py:216
  87.0 8.5 %collective-permute-start.3 = (bf16[1,256,384]{2,1,0:T(8,128)(2,1)}, bf16[1,256,384]{2,1,0:T(8,128)(2,1)}, u32[]{:S(2)}, u32[]{:S(2)}) collective-permute-start(bf16[1,256,384]{2,1,0:T(8,128)(2,1)} %copy-done.6), channel_id=1, source_target_pairs={{0,24},{2,26},{4,28},{6,30},{8,16},{10,18},{12,20},{14,22},{16,8},... | collective-permute-start | bytes 589832 | tf_op jit(solution)/shard_map/ppermute | solution.py:216
  95.5 20.4 %collective-permute-start.14 = (bf16[4,2,256,128]{3,2,1,0:T(8,128)(2,1)S(1)}, bf16[4,2,256,128]{3,2,1,0:T(8,128)(2,1)S(1)}, u32[]{:S(2)}, u32[]{:S(2)}) collective-permute-start(bf16[4,2,256,128]{3,2,1,0:T(8,128)(2,1)S(1)} %pad_maximum_fusion.1.refs_4_), channel_id=1, source_target_pairs={{0,2},{2,0},{4,6},{6,4},{8,10},{10,8},{12,14},{14,12},{16,18},{18,... | collective-permute-start | bytes 1572872 | tf_op jit(solution)/shard_map/ppermute | solution.py:230
  95.5 33.1 %collective-permute-start.20 = (bf16[4,2,256,128]{3,2,1,0:T(8,128)(2,1)S(1)}, bf16[4,2,256,128]{3,2,1,0:T(8,128)(2,1)S(1)}, u32[]{:S(2)}, u32[]{:S(2)}) collective-permute-start(bf16[4,2,256,128]{3,2,1,0:T(8,128)(2,1)S(1)} %pad_maximum_fusion.2.refs_4_), channel_id=1, source_target_pairs={{0,2},{2,0},{4,6},{6,4},{8,10},{10,8},{12,14},{14,12},{16,18},{18,... | collective-permute-start | bytes 1572872 | tf_op jit(solution)/shard_map/ppermute | solution.py:230
  96.0 7.6 %collective-permute-start.9 = (bf16[4,2,256,128]{3,2,1,0:T(8,128)(2,1)}, bf16[4,2,256,128]{3,2,1,0:T(8,128)(2,1)S(1)}, u32[]{:S(2)}, u32[]{:S(2)}) collective-permute-start(bf16[4,2,256,128]{3,2,1,0:T(8,128)(2,1)} %collective-permute-done.7.refs_5_), channel_id=1, source_target_pairs={{0,2},{2,0},{4,6},{6,4},{8,10},{10,8},{12,14},{14,12},{16,18},{18,... | collective-permute-start | bytes 1572872 | tf_op jit(solution)/shard_map/ppermute | solution.py:231
  96.2 21.7 %collective-permute-start.15 = (bf16[4,2,256,128]{3,2,1,0:T(8,128)(2,1)S(1)}, bf16[4,2,256,128]{3,2,1,0:T(8,128)(2,1)S(1)}, u32[]{:S(2)}, u32[]{:S(2)}) collective-permute-start(bf16[4,2,256,128]{3,2,1,0:T(8,128)(2,1)S(1)} %collective-permute-done.13.refs_5_), channel_id=1, source_target_pairs={{0,2},{2,0},{4,6},{6,4},{8,10},{10,8},{12,14},{14,12},{16,18},{18,... | collective-permute-start | bytes 1572872 | tf_op jit(solution)/shard_map/ppermute | solution.py:231
  103.5 25.9 %collective-permute-start.21 = (bf16[4,2,256,128]{3,2,1,0:T(8,128)(2,1)S(1)}, bf16[4,2,256,128]{3,2,1,0:T(8,128)(2,1)S(1)}, u32[]{:S(2)}, u32[]{:S(2)}) collective-permute-start(bf16[4,2,256,128]{3,2,1,0:T(8,128)(2,1)S(1)} %collective-permute-done.19.refs_5_), channel_id=1, source_target_pairs={{0,2},{2,0},{4,6},{6,4},{8,10},{10,8},{12,14},{14,12},{16,18},{18,... | collective-permute-start | bytes 1572872 | tf_op jit(solution)/shard_map/ppermute | solution.py:231
  104.5 47.2 %slice-start = ((s8[9437184]{0:T(1024)(128)(4,1)}), s8[4194304]{0:T(1024)(128)(4,1)S(1)}, s32[]{:S(2)}) async-start(s8[9437184]{0:T(1024)(128)(4,1)} %bitcast.33), calls=%async_computation | async-start | bytes 8388608
  114.0 26.8 %collective-permute-start.22 = (bf16[256,128]{1,0:T(8,128)(2,1)S(1)}, bf16[256,128]{1,0:T(8,128)(2,1)S(1)}, u32[]{:S(2)}, u32[]{:S(2)}) collective-permute-start(bf16[256,128]{1,0:T(8,128)(2,1)S(1)} %get-tuple-element.52), channel_id=1, source_target_pairs={{0,8},{2,10},{4,12},{6,14},{8,0},{10,2},{12,4},{14,6},{16,24},{18,... | collective-permute-start | bytes 196616 | tf_op jit(solution)/shard_map/ppermute | solution.py:216
  115.9 26.4 %collective-permute-start.25 = (bf16[256,128]{1,0:T(8,128)(2,1)S(1)}, bf16[256,128]{1,0:T(8,128)(2,1)S(1)}, u32[]{:S(2)}, u32[]{:S(2)}) collective-permute-start(bf16[256,128]{1,0:T(8,128)(2,1)S(1)} %get-tuple-element.55), channel_id=1, source_target_pairs={{0,16},{2,18},{4,20},{6,22},{8,24},{10,26},{12,28},{14,30},{16,0},... | collective-permute-start | bytes 196616 | tf_op jit(solution)/shard_map/ppermute | solution.py:216
  117.9 33.7 %slice-start.1 = ((s8[9437184]{0:T(1024)(128)(4,1)}), s8[4194304]{0:T(1024)(128)(4,1)S(1)}, s32[]{:S(2)}) async-start(s8[9437184]{0:T(1024)(128)(4,1)} %bitcast.33), calls=%async_computation.1 | async-start | bytes 8388608
  117.9 24.4 %collective-permute-start.28 = (bf16[256,128]{1,0:T(8,128)(2,1)S(1)}, bf16[256,128]{1,0:T(8,128)(2,1)S(1)}, u32[]{:S(2)}, u32[]{:S(2)}) collective-permute-start(bf16[256,128]{1,0:T(8,128)(2,1)S(1)} %get-tuple-element.58), channel_id=1, source_target_pairs={{0,24},{2,26},{4,28},{6,30},{8,16},{10,18},{12,20},{14,22},{16,8},... | collective-permute-start | bytes 196616 | tf_op jit(solution)/shard_map/ppermute | solution.py:216
  128.6 16.7 %collective-permute-start.23 = (bf16[256,128]{1,0:T(8,128)(2,1)S(1)}, bf16[256,128]{1,0:T(8,128)(2,1)S(1)}, u32[]{:S(2)}, u32[]{:S(2)}) collective-permute-start(bf16[256,128]{1,0:T(8,128)(2,1)S(1)} %get-tuple-element.53), channel_id=1, source_target_pairs={{0,8},{2,10},{4,12},{6,14},{8,0},{10,2},{12,4},{14,6},{16,24},{18,... | collective-permute-start | bytes 196616 | tf_op jit(solution)/shard_map/ppermute | solution.py:216
  129.3 22.3 %slice-start.2 = ((s8[9437184]{0:T(1024)(128)(4,1)}), s8[1048576]{0:T(1024)(128)(4,1)S(1)}, s32[]{:S(2)}) async-start(s8[9437184]{0:T(1024)(128)(4,1)} %bitcast.33), calls=%async_computation.2 | async-start | bytes 2097152
  129.3 17.4 %collective-permute-start.26 = (bf16[256,128]{1,0:T(8,128)(2,1)S(1)}, bf16[256,128]{1,0:T(8,128)(2,1)S(1)}, u32[]{:S(2)}, u32[]{:S(2)}) collective-permute-start(bf16[256,128]{1,0:T(8,128)(2,1)S(1)} %get-tuple-element.56), channel_id=1, source_target_pairs={{0,16},{2,18},{4,20},{6,22},{8,24},{10,26},{12,28},{14,30},{16,0},... | collective-permute-start | bytes 196616 | tf_op jit(solution)/shard_map/ppermute | solution.py:216
  140.8 6.9 %collective-permute-start.29 = (bf16[256,128]{1,0:T(8,128)(2,1)S(1)}, bf16[256,128]{1,0:T(8,128)(2,1)S(1)}, u32[]{:S(2)}, u32[]{:S(2)}) collective-permute-start(bf16[256,128]{1,0:T(8,128)(2,1)S(1)} %get-tuple-element.59), channel_id=1, source_target_pairs={{0,24},{2,26},{4,28},{6,30},{8,16},{10,18},{12,20},{14,22},{16,8},... | collective-permute-start | bytes 196616 | tf_op jit(solution)/shard_map/ppermute | solution.py:216
  142.3 5.4 %collective-permute-start.24 = (bf16[256,128]{1,0:T(8,128)(2,1)S(1)}, bf16[256,128]{1,0:T(8,128)(2,1)S(1)}, u32[]{:S(2)}, u32[]{:S(2)}) collective-permute-start(bf16[256,128]{1,0:T(8,128)(2,1)S(1)} %get-tuple-element.54), channel_id=1, source_target_pairs={{0,8},{2,10},{4,12},{6,14},{8,0},{10,2},{12,4},{14,6},{16,24},{18,... | collective-permute-start | bytes 196616 | tf_op jit(solution)/shard_map/ppermute | solution.py:216
  142.3 9.3 %collective-permute-start.27 = (bf16[256,128]{1,0:T(8,128)(2,1)S(1)}, bf16[256,128]{1,0:T(8,128)(2,1)S(1)}, u32[]{:S(2)}, u32[]{:S(2)}) collective-permute-start(bf16[256,128]{1,0:T(8,128)(2,1)S(1)} %get-tuple-element.57), channel_id=1, source_target_pairs={{0,16},{2,18},{4,20},{6,22},{8,24},{10,26},{12,28},{14,30},{16,0},... | collective-permute-start | bytes 196616 | tf_op jit(solution)/shard_map/ppermute | solution.py:216
  145.3 6.4 %collective-permute-start.30 = (bf16[256,128]{1,0:T(8,128)(2,1)S(1)}, bf16[256,128]{1,0:T(8,128)(2,1)S(1)}, u32[]{:S(2)}, u32[]{:S(2)}) collective-permute-start(bf16[256,128]{1,0:T(8,128)(2,1)S(1)} %get-tuple-element.60), channel_id=1, source_target_pairs={{0,24},{2,26},{4,28},{6,30},{8,16},{10,18},{12,20},{14,22},{16,8},... | collective-permute-start | bytes 196616 | tf_op jit(solution)/shard_map/ppermute | solution.py:216
  154.5 17.4 %collective-permute-start.31 = (bf16[256,1536]{1,0:T(8,128)(2,1)S(1)}, bf16[256,1536]{1,0:T(8,128)(2,1)S(1)}, u32[]{:S(2)}, u32[]{:S(2)}) collective-permute-start(bf16[256,1536]{1,0:T(8,128)(2,1)S(1)} %shard_map.81), channel_id=1, source_target_pairs={{0,1},{1,0},{2,3},{3,2},{4,5},{5,4},{6,7},{7,6},{8,9},{9,8},{10,11... | collective-permute-start | bytes 2359304 | tf_op jit(solution)/shard_map/ppermute | solution.py:241
  (3 other events, 5.7 us)

commit v2 on v1

--- a/solution.py
+++ b/solution.py
@@ -32,61 +32,67 @@
     return pltpu.CompilerParams(vmem_limit_bytes=mib * MIB)
 
 
-def project(where, own, other, weights, width, first):
+def project(where, own, other, weights, groups, heads, group_heads):
     rows, half = own.shape
     kinds = len(weights)
-
-    def column(i, s):
-        return (s[1] ^ i) * first[1] + first[0]
+    count = len(heads)
 
     def body(s, own_ref, other_ref, *refs):
         mine, theirs = refs[:kinds], refs[kinds : 2 * kinds]
         outs = refs[2 * kinds :]
-        step = pl.program_id(0)
         w_mine = jnp.concatenate([r[...] for r in mine], axis=1)
         w_theirs = jnp.concatenate([r[...] for r in theirs], axis=1)
         total = jnp.dot(own_ref[...], w_mine, preferred_element_type=F32)
         total += jnp.dot(other_ref[...], w_theirs, preferred_element_type=F32)
         total = total.astype(BF16)
-        for i in range(Z):
-
-            @pl.when(step == i)
+        for i in range(len(groups)):
+
+            @pl.when(pl.program_id(0) == i)
             def _(i=i):
                 for k in range(kinds):
-                    outs[i][k] = total[:, k * width : (k + 1) * width]
-
-    row_spec = pl.BlockSpec((rows, half), lambda i, s: (0, 0))
-    mine_spec = pl.BlockSpec((half, width), lambda i, s: (s[0], column(i, s)))
-    theirs_spec = pl.BlockSpec((half, width), lambda i, s: (1 - s[0], column(i, s)))
+                    outs[i][k * count + pl.program_id(1)] = total[:, k * HEAD_DIM : (k + 1) * HEAD_DIM]
+
+    def column(i, h, s):
+        flip = groups[0] if len(groups) == 1 else groups[0] ^ (i * (groups[0] ^ groups[1]))
+        return (s[1] ^ flip) * group_heads + heads[0] + h
+
+    row_spec = pl.BlockSpec((rows, half), lambda i, h, s: (0, 0))
+    mine_spec = pl.BlockSpec((half, HEAD_DIM), lambda i, h, s: (s[0], column(i, h, s)))
+    theirs_spec = pl.BlockSpec((half, HEAD_DIM), lambda i, h, s: (1 - s[0], column(i, h, s)))
+    out = (kinds * count, rows, HEAD_DIM)
+    blocks = kinds * len(groups) * count
     return pl.pallas_call(
         body,
         grid_spec=pltpu.PrefetchScalarGridSpec(
             num_scalar_prefetch=1,
-            grid=(Z,),
+            grid=(len(groups), count),
             in_specs=[row_spec, row_spec] + [mine_spec] * kinds + [theirs_spec] * kinds,
-            out_specs=[pl.BlockSpec((kinds, rows, width), lambda i, s: (0, 0, 0))] * Z,
-        ),
-        out_shape=[jax.ShapeDtypeStruct((kinds, rows, width), BF16)] * Z,
-        compiler_params=params(24),
+            out_specs=[pl.BlockSpec(out, lambda i, h, s: (0, 0, 0))] * len(groups),
+        ),
+        out_shape=[jax.ShapeDtypeStruct(out, BF16)] * len(groups),
+        compiler_params=params(56),
         cost_estimate=pl.CostEstimate(
-            flops=2 * rows * 2 * half * width * kinds * Z,
-            bytes_accessed=2 * 2 * half * width * kinds * Z,
+            flops=4 * rows * half * HEAD_DIM * blocks,
+            bytes_accessed=4 * half * HEAD_DIM * blocks,
             transcendentals=0,
         ),
     )(where, own, other, *weights, *weights)
 
 
-def attend(queries, parts, bias, head):
-    rows = queries[0].shape[1]
-    tile = parts[0].shape[2]
-    tiles = len(parts) * Z
+def attend(queries, parts, bias):
+    rows = queries[0][0].shape[1]
+    tile = parts[0][0].shape[2]
+    where_tile = [(i, b) for i, p in enumerate(parts) for b in range(p[0].shape[0])]
+    tiles = len(where_tile)
     key_count = tiles * tile
     scale = math.log2(math.e) / math.sqrt(HEAD_DIM)
     per = rows // BLOCK
+    n = len(parts)
 
     def body(*refs):
-        q_refs, kv_refs, bias_ref = refs[:Z], refs[Z : Z + len(parts)], refs[Z + len(parts)]
-        outs = refs[Z + len(parts) + 1 : Z + len(parts) + 1 + Z]
+        q_refs, k_refs, v_refs = refs[:Z], refs[Z : Z + n], refs[Z + n : Z + 2 * n]
+        bias_ref = refs[Z + 2 * n]
+        outs = refs[Z + 2 * n + 1 : Z + 2 * n + 1 + Z]
         s_ref, q_ref = refs[-2:]
         step = pl.program_id(0)
         for i in range(Z):
@@ -98,7 +104,7 @@
         query = q_ref[...]
         top = jnp.full((rows, 1), -jnp.inf, F32)
         for t in range(tiles):
-            key = kv_refs[t // Z][t % Z, 0]
+            key = k_refs[where_tile[t][0]][where_tile[t][1], 0]
             score = lax.dot_general(
                 query, key, (((1,), (1,)), ((), ())), preferred_element_type=F32
             )
@@ -118,7 +124,9 @@
             weight = jnp.exp2(s_ref[:, t * tile : (t + 1) * tile] * scale - shift)
             total += jnp.sum(weight, axis=1, keepdims=True)
             accum += jnp.dot(
-                weight.astype(BF16), kv_refs[t // Z][t % Z, 1], preferred_element_type=F32
+                weight.astype(BF16),
+                v_refs[where_tile[t][0]][where_tile[t][1], 0],
+                preferred_element_type=F32,
             )
         result = (accum / total).astype(BF16)
         for i in range(Z):
@@ -127,11 +135,18 @@
             def _(i=i):
                 outs[i][...] = result
 
+    def query_spec(index):
+        return pl.BlockSpec((1, rows, HEAD_DIM), lambda i: (index, 0, 0))
+
+    def part_spec(part, index):
+        return pl.BlockSpec((part.shape[0], 1, tile, HEAD_DIM), lambda i: (0, index, 0, 0))
+
     return pl.pallas_call(
         body,
         grid=(Z,),
-        in_specs=[pl.BlockSpec((1, rows, HEAD_DIM), lambda i: (0, 0, head))] * Z
-        + [pl.BlockSpec(p.shape, lambda i: (0, 0, 0, 0)) for p in parts]
+        in_specs=[query_spec(at) for _, at in queries]
+        + [part_spec(p, k) for p, k, _ in parts]
+        + [part_spec(p, v) for p, _, v in parts]
         + [pl.BlockSpec(bias.shape, lambda i: (0, 0))],
         out_specs=[pl.BlockSpec((rows, HEAD_DIM), lambda i: (0, 0))] * Z,
         out_shape=[jax.ShapeDtypeStruct((rows, HEAD_DIM), BF16)] * Z,
@@ -142,7 +157,7 @@
             bytes_accessed=4 * key_count * HEAD_DIM,
             transcendentals=Z * rows * key_count,
         ),
-    )(*queries, *parts, bias)
+    )(*[q for q, _ in queries], *[p for p, _, _ in parts], *[p for p, _, _ in parts], bias)
 
 
 def mix(where, attended, w_out, flip, step_width):
@@ -187,19 +202,32 @@
     group_heads = w_query.shape[1] // HEAD_DIM // Z
     block_count = block_order.shape[0]
     per = rows // BLOCK
+    cut = rows // 2
     ctx = lax.axis_index("ctx")
     y = lax.axis_index("head")
     z, x, c = ctx // (X * C), (ctx // C) % X, ctx % C
     where = jnp.stack([y, z]).astype(jnp.int32)
-
-    other = lax.ppermute(tokens, "head", [(0, 1), (1, 0)])
+    weights = (w_query, w_key, w_value)
+
+    def over_y(a):
+        return lax.ppermute(a, "head", [(0, 1), (1, 0)])
+
+    def over(a, dz, dx, dc):
+        return lax.ppermute(a, "ctx", hop(dz, dx, dc))
+
+    other = over_y(tokens)
+    far = [over(tokens[i * cut : (i + 1) * cut], 2, 0, 0) for i in range(2)]
+    far_other = [over_y(f) for f in far]
 
     def blocks(pairs):
         first = jnp.stack([place(z ^ dz, x ^ dx, c ^ dc) for dz, dx, dc in pairs]) * per
         return (first[:, None] + jnp.arange(per)[None, :]).reshape(-1)
 
+    sides = ((0, 0), (1, 0), (0, 1), (1, 1))
     query_blocks = blocks([(dz, 0, 0) for dz in range(Z)])
-    key_blocks = blocks([(dz, dx, dc) for dc, dx in ((0, 0), (0, 1), (1, 0), (1, 1)) for dz in range(Z)])
+    key_blocks = blocks(
+        [(dz + near, dx, dc) for near in (0, 2) for dx, dc in sides for dz in range(2)]
+    )
     frames = jnp.arange(block_count, dtype=jnp.int32)
     order_hot = (block_order[:, None] == frames[None, :]).astype(F32)
 
@@ -207,38 +235,37 @@
         place_hot = (wanted[:, None] == frames[None, :]).astype(F32)
         return jnp.dot(place_hot, order_hot)
 
-    live = jnp.dot(
-        jnp.dot(pick(query_blocks), block_mask.astype(F32)), pick(key_blocks).T
-    )
+    live = jnp.dot(jnp.dot(pick(query_blocks), block_mask.astype(F32)), pick(key_blocks).T)
     bias = jnp.repeat(jnp.where(live > 0.5, 0.0, -1e30).astype(F32), BLOCK, axis=1)
 
-    def share(pieces):
-        return [pieces[0]] + [lax.ppermute(pieces[dz], "ctx", hop(dz, 0, 0)) for dz in range(1, Z)]
-
-    gathered = []
-    queries = None
+    def spread(part):
+        across = over(part, 0, 1, 0)
+        return [part, across, over(part, 0, 0, 1), over(across, 0, 0, 1)]
+
+    kept, sent = project(where, tokens, other, weights, (0, 1), range(group_heads), group_heads)
+    came = over(sent, 1, 0, 0)
+    near = [spread(a[None, group_heads:]) for a in (kept, came)]
+    near_queries = [kept, came]
+
+    far = jnp.concatenate(far, axis=0)
+    far_other = jnp.concatenate(far_other, axis=0)
+    results = []
+    far_queries, far_parts = [], []
     for j in range(group_heads):
-        pieces = share(
-            project(where, tokens, other, (w_key, w_value), HEAD_DIM, (j, group_heads))
-        )
-        part = jnp.stack(pieces)
-        across = lax.ppermute(part, "ctx", hop(0, 1, 0))
-        gathered.append(
-            (
-                part,
-                across,
-                lax.ppermute(part, "ctx", hop(0, 0, 1)),
-                lax.ppermute(across, "ctx", hop(0, 0, 1)),
-            )
-        )
-        if j == 0:
-            queries = share(
-                project(where, tokens, other, (w_query,), HEAD_DIM * group_heads, (0, 1))
-            )
-    results = [share(attend(queries, gathered[j], bias, j)) for j in range(group_heads)]
+        kept, sent = project(where, far, far_other, weights, (0, 1), (j,), group_heads)
+        came = over(sent, 1, 0, 0)
+        far_queries.append((kept, came))
+        far_parts.append(spread(jnp.stack([kept[1:], came[1:]])))
+    for j in range(group_heads):
+        queries = [(a, j) for a in near_queries] + [(a, 0) for a in far_queries[j]]
+        parts = [(near[i][side], j, group_heads + j) for side in range(4) for i in range(2)]
+        parts += [(a, 0, 1) for a in far_parts[j]]
+        results.append(attend(queries, parts, bias))
+    results = [
+        [r[0]] + [over(r[dz], dz, 0, 0) for dz in range(1, Z)] for r in results
+    ]
     attended = [results[j][dz] for dz in range(Z) for j in range(group_heads)]
-    away = mix(where, attended, w_out, True, 512)
-    arrived = lax.ppermute(away, "head", [(0, 1), (1, 0)])
+    arrived = over_y(mix(where, attended, w_out, True, 512))
     home = mix(where, attended, w_out, False, 512)
     return (home.astype(F32) + arrived.astype(F32)).astype(BF16)
 

time: 173 us -> 201 us (1.16)
  waiting for transfers between devices: 61.9 us -> 92.5 us
  Pallas kernels: 52.7 us -> 64.2 us
  starting transfers between devices: 42.4 us -> 31.5 us
  local copies, waits for them, and re-layouts: 13.6 us -> 7.43 us
    ppermute x32 -> x34, waiting for transfers between devices: 61.9 us -> 92.5 us  [the longest x30 79.8 us: over(): return lax.ppermute(a, 'ctx', hop(dz, dx, dc))]
    ppermute x32 -> x34, starting transfers between devices: 42.4 us -> 31.5 us  [the longest x30 26.1 us: over(): return lax.ppermute(a, 'ctx', hop(dz, dx, dc))]
    pallas_call x4, Pallas kernels: 19.2 us -> 30 us  [project(): pl.pallas_call(body, grid_spec=pltpu.PrefetchScalarGridSpec(num_scalar_pr...]
    unnamed x38 -> x48, local copies, waits for them, and re-layouts: 13.1 us -> 3.77 us
  transfers between devices with their start and end apart: 32 -> 34, of which waited for: 11 -> 14; matrix products, arithmetic and copies ran while one was open for 1% -> 4% of each run, Pallas kernels for 26% -> 31%
where the time goes in v2:
time: 201 us
  waiting for transfers between devices  92.5 us (46%)
  Pallas kernels  64.2 us (32%)
  starting transfers between devices  31.5 us (16%)
  local copies, waits for them, and re-layouts  7.43 us (4%)
  other arithmetic  3.39 us (2%)
    ppermute x30, waiting for transfers between devices, over(): return lax.ppermute(a, 'ctx', hop(dz, dx, dc))  79.8 us
    pallas_call x4, Pallas kernels, project(): pl.pallas_call(body, grid_spec=pltpu.PrefetchScalarGridSpec(num_scalar_pr...  30 us
    pallas_call x3, Pallas kernels, attend(): pl.pallas_call(body, grid=(Z,), in_specs=[query_spec(at) for _, at in que...  28.6 us
    ppermute x30, starting transfers between devices, over(): return lax.ppermute(a, 'ctx', hop(dz, dx, dc))  26.1 us
    ppermute x4, waiting for transfers between devices, over_y(): return lax.ppermute(a, 'head', [(0, 1), (1, 0)])  12.7 us
    pallas_call x2, Pallas kernels, mix(): pl.pallas_call(body, grid_spec=pltpu.PrefetchScalarGridSpec(num_scalar_pr...  5.64 us
    ppermute x4, starting transfers between devices, over_y(): return lax.ppermute(a, 'head', [(0, 1), (1, 0)])  5.38 us
  transfers between devices with their start and end apart: 34, of which 14 were waited for; matrix products, arithmetic and copies ran while one was open for 4% of the time, Pallas kernels for 31%

profile of v2, /device:TPU:0, one launch (start us, length us, event | category | flops | bytes accessed | tf_op | source)
XLA Modules:
  0.0 200.7 jit_solution(6052475446918309481)
XLA Ops:
  0.0 3.0 %collective-permute-start = (bf16[256,1536]{1,0:T(8,128)(2,1)}, bf16[256,1536]{1,0:T(8,128)(2,1)S(1)}, u32[]{:S(2)}, u32[]{:S(2)}) collective-permute-start(bf16[256,1536]{1,0:T(8,128)(2,1)} %own_ref.1), channel_id=1, source_target_pairs={{0,1},{1,0},{2,3},{3,2},{4,5},{5,4},{6,7},{7,6},{8,9},{9,8},{10,11... | collective-permute-start | bytes 2359304 | tf_op jit(solution)/shard_map/ppermute | solution.py:213
  3.0 1.2 fusion.21
  4.1 2.7 %collective-permute-start.2 = (bf16[128,1536]{1,0:T(8,128)(2,1)S(1)}, bf16[128,1536]{1,0:T(8,128)(2,1)S(1)}, u32[]{:S(2)}, u32[]{:S(2)}) collective-permute-start(bf16[128,1536]{1,0:T(8,128)(2,1)S(1)} %get-tuple-element.46), channel_id=1, source_target_pairs={{0,16},{2,18},{4,20},{6,22},{8,24},{10,26},{12,28},{14,30},{16,0},... | collective-permute-start | bytes 1179656 | tf_op jit(solution)/shard_map/ppermute | solution.py:216
  7.5 0.6 pad_add_fusion.s
  8.1 1.0 fusion.3
  9.1 24.6 %collective-permute-done.2 = bf16[128,1536]{1,0:T(8,128)(2,1)S(1)} collective-permute-done((bf16[128,1536]{1,0:T(8,128)(2,1)S(1)}, bf16[128,1536]{1,0:T(8,128)(2,1)S(1)}, u32[]{:S(2)}, u32[]{:S(2)}) %collective-permute-start.2) | collective-permute-done | bytes 393248 | tf_op jit(solution)/shard_map/ppermute | solution.py:216
  34.1 6.8 %collective-permute-done.3 = bf16[128,1536]{1,0:T(8,128)(2,1)S(1)} collective-permute-done((bf16[128,1536]{1,0:T(8,128)(2,1)S(1)}, bf16[128,1536]{1,0:T(8,128)(2,1)S(1)}, u32[]{:S(2)}, u32[]{:S(2)}) %collective-permute-start.3) | collective-permute-done | bytes 393248 | tf_op jit(solution)/shard_map/ppermute | solution.py:216
  41.5 0.9 copy-done.15
  42.4 11.8 %shard_map.73 = (bf16[9,256,128]{2,1,0:T(8,128)(2,1)}, bf16[9,256,128]{2,1,0:T(8,128)(2,1)}) custom-call(s32[2]{0:T(128)} %pad_add_fusion.s, bf16[256,1536]{1,0:T(8,128)(2,1)} %own_ref.1, bf16[256,1536]{1,0:T(8,128)(2,1)} %copy-done.15, bf16[3072,1536]{1,0:T(8,128)(2,1)} %refs_3_.7, bf16[3072,1536]{1,0:T(8,128)(2,1)} %refs_4_.7, bf16[3072,1536]{1,0:T(8,128)(2,1)} %refs_5_.7, ...), custom_call_target="tpu_custom_call" | custom-call | flops 3623878656 | bytes 14155776 | tf_op jit(solution)/shard_map/pallas_call | solution.py:64
  54.3 1.0 slice_bitcast_fusion.1.refs_4_.refs_16_
  55.3 1.6 collective-permute-start.7
  57.0 0.9 copy-done.13
  57.9 6.0 %shard_map.78 = (bf16[3,256,128]{2,1,0:T(8,128)(2,1)}, bf16[3,256,128]{2,1,0:T(8,128)(2,1)}) custom-call(s32[2]{0:T(128)} %pad_add_fusion.s, bf16[256,1536]{1,0:T(8,128)(2,1)} %copy-done.14, bf16[256,1536]{1,0:T(8,128)(2,1)} %copy-done.13, bf16[3072,1536]{1,0:T(8,128)(2,1)} %refs_3_.7, bf16[3072,1536]{1,0:T(8,128)(2,1)} %refs_4_.7, ...), custom_call_target="tpu_custom_call" | custom-call | flops 1207959552 | bytes 4718592 | tf_op jit(solution)/shard_map/pallas_call | solution.py:64
  63.9 6.0 %shard_map.76 = (bf16[3,256,128]{2,1,0:T(8,128)(2,1)}, bf16[3,256,128]{2,1,0:T(8,128)(2,1)}) custom-call(s32[2]{0:T(128)} %pad_add_fusion.s, bf16[256,1536]{1,0:T(8,128)(2,1)} %copy-done.14, bf16[256,1536]{1,0:T(8,128)(2,1)} %copy-done.13, bf16[3072,1536]{1,0:T(8,128)(2,1)} %refs_3_.7, bf16[3072,1536]{1,0:T(8,128)(2,1)} %refs_4_.7, ...), custom_call_target="tpu_custom_call" | custom-call | flops 1207959552 | bytes 4718592 | tf_op jit(solution)/shard_map/pallas_call | solution.py:64
  69.9 6.1 %shard_map.74 = (bf16[3,256,128]{2,1,0:T(8,128)(2,1)}, bf16[3,256,128]{2,1,0:T(8,128)(2,1)}) custom-call(s32[2]{0:T(128)} %pad_add_fusion.s, bf16[256,1536]{1,0:T(8,128)(2,1)} %copy-done.14, bf16[256,1536]{1,0:T(8,128)(2,1)} %copy-done.13, bf16[3072,1536]{1,0:T(8,128)(2,1)} %refs_3_.7, bf16[3072,1536]{1,0:T(8,128)(2,1)} %refs_4_.7, ...), custom_call_target="tpu_custom_call" | custom-call | flops 1207959552 | bytes 4718592 | tf_op jit(solution)/shard_map/pallas_call | solution.py:64
  76.0 0.7 collective-permute-start.20
  76.8 1.4 collective-permute-start.1
  78.2 0.7 collective-permute-start.16
  78.9 0.9 slice_bitcast_fusion.7
  79.8 4.0 %collective-permute-done.20.refs_3_ = bf16[3,256,128]{2,1,0:T(8,128)(2,1)S(1)} collective-permute-done((bf16[3,256,128]{2,1,0:T(8,128)(2,1)S(1)}, bf16[3,256,128]{2,1,0:T(8,128)(2,1)S(1)}, u32[]{:S(2)}, u32[]{:S(2)}) %collective-permute-start.20) | collective-permute-done | bytes 196640 | tf_op jit(solution)/shard_map/ppermute | solution.py:216
  83.8 0.7 collective-permute-start.6
  84.5 0.7 pad_maximum_fusion.2.refs_12_.refs_24_
  85.2 15.4 %collective-permute-done.16.refs_3_ = bf16[3,256,128]{2,1,0:T(8,128)(2,1)S(1)} collective-permute-done((bf16[3,256,128]{2,1,0:T(8,128)(2,1)S(1)}, bf16[3,256,128]{2,1,0:T(8,128)(2,1)S(1)}, u32[]{:S(2)}, u32[]{:S(2)}) %collective-permute-start.16) | collective-permute-done | bytes 196640 | tf_op jit(solution)/shard_map/ppermute | solution.py:216
  101.2 3.3 %collective-permute-done.6.refs_3_ = bf16[3,256,128]{2,1,0:T(8,128)(2,1)S(1)} collective-permute-done((bf16[3,256,128]{2,1,0:T(8,128)(2,1)}, bf16[3,256,128]{2,1,0:T(8,128)(2,1)S(1)}, u32[]{:S(2)}, u32[]{:S(2)}) %collective-permute-start.6) | collective-permute-done | bytes 196640 | tf_op jit(solution)/shard_map/ppermute | solution.py:216
  104.5 0.7 pad_maximum_fusion.1.refs_12_.refs_24_
  105.9 1.6 collective-permute-start.13
  107.5 1.0 collective-permute-done.21.refs_13_.refs_25_
  109.9 4.9 %collective-permute-done.17.refs_13_.refs_25_ = bf16[2,2,256,128]{3,2,1,0:T(8,128)(2,1)} collective-permute-done((bf16[2,2,256,128]{3,2,1,0:T(8,128)(2,1)}, bf16[2,2,256,128]{3,2,1,0:T(8,128)(2,1)}, u32[]{:S(2)}, u32[]{:S(2)}) %collective-permute-start.17) | collective-permute-done | bytes 262176 | tf_op jit(solution)/shard_map/ppermute | solution.py:216
  114.8 5.6 %collective-permute-done.13.refs_13_.refs_25_ = bf16[2,2,256,128]{3,2,1,0:T(8,128)(2,1)} collective-permute-done((bf16[2,2,256,128]{3,2,1,0:T(8,128)(2,1)S(1)}, bf16[2,2,256,128]{3,2,1,0:T(8,128)(2,1)}, u32[]{:S(2)}, u32[]{:S(2)}) %collective-permute-start.13) | collective-permute-done | bytes 262176 | tf_op jit(solution)/shard_map/ppermute | solution.py:216
  120.9 7.4 %collective-permute-done.8.refs_7_.refs_19_ = bf16[1,6,256,128]{3,2,1,0:T(8,128)(2,1)S(1)} collective-permute-done((bf16[1,6,256,128]{3,2,1,0:T(8,128)(2,1)S(1)}, bf16[1,6,256,128]{3,2,1,0:T(8,128)(2,1)S(1)}, u32[]{:S(2)}, u32[]{:S(2)}) %collective-permute-start.8) | collective-permute-done | bytes 393248 | tf_op jit(solution)/shard_map/ppermute | solution.py:216
  129.1 0.9 collective-permute-done.12.refs_11_.refs_23_
  130.1 0.9 copy-done.9
  131.0 0.9 copy-done.11
  131.9 9.7 %shard_map.79 = (bf16[256,128]{1,0:T(8,128)(2,1)S(1)}, bf16[256,128]{1,0:T(8,128)(2,1)S(1)}, bf16[256,128]{1,0:T(8,128)(2,1)S(1)}, bf16[256,128]{1,0:T(8,128)(2,1)S(1)}) custom-call(bf16[9,256,128]{2,1,0:T(8,128)(2,1)S(1)} %copy-done, bf16[9,256,128]{2,1,0:T(8,128)(2,1)S(1)} %collective-permute-done.1.refs_1_, bf16[3,256,128]{2,1,0:T(8,128)(2,1)S(1)} %copy-done.9, ...), custom_call_target="tpu_custom_call" | custom-call | flops 2147483648 | bytes 2097152 | tf_op jit(solution)/shard_map/pallas_call | solution.py:144
  141.6 0.7 collective-permute-start.26
  142.3 3.4 %collective-permute-start.29 = (bf16[256,128]{1,0:T(8,128)(2,1)S(1)}, bf16[256,128]{1,0:T(8,128)(2,1)S(1)}, u32[]{:S(2)}, u32[]{:S(2)}) collective-permute-start(bf16[256,128]{1,0:T(8,128)(2,1)S(1)} %get-tuple-element.41), channel_id=1, source_target_pairs={{0,16},{2,18},{4,20},{6,22},{8,24},{10,26},{12,28},{14,30},{16,0},... | collective-permute-start | bytes 196616 | tf_op jit(solution)/shard_map/ppermute | solution.py:216
  146.1 9.6 %shard_map.77 = (bf16[256,128]{1,0:T(8,128)(2,1)S(1)}, bf16[256,128]{1,0:T(8,128)(2,1)S(1)}, bf16[256,128]{1,0:T(8,128)(2,1)S(1)}, bf16[256,128]{1,0:T(8,128)(2,1)S(1)}) custom-call(bf16[9,256,128]{2,1,0:T(8,128)(2,1)S(1)} %copy-done, bf16[9,256,128]{2,1,0:T(8,128)(2,1)S(1)} %collective-permute-done.1.refs_1_, bf16[3,256,128]{2,1,0:T(8,128)(2,1)S(1)} %copy-done.3, ...), custom_call_target="tpu_custom_call" | custom-call | flops 2147483648 | bytes 2097152 | tf_op jit(solution)/shard_map/pallas_call | solution.py:144
  156.1 3.6 %collective-permute-start.28 = (bf16[256,128]{1,0:T(8,128)(2,1)S(1)}, bf16[256,128]{1,0:T(8,128)(2,1)S(1)}, u32[]{:S(2)}, u32[]{:S(2)}) collective-permute-start(bf16[256,128]{1,0:T(8,128)(2,1)S(1)} %get-tuple-element.40), channel_id=1, source_target_pairs={{0,16},{2,18},{4,20},{6,22},{8,24},{10,26},{12,28},{14,30},{16,0},... | collective-permute-start | bytes 196616 | tf_op jit(solution)/shard_map/ppermute | solution.py:216
  159.8 9.3 %shard_map.75 = (bf16[256,128]{1,0:T(8,128)(2,1)S(1)}, bf16[256,128]{1,0:T(8,128)(2,1)S(1)}, bf16[256,128]{1,0:T(8,128)(2,1)S(1)}, bf16[256,128]{1,0:T(8,128)(2,1)S(1)}) custom-call(bf16[9,256,128]{2,1,0:T(8,128)(2,1)S(1)} %copy-done, bf16[9,256,128]{2,1,0:T(8,128)(2,1)S(1)} %collective-permute-done.1.refs_1_, bf16[3,256,128]{2,1,0:T(8,128)(2,1)S(1)} %copy-done.1, ...), custom_call_target="tpu_custom_call" | custom-call | flops 2147483648 | bytes 2097152 | tf_op jit(solution)/shard_map/pallas_call | solution.py:144
  170.0 3.5 %collective-permute-start.27 = (bf16[256,128]{1,0:T(8,128)(2,1)S(1)}, bf16[256,128]{1,0:T(8,128)(2,1)S(1)}, u32[]{:S(2)}, u32[]{:S(2)}) collective-permute-start(bf16[256,128]{1,0:T(8,128)(2,1)S(1)} %get-tuple-element.39), channel_id=1, source_target_pairs={{0,16},{2,18},{4,20},{6,22},{8,24},{10,26},{12,28},{14,30},{16,0},... | collective-permute-start | bytes 196616 | tf_op jit(solution)/shard_map/ppermute | solution.py:216
  174.0 1.2 collective-permute-done.31.refs_10_
  175.2 3.2 %collective-permute-done.27.refs_6_ = bf16[256,128]{1,0:T(8,128)(2,1)S(1)} collective-permute-done((bf16[256,128]{1,0:T(8,128)(2,1)S(1)}, bf16[256,128]{1,0:T(8,128)(2,1)S(1)}, u32[]{:S(2)}, u32[]{:S(2)}) %collective-permute-start.27) | collective-permute-done | bytes 65568 | tf_op jit(solution)/shard_map/ppermute | solution.py:216
  178.4 1.3 collective-permute-done.30.refs_9_
  179.8 2.8 %shard_map.81 = bf16[256,1536]{1,0:T(8,128)(2,1)S(1)} custom-call(s32[2]{0:T(128)S(1)} %copy-done.12, bf16[256,128]{1,0:T(8,128)(2,1)S(1)} %get-tuple-element.29.refs_0_, bf16[256,128]{1,0:T(8,128)(2,1)S(1)} %get-tuple-element.32.refs_1_, bf16[256,128]{1,0:T(8,128)(2,1)S(1)} %get-tuple-element.35.refs_2_, ...), custom_call_target="tpu_custom_call" | custom-call | flops 1207959552 | bytes 4718592 | tf_op jit(solution)/shard_map/pallas_call | solution.py:181
  182.6 1.5 collective-permute-start.33
  184.1 2.8 %shard_map.80 = bf16[256,1536]{1,0:T(8,128)(2,1)S(1)} custom-call(s32[2]{0:T(128)S(1)} %copy-done.12, bf16[256,128]{1,0:T(8,128)(2,1)S(1)} %get-tuple-element.29.refs_0_, bf16[256,128]{1,0:T(8,128)(2,1)S(1)} %get-tuple-element.32.refs_1_, bf16[256,128]{1,0:T(8,128)(2,1)S(1)} %get-tuple-element.35.refs_2_, ...), custom_call_target="tpu_custom_call" | custom-call | flops 1207959552 | bytes 4718592 | tf_op jit(solution)/shard_map/pallas_call | solution.py:181
  186.9 12.7 %collective-permute-done.33 = bf16[256,1536]{1,0:T(8,128)(2,1)S(1)} collective-permute-done((bf16[256,1536]{1,0:T(8,128)(2,1)S(1)}, bf16[256,1536]{1,0:T(8,128)(2,1)S(1)}, u32[]{:S(2)}, u32[]{:S(2)}) %collective-permute-start.33) | collective-permute-done | bytes 786464 | tf_op jit(solution)/shard_map/ppermute | solution.py:213
  199.6 1.1 add_convert_fusion
  (105 shorter events, 7.6 us)
Async XLA Ops:
  0.0 41.5 %collective-permute-start = (bf16[256,1536]{1,0:T(8,128)(2,1)}, bf16[256,1536]{1,0:T(8,128)(2,1)S(1)}, u32[]{:S(2)}, u32[]{:S(2)}) collective-permute-start(bf16[256,1536]{1,0:T(8,128)(2,1)} %own_ref.1), channel_id=1, source_target_pairs={{0,1},{1,0},{2,3},{3,2},{4,5},{5,4},{6,7},{7,6},{8,9},{9,8},{10,11... | collective-permute-start | bytes 2359304 | tf_op jit(solution)/shard_map/ppermute | solution.py:213
  4.1 29.6 %collective-permute-start.2 = (bf16[128,1536]{1,0:T(8,128)(2,1)S(1)}, bf16[128,1536]{1,0:T(8,128)(2,1)S(1)}, u32[]{:S(2)}, u32[]{:S(2)}) collective-permute-start(bf16[128,1536]{1,0:T(8,128)(2,1)S(1)} %get-tuple-element.46), channel_id=1, source_target_pairs={{0,16},{2,18},{4,20},{6,22},{8,24},{10,26},{12,28},{14,30},{16,0},... | collective-permute-start | bytes 1179656 | tf_op jit(solution)/shard_map/ppermute | solution.py:216
  6.8 34.2 %collective-permute-start.3 = (bf16[128,1536]{1,0:T(8,128)(2,1)S(1)}, bf16[128,1536]{1,0:T(8,128)(2,1)S(1)}, u32[]{:S(2)}, u32[]{:S(2)}) collective-permute-start(bf16[128,1536]{1,0:T(8,128)(2,1)S(1)} %get-tuple-element.45), channel_id=1, source_target_pairs={{0,16},{2,18},{4,20},{6,22},{8,24},{10,26},{12,28},{14,30},{16,0},... | collective-permute-start | bytes 1179656 | tf_op jit(solution)/shard_map/ppermute | solution.py:216
  33.7 23.2 %collective-permute-start.4 = (bf16[128,1536]{1,0:T(8,128)(2,1)S(1)}, bf16[128,1536]{1,0:T(8,128)(2,1)S(1)}, u32[]{:S(2)}, u32[]{:S(2)}) collective-permute-start(bf16[128,1536]{1,0:T(8,128)(2,1)S(1)} %collective-permute-done.2), channel_id=1, source_target_pairs={{0,1},{1,0},{2,3},{3,2},{4,5},{5,4},{6,7},{7,6},{8,9},{9,8},{10,11... | collective-permute-start | bytes 1179656 | tf_op jit(solution)/shard_map/ppermute | solution.py:213
  41.0 16.0 %collective-permute-start.5 = (bf16[128,1536]{1,0:T(8,128)(2,1)S(1)}, bf16[128,1536]{1,0:T(8,128)(2,1)S(1)}, u32[]{:S(2)}, u32[]{:S(2)}) collective-permute-start(bf16[128,1536]{1,0:T(8,128)(2,1)S(1)} %collective-permute-done.3), channel_id=1, source_target_pairs={{0,1},{1,0},{2,3},{3,2},{4,5},{5,4},{6,7},{7,6},{8,9},{9,8},{10,11... | collective-permute-start | bytes 1179656 | tf_op jit(solution)/shard_map/ppermute | solution.py:213
  41.5 12.8 %copy-start.14 = (bf16[256,1536]{1,0:T(8,128)(2,1)}, bf16[256,1536]{1,0:T(8,128)(2,1)S(1)}, u32[]{:S(2)}) copy-start(bf16[256,1536]{1,0:T(8,128)(2,1)S(1)} %constant_dynamic-update-slice_fusion.own_ref) | copy-start | bytes 2359300
  55.3 50.6 %collective-permute-start.7 = (bf16[1,6,256,128]{3,2,1,0:T(8,128)(2,1)S(1)}, bf16[1,6,256,128]{3,2,1,0:T(8,128)(2,1)S(1)}, u32[]{:S(2)}, u32[]{:S(2)}) collective-permute-start(bf16[1,6,256,128]{3,2,1,0:T(8,128)(2,1)S(1)} %slice_bitcast_fusion.1.refs_4_.refs_16_), channel_id=1, source_target_pairs={{0,4},{2,6},{4,0},{6,2},{8,12},{10,14},{12,8},{14,10},{16,20},{18,... | collective-permute-start | bytes 1179656 | tf_op jit(solution)/shard_map/ppermute | solution.py:216
  56.9 51.7 %collective-permute-start.9 = (bf16[1,6,256,128]{3,2,1,0:T(8,128)(2,1)S(1)}, bf16[1,6,256,128]{3,2,1,0:T(8,128)(2,1)S(1)}, u32[]{:S(2)}, u32[]{:S(2)}) collective-permute-start(bf16[1,6,256,128]{3,2,1,0:T(8,128)(2,1)S(1)} %slice_bitcast_fusion.1.refs_4_.refs_16_), channel_id=1, source_target_pairs={{0,2},{2,0},{4,6},{6,4},{8,10},{10,8},{12,14},{14,12},{16,18},{18,... | collective-permute-start | bytes 1179656 | tf_op jit(solution)/shard_map/ppermute | solution.py:216
  69.9 8.4 %copy-start.17 = (bf16[3,256,128]{2,1,0:T(8,128)(2,1)S(1)}, bf16[3,256,128]{2,1,0:T(8,128)(2,1)}, u32[]{:S(2)}) copy-start(bf16[3,256,128]{2,1,0:T(8,128)(2,1)} %get-tuple-element.31) | copy-start | bytes 589828
  69.9 9.0 %copy-start.2 = (bf16[3,256,128]{2,1,0:T(8,128)(2,1)S(1)}, bf16[3,256,128]{2,1,0:T(8,128)(2,1)}, u32[]{:S(2)}) copy-start(bf16[3,256,128]{2,1,0:T(8,128)(2,1)} %get-tuple-element.30.refs_2_) | copy-start | bytes 589828
  69.9 39.4 %copy-start.19 = (s32[32]{0:T(128)S(1)}, s32[32]{0:T(128)}, u32[]{:S(2)}) copy-start(s32[32]{0:T(128)} %param.8) | copy-start | bytes 388
  69.9 60.2 %copy-start = (bf16[9,256,128]{2,1,0:T(8,128)(2,1)S(1)}, bf16[9,256,128]{2,1,0:T(8,128)(2,1)}, u32[]{:S(2)}) copy-start(bf16[9,256,128]{2,1,0:T(8,128)(2,1)} %get-tuple-element.25.refs_0_) | copy-start | bytes 1769476
  76.0 7.8 %collective-permute-start.20 = (bf16[3,256,128]{2,1,0:T(8,128)(2,1)S(1)}, bf16[3,256,128]{2,1,0:T(8,128)(2,1)S(1)}, u32[]{:S(2)}, u32[]{:S(2)}) collective-permute-start(bf16[3,256,128]{2,1,0:T(8,128)(2,1)S(1)} %copy-done.18), channel_id=1, source_target_pairs={{0,8},{2,10},{4,12},{6,14},{8,0},{10,2},{12,4},{14,6},{16,24},{18,... | collective-permute-start | bytes 589832 | tf_op jit(solution)/shard_map/ppermute | solution.py:216
  76.8 28.5 %collective-permute-start.1 = (bf16[9,256,128]{2,1,0:T(8,128)(2,1)S(1)}, bf16[9,256,128]{2,1,0:T(8,128)(2,1)S(1)}, u32[]{:S(2)}, u32[]{:S(2)}) collective-permute-start(bf16[9,256,128]{2,1,0:T(8,128)(2,1)S(1)} %copy-done.16), channel_id=1, source_target_pairs={{0,8},{2,10},{4,12},{6,14},{8,0},{10,2},{12,4},{14,6},{16,24},{18,... | collective-permute-start | bytes 1769480 | tf_op jit(solution)/shard_map/ppermute | solution.py:216
  78.2 22.4 %collective-permute-start.16 = (bf16[3,256,128]{2,1,0:T(8,128)(2,1)S(1)}, bf16[3,256,128]{2,1,0:T(8,128)(2,1)S(1)}, u32[]{:S(2)}, u32[]{:S(2)}) collective-permute-start(bf16[3,256,128]{2,1,0:T(8,128)(2,1)S(1)} %copy-done.17), channel_id=1, source_target_pairs={{0,8},{2,10},{4,12},{6,14},{8,0},{10,2},{12,4},{14,6},{16,24},{18,... | collective-permute-start | bytes 589832 | tf_op jit(solution)/shard_map/ppermute | solution.py:216
  83.8 24.7 %copy-start.10 = (bf16[3,256,128]{2,1,0:T(8,128)(2,1)}, bf16[3,256,128]{2,1,0:T(8,128)(2,1)S(1)}, u32[]{:S(2)}) copy-start(bf16[3,256,128]{2,1,0:T(8,128)(2,1)S(1)} %collective-permute-done.20.refs_3_) | copy-start | bytes 589828
  83.8 20.7 %collective-permute-start.6 = (bf16[3,256,128]{2,1,0:T(8,128)(2,1)}, bf16[3,256,128]{2,1,0:T(8,128)(2,1)S(1)}, u32[]{:S(2)}, u32[]{:S(2)}) collective-permute-start(bf16[3,256,128]{2,1,0:T(8,128)(2,1)} %get-tuple-element.28), channel_id=1, source_target_pairs={{0,8},{2,10},{4,12},{6,14},{8,0},{10,2},{12,4},{14,6},{16,24},{18,... | collective-permute-start | bytes 589832 | tf_op jit(solution)/shard_map/ppermute | solution.py:216
  100.7 7.9 %collective-permute-start.21 = (bf16[2,2,256,128]{3,2,1,0:T(8,128)(2,1)}, bf16[2,2,256,128]{3,2,1,0:T(8,128)(2,1)}, u32[]{:S(2)}, u32[]{:S(2)}) collective-permute-start(bf16[2,2,256,128]{3,2,1,0:T(8,128)(2,1)} %pad_maximum_fusion.2.refs_12_.refs_24_), channel_id=1, source_target_pairs={{0,4},{2,6},{4,0},{6,2},{8,12},{10,14},{12,8},{14,10},{16,20},{18,... | collective-permute-start | bytes 786440 | tf_op jit(solution)/shard_map/ppermute | solution.py:216
  104.5 5.2 %collective-permute-start.22 = (bf16[2,2,256,128]{3,2,1,0:T(8,128)(2,1)}, bf16[2,2,256,128]{3,2,1,0:T(8,128)(2,1)}, u32[]{:S(2)}, u32[]{:S(2)}) collective-permute-start(bf16[2,2,256,128]{3,2,1,0:T(8,128)(2,1)} %pad_maximum_fusion.2.refs_12_.refs_24_), channel_id=1, source_target_pairs={{0,2},{2,0},{4,6},{6,4},{8,10},{10,8},{12,14},{14,12},{16,18},{18,... | collective-permute-start | bytes 786440 | tf_op jit(solution)/shard_map/ppermute | solution.py:216
  105.3 9.5 %collective-permute-start.17 = (bf16[2,2,256,128]{3,2,1,0:T(8,128)(2,1)}, bf16[2,2,256,128]{3,2,1,0:T(8,128)(2,1)}, u32[]{:S(2)}, u32[]{:S(2)}) collective-permute-start(bf16[2,2,256,128]{3,2,1,0:T(8,128)(2,1)} %pad_maximum_fusion.1.refs_12_.refs_24_), channel_id=1, source_target_pairs={{0,4},{2,6},{4,0},{6,2},{8,12},{10,14},{12,8},{14,10},{16,20},{18,... | collective-permute-start | bytes 786440 | tf_op jit(solution)/shard_map/ppermute | solution.py:216
  105.9 14.5 %collective-permute-start.13 = (bf16[2,2,256,128]{3,2,1,0:T(8,128)(2,1)S(1)}, bf16[2,2,256,128]{3,2,1,0:T(8,128)(2,1)}, u32[]{:S(2)}, u32[]{:S(2)}) collective-permute-start(bf16[2,2,256,128]{3,2,1,0:T(8,128)(2,1)S(1)} %pad_maximum_fusion.refs_12_.refs_24_), channel_id=1, source_target_pairs={{0,4},{2,6},{4,0},{6,2},{8,12},{10,14},{12,8},{14,10},{16,20},{18,... | collective-permute-start | bytes 786440 | tf_op jit(solution)/shard_map/ppermute | solution.py:216
  108.5 11.9 %collective-permute-start.23 = (bf16[2,2,256,128]{3,2,1,0:T(8,128)(2,1)}, bf16[2,2,256,128]{3,2,1,0:T(8,128)(2,1)}, u32[]{:S(2)}, u32[]{:S(2)}) collective-permute-start(bf16[2,2,256,128]{3,2,1,0:T(8,128)(2,1)} %collective-permute-done.21.refs_13_.refs_25_), channel_id=1, source_target_pairs={{0,2},{2,0},{4,6},{6,4},{8,10},{10,8},{12,14},{14,12},{16,18},{18,... | collective-permute-start | bytes 786440 | tf_op jit(solution)/shard_map/ppermute | solution.py:216
  108.5 19.8 %collective-permute-start.8 = (bf16[1,6,256,128]{3,2,1,0:T(8,128)(2,1)S(1)}, bf16[1,6,256,128]{3,2,1,0:T(8,128)(2,1)S(1)}, u32[]{:S(2)}, u32[]{:S(2)}) collective-permute-start(bf16[1,6,256,128]{3,2,1,0:T(8,128)(2,1)S(1)} %slice_bitcast_fusion.refs_5_.refs_17_), channel_id=1, source_target_pairs={{0,4},{2,6},{4,0},{6,2},{8,12},{10,14},{12,8},{14,10},{16,20},{18,... | collective-permute-start | bytes 1179656 | tf_op jit(solution)/shard_map/ppermute | solution.py:216
  109.7 36.5 %copy-start.3 = (bf16[3,256,128]{2,1,0:T(8,128)(2,1)S(1)}, bf16[3,256,128]{2,1,0:T(8,128)(2,1)}, u32[]{:S(2)}) copy-start(bf16[3,256,128]{2,1,0:T(8,128)(2,1)} %get-tuple-element.30.refs_2_) | copy-start | bytes 589828
  109.7 36.5 %copy-start.7 = (bf16[3,256,128]{2,1,0:T(8,128)(2,1)S(1)}, bf16[3,256,128]{2,1,0:T(8,128)(2,1)}, u32[]{:S(2)}) copy-start(bf16[3,256,128]{2,1,0:T(8,128)(2,1)} %copy-done.6) | copy-start | bytes 589828
  109.7 32.6 %collective-permute-start.18 = (bf16[2,2,256,128]{3,2,1,0:T(8,128)(2,1)}, bf16[2,2,256,128]{3,2,1,0:T(8,128)(2,1)S(1)}, u32[]{:S(2)}, u32[]{:S(2)}) collective-permute-start(bf16[2,2,256,128]{3,2,1,0:T(8,128)(2,1)} %pad_maximum_fusion.1.refs_12_.refs_24_), channel_id=1, source_target_pairs={{0,2},{2,0},{4,6},{6,4},{8,10},{10,8},{12,14},{14,12},{16,18},{18,... | collective-permute-start | bytes 786440 | tf_op jit(solution)/shard_map/ppermute | solution.py:216
  114.8 13.7 %collective-permute-start.11 = (bf16[1,6,256,128]{3,2,1,0:T(8,128)(2,1)S(1)}, bf16[1,6,256,128]{3,2,1,0:T(8,128)(2,1)S(1)}, u32[]{:S(2)}, u32[]{:S(2)}) collective-permute-start(bf16[1,6,256,128]{3,2,1,0:T(8,128)(2,1)S(1)} %collective-permute-done.7.refs_6_.refs_18_), channel_id=1, source_target_pairs={{0,2},{2,0},{4,6},{6,4},{8,10},{10,8},{12,14},{14,12},{16,18},{18,... | collective-permute-start | bytes 1179656 | tf_op jit(solution)/shard_map/ppermute | solution.py:216
  120.4 25.3 %collective-permute-start.19 = (bf16[2,2,256,128]{3,2,1,0:T(8,128)(2,1)}, bf16[2,2,256,128]{3,2,1,0:T(8,128)(2,1)S(1)}, u32[]{:S(2)}, u32[]{:S(2)}) collective-permute-start(bf16[2,2,256,128]{3,2,1,0:T(8,128)(2,1)} %collective-permute-done.17.refs_13_.refs_25_), channel_id=1, source_target_pairs={{0,2},{2,0},{4,6},{6,4},{8,10},{10,8},{12,14},{14,12},{16,18},{18,... | collective-permute-start | bytes 786440 | tf_op jit(solution)/shard_map/ppermute | solution.py:216
  120.4 8.6 %collective-permute-start.10 = (bf16[1,6,256,128]{3,2,1,0:T(8,128)(2,1)S(1)}, bf16[1,6,256,128]{3,2,1,0:T(8,128)(2,1)S(1)}, u32[]{:S(2)}, u32[]{:S(2)}) collective-permute-start(bf16[1,6,256,128]{3,2,1,0:T(8,128)(2,1)S(1)} %slice_bitcast_fusion.refs_5_.refs_17_), channel_id=1, source_target_pairs={{0,2},{2,0},{4,6},{6,4},{8,10},{10,8},{12,14},{14,12},{16,18},{18,... | collective-permute-start | bytes 1179656 | tf_op jit(solution)/shard_map/ppermute | solution.py:216
  128.3 1.7 collective-permute-start.12
  128.4 31.3 %copy-start.1 = (bf16[3,256,128]{2,1,0:T(8,128)(2,1)S(1)}, bf16[3,256,128]{2,1,0:T(8,128)(2,1)}, u32[]{:S(2)}) copy-start(bf16[3,256,128]{2,1,0:T(8,128)(2,1)} %get-tuple-element.27.refs_2_) | copy-start | bytes 589828
  128.4 31.3 %copy-start.5 = (bf16[3,256,128]{2,1,0:T(8,128)(2,1)S(1)}, bf16[3,256,128]{2,1,0:T(8,128)(2,1)}, u32[]{:S(2)}) copy-start(bf16[3,256,128]{2,1,0:T(8,128)(2,1)} %copy-done.4) | copy-start | bytes 589828
  128.5 27.3 %collective-permute-start.14 = (bf16[2,2,256,128]{3,2,1,0:T(8,128)(2,1)S(1)}, bf16[2,2,256,128]{3,2,1,0:T(8,128)(2,1)S(1)}, u32[]{:S(2)}, u32[]{:S(2)}) collective-permute-start(bf16[2,2,256,128]{3,2,1,0:T(8,128)(2,1)S(1)} %pad_maximum_fusion.refs_12_.refs_24_), channel_id=1, source_target_pairs={{0,2},{2,0},{4,6},{6,4},{8,10},{10,8},{12,14},{14,12},{16,18},{18,... | collective-permute-start | bytes 786440 | tf_op jit(solution)/shard_map/ppermute | solution.py:216
  129.0 27.1 %collective-permute-start.15 = (bf16[2,2,256,128]{3,2,1,0:T(8,128)(2,1)}, bf16[2,2,256,128]{3,2,1,0:T(8,128)(2,1)S(1)}, u32[]{:S(2)}, u32[]{:S(2)}) collective-permute-start(bf16[2,2,256,128]{3,2,1,0:T(8,128)(2,1)} %collective-permute-done.13.refs_13_.refs_25_), channel_id=1, source_target_pairs={{0,2},{2,0},{4,6},{6,4},{8,10},{10,8},{12,14},{14,12},{16,18},{18,... | collective-permute-start | bytes 786440 | tf_op jit(solution)/shard_map/ppermute | solution.py:216
  141.6 27.5 %collective-permute-start.26 = (bf16[256,128]{1,0:T(8,128)(2,1)S(1)}, bf16[256,128]{1,0:T(8,128)(2,1)S(1)}, u32[]{:S(2)}, u32[]{:S(2)}) collective-permute-start(bf16[256,128]{1,0:T(8,128)(2,1)S(1)} %get-tuple-element.38), channel_id=1, source_target_pairs={{0,8},{2,10},{4,12},{6,14},{8,0},{10,2},{12,4},{14,6},{16,24},{18,... | collective-permute-start | bytes 196616 | tf_op jit(solution)/shard_map/ppermute | solution.py:216
  142.3 27.3 %collective-permute-start.29 = (bf16[256,128]{1,0:T(8,128)(2,1)S(1)}, bf16[256,128]{1,0:T(8,128)(2,1)S(1)}, u32[]{:S(2)}, u32[]{:S(2)}) collective-permute-start(bf16[256,128]{1,0:T(8,128)(2,1)S(1)} %get-tuple-element.41), channel_id=1, source_target_pairs={{0,16},{2,18},{4,20},{6,22},{8,24},{10,26},{12,28},{14,30},{16,0},... | collective-permute-start | bytes 196616 | tf_op jit(solution)/shard_map/ppermute | solution.py:216
  145.8 34.0 %slice-start = ((s8[9437184]{0:T(1024)(128)(4,1)}), s8[4194304]{0:T(1024)(128)(4,1)S(1)}, s32[]{:S(2)}) async-start(s8[9437184]{0:T(1024)(128)(4,1)} %bitcast.37), calls=%async_computation | async-start | bytes 8388608
  145.8 34.0 %slice-start.1 = ((s8[9437184]{0:T(1024)(128)(4,1)}), s8[4194304]{0:T(1024)(128)(4,1)S(1)}, s32[]{:S(2)}) async-start(s8[9437184]{0:T(1024)(128)(4,1)} %bitcast.37), calls=%async_computation.1 | async-start | bytes 8388608
  145.8 34.0 %copy-start.12 = (s32[2]{0:T(128)S(1)}, s32[2]{0:T(128)}, u32[]{:S(2)}) copy-start(s32[2]{0:T(128)} %pad_add_fusion.s) | copy-start | bytes 28
  145.8 24.2 %collective-permute-start.32 = (bf16[256,128]{1,0:T(8,128)(2,1)S(1)}, bf16[256,128]{1,0:T(8,128)(2,1)S(1)}, u32[]{:S(2)}, u32[]{:S(2)}) collective-permute-start(bf16[256,128]{1,0:T(8,128)(2,1)S(1)} %get-tuple-element.44), channel_id=1, source_target_pairs={{0,24},{2,26},{4,28},{6,30},{8,16},{10,18},{12,20},{14,22},{16,8},... | collective-permute-start | bytes 196616 | tf_op jit(solution)/shard_map/ppermute | solution.py:216
  155.7 17.8 %collective-permute-start.25 = (bf16[256,128]{1,0:T(8,128)(2,1)S(1)}, bf16[256,128]{1,0:T(8,128)(2,1)S(1)}, u32[]{:S(2)}, u32[]{:S(2)}) collective-permute-start(bf16[256,128]{1,0:T(8,128)(2,1)S(1)} %get-tuple-element.37), channel_id=1, source_target_pairs={{0,8},{2,10},{4,12},{6,14},{8,0},{10,2},{12,4},{14,6},{16,24},{18,... | collective-permute-start | bytes 196616 | tf_op jit(solution)/shard_map/ppermute | solution.py:216
  156.1 23.6 %slice-start.2 = ((s8[9437184]{0:T(1024)(128)(4,1)}), s8[1048576]{0:T(1024)(128)(4,1)S(1)}, s32[]{:S(2)}) async-start(s8[9437184]{0:T(1024)(128)(4,1)} %bitcast.37), calls=%async_computation.2 | async-start | bytes 2097152
  156.1 17.9 %collective-permute-start.28 = (bf16[256,128]{1,0:T(8,128)(2,1)S(1)}, bf16[256,128]{1,0:T(8,128)(2,1)S(1)}, u32[]{:S(2)}, u32[]{:S(2)}) collective-permute-start(bf16[256,128]{1,0:T(8,128)(2,1)S(1)} %get-tuple-element.40), channel_id=1, source_target_pairs={{0,16},{2,18},{4,20},{6,22},{8,24},{10,26},{12,28},{14,30},{16,0},... | collective-permute-start | bytes 196616 | tf_op jit(solution)/shard_map/ppermute | solution.py:216
  169.1 6.1 %collective-permute-start.31 = (bf16[256,128]{1,0:T(8,128)(2,1)S(1)}, bf16[256,128]{1,0:T(8,128)(2,1)S(1)}, u32[]{:S(2)}, u32[]{:S(2)}) collective-permute-start(bf16[256,128]{1,0:T(8,128)(2,1)S(1)} %get-tuple-element.43), channel_id=1, source_target_pairs={{0,24},{2,26},{4,28},{6,30},{8,16},{10,18},{12,20},{14,22},{16,8},... | collective-permute-start | bytes 196616 | tf_op jit(solution)/shard_map/ppermute | solution.py:216
  169.6 5.6 %collective-permute-start.24 = (bf16[256,128]{1,0:T(8,128)(2,1)S(1)}, bf16[256,128]{1,0:T(8,128)(2,1)S(1)}, u32[]{:S(2)}, u32[]{:S(2)}) collective-permute-start(bf16[256,128]{1,0:T(8,128)(2,1)S(1)} %get-tuple-element.36), channel_id=1, source_target_pairs={{0,8},{2,10},{4,12},{6,14},{8,0},{10,2},{12,4},{14,6},{16,24},{18,... | collective-permute-start | bytes 196616 | tf_op jit(solution)/shard_map/ppermute | solution.py:216
  170.0 8.4 %collective-permute-start.27 = (bf16[256,128]{1,0:T(8,128)(2,1)S(1)}, bf16[256,128]{1,0:T(8,128)(2,1)S(1)}, u32[]{:S(2)}, u32[]{:S(2)}) collective-permute-start(bf16[256,128]{1,0:T(8,128)(2,1)S(1)} %get-tuple-element.39), channel_id=1, source_target_pairs={{0,16},{2,18},{4,20},{6,22},{8,24},{10,26},{12,28},{14,30},{16,0},... | collective-permute-start | bytes 196616 | tf_op jit(solution)/shard_map/ppermute | solution.py:216
  173.6 6.2 %collective-permute-start.30 = (bf16[256,128]{1,0:T(8,128)(2,1)S(1)}, bf16[256,128]{1,0:T(8,128)(2,1)S(1)}, u32[]{:S(2)}, u32[]{:S(2)}) collective-permute-start(bf16[256,128]{1,0:T(8,128)(2,1)S(1)} %get-tuple-element.42), channel_id=1, source_target_pairs={{0,24},{2,26},{4,28},{6,30},{8,16},{10,18},{12,20},{14,22},{16,8},... | collective-permute-start | bytes 196616 | tf_op jit(solution)/shard_map/ppermute | solution.py:216
  182.6 17.0 %collective-permute-start.33 = (bf16[256,1536]{1,0:T(8,128)(2,1)S(1)}, bf16[256,1536]{1,0:T(8,128)(2,1)S(1)}, u32[]{:S(2)}, u32[]{:S(2)}) collective-permute-start(bf16[256,1536]{1,0:T(8,128)(2,1)S(1)} %shard_map.81), channel_id=1, source_target_pairs={{0,1},{1,0},{2,3},{3,2},{4,5},{5,4},{6,7},{7,6},{8,9},{9,8},{10,11... | collective-permute-start | bytes 2359304 | tf_op jit(solution)/shard_map/ppermute | solution.py:213
  (9 other events, 29.2 us)

commit v3 on v2

v3 whole, which is shorter than its diff:
```python
import functools
import math

import jax
import jax.numpy as jnp
from jax import lax
from jax.experimental import pallas as pl
from jax.experimental.pallas import tpu as pltpu
from jax.sharding import PartitionSpec as P

HEAD_DIM = 128
BLOCK = 128
Z, X, C = 4, 2, 2
MIB = 1 << 20
BF16, F32 = jnp.bfloat16, jnp.float32
LIGHT = pl.CostEstimate(flops=1024, bytes_accessed=1024, transcendentals=0)


def place(z, x, c):
    return (z * X + x) * C + c


def hop(dz, dx, dc):
    return [
        (place(z, x, c), place(z ^ dz, x ^ dx, c ^ dc))
        for z in range(Z)
        for x in range(X)
        for c in range(C)
    ]


def params(mib):
    return pltpu.CompilerParams(vmem_limit_bytes=mib * MIB)


def after(value, *others):
    return lax.optimization_barrier((value, *others))[0]


def whole(count):
    return [pl.BlockSpec(memory_space=pltpu.VMEM)] * count


def fetch(where, weights, width):
    depth = weights[0].shape[0]
    half = depth // 2
    kinds = len(weights)

    def body(s, *refs):
        out, sems = refs[kinds], refs[kinds + 1]
        copies = []
        for g in range(2):
            columns = pl.ds(pl.multiple_of((s[1] ^ g) * width, width), width)
            for k in range(kinds):
                for part in range(2):
                    rows = pl.ds(pl.multiple_of((s[0] ^ part) * half, half), half)
                    copies.append(
                        pltpu.make_async_copy(
                            refs[k].at[rows, columns],
                            out.at[g * kinds + k, pl.ds(part * half, half)],
                            sems.at[len(copies)],
                        )
                    )
        for copy in copies:
            copy.start()
        for copy in copies:
            copy.wait()

    return pl.pallas_call(
        body,
        grid_spec=pltpu.PrefetchScalarGridSpec(
            num_scalar_prefetch=1,
            grid=(),
            in_specs=[pl.BlockSpec(memory_space=pl.ANY)] * kinds,
            out_specs=pl.BlockSpec(memory_space=pltpu.VMEM),
            scratch_shapes=[pltpu.SemaphoreType.DMA((4 * kinds,))],
        ),
        out_shape=pltpu.VMEM((2 * kinds, depth, width), BF16),
        compiler_params=params(4),
        cost_estimate=LIGHT,
    )(where, *weights)


def project(own, other, held, outputs):
    rows = own.shape[0]
    kinds = held.shape[0] // 2
    flat = [block for blocks in outputs for block in blocks]

    def body(own_ref, other_ref, held_ref, *outs):
        tokens = jnp.concatenate([own_ref[...], other_ref[...]], axis=1)
        at = [(o, i) for o, blocks in enumerate(outputs) for i in range(len(blocks))]
        for start in range(0, len(flat), 2):
            pair = flat[start : start + 2]
            weight = [
                held_ref[g * kinds + k, :, h * HEAD_DIM : (h + 1) * HEAD_DIM] for g, k, h in pair
            ]
            total = jnp.dot(
                tokens, jnp.concatenate(weight, axis=1), preferred_element_type=F32
            ).astype(BF16)
            for i in range(len(pair)):
                o, place_in = at[start + i]
                outs[o][place_in] = total[:, i * HEAD_DIM : (i + 1) * HEAD_DIM]

    return pl.pallas_call(
        body,
        in_specs=whole(3),
        out_specs=whole(len(outputs)),
        out_shape=[jax.ShapeDtypeStruct((len(b), rows, HEAD_DIM), BF16) for b in outputs],
        compiler_params=params(16),
        cost_estimate=LIGHT,
    )(own, other, held)


def attend(queries, parts, bias, fence):
    rows = queries[0][0].shape[1]
    tile = parts[0][0].shape[1]
    n = len(parts)
    group = 4
    scale = math.log2(math.e) / math.sqrt(HEAD_DIM)
    per = rows // BLOCK
    both = 2 * rows

    def body(*refs):
        q_refs, k_refs, v_refs = refs[:Z], refs[Z : Z + n], refs[Z + n : Z + 2 * n]
        bias_ref = refs[Z + 2 * n]
        outs = refs[Z + 2 * n + 2 : Z + 2 * n + 2 + Z]
        q_ref = refs[-1]
        step = pl.program_id(0)
        for i in range(Z // 2):

            @pl.when(step == i)
            def _(i=i):
                q_ref[:rows] = q_refs[2 * i][0]
                q_ref[rows:] = q_refs[2 * i + 1][0]

        query = q_ref[...]
        top = jnp.full((both, 1), -1e30, F32)
        total = jnp.zeros((both, HEAD_DIM), F32)
        accum = jnp.zeros((both, HEAD_DIM), F32)
        for t in range(0, n, group):
            key = jnp.concatenate([k_refs[u][0] for u in range(t, t + group)], axis=0)
            value = jnp.concatenate([v_refs[u][0] for u in range(t, t + group)], axis=0)
            width = group * tile
            score = lax.dot_general(
                query, key, (((1,), (1,)), ((), ())), preferred_element_type=F32
            )
            keep = [
                jnp.broadcast_to(
                    bias_ref[pl.ds(step * 2 * per + r, 1), t * tile : t * tile + width],
                    (BLOCK, width),
                )
                for r in range(2 * per)
            ]
            score = score + jnp.concatenate(keep, axis=0)
            best = score[:, :HEAD_DIM]
            for u in range(HEAD_DIM, width, HEAD_DIM):
                best = jnp.maximum(best, score[:, u : u + HEAD_DIM])
            top_next = jnp.maximum(top, jnp.max(best, axis=1, keepdims=True))
            factor = jnp.exp2((top - top_next) * scale)
            top = top_next
            weight = jnp.exp2(score * scale - top * scale)
            add = weight[:, :HEAD_DIM]
            for u in range(HEAD_DIM, width, HEAD_DIM):
                add = add + weight[:, u : u + HEAD_DIM]
            total = total * factor + add
            accum = accum * factor + jnp.dot(
                weight.astype(BF16), value, preferred_element_type=F32
            )
        result = (accum / jnp.sum(total, axis=1, keepdims=True)).astype(BF16)
        for i in range(Z // 2):

            @pl.when(step == i)
            def _(i=i):
                outs[2 * i][...] = result[:rows]
                outs[2 * i + 1][...] = result[rows:]

    def block_spec(index):
        return pl.BlockSpec((1, rows, HEAD_DIM), lambda i: (index, 0, 0))

    return pl.pallas_call(
        body,
        grid=(Z // 2,),
        in_specs=[block_spec(at) for _, at in queries]
        + [block_spec(k) for _, k, _ in parts]
        + [block_spec(v) for _, _, v in parts]
        + [pl.BlockSpec(bias.shape, lambda i: (0, 0)), pl.BlockSpec(memory_space=pl.ANY)],
        out_specs=[pl.BlockSpec((rows, HEAD_DIM), lambda i: (0, 0))] * Z,
        out_shape=[jax.ShapeDtypeStruct((rows, HEAD_DIM), BF16)] * Z,
        scratch_shapes=[pltpu.VMEM((both, HEAD_DIM), BF16)],
        compiler_params=params(24),
        cost_estimate=LIGHT,
    )(*[q for q, _ in queries], *[p for p, _, _ in parts], *[p for p, _, _ in parts], bias, fence)


def mix(where, attended, w_out, flip, step_width):
    rows = attended[0].shape[0]
    depth = w_out.shape[0] // Z
    half = w_out.shape[1] // 2
    steps = half // step_width
    count = len(attended)

    def body(s, *refs):
        rows_all = jnp.concatenate([r[...] for r in refs[:count]], axis=1)
        weight = jnp.concatenate([r[...] for r in refs[count : count + Z]], axis=0)
        refs[-1][...] = jnp.dot(rows_all, weight, preferred_element_type=F32).astype(BF16)

    def weight_spec(dz):
        return pl.BlockSpec(
            (depth, step_width),
            lambda i, s: (s[1] ^ dz, (1 - s[0] if flip else s[0]) * steps + i),
        )

    return pl.pallas_call(
        body,
        grid_spec=pltpu.PrefetchScalarGridSpec(
            num_scalar_prefetch=1,
            grid=(steps,),
            in_specs=[pl.BlockSpec(a.shape, lambda i, s: (0, 0)) for a in attended]
            + [weight_spec(dz) for dz in range(Z)],
            out_specs=pl.BlockSpec((rows, step_width), lambda i, s: (0, i)),
        ),
        out_shape=jax.ShapeDtypeStruct((rows, half), BF16),
        compiler_params=params(24),
        cost_estimate=LIGHT,
    )(where, *attended, *([w_out] * Z))


def split_heads(tokens, block_order, block_mask, w_query, w_key, w_value, w_out):
    rows, half = tokens.shape
    group_heads = w_query.shape[1] // HEAD_DIM // Z
    block_count = block_order.shape[0]
    per = rows // BLOCK
    cut = rows // 2
    ctx = lax.axis_index("ctx")
    y = lax.axis_index("head")
    z, x, c = ctx // (X * C), (ctx // C) % X, ctx % C
    where = jnp.stack([y, z]).astype(jnp.int32)
    weights = (w_query, w_key, w_value)

    def over_y(a):
        return lax.ppermute(a, "head", [(0, 1), (1, 0)])

    def over(a, dz, dx, dc):
        return lax.ppermute(a, "ctx", hop(dz, dx, dc))

    held = [pltpu.with_memory_space_constraint(w, pltpu.HBM) for w in weights]
    other = over_y(tokens)
    far = [over(tokens[i * cut : (i + 1) * cut], 2, 0, 0) for i in range(2)]

    def blocks(pairs):
        first = jnp.stack([place(z ^ dz, x ^ dx, c ^ dc) for dz, dx, dc in pairs]) * per
        return (first[:, None] + jnp.arange(per)[None, :]).reshape(-1)

    sides = ((0, 0), (1, 0), (0, 1), (1, 1))
    query_blocks = blocks([(dz, 0, 0) for dz in range(Z)])
    key_blocks = blocks([(dz, dx, dc) for dz in range(Z) for dx, dc in sides])
    frames = jnp.arange(block_count, dtype=jnp.int32)
    order_hot = (block_order[:, None] == frames[None, :]).astype(F32)

    def pick(wanted):
        place_hot = (wanted[:, None] == frames[None, :]).astype(F32)
        return jnp.dot(place_hot, order_hot)

    live = jnp.dot(jnp.dot(pick(query_blocks), block_mask.astype(F32)), pick(key_blocks).T)
    bias = jnp.repeat(jnp.where(live > 0.5, 0.0, -1e30).astype(F32), BLOCK, axis=1)

    heads = range(group_heads)
    span = group_heads * HEAD_DIM

    def pairs(group, wanted):
        return [(group, kind, h) for kind in (1, 2) for h in wanted]

    def singles(group):
        return [(group, 0, h) for h in heads]

    held = fetch(where, held, span)

    far_other = [over_y(far[0])]
    own_q, own_kv, sent_q, sent_kv = project(
        after(tokens, far[0]),
        other,
        held,
        [singles(0), pairs(0, heads), singles(1), pairs(1, heads)],
    )
    came_kv = over(sent_kv, 1, 0, 0)
    came_q = over(sent_q, 1, 0, 0)
    own_across = over(own_kv, 0, 1, 0)
    own_core = over(own_kv, 0, 0, 1)
    far_other.append(over_y(after(far[1], own_kv)))
    came_kv = after(came_kv, far[1])
    came_across = over(came_kv, 0, 1, 0)
    came_core = over(came_kv, 0, 0, 1)
    own_across_core = over(after(own_across, came_kv), 0, 0, 1)

    far = after(jnp.concatenate(far, axis=0), came_kv, own_across)
    far_other = jnp.concatenate(far_other, axis=0)
    first, rest = (0,), tuple(heads)[1:]
    far_sent_kv, far_sent_q = project(far, far_other, held, [pairs(1, first), singles(1)])
    far_came_kv = over(far_sent_kv, 1, 0, 0)
    far_came_q = over(far_sent_q, 1, 0, 0)
    (far_sent_kv2,) = project(after(far, far_sent_kv), far_other, held, [pairs(1, rest)])
    far_came_kv2 = over(far_sent_kv2, 1, 0, 0)
    far_q, far_kv = project(
        after(far, far_sent_kv2), far_other, held, [singles(0), pairs(0, heads)]
    )

    def spread(part):
        across = over(part, 0, 1, 0)
        return [part, across, over(part, 0, 0, 1), over(across, 0, 0, 1)]

    far_kept = spread(far_kv)
    came_across_core = over(came_across, 0, 0, 1)
    far_first = spread(after(far_came_kv, far_kv))
    far_rest = spread(after(far_came_kv2, far_first[0]))
    near = [[own_kv, own_across, own_core, own_across_core]]
    near.append([came_kv, came_across, came_core, came_across_core])

    results = []
    for j in heads:
        queries = [(own_q, j), (came_q, j), (far_q, j), (far_came_q, j)]
        parts = [(a, j, group_heads + j) for a in near[0] + near[1] + far_kept]
        if j == 0:
            parts += [(a, 0, 1) for a in far_first]
        else:
            parts += [(a, j - 1, group_heads - 1 + j - 1) for a in far_rest]
        results.append(attend(queries, parts, bias, results[-1][0] if j else far_rest[1]))
    results = [[r[0]] + [over(r[dz], dz, 0, 0) for dz in range(1, Z)] for r in results]
    attended = [results[j][dz] for dz in range(Z) for j in range(group_heads)]
    arrived = over_y(mix(where, attended, w_out, True, 512))
    home = mix(where, attended, w_out, False, 512)
    return (home.astype(F32) + arrived.astype(F32)).astype(BF16)


def gather_all(tokens, block_order, block_mask, w_query, w_key, w_value, w_out):
    row_count = tokens.shape[0]
    local_width = w_query.shape[1]
    local_heads = local_width // HEAD_DIM
    block_count = block_order.shape[0]
    portion = lax.all_gather(tokens, "head", axis=1, tiled=True)
    query_rows, key_rows, value_rows = [
        jnp.dot(portion, weight, preferred_element_type=F32)
        .astype(BF16)
        .reshape(row_count, local_heads, HEAD_DIM)
        for weight in (w_query, w_key, w_value)
    ]
    cycle_live = block_mask[block_order][:, block_order]
    row_blocks = (
        lax.axis_index("ctx") * row_count + jnp.arange(row_count, dtype=jnp.int32)
    ) // BLOCK
    live_columns = cycle_live[row_blocks].T
    inv_root = 1.0 / HEAD_DIM**0.5

    def advance(state, inputs):
        key_tile, value_tile, offset = inputs
        keep = lax.dynamic_index_in_dim(live_columns, offset, 0, keepdims=False) > 0
        top_now, total_now, accum = state
        scores = (
            jnp.einsum("qhd,khd->hqk", query_rows, key_tile, preferred_element_type=F32)
            * inv_root
        )
        allowed = keep[None, :, None]
        top_next = jnp.maximum(top_now, jnp.max(jnp.where(allowed, scores, -1e30), axis=-1))
        factor = jnp.exp(top_now - top_next)
        weights = jnp.where(allowed, jnp.exp(scores - top_next[..., None]), 0.0)
        total_next = total_now * factor + jnp.sum(weights, axis=-1)
        accum = accum * factor[..., None] + jnp.einsum(
            "hqk,khd->hqd", weights.astype(BF16), value_tile, preferred_element_type=F32
        )
        return (top_next, total_next, accum), None

    initial = (
        jnp.full((local_heads, row_count), -1e30, F32),
        jnp.zeros((local_heads, row_count), F32),
        jnp.zeros((local_heads, row_count, HEAD_DIM), F32),
    )
    tiles = [
        lax.all_gather(part, "ctx", axis=0, tiled=True).reshape(
            block_count, BLOCK, local_heads, HEAD_DIM
        )
        for part in (key_rows, value_rows)
    ]
    (_, total, accum), _ = lax.scan(
        advance, initial, (*tiles, jnp.arange(block_count, dtype=jnp.int32))
    )
    attended = (
        (accum / total[..., None]).transpose(1, 0, 2).reshape(row_count, local_width).astype(BF16)
    )
    partial_out = jnp.dot(attended, w_out, preferred_element_type=F32)
    return lax.psum_scatter(partial_out.astype(BF16), "head", scatter_dimension=1, tiled=True)


def solution(mesh):
    in_specs = (
        P("ctx", "head"),
        P(),
        P(),
        P(None, "head"),
        P(None, "head"),
        P(None, "head"),
        P("head", None),
    )

    def per_device(tokens, block_order, block_mask, w_query, w_key, w_value, w_out):
        args = (tokens, block_order, block_mask, w_query, w_key, w_value, w_out)
        heads = w_query.shape[1] // HEAD_DIM
        fits = mesh.shape["ctx"] == Z * X * C and mesh.shape["head"] == 2 and heads % Z == 0
        return split_heads(*args) if fits else gather_all(*args)

    return jax.shard_map(
        per_device, mesh=mesh, in_specs=in_specs, out_specs=P("ctx", "head"), check_vma=False
    )
```

time: 201 us -> 191 us (0.950); the launches traced: 201 us -> 188 us
  waiting for transfers between devices: 92.5 us -> 70.5 us
  local copies, waits for them, and re-layouts: 7.43 us -> 28.6 us
  Pallas kernels: 64.2 us -> 45.1 us
  starting transfers between devices: 31.5 us -> 38.5 us
    ppermute x30 -> x31, waiting for transfers between devices: 79.8 us -> 55.1 us  [over(): return lax.ppermute(a, 'ctx', hop(dz, dx, dc))]
    unnamed x48 -> x45, local copies, waits for them, and re-layouts: 3.77 us -> 25.6 us
    pallas_call x7 -> x8, Pallas kernels: 58.5 us -> 39.4 us  [the longest x3 24 us: attend(): pl.pallas_call(body, grid=(Z // 2,), in_specs=[block_spec(at) for _, at i...]
    ppermute x30 -> x31, starting transfers between devices: 26.1 us -> 32 us  [over(): return lax.ppermute(a, 'ctx', hop(dz, dx, dc))]
    ppermute x4, waiting for transfers between devices: 12.7 us -> 15.4 us  [over_y(): return lax.ppermute(a, 'head', [(0, 1), (1, 0)])]
  transfers between devices with their start and end apart: 34 -> 35, of which waited for: 14 -> 12; matrix products, arithmetic and copies ran while one was open for 4% -> 4% of each run, Pallas kernels for 31% -> 21%
where the time goes in v3:
time: 191 us; the launch traced here: 188 us
  waiting for transfers between devices  70.5 us (37%)
  Pallas kernels  45.1 us (24%)
  starting transfers between devices  38.5 us (20%)
  local copies, waits for them, and re-layouts  28.6 us (15%)
  matrix products  2.57 us (1%)
  other arithmetic  2.45 us (1%)
    ppermute x31, waiting for transfers between devices, over(): return lax.ppermute(a, 'ctx', hop(dz, dx, dc))  55.1 us
    ppermute x31, starting transfers between devices, over(): return lax.ppermute(a, 'ctx', hop(dz, dx, dc))  32 us
    unnamed x45, local copies, waits for them, and re-layouts  25.6 us
    pallas_call x3, Pallas kernels, attend(): pl.pallas_call(body, grid=(Z // 2,), in_specs=[block_spec(at) for _, at i...  24 us
    ppermute x4, waiting for transfers between devices, over_y(): return lax.ppermute(a, 'head', [(0, 1), (1, 0)])  15.4 us
    pallas_call x4, Pallas kernels, project(): pl.pallas_call(body, in_specs=whole(3), out_specs=whole(len(outputs)), ou...  9.6 us
    ppermute x4, starting transfers between devices, over_y(): return lax.ppermute(a, 'head', [(0, 1), (1, 0)])  6.5 us
    pallas_call x1, Pallas kernels, fetch(): pl.pallas_call(body, grid_spec=pltpu.PrefetchScalarGridSpec(num_scalar_pr...  5.84 us
  transfers between devices with their start and end apart: 35, of which 12 were waited for; matrix products, arithmetic and copies ran while one was open for 4% of the time, Pallas kernels for 21%

profile of v3, /device:TPU:0, one launch (start us, length us, event | category | flops | bytes accessed | tf_op | source)
XLA Modules:
  0.0 187.9 jit_solution(13841345335034122516)
XLA Ops:
  0.0 3.0 %collective-permute-start.1 = (bf16[256,1536]{1,0:T(8,128)(2,1)}, bf16[256,1536]{1,0:T(8,128)(2,1)S(1)}, u32[]{:S(2)}, u32[]{:S(2)}) collective-permute-start(bf16[256,1536]{1,0:T(8,128)(2,1)} %own_ref), channel_id=1, source_target_pairs={{0,1},{1,0},{2,3},{3,2},{4,5},{5,4},{6,7},{7,6},{8,9},{9,8},{10,11... | collective-permute-start | bytes 2359304 | tf_op jit(solution)/shard_map/ppermute | solution.py:241
  3.0 1.2 fusion.21
  4.1 2.7 %collective-permute-start = (bf16[128,1536]{1,0:T(8,128)(2,1)S(1)}, bf16[128,1536]{1,0:T(8,128)(2,1)S(1)}, u32[]{:S(2)}, u32[]{:S(2)}) collective-permute-start(bf16[128,1536]{1,0:T(8,128)(2,1)S(1)} %get-tuple-element.64), channel_id=1, source_target_pairs={{0,16},{2,18},{4,20},{6,22},{8,24},{10,26},{12,28},{14,30},{16,0},... | collective-permute-start | bytes 1179656 | tf_op jit(solution)/shard_map/ppermute | solution.py:244
  7.1 26.6 %collective-permute-done = bf16[128,1536]{1,0:T(8,128)(2,1)S(1)} collective-permute-done((bf16[128,1536]{1,0:T(8,128)(2,1)S(1)}, bf16[128,1536]{1,0:T(8,128)(2,1)S(1)}, u32[]{:S(2)}, u32[]{:S(2)}) %collective-permute-start) | collective-permute-done | bytes 393248 | tf_op jit(solution)/shard_map/ppermute | solution.py:244
  34.2 5.8 %shard_map.73.held_ref = bf16[6,3072,384]{2,1,0:T(8,128)(2,1)S(1)} custom-call(s32[2]{0:T(128)S(1)} %pad_add_fusion.s, bf16[3072,1536]{1,0:T(8,128)(2,1)} %refs_0_.1, bf16[3072,1536]{1,0:T(8,128)(2,1)} %refs_1_.1, bf16[3072,1536]{1,0:T(8,128)(2,1)} %refs_2_.1), custom_call_target="tpu_custom_call" | custom-call | flops 1024 | bytes 1024 | tf_op jit(solution)/shard_map/pallas_call | solution.py:69
  40.1 5.0 %copy-done = bf16[6,3072,384]{2,1,0:T(8,128)(2,1)} copy-done((bf16[6,3072,384]{2,1,0:T(8,128)(2,1)}, bf16[6,3072,384]{2,1,0:T(8,128)(2,1)S(1)}, u32[]{:S(2)}) %copy-start) | copy-done | bytes 14155800
  45.2 5.0 %copy-done.1 = bf16[6,3072,384]{2,1,0:T(8,128)(2,1)S(1)} copy-done((bf16[6,3072,384]{2,1,0:T(8,128)(2,1)S(1)}, bf16[6,3072,384]{2,1,0:T(8,128)(2,1)}, u32[]{:S(2)}) %copy-start.1) | copy-done | bytes 14155800
  50.2 3.8 %shard_map.74 = (bf16[3,256,128]{2,1,0:T(8,128)(2,1)S(1)}, bf16[6,256,128]{2,1,0:T(8,128)(2,1)S(1)}, bf16[3,256,128]{2,1,0:T(8,128)(2,1)S(1)}, bf16[6,256,128]{2,1,0:T(8,128)(2,1)S(1)}) custom-call(bf16[256,1536]{1,0:T(8,128)(2,1)S(1)} %copy-done.3, bf16[256,1536]{1,0:T(8,128)(2,1)S(1)} %collective-permute-done.1.other_ref, bf16[6,3072,384]{2,1,0:T(8,128)(2,1)S(1)} %copy-done.1), custom_call_target="tpu_custom_call" | custom-call | flops 1024 | bytes 1024 | tf_op jit(solution)/shard_map/pallas_call | solution.py:104
  54.1 1.6 collective-permute-start.5
  55.7 1.5 collective-permute-start.7
  57.3 1.1 pad_maximum_fusion.own_ref
  58.4 1.0 constant_dynamic-update-slice_fusion.1
  59.4 3.3 %collective-permute-done.4.refs_8_.refs_24_ = bf16[6,256,128]{2,1,0:T(8,128)(2,1)S(1)} collective-permute-done((bf16[6,256,128]{2,1,0:T(8,128)(2,1)S(1)}, bf16[6,256,128]{2,1,0:T(8,128)(2,1)S(1)}, u32[]{:S(2)}, u32[]{:S(2)}) %collective-permute-start.4) | collective-permute-done | bytes 393248 | tf_op jit(solution)/shard_map/ppermute | solution.py:244
  62.7 1.5 collective-permute-done.5.refs_5_.refs_21_
  64.2 1.4 collective-permute-done.7
  65.6 1.9 %shard_map.75 = (bf16[2,256,128]{2,1,0:T(8,128)(2,1)}, bf16[3,256,128]{2,1,0:T(8,128)(2,1)S(1)}) custom-call(bf16[256,1536]{1,0:T(8,128)(2,1)S(1)} %pad_maximum_fusion.own_ref, bf16[256,1536]{1,0:T(8,128)(2,1)S(1)} %constant_dynamic-update-slice_fusion.other_ref, bf16[6,3072,384]{2,1,0:T(8,128)(2,1)S(1)} %copy-done.1), custom_call_target="tpu_custom_call" | custom-call | flops 1024 | bytes 1024 | tf_op jit(solution)/shard_map/pallas_call | solution.py:104
  68.6 1.7 shard_map.76
  70.3 1.7 collective-permute-start.21
  72.3 5.0 %copy-done.2 = bf16[6,3072,384]{2,1,0:T(8,128)(2,1)S(1)} copy-done((bf16[6,3072,384]{2,1,0:T(8,128)(2,1)S(1)}, bf16[6,3072,384]{2,1,0:T(8,128)(2,1)}, u32[]{:S(2)}) %copy-start.2) | copy-done | bytes 14155800
  77.3 2.2 %shard_map.77 = (bf16[3,256,128]{2,1,0:T(8,128)(2,1)S(1)}, bf16[6,256,128]{2,1,0:T(8,128)(2,1)S(1)}) custom-call(bf16[256,1536]{1,0:T(8,128)(2,1)S(1)} %pad_maximum_fusion.own_ref, bf16[256,1536]{1,0:T(8,128)(2,1)S(1)} %constant_dynamic-update-slice_fusion.other_ref, bf16[6,3072,384]{2,1,0:T(8,128)(2,1)S(1)} %copy-done.2), custom_call_target="tpu_custom_call" | custom-call | flops 1024 | bytes 1024 | tf_op jit(solution)/shard_map/pallas_call | solution.py:104
  80.7 1.6 fusion.3
  82.7 1.7 collective-permute-start.8
  84.3 2.0 %collective-permute-done.18.refs_17_.refs_33_ = bf16[2,256,128]{2,1,0:T(8,128)(2,1)} collective-permute-done((bf16[2,256,128]{2,1,0:T(8,128)(2,1)}, bf16[2,256,128]{2,1,0:T(8,128)(2,1)}, u32[]{:S(2)}, u32[]{:S(2)}) %collective-permute-start.18) | collective-permute-done | bytes 131104 | tf_op jit(solution)/shard_map/ppermute | solution.py:244
  86.9 3.4 %collective-permute-done.2.refs_1_ = bf16[3,256,128]{2,1,0:T(8,128)(2,1)S(1)} collective-permute-done((bf16[3,256,128]{2,1,0:T(8,128)(2,1)}, bf16[3,256,128]{2,1,0:T(8,128)(2,1)S(1)}, u32[]{:S(2)}, u32[]{:S(2)}) %collective-permute-start.2) | collective-permute-done | bytes 196640 | tf_op jit(solution)/shard_map/ppermute | solution.py:244
  90.9 1.5 collective-permute-start.11
  92.4 1.3 collective-permute-done.8.refs_3_
  94.4 1.5 collective-permute-start.14
  97.9 1.0 fusion.9
  99.8 3.2 %collective-permute-done.11.refs_9_.refs_25_ = bf16[6,256,128]{2,1,0:T(8,128)(2,1)S(1)} collective-permute-done((bf16[6,256,128]{2,1,0:T(8,128)(2,1)S(1)}, bf16[6,256,128]{2,1,0:T(8,128)(2,1)S(1)}, u32[]{:S(2)}, u32[]{:S(2)}) %collective-permute-start.11) | collective-permute-done | bytes 393248 | tf_op jit(solution)/shard_map/ppermute | solution.py:244
  103.5 7.9 %collective-permute-done.14.refs_13_.refs_29_ = bf16[6,256,128]{2,1,0:T(8,128)(2,1)S(1)} collective-permute-done((bf16[6,256,128]{2,1,0:T(8,128)(2,1)S(1)}, bf16[6,256,128]{2,1,0:T(8,128)(2,1)S(1)}, u32[]{:S(2)}, u32[]{:S(2)}) %collective-permute-start.14) | collective-permute-done | bytes 393248 | tf_op jit(solution)/shard_map/ppermute | solution.py:244
  111.4 3.4 %collective-permute-done.22.refs_37_.refs_17_.refs_33_ = bf16[4,256,128]{2,1,0:T(8,128)(2,1)} collective-permute-done((bf16[4,256,128]{2,1,0:T(8,128)(2,1)}, bf16[4,256,128]{2,1,0:T(8,128)(2,1)}, u32[]{:S(2)}, u32[]{:S(2)}) %collective-permute-start.22) | collective-permute-done | bytes 262176 | tf_op jit(solution)/shard_map/ppermute | solution.py:244
  116.6 0.9 copy-done.7
  117.5 0.9 copy-done.9
  121.1 7.9 %shard_map.78 = (bf16[256,128]{1,0:T(8,128)(2,1)S(1)}, bf16[256,128]{1,0:T(8,128)(2,1)S(1)}, bf16[256,128]{1,0:T(8,128)(2,1)S(1)}, bf16[256,128]{1,0:T(8,128)(2,1)S(1)}) custom-call(bf16[3,256,128]{2,1,0:T(8,128)(2,1)S(1)} %copy-done.5, bf16[3,256,128]{2,1,0:T(8,128)(2,1)S(1)} %copy-done.9, bf16[3,256,128]{2,1,0:T(8,128)(2,1)S(1)} %copy-done.7, ...), custom_call_target="tpu_custom_call" | custom-call | flops 1024 | bytes 1024 | tf_op jit(solution)/shard_map/pallas_call | solution.py:180
  129.5 8.1 %shard_map.79 = (bf16[256,128]{1,0:T(8,128)(2,1)S(1)}, bf16[256,128]{1,0:T(8,128)(2,1)S(1)}, bf16[256,128]{1,0:T(8,128)(2,1)S(1)}, bf16[256,128]{1,0:T(8,128)(2,1)S(1)}) custom-call(bf16[3,256,128]{2,1,0:T(8,128)(2,1)S(1)} %copy-done.5, bf16[3,256,128]{2,1,0:T(8,128)(2,1)S(1)} %copy-done.9, bf16[3,256,128]{2,1,0:T(8,128)(2,1)S(1)} %copy-done.7, ...), custom_call_target="tpu_custom_call" | custom-call | flops 1024 | bytes 1024 | tf_op jit(solution)/shard_map/pallas_call | solution.py:180
  137.6 1.7 collective-permute-start.26
  139.4 8.0 %shard_map.80 = (bf16[256,128]{1,0:T(8,128)(2,1)S(1)}, bf16[256,128]{1,0:T(8,128)(2,1)S(1)}, bf16[256,128]{1,0:T(8,128)(2,1)S(1)}, bf16[256,128]{1,0:T(8,128)(2,1)S(1)}) custom-call(bf16[3,256,128]{2,1,0:T(8,128)(2,1)S(1)} %copy-done.5, bf16[3,256,128]{2,1,0:T(8,128)(2,1)S(1)} %copy-done.9, bf16[3,256,128]{2,1,0:T(8,128)(2,1)S(1)} %copy-done.7, ...), custom_call_target="tpu_custom_call" | custom-call | flops 1024 | bytes 1024 | tf_op jit(solution)/shard_map/pallas_call | solution.py:180
  147.8 3.4 %collective-permute-start.28 = (bf16[256,128]{1,0:T(8,128)(2,1)S(1)}, bf16[256,128]{1,0:T(8,128)(2,1)S(1)}, u32[]{:S(2)}, u32[]{:S(2)}) collective-permute-start(bf16[256,128]{1,0:T(8,128)(2,1)S(1)} %get-tuple-element.57), channel_id=1, source_target_pairs={{0,16},{2,18},{4,20},{6,22},{8,24},{10,26},{12,28},{14,30},{16,0},... | collective-permute-start | bytes 196616 | tf_op jit(solution)/shard_map/ppermute | solution.py:244
  151.2 2.9 %collective-permute-start.30 = (bf16[256,128]{1,0:T(8,128)(2,1)S(1)}, bf16[256,128]{1,0:T(8,128)(2,1)S(1)}, u32[]{:S(2)}, u32[]{:S(2)}) collective-permute-start(bf16[256,128]{1,0:T(8,128)(2,1)S(1)} %get-tuple-element.59), channel_id=1, source_target_pairs={{0,16},{2,18},{4,20},{6,22},{8,24},{10,26},{12,28},{14,30},{16,0},... | collective-permute-start | bytes 196616 | tf_op jit(solution)/shard_map/ppermute | solution.py:244
  154.1 1.2 collective-permute-start.31
  155.3 2.7 %collective-permute-start.32 = (bf16[256,128]{1,0:T(8,128)(2,1)S(1)}, bf16[256,128]{1,0:T(8,128)(2,1)S(1)}, u32[]{:S(2)}, u32[]{:S(2)}) collective-permute-start(bf16[256,128]{1,0:T(8,128)(2,1)S(1)} %get-tuple-element.61), channel_id=1, source_target_pairs={{0,24},{2,26},{4,28},{6,30},{8,16},{10,18},{12,20},{14,22},{16,8},... | collective-permute-start | bytes 196616 | tf_op jit(solution)/shard_map/ppermute | solution.py:244
  157.9 5.1 %collective-permute-start.33 = (bf16[256,128]{1,0:T(8,128)(2,1)S(1)}, bf16[256,128]{1,0:T(8,128)(2,1)S(1)}, u32[]{:S(2)}, u32[]{:S(2)}) collective-permute-start(bf16[256,128]{1,0:T(8,128)(2,1)S(1)} %get-tuple-element.62), channel_id=1, source_target_pairs={{0,24},{2,26},{4,28},{6,30},{8,16},{10,18},{12,20},{14,22},{16,8},... | collective-permute-start | bytes 196616 | tf_op jit(solution)/shard_map/ppermute | solution.py:244
  163.1 2.5 %collective-permute-done.30.refs_8_ = bf16[256,128]{1,0:T(8,128)(2,1)S(1)} collective-permute-done((bf16[256,128]{1,0:T(8,128)(2,1)S(1)}, bf16[256,128]{1,0:T(8,128)(2,1)S(1)}, u32[]{:S(2)}, u32[]{:S(2)}) %collective-permute-start.30) | collective-permute-done | bytes 65568 | tf_op jit(solution)/shard_map/ppermute | solution.py:244
  165.6 2.8 %shard_map.82 = bf16[256,1536]{1,0:T(8,128)(2,1)S(1)} custom-call(s32[2]{0:T(128)S(1)} %pad_add_fusion.s, bf16[256,128]{1,0:T(8,128)(2,1)S(1)} %get-tuple-element.51.refs_37_.refs_0_, bf16[256,128]{1,0:T(8,128)(2,1)S(1)} %get-tuple-element.52.refs_37_.refs_1_, bf16[256,128]{1,0:T(8,128)(2,1)S(1)} %get-tuple-element.53.refs_2_, ...), custom_call_target="tpu_custom_call" | custom-call | flops 1024 | bytes 1024 | tf_op jit(solution)/shard_map/pallas_call | solution.py:213
  168.5 1.6 collective-permute-start.34
  170.0 2.8 %shard_map.81 = bf16[256,1536]{1,0:T(8,128)(2,1)S(1)} custom-call(s32[2]{0:T(128)S(1)} %pad_add_fusion.s, bf16[256,128]{1,0:T(8,128)(2,1)S(1)} %get-tuple-element.51.refs_37_.refs_0_, bf16[256,128]{1,0:T(8,128)(2,1)S(1)} %get-tuple-element.52.refs_37_.refs_1_, bf16[256,128]{1,0:T(8,128)(2,1)S(1)} %get-tuple-element.53.refs_2_, ...), custom_call_target="tpu_custom_call" | custom-call | flops 1024 | bytes 1024 | tf_op jit(solution)/shard_map/pallas_call | solution.py:213
  172.9 14.0 %collective-permute-done.34 = bf16[256,1536]{1,0:T(8,128)(2,1)S(1)} collective-permute-done((bf16[256,1536]{1,0:T(8,128)(2,1)S(1)}, bf16[256,1536]{1,0:T(8,128)(2,1)S(1)}, u32[]{:S(2)}, u32[]{:S(2)}) %collective-permute-start.34) | collective-permute-done | bytes 786464 | tf_op jit(solution)/shard_map/ppermute | solution.py:241
  186.8 1.1 add_convert_fusion
  (94 shorter events, 14.7 us)
Async XLA Ops:
  0.0 45.2 %collective-permute-start.1 = (bf16[256,1536]{1,0:T(8,128)(2,1)}, bf16[256,1536]{1,0:T(8,128)(2,1)S(1)}, u32[]{:S(2)}, u32[]{:S(2)}) collective-permute-start(bf16[256,1536]{1,0:T(8,128)(2,1)} %own_ref), channel_id=1, source_target_pairs={{0,1},{1,0},{2,3},{3,2},{4,5},{5,4},{6,7},{7,6},{8,9},{9,8},{10,11... | collective-permute-start | bytes 2359304 | tf_op jit(solution)/shard_map/ppermute | solution.py:241
  4.1 29.6 %collective-permute-start = (bf16[128,1536]{1,0:T(8,128)(2,1)S(1)}, bf16[128,1536]{1,0:T(8,128)(2,1)S(1)}, u32[]{:S(2)}, u32[]{:S(2)}) collective-permute-start(bf16[128,1536]{1,0:T(8,128)(2,1)S(1)} %get-tuple-element.64), channel_id=1, source_target_pairs={{0,16},{2,18},{4,20},{6,22},{8,24},{10,26},{12,28},{14,30},{16,0},... | collective-permute-start | bytes 1179656 | tf_op jit(solution)/shard_map/ppermute | solution.py:244
  6.8 49.0 %collective-permute-start.3 = (bf16[128,1536]{1,0:T(8,128)(2,1)S(1)}, bf16[128,1536]{1,0:T(8,128)(2,1)}, u32[]{:S(2)}, u32[]{:S(2)}) collective-permute-start(bf16[128,1536]{1,0:T(8,128)(2,1)S(1)} %get-tuple-element.63), channel_id=1, source_target_pairs={{0,16},{2,18},{4,20},{6,22},{8,24},{10,26},{12,28},{14,30},{16,0},... | collective-permute-start | bytes 1179656 | tf_op jit(solution)/shard_map/ppermute | solution.py:244
  33.7 24.7 %collective-permute-start.6 = (bf16[128,1536]{1,0:T(8,128)(2,1)S(1)}, bf16[128,1536]{1,0:T(8,128)(2,1)}, u32[]{:S(2)}, u32[]{:S(2)}) collective-permute-start(bf16[128,1536]{1,0:T(8,128)(2,1)S(1)} %collective-permute-done), channel_id=1, source_target_pairs={{0,1},{1,0},{2,3},{3,2},{4,5},{5,4},{6,7},{7,6},{8,9},{9,8},{10,11... | collective-permute-start | bytes 1179656 | tf_op jit(solution)/shard_map/ppermute | solution.py:241
  34.2 11.0 %copy-start.3 = (bf16[256,1536]{1,0:T(8,128)(2,1)S(1)}, bf16[256,1536]{1,0:T(8,128)(2,1)}, u32[]{:S(2)}) copy-start(bf16[256,1536]{1,0:T(8,128)(2,1)} %own_ref) | copy-start | bytes 2359300
  40.0 5.0 %copy-start = (bf16[6,3072,384]{2,1,0:T(8,128)(2,1)}, bf16[6,3072,384]{2,1,0:T(8,128)(2,1)S(1)}, u32[]{:S(2)}) copy-start(bf16[6,3072,384]{2,1,0:T(8,128)(2,1)S(1)} %shard_map.73.held_ref) | copy-start | bytes 42467332
  45.2 5.0 %copy-start.1 = (bf16[6,3072,384]{2,1,0:T(8,128)(2,1)S(1)}, bf16[6,3072,384]{2,1,0:T(8,128)(2,1)}, u32[]{:S(2)}) copy-start(bf16[6,3072,384]{2,1,0:T(8,128)(2,1)} %copy-done) | copy-start | bytes 42467332
  54.0 10.2 %copy-start.4 = (bf16[3,256,128]{2,1,0:T(8,128)(2,1)}, bf16[3,256,128]{2,1,0:T(8,128)(2,1)S(1)}, u32[]{:S(2)}) copy-start(bf16[3,256,128]{2,1,0:T(8,128)(2,1)S(1)} %get-tuple-element.35.refs_0_) | copy-start | bytes 589828
  54.0 11.6 %copy-start.16 = (bf16[3,256,128]{2,1,0:T(8,128)(2,1)}, bf16[3,256,128]{2,1,0:T(8,128)(2,1)S(1)}, u32[]{:S(2)}) copy-start(bf16[3,256,128]{2,1,0:T(8,128)(2,1)S(1)} %get-tuple-element.36) | copy-start | bytes 589828
  54.0 8.7 %collective-permute-start.4 = (bf16[6,256,128]{2,1,0:T(8,128)(2,1)S(1)}, bf16[6,256,128]{2,1,0:T(8,128)(2,1)S(1)}, u32[]{:S(2)}, u32[]{:S(2)}) collective-permute-start(bf16[6,256,128]{2,1,0:T(8,128)(2,1)S(1)} %get-tuple-element.37), channel_id=1, source_target_pairs={{0,8},{2,10},{4,12},{6,14},{8,0},{10,2},{12,4},{14,6},{16,24},{18,... | collective-permute-start | bytes 1179656 | tf_op jit(solution)/shard_map/ppermute | solution.py:244
  54.1 10.1 %collective-permute-start.5 = (bf16[6,256,128]{2,1,0:T(8,128)(2,1)S(1)}, bf16[6,256,128]{2,1,0:T(8,128)(2,1)S(1)}, u32[]{:S(2)}, u32[]{:S(2)}) collective-permute-start(bf16[6,256,128]{2,1,0:T(8,128)(2,1)S(1)} %get-tuple-element.39.refs_4_.refs_20_), channel_id=1, source_target_pairs={{0,4},{2,6},{4,0},{6,2},{8,12},{10,14},{12,8},{14,10},{16,20},{18,... | collective-permute-start | bytes 1179656 | tf_op jit(solution)/shard_map/ppermute | solution.py:244
  55.7 9.8 %collective-permute-start.7 = (bf16[128,1536]{1,0:T(8,128)(2,1)}, bf16[128,1536]{1,0:T(8,128)(2,1)S(1)}, u32[]{:S(2)}, u32[]{:S(2)}) collective-permute-start(bf16[128,1536]{1,0:T(8,128)(2,1)} %collective-permute-done.3), channel_id=1, source_target_pairs={{0,1},{1,0},{2,3},{3,2},{4,5},{5,4},{6,7},{7,6},{8,9},{9,8},{10,11... | collective-permute-start | bytes 1179656 | tf_op jit(solution)/shard_map/ppermute | solution.py:241
  68.2 11.9 %collective-permute-start.17 = (bf16[2,256,128]{2,1,0:T(8,128)(2,1)}, bf16[2,256,128]{2,1,0:T(8,128)(2,1)}, u32[]{:S(2)}, u32[]{:S(2)}) collective-permute-start(bf16[2,256,128]{2,1,0:T(8,128)(2,1)} %get-tuple-element.42), channel_id=1, source_target_pairs={{0,8},{2,10},{4,12},{6,14},{8,0},{10,2},{12,4},{14,6},{16,24},{18,... | collective-permute-start | bytes 393224 | tf_op jit(solution)/shard_map/ppermute | solution.py:244
  70.3 16.1 %collective-permute-start.21 = (bf16[4,256,128]{2,1,0:T(8,128)(2,1)}, bf16[4,256,128]{2,1,0:T(8,128)(2,1)}, u32[]{:S(2)}, u32[]{:S(2)}) collective-permute-start(bf16[4,256,128]{2,1,0:T(8,128)(2,1)} %shard_map.76), channel_id=1, source_target_pairs={{0,8},{2,10},{4,12},{6,14},{8,0},{10,2},{12,4},{14,6},{16,24},{18,... | collective-permute-start | bytes 786440 | tf_op jit(solution)/shard_map/ppermute | solution.py:244
  72.2 20.2 %collective-permute-start.9 = (bf16[6,256,128]{2,1,0:T(8,128)(2,1)S(1)}, bf16[6,256,128]{2,1,0:T(8,128)(2,1)S(1)}, u32[]{:S(2)}, u32[]{:S(2)}) collective-permute-start(bf16[6,256,128]{2,1,0:T(8,128)(2,1)S(1)} %get-tuple-element.39.refs_4_.refs_20_), channel_id=1, source_target_pairs={{0,2},{2,0},{4,6},{6,4},{8,10},{10,8},{12,14},{14,12},{16,18},{18,... | collective-permute-start | bytes 1179656 | tf_op jit(solution)/shard_map/ppermute | solution.py:244
  72.3 5.0 %copy-start.2 = (bf16[6,3072,384]{2,1,0:T(8,128)(2,1)S(1)}, bf16[6,3072,384]{2,1,0:T(8,128)(2,1)}, u32[]{:S(2)}) copy-start(bf16[6,3072,384]{2,1,0:T(8,128)(2,1)} %copy-done) | copy-start | bytes 42467332
  77.3 3.4 %copy-start.18 = (s32[32]{0:T(128)S(1)}, s32[32]{0:T(128)}, u32[]{:S(2)}) copy-start(s32[32]{0:T(128)} %param.8) | copy-start | bytes 388
  80.2 6.2 %collective-permute-start.18 = (bf16[2,256,128]{2,1,0:T(8,128)(2,1)}, bf16[2,256,128]{2,1,0:T(8,128)(2,1)}, u32[]{:S(2)}, u32[]{:S(2)}) collective-permute-start(bf16[2,256,128]{2,1,0:T(8,128)(2,1)} %collective-permute-done.17.refs_16_.refs_32_), channel_id=1, source_target_pairs={{0,4},{2,6},{4,0},{6,2},{8,12},{10,14},{12,8},{14,10},{16,20},{18,... | collective-permute-start | bytes 393224 | tf_op jit(solution)/shard_map/ppermute | solution.py:244
  82.3 7.9 %collective-permute-start.2 = (bf16[3,256,128]{2,1,0:T(8,128)(2,1)}, bf16[3,256,128]{2,1,0:T(8,128)(2,1)S(1)}, u32[]{:S(2)}, u32[]{:S(2)}) collective-permute-start(bf16[3,256,128]{2,1,0:T(8,128)(2,1)} %copy-done.16), channel_id=1, source_target_pairs={{0,8},{2,10},{4,12},{6,14},{8,0},{10,2},{12,4},{14,6},{16,24},{18,... | collective-permute-start | bytes 589832 | tf_op jit(solution)/shard_map/ppermute | solution.py:244
  82.7 11.1 %collective-permute-start.8 = (bf16[3,256,128]{2,1,0:T(8,128)(2,1)}, bf16[3,256,128]{2,1,0:T(8,128)(2,1)S(1)}, u32[]{:S(2)}, u32[]{:S(2)}) collective-permute-start(bf16[3,256,128]{2,1,0:T(8,128)(2,1)} %copy-done.17), channel_id=1, source_target_pairs={{0,8},{2,10},{4,12},{6,14},{8,0},{10,2},{12,4},{14,6},{16,24},{18,... | collective-permute-start | bytes 589832 | tf_op jit(solution)/shard_map/ppermute | solution.py:244
  86.4 9.5 %collective-permute-start.19 = (bf16[2,256,128]{2,1,0:T(8,128)(2,1)}, bf16[2,256,128]{2,1,0:T(8,128)(2,1)S(1)}, u32[]{:S(2)}, u32[]{:S(2)}) collective-permute-start(bf16[2,256,128]{2,1,0:T(8,128)(2,1)} %collective-permute-done.17.refs_16_.refs_32_), channel_id=1, source_target_pairs={{0,2},{2,0},{4,6},{6,4},{8,10},{10,8},{12,14},{14,12},{16,18},{18,... | collective-permute-start | bytes 393224 | tf_op jit(solution)/shard_map/ppermute | solution.py:244
  86.4 10.2 %collective-permute-start.20 = (bf16[2,256,128]{2,1,0:T(8,128)(2,1)}, bf16[2,256,128]{2,1,0:T(8,128)(2,1)S(1)}, u32[]{:S(2)}, u32[]{:S(2)}) collective-permute-start(bf16[2,256,128]{2,1,0:T(8,128)(2,1)} %collective-permute-done.18.refs_17_.refs_33_), channel_id=1, source_target_pairs={{0,2},{2,0},{4,6},{6,4},{8,10},{10,8},{12,14},{14,12},{16,18},{18,... | collective-permute-start | bytes 393224 | tf_op jit(solution)/shard_map/ppermute | solution.py:244
  90.9 12.1 %collective-permute-start.11 = (bf16[6,256,128]{2,1,0:T(8,128)(2,1)S(1)}, bf16[6,256,128]{2,1,0:T(8,128)(2,1)S(1)}, u32[]{:S(2)}, u32[]{:S(2)}) collective-permute-start(bf16[6,256,128]{2,1,0:T(8,128)(2,1)S(1)} %collective-permute-done.4.refs_8_.refs_24_), channel_id=1, source_target_pairs={{0,4},{2,6},{4,0},{6,2},{8,12},{10,14},{12,8},{14,10},{16,20},{18,... | collective-permute-start | bytes 1179656 | tf_op jit(solution)/shard_map/ppermute | solution.py:244
  92.4 10.6 %collective-permute-start.12 = (bf16[6,256,128]{2,1,0:T(8,128)(2,1)S(1)}, bf16[6,256,128]{2,1,0:T(8,128)(2,1)S(1)}, u32[]{:S(2)}, u32[]{:S(2)}) collective-permute-start(bf16[6,256,128]{2,1,0:T(8,128)(2,1)S(1)} %collective-permute-done.4.refs_8_.refs_24_), channel_id=1, source_target_pairs={{0,2},{2,0},{4,6},{6,4},{8,10},{10,8},{12,14},{14,12},{16,18},{18,... | collective-permute-start | bytes 1179656 | tf_op jit(solution)/shard_map/ppermute | solution.py:244
  94.4 17.0 %collective-permute-start.14 = (bf16[6,256,128]{2,1,0:T(8,128)(2,1)S(1)}, bf16[6,256,128]{2,1,0:T(8,128)(2,1)S(1)}, u32[]{:S(2)}, u32[]{:S(2)}) collective-permute-start(bf16[6,256,128]{2,1,0:T(8,128)(2,1)S(1)} %get-tuple-element.48.refs_12_.refs_28_), channel_id=1, source_target_pairs={{0,4},{2,6},{4,0},{6,2},{8,12},{10,14},{12,8},{14,10},{16,20},{18,... | collective-permute-start | bytes 1179656 | tf_op jit(solution)/shard_map/ppermute | solution.py:244
  96.6 3.0 %collective-permute-start.10 = (bf16[6,256,128]{2,1,0:T(8,128)(2,1)S(1)}, bf16[6,256,128]{2,1,0:T(8,128)(2,1)S(1)}, u32[]{:S(2)}, u32[]{:S(2)}) collective-permute-start(bf16[6,256,128]{2,1,0:T(8,128)(2,1)S(1)} %collective-permute-done.5.refs_5_.refs_21_), channel_id=1, source_target_pairs={{0,2},{2,0},{4,6},{6,4},{8,10},{10,8},{12,14},{14,12},{16,18},{18,... | collective-permute-start | bytes 1179656 | tf_op jit(solution)/shard_map/ppermute | solution.py:244
  97.2 17.6 %collective-permute-start.22 = (bf16[4,256,128]{2,1,0:T(8,128)(2,1)}, bf16[4,256,128]{2,1,0:T(8,128)(2,1)}, u32[]{:S(2)}, u32[]{:S(2)}) collective-permute-start(bf16[4,256,128]{2,1,0:T(8,128)(2,1)} %collective-permute-done.21.refs_16_.refs_32_), channel_id=1, source_target_pairs={{0,4},{2,6},{4,0},{6,2},{8,12},{10,14},{12,8},{14,10},{16,20},{18,... | collective-permute-start | bytes 786440 | tf_op jit(solution)/shard_map/ppermute | solution.py:244
  99.6 16.0 %collective-permute-start.15 = (bf16[6,256,128]{2,1,0:T(8,128)(2,1)S(1)}, bf16[6,256,128]{2,1,0:T(8,128)(2,1)S(1)}, u32[]{:S(2)}, u32[]{:S(2)}) collective-permute-start(bf16[6,256,128]{2,1,0:T(8,128)(2,1)S(1)} %get-tuple-element.48.refs_12_.refs_28_), channel_id=1, source_target_pairs={{0,2},{2,0},{4,6},{6,4},{8,10},{10,8},{12,14},{14,12},{16,18},{18,... | collective-permute-start | bytes 1179656 | tf_op jit(solution)/shard_map/ppermute | solution.py:244
  103.0 26.5 %collective-permute-start.23 = (bf16[4,256,128]{2,1,0:T(8,128)(2,1)}, bf16[4,256,128]{2,1,0:T(8,128)(2,1)S(1)}, u32[]{:S(2)}, u32[]{:S(2)}) collective-permute-start(bf16[4,256,128]{2,1,0:T(8,128)(2,1)} %collective-permute-done.21.refs_16_.refs_32_), channel_id=1, source_target_pairs={{0,2},{2,0},{4,6},{6,4},{8,10},{10,8},{12,14},{14,12},{16,18},{18,... | collective-permute-start | bytes 786440 | tf_op jit(solution)/shard_map/ppermute | solution.py:244
  103.0 12.6 %collective-permute-start.13 = (bf16[6,256,128]{2,1,0:T(8,128)(2,1)S(1)}, bf16[6,256,128]{2,1,0:T(8,128)(2,1)S(1)}, u32[]{:S(2)}, u32[]{:S(2)}) collective-permute-start(bf16[6,256,128]{2,1,0:T(8,128)(2,1)S(1)} %collective-permute-done.11.refs_9_.refs_25_), channel_id=1, source_target_pairs={{0,2},{2,0},{4,6},{6,4},{8,10},{10,8},{12,14},{14,12},{16,18},{18,... | collective-permute-start | bytes 1179656 | tf_op jit(solution)/shard_map/ppermute | solution.py:244
  111.4 4.2 %collective-permute-start.16 = (bf16[6,256,128]{2,1,0:T(8,128)(2,1)S(1)}, bf16[6,256,128]{2,1,0:T(8,128)(2,1)S(1)}, u32[]{:S(2)}, u32[]{:S(2)}) collective-permute-start(bf16[6,256,128]{2,1,0:T(8,128)(2,1)S(1)} %collective-permute-done.14.refs_13_.refs_29_), channel_id=1, source_target_pairs={{0,2},{2,0},{4,6},{6,4},{8,10},{10,8},{12,14},{14,12},{16,18},{18,... | collective-permute-start | bytes 1179656 | tf_op jit(solution)/shard_map/ppermute | solution.py:244
  114.8 14.7 %collective-permute-start.24 = (bf16[4,256,128]{2,1,0:T(8,128)(2,1)}, bf16[4,256,128]{2,1,0:T(8,128)(2,1)S(1)}, u32[]{:S(2)}, u32[]{:S(2)}) collective-permute-start(bf16[4,256,128]{2,1,0:T(8,128)(2,1)} %collective-permute-done.22.refs_37_.refs_17_.refs_33_), channel_id=1, source_target_pairs={{0,2},{2,0},{4,6},{6,4},{8,10},{10,8},{12,14},{14,12},{16,18},{18,... | collective-permute-start | bytes 786440 | tf_op jit(solution)/shard_map/ppermute | solution.py:244
  115.6 0.9 copy-start.5
  116.6 0.9 copy-start.7
  117.5 0.9 copy-start.9
  129.1 22.1 %collective-permute-start.25 = (bf16[256,128]{1,0:T(8,128)(2,1)S(1)}, bf16[256,128]{1,0:T(8,128)(2,1)S(1)}, u32[]{:S(2)}, u32[]{:S(2)}) collective-permute-start(bf16[256,128]{1,0:T(8,128)(2,1)S(1)} %get-tuple-element.54), channel_id=1, source_target_pairs={{0,8},{2,10},{4,12},{6,14},{8,0},{10,2},{12,4},{14,6},{16,24},{18,... | collective-permute-start | bytes 196616 | tf_op jit(solution)/shard_map/ppermute | solution.py:244
  129.5 36.1 %slice-start = ((s8[9437184]{0:T(1024)(128)(4,1)}), s8[4194304]{0:T(1024)(128)(4,1)S(1)}, s32[]{:S(2)}) async-start(s8[9437184]{0:T(1024)(128)(4,1)} %bitcast.21), calls=%async_computation | async-start | bytes 8388608
  129.5 36.1 %slice-start.1 = ((s8[9437184]{0:T(1024)(128)(4,1)}), s8[4194304]{0:T(1024)(128)(4,1)S(1)}, s32[]{:S(2)}) async-start(s8[9437184]{0:T(1024)(128)(4,1)} %bitcast.21), calls=%async_computation.1 | async-start | bytes 8388608
  137.6 16.5 %collective-permute-start.26 = (bf16[256,128]{1,0:T(8,128)(2,1)S(1)}, bf16[256,128]{1,0:T(8,128)(2,1)S(1)}, u32[]{:S(2)}, u32[]{:S(2)}) collective-permute-start(bf16[256,128]{1,0:T(8,128)(2,1)S(1)} %get-tuple-element.55), channel_id=1, source_target_pairs={{0,8},{2,10},{4,12},{6,14},{8,0},{10,2},{12,4},{14,6},{16,24},{18,... | collective-permute-start | bytes 196616 | tf_op jit(solution)/shard_map/ppermute | solution.py:244
  139.4 26.3 %slice-start.2 = ((s8[9437184]{0:T(1024)(128)(4,1)}), s8[1048576]{0:T(1024)(128)(4,1)S(1)}, s32[]{:S(2)}) async-start(s8[9437184]{0:T(1024)(128)(4,1)} %bitcast.21), calls=%async_computation.2 | async-start | bytes 2097152
  147.4 7.9 %collective-permute-start.27 = (bf16[256,128]{1,0:T(8,128)(2,1)S(1)}, bf16[256,128]{1,0:T(8,128)(2,1)S(1)}, u32[]{:S(2)}, u32[]{:S(2)}) collective-permute-start(bf16[256,128]{1,0:T(8,128)(2,1)S(1)} %get-tuple-element.56), channel_id=1, source_target_pairs={{0,8},{2,10},{4,12},{6,14},{8,0},{10,2},{12,4},{14,6},{16,24},{18,... | collective-permute-start | bytes 196616 | tf_op jit(solution)/shard_map/ppermute | solution.py:244
  147.8 10.1 %collective-permute-start.28 = (bf16[256,128]{1,0:T(8,128)(2,1)S(1)}, bf16[256,128]{1,0:T(8,128)(2,1)S(1)}, u32[]{:S(2)}, u32[]{:S(2)}) collective-permute-start(bf16[256,128]{1,0:T(8,128)(2,1)S(1)} %get-tuple-element.57), channel_id=1, source_target_pairs={{0,16},{2,18},{4,20},{6,22},{8,24},{10,26},{12,28},{14,30},{16,0},... | collective-permute-start | bytes 196616 | tf_op jit(solution)/shard_map/ppermute | solution.py:244
  151.2 11.9 %collective-permute-start.29 = (bf16[256,128]{1,0:T(8,128)(2,1)S(1)}, bf16[256,128]{1,0:T(8,128)(2,1)S(1)}, u32[]{:S(2)}, u32[]{:S(2)}) collective-permute-start(bf16[256,128]{1,0:T(8,128)(2,1)S(1)} %get-tuple-element.58), channel_id=1, source_target_pairs={{0,16},{2,18},{4,20},{6,22},{8,24},{10,26},{12,28},{14,30},{16,0},... | collective-permute-start | bytes 196616 | tf_op jit(solution)/shard_map/ppermute | solution.py:244
  151.2 14.4 %collective-permute-start.30 = (bf16[256,128]{1,0:T(8,128)(2,1)S(1)}, bf16[256,128]{1,0:T(8,128)(2,1)S(1)}, u32[]{:S(2)}, u32[]{:S(2)}) collective-permute-start(bf16[256,128]{1,0:T(8,128)(2,1)S(1)} %get-tuple-element.59), channel_id=1, source_target_pairs={{0,16},{2,18},{4,20},{6,22},{8,24},{10,26},{12,28},{14,30},{16,0},... | collective-permute-start | bytes 196616 | tf_op jit(solution)/shard_map/ppermute | solution.py:244
  154.1 11.5 %collective-permute-start.31 = (bf16[256,128]{1,0:T(8,128)(2,1)S(1)}, bf16[256,128]{1,0:T(8,128)(2,1)S(1)}, u32[]{:S(2)}, u32[]{:S(2)}) collective-permute-start(bf16[256,128]{1,0:T(8,128)(2,1)S(1)} %get-tuple-element.60), channel_id=1, source_target_pairs={{0,24},{2,26},{4,28},{6,30},{8,16},{10,18},{12,20},{14,22},{16,8},... | collective-permute-start | bytes 196616 | tf_op jit(solution)/shard_map/ppermute | solution.py:244
  155.3 10.3 %collective-permute-start.32 = (bf16[256,128]{1,0:T(8,128)(2,1)S(1)}, bf16[256,128]{1,0:T(8,128)(2,1)S(1)}, u32[]{:S(2)}, u32[]{:S(2)}) collective-permute-start(bf16[256,128]{1,0:T(8,128)(2,1)S(1)} %get-tuple-element.61), channel_id=1, source_target_pairs={{0,24},{2,26},{4,28},{6,30},{8,16},{10,18},{12,20},{14,22},{16,8},... | collective-permute-start | bytes 196616 | tf_op jit(solution)/shard_map/ppermute | solution.py:244
  157.9 7.7 %collective-permute-start.33 = (bf16[256,128]{1,0:T(8,128)(2,1)S(1)}, bf16[256,128]{1,0:T(8,128)(2,1)S(1)}, u32[]{:S(2)}, u32[]{:S(2)}) collective-permute-start(bf16[256,128]{1,0:T(8,128)(2,1)S(1)} %get-tuple-element.62), channel_id=1, source_target_pairs={{0,24},{2,26},{4,28},{6,30},{8,16},{10,18},{12,20},{14,22},{16,8},... | collective-permute-start | bytes 196616 | tf_op jit(solution)/shard_map/ppermute | solution.py:244
  168.5 18.4 %collective-permute-start.34 = (bf16[256,1536]{1,0:T(8,128)(2,1)S(1)}, bf16[256,1536]{1,0:T(8,128)(2,1)S(1)}, u32[]{:S(2)}, u32[]{:S(2)}) collective-permute-start(bf16[256,1536]{1,0:T(8,128)(2,1)S(1)} %shard_map.82), channel_id=1, source_target_pairs={{0,1},{1,0},{2,3},{3,2},{4,5},{5,4},{6,7},{7,6},{8,9},{9,8},{10,11... | collective-permute-start | bytes 2359304 | tf_op jit(solution)/shard_map/ppermute | solution.py:241
  (9 other events, 6.7 us)

commit v4 on v3

--- a/solution.py
+++ b/solution.py
@@ -41,13 +41,13 @@
     return [pl.BlockSpec(memory_space=pltpu.VMEM)] * count
 
 
-def fetch(where, weights, width):
+def fetch(where, weights, width, fence):
     depth = weights[0].shape[0]
     half = depth // 2
     kinds = len(weights)
 
     def body(s, *refs):
-        out, sems = refs[kinds], refs[kinds + 1]
+        out, sems = refs[kinds + 1], refs[kinds + 2]
         copies = []
         for g in range(2):
             columns = pl.ds(pl.multiple_of((s[1] ^ g) * width, width), width)
@@ -71,23 +71,31 @@
         grid_spec=pltpu.PrefetchScalarGridSpec(
             num_scalar_prefetch=1,
             grid=(),
-            in_specs=[pl.BlockSpec(memory_space=pl.ANY)] * kinds,
+            in_specs=[pl.BlockSpec(memory_space=pl.ANY)] * (kinds + 1),
             out_specs=pl.BlockSpec(memory_space=pltpu.VMEM),
             scratch_shapes=[pltpu.SemaphoreType.DMA((4 * kinds,))],
         ),
         out_shape=pltpu.VMEM((2 * kinds, depth, width), BF16),
         compiler_params=params(4),
         cost_estimate=LIGHT,
-    )(where, *weights)
+    )(where, *weights, fence)
 
 
 def project(own, other, held, outputs):
-    rows = own.shape[0]
+    pieces = len(own)
+    rows = sum(a.shape[0] for a in own)
     kinds = held.shape[0] // 2
     flat = [block for blocks in outputs for block in blocks]
 
-    def body(own_ref, other_ref, held_ref, *outs):
-        tokens = jnp.concatenate([own_ref[...], other_ref[...]], axis=1)
+    def body(*refs):
+        held_ref, outs = refs[2 * pieces], refs[2 * pieces + 1 :]
+        tokens = jnp.concatenate(
+            [
+                jnp.concatenate([r[...] for r in refs[:pieces]], axis=0),
+                jnp.concatenate([r[...] for r in refs[pieces : 2 * pieces]], axis=0),
+            ],
+            axis=1,
+        )
         at = [(o, i) for o, blocks in enumerate(outputs) for i in range(len(blocks))]
         for start in range(0, len(flat), 2):
             pair = flat[start : start + 2]
@@ -103,52 +111,104 @@
 
     return pl.pallas_call(
         body,
-        in_specs=whole(3),
+        in_specs=whole(2 * pieces + 1),
         out_specs=whole(len(outputs)),
         out_shape=[jax.ShapeDtypeStruct((len(b), rows, HEAD_DIM), BF16) for b in outputs],
         compiler_params=params(16),
         cost_estimate=LIGHT,
-    )(own, other, held)
-
-
-def attend(queries, parts, bias, fence):
-    rows = queries[0][0].shape[1]
-    tile = parts[0][0].shape[1]
-    n = len(parts)
+    )(*own, *other, held)
+
+
+def mask_rows(where, block_order, block_mask, rows):
+    blocks = block_order.shape[0]
+    per = rows // BLOCK
+    keys = blocks * BLOCK
+
+    def body(s, order_ref, mask_ref, out_ref):
+        def ids(shape, axis, shift):
+            at = lax.broadcasted_iota(jnp.int32, shape, axis) >> shift
+            piece = at >> (per.bit_length() - 1)
+            return at & (per - 1), piece
+
+        hot = (order_ref[...] == lax.broadcasted_iota(jnp.int32, (blocks, blocks), 0)).astype(F32)
+        low, piece = ids((Z * per, blocks), 0, 0)
+        want = (place(s[1] ^ piece, s[2], s[3])) * per + low
+        query = (want == lax.broadcasted_iota(jnp.int32, (Z * per, blocks), 1)).astype(F32)
+        low, piece = ids((blocks, keys), 1, BLOCK.bit_length() - 1)
+        want = place(s[1] ^ (piece >> 2), s[2] ^ (piece & 1), s[3] ^ ((piece >> 1) & 1)) * per + low
+        key = (want == lax.broadcasted_iota(jnp.int32, (blocks, keys), 0)).astype(F32)
+        frames = lax.dot_general(query, hot, (((1,), (1,)), ((), ())), preferred_element_type=F32)
+        live = jnp.dot(frames, mask_ref[...].astype(F32), preferred_element_type=F32)
+        live = jnp.dot(live, hot, preferred_element_type=F32)
+        live = jnp.dot(live, key, preferred_element_type=F32)
+        out_ref[...] = jnp.where(live > 0.5, 0.0, -1e30)
+
+    return pl.pallas_call(
+        body,
+        grid_spec=pltpu.PrefetchScalarGridSpec(
+            num_scalar_prefetch=1, grid=(), in_specs=whole(2), out_specs=whole(1)[0]
+        ),
+        out_shape=jax.ShapeDtypeStruct((Z * per, keys), F32),
+        compiler_params=params(8),
+        cost_estimate=LIGHT,
+    )(where, block_order[None, :], block_mask)
+
+
+def attend(queries, parts, states, bias, query_at, key_at, last, fences):
+    rows = queries[0][0][0].shape[1]
+    tile = parts[0][0][0].shape[1]
+    n = len(parts[0])
     group = 4
     scale = math.log2(math.e) / math.sqrt(HEAD_DIM)
     per = rows // BLOCK
     both = 2 * rows
+    steps = len(queries)
+    same_parts = len(parts) == 1
 
     def body(*refs):
-        q_refs, k_refs, v_refs = refs[:Z], refs[Z : Z + n], refs[Z + n : Z + 2 * n]
-        bias_ref = refs[Z + 2 * n]
-        outs = refs[Z + 2 * n + 2 : Z + 2 * n + 2 + Z]
-        q_ref = refs[-1]
+        refs = list(refs)
+
+        def take(count):
+            got = refs[:count]
+            del refs[:count]
+            return got
+
+        q_refs = take(2 * steps)
+        k_refs, v_refs = take(n), take(n)
+        state_refs = [take(3) for _ in states]
+        (bias_ref,) = take(1)
+        take(len(fences))
+        outs = take(2 * steps if last else 3)
+        q_ref = refs[0]
         step = pl.program_id(0)
-        for i in range(Z // 2):
+        for i in range(steps):
 
             @pl.when(step == i)
             def _(i=i):
                 q_ref[:rows] = q_refs[2 * i][0]
                 q_ref[rows:] = q_refs[2 * i + 1][0]
+                if states:
+                    for held, ref in zip(refs[1:], state_refs[i]):
+                        held[...] = ref[0]
 
         query = q_ref[...]
-        top = jnp.full((both, 1), -1e30, F32)
-        total = jnp.zeros((both, HEAD_DIM), F32)
-        accum = jnp.zeros((both, HEAD_DIM), F32)
+        if states:
+            top, total, accum = refs[1][:, :1], refs[2][...], refs[3][...]
+        else:
+            top = jnp.full((both, 1), -1e30, F32)
+            total = jnp.zeros((both, HEAD_DIM), F32)
+            accum = jnp.zeros((both, HEAD_DIM), F32)
+        first_row = (query_at[0] + step * query_at[1]) * per
         for t in range(0, n, group):
             key = jnp.concatenate([k_refs[u][0] for u in range(t, t + group)], axis=0)
             value = jnp.concatenate([v_refs[u][0] for u in range(t, t + group)], axis=0)
             width = group * tile
+            at = (key_at + t) * tile
             score = lax.dot_general(
                 query, key, (((1,), (1,)), ((), ())), preferred_element_type=F32
             )
             keep = [
-                jnp.broadcast_to(
-                    bias_ref[pl.ds(step * 2 * per + r, 1), t * tile : t * tile + width],
-                    (BLOCK, width),
-                )
+                jnp.broadcast_to(bias_ref[pl.ds(first_row + r, 1), at : at + width], (BLOCK, width))
                 for r in range(2 * per)
             ]
             score = score + jnp.concatenate(keep, axis=0)
@@ -166,30 +226,62 @@
             accum = accum * factor + jnp.dot(
                 weight.astype(BF16), value, preferred_element_type=F32
             )
-        result = (accum / jnp.sum(total, axis=1, keepdims=True)).astype(BF16)
-        for i in range(Z // 2):
-
-            @pl.when(step == i)
-            def _(i=i):
-                outs[2 * i][...] = result[:rows]
-                outs[2 * i + 1][...] = result[rows:]
-
-    def block_spec(index):
-        return pl.BlockSpec((1, rows, HEAD_DIM), lambda i: (index, 0, 0))
-
+        if last:
+            result = (accum / jnp.sum(total, axis=1, keepdims=True)).astype(BF16)
+            for i in range(steps):
+
+                @pl.when(step == i)
+                def _(i=i):
+                    outs[2 * i][...] = result[:rows]
+                    outs[2 * i + 1][...] = result[rows:]
+
+        else:
+            outs[0][0] = jnp.broadcast_to(top, (both, HEAD_DIM))
+            outs[1][0] = total
+            outs[2][0] = accum
+
+    def fixed(block, index):
+        return pl.BlockSpec(block, lambda i: (index,) + (0,) * (len(block) - 1))
+
+    def part_spec(kind):
+        def one(u):
+            base = parts[0][u][kind]
+            stride = 0 if same_parts else 1
+            return pl.BlockSpec((1, tile, HEAD_DIM), lambda i: (base + i * stride, 0, 0))
+
+        return [one(u) for u in range(n)]
+
+    arrays = [p[0] for p in parts[0]]
+    state_block = (1, both, HEAD_DIM)
+    if last:
+        out_specs = [pl.BlockSpec((rows, HEAD_DIM), lambda i: (0, 0))] * (2 * steps)
+        out_shape = [jax.ShapeDtypeStruct((rows, HEAD_DIM), BF16)] * (2 * steps)
+    else:
+        out_specs = [pl.BlockSpec(state_block, lambda i: (i, 0, 0))] * 3
+        out_shape = [jax.ShapeDtypeStruct((steps, both, HEAD_DIM), F32)] * 3
     return pl.pallas_call(
         body,
-        grid=(Z // 2,),
-        in_specs=[block_spec(at) for _, at in queries]
-        + [block_spec(k) for _, k, _ in parts]
-        + [block_spec(v) for _, _, v in parts]
-        + [pl.BlockSpec(bias.shape, lambda i: (0, 0)), pl.BlockSpec(memory_space=pl.ANY)],
-        out_specs=[pl.BlockSpec((rows, HEAD_DIM), lambda i: (0, 0))] * Z,
-        out_shape=[jax.ShapeDtypeStruct((rows, HEAD_DIM), BF16)] * Z,
-        scratch_shapes=[pltpu.VMEM((both, HEAD_DIM), BF16)],
+        grid=(steps,),
+        in_specs=[fixed((1, rows, HEAD_DIM), at) for row in queries for _, at in row]
+        + part_spec(1)
+        + part_spec(2)
+        + [fixed(state_block, at) for _, at in states for _ in range(3)]
+        + [pl.BlockSpec(bias.shape, lambda i: (0, 0))]
+        + [pl.BlockSpec(memory_space=pl.ANY)] * len(fences),
+        out_specs=out_specs,
+        out_shape=out_shape,
+        scratch_shapes=[pltpu.VMEM((both, HEAD_DIM), BF16)]
+        + [pltpu.VMEM((both, HEAD_DIM), F32)] * (3 if states else 0),
         compiler_params=params(24),
         cost_estimate=LIGHT,
-    )(*[q for q, _ in queries], *[p for p, _, _ in parts], *[p for p, _, _ in parts], bias, fence)
+    )(
+        *[a for row in queries for a, _ in row],
+        *arrays,
+        *arrays,
+        *[a for held, _ in states for a in held],
+        bias,
+        *fences,
+    )
 
 
 def mix(where, attended, w_out, flip, step_width):
@@ -228,14 +320,14 @@
 def split_heads(tokens, block_order, block_mask, w_query, w_key, w_value, w_out):
     rows, half = tokens.shape
     group_heads = w_query.shape[1] // HEAD_DIM // Z
-    block_count = block_order.shape[0]
-    per = rows // BLOCK
     cut = rows // 2
     ctx = lax.axis_index("ctx")
     y = lax.axis_index("head")
-    z, x, c = ctx // (X * C), (ctx // C) % X, ctx % C
-    where = jnp.stack([y, z]).astype(jnp.int32)
-    weights = (w_query, w_key, w_value)
+    where = jnp.stack([y, ctx // (X * C), (ctx // C) % X, ctx % C]).astype(jnp.int32)
+    weights = [pltpu.with_memory_space_constraint(w, pltpu.HBM) for w in (w_query, w_key, w_value)]
+    w_out = pltpu.with_memory_space_constraint(w_out, pltpu.HBM)
+    heads = range(group_heads)
+    span = group_heads * HEAD_DIM
 
     def over_y(a):
         return lax.ppermute(a, "head", [(0, 1), (1, 0)])
@@ -243,89 +335,109 @@
     def over(a, dz, dx, dc):
         return lax.ppermute(a, "ctx", hop(dz, dx, dc))
 
-    held = [pltpu.with_memory_space_constraint(w, pltpu.HBM) for w in weights]
-    other = over_y(tokens)
-    far = [over(tokens[i * cut : (i + 1) * cut], 2, 0, 0) for i in range(2)]
-
-    def blocks(pairs):
-        first = jnp.stack([place(z ^ dz, x ^ dx, c ^ dc) for dz, dx, dc in pairs]) * per
-        return (first[:, None] + jnp.arange(per)[None, :]).reshape(-1)
-
-    sides = ((0, 0), (1, 0), (0, 1), (1, 1))
-    query_blocks = blocks([(dz, 0, 0) for dz in range(Z)])
-    key_blocks = blocks([(dz, dx, dc) for dz in range(Z) for dx, dc in sides])
-    frames = jnp.arange(block_count, dtype=jnp.int32)
-    order_hot = (block_order[:, None] == frames[None, :]).astype(F32)
-
-    def pick(wanted):
-        place_hot = (wanted[:, None] == frames[None, :]).astype(F32)
-        return jnp.dot(place_hot, order_hot)
-
-    live = jnp.dot(jnp.dot(pick(query_blocks), block_mask.astype(F32)), pick(key_blocks).T)
-    bias = jnp.repeat(jnp.where(live > 0.5, 0.0, -1e30).astype(F32), BLOCK, axis=1)
-
-    heads = range(group_heads)
-    span = group_heads * HEAD_DIM
-
     def pairs(group, wanted):
         return [(group, kind, h) for kind in (1, 2) for h in wanted]
 
     def singles(group):
         return [(group, 0, h) for h in heads]
 
-    held = fetch(where, held, span)
-
+    other = over_y(tokens)
+    far = [over(tokens[:cut], 2, 0, 0)]
+    bias = mask_rows(where, block_order, block_mask, rows)
+    held = fetch(where, weights, span, bias)
+
+    other = after(other, held)
+    far[0] = after(far[0], held)
+    far.append(over(after(tokens[cut:], far[0]), 2, 0, 0))
     far_other = [over_y(far[0])]
-    own_q, own_kv, sent_q, sent_kv = project(
-        after(tokens, far[0]),
-        other,
-        held,
-        [singles(0), pairs(0, heads), singles(1), pairs(1, heads)],
+    own_kv, sent_kv = project(
+        [after(tokens, far[0])], [other], held, [pairs(0, heads), pairs(1, heads)]
     )
     came_kv = over(sent_kv, 1, 0, 0)
-    came_q = over(sent_q, 1, 0, 0)
     own_across = over(own_kv, 0, 1, 0)
     own_core = over(own_kv, 0, 0, 1)
-    far_other.append(over_y(after(far[1], own_kv)))
-    came_kv = after(came_kv, far[1])
+    own_q, sent_q = project(
+        [after(tokens, sent_kv)], [other], held, [singles(0), singles(1)]
+    )
+    came_q = over(sent_q, 1, 0, 0)
+    far[1] = after(far[1], sent_q)
+    far_other.append(over_y(after(far[1], far_other[0])))
+    own_across_core = over(own_across, 0, 0, 1)
+    came_kv = after(came_kv, own_across)
     came_across = over(came_kv, 0, 1, 0)
     came_core = over(came_kv, 0, 0, 1)
-    own_across_core = over(after(own_across, came_kv), 0, 0, 1)
-
-    far = after(jnp.concatenate(far, axis=0), came_kv, own_across)
-    far_other = jnp.concatenate(far_other, axis=0)
+
+    far[1] = after(far[1], came_kv)
+    far_other[1] = after(far_other[1], came_kv)
     first, rest = (0,), tuple(heads)[1:]
     far_sent_kv, far_sent_q = project(far, far_other, held, [pairs(1, first), singles(1)])
     far_came_kv = over(far_sent_kv, 1, 0, 0)
     far_came_q = over(far_sent_q, 1, 0, 0)
-    (far_sent_kv2,) = project(after(far, far_sent_kv), far_other, held, [pairs(1, rest)])
+    (far_kv,) = project(
+        [far[0], after(far[1], far_sent_kv)], far_other, held, [pairs(0, heads)]
+    )
+    far_across = over(far_kv, 0, 1, 0)
+    far_core = over(far_kv, 0, 0, 1)
+    far_sent_kv2, far_q = project(
+        [far[0], after(far[1], far_kv)], far_other, held, [pairs(1, rest), singles(0)]
+    )
     far_came_kv2 = over(far_sent_kv2, 1, 0, 0)
-    far_q, far_kv = project(
-        after(far, far_sent_kv2), far_other, held, [singles(0), pairs(0, heads)]
-    )
-
-    def spread(part):
-        across = over(part, 0, 1, 0)
-        return [part, across, over(part, 0, 0, 1), over(across, 0, 0, 1)]
-
-    far_kept = spread(far_kv)
+    came_across = after(came_across, far_q)
     came_across_core = over(came_across, 0, 0, 1)
-    far_first = spread(after(far_came_kv, far_kv))
-    far_rest = spread(after(far_came_kv2, far_first[0]))
-    near = [[own_kv, own_across, own_core, own_across_core]]
-    near.append([came_kv, came_across, came_core, came_across_core])
+
+    near = [own_kv, own_across, own_core, own_across_core]
+    near += [came_kv, came_across, came_core, came_across_core]
+    near_parts = [[(a, 0, group_heads) for a in near], None]
+    state_near = attend(
+        [[(own_q, j), (came_q, j)] for j in heads], near_parts, [], bias, (0, 0), 0, False, []
+    )
+    far_came_kv = after(far_came_kv, state_near[0])
+    first_across = over(far_came_kv, 0, 1, 0)
+    first_core = over(far_came_kv, 0, 0, 1)
+    far_came_kv2 = after(far_came_kv2, far_came_kv)
+    rest_across = over(far_came_kv2, 0, 1, 0)
+    rest_core = over(far_came_kv2, 0, 0, 1)
+    far_across = after(far_across, far_came_kv2)
+    far_across_core = over(far_across, 0, 0, 1)
+    state_far = attend(
+        [[(far_q, j), (far_came_q, j)] for j in heads],
+        near_parts,
+        [],
+        bias,
+        (2, 0),
+        0,
+        False,
+        [far_across, far_came_kv2],
+    )
+    first_across = after(first_across, state_far[0])
+    first_across_core = over(first_across, 0, 0, 1)
+    rest_across = after(rest_across, first_across_core)
+    rest_across_core = over(rest_across, 0, 0, 1)
+    kept = [far_kv, far_across, far_core, far_across_core]
+    far_first = [far_came_kv, first_across, first_core, first_across_core]
+    far_rest = [far_came_kv2, rest_across, rest_core, rest_across_core]
 
     results = []
     for j in heads:
-        queries = [(own_q, j), (came_q, j), (far_q, j), (far_came_q, j)]
-        parts = [(a, j, group_heads + j) for a in near[0] + near[1] + far_kept]
+        parts = [(a, j, group_heads + j) for a in kept]
         if j == 0:
             parts += [(a, 0, 1) for a in far_first]
         else:
             parts += [(a, j - 1, group_heads - 1 + j - 1) for a in far_rest]
-        results.append(attend(queries, parts, bias, results[-1][0] if j else far_rest[1]))
+        results.append(
+            attend(
+                [[(own_q, j), (came_q, j)], [(far_q, j), (far_came_q, j)]],
+                [parts],
+                [(state_near, j), (state_far, j)],
+                bias,
+                (0, 2),
+                len(near),
+                True,
+                [results[-1][0]] if j else [],
+            )
+        )
     results = [[r[0]] + [over(r[dz], dz, 0, 0) for dz in range(1, Z)] for r in results]
-    attended = [results[j][dz] for dz in range(Z) for j in range(group_heads)]
+    attended = [results[j][dz] for dz in range(Z) for j in heads]
     arrived = over_y(mix(where, attended, w_out, True, 512))
     home = mix(where, attended, w_out, False, 512)
     return (home.astype(F32) + arrived.astype(F32)).astype(BF16)

time: 191 us -> 140 us (0.73); the launches traced: 188 us -> 139 us
  local copies, waits for them, and re-layouts: 28.6 us -> 2.54 us
  waiting for transfers between devices: 70.5 us -> 48.6 us
  Pallas kernels: 45.1 us -> 50.2 us
  matrix products: 2.57 us -> 0 us
  starting transfers between devices: 38.5 us -> 36.5 us
    unnamed x45 -> x6, local copies, waits for them, and re-layouts: 25.6 us -> 1.38 us
    ppermute x31, waiting for transfers between devices: 55.1 us -> 32.9 us  [over(): return lax.ppermute(a, 'ctx', hop(dz, dx, dc))]
    pallas_call x2, Pallas kernels: 5.62 us -> 9.01 us  [mix(): pl.pallas_call(body, grid_spec=pltpu.PrefetchScalarGridSpec(num_scalar_pr...]
    dot_general x2 -> x0, matrix products: 2.57 us -> none  [the longest x1 1.6 us: split_heads(): jnp.dot(pick(query_blocks), block_mask.astype(F32))]
    pallas_call x7 -> x11, Pallas kernels: 33.6 us -> 35.3 us  [the longest x5 25.7 us: attend(): pl.pallas_call(body, grid=(steps,), in_specs=[fixed((1, rows, HEAD_DIM),...]
  transfers between devices with their start and end apart: 35 -> 35, of which waited for: 12 -> 12; matrix products, arithmetic and copies ran while one was open for 4% -> 1% of each run, Pallas kernels for 21% -> 33%
where the time goes in v4:
time: 140 us; the launch traced here: 139 us
  Pallas kernels  50.2 us (36%)
  waiting for transfers between devices  48.6 us (35%)
  starting transfers between devices  36.5 us (26%)
  local copies, waits for them, and re-layouts  2.54 us (2%)
    ppermute x31, waiting for transfers between devices, over(): return lax.ppermute(a, 'ctx', hop(dz, dx, dc))  32.9 us
    ppermute x31, starting transfers between devices, over(): return lax.ppermute(a, 'ctx', hop(dz, dx, dc))  31.7 us
    pallas_call x5, Pallas kernels, attend(): pl.pallas_call(body, grid=(steps,), in_specs=[fixed((1, rows, HEAD_DIM),...  25.7 us
    ppermute x4, waiting for transfers between devices, over_y(): return lax.ppermute(a, 'head', [(0, 1), (1, 0)])  15.6 us
    pallas_call x2, Pallas kernels, mix(): pl.pallas_call(body, grid_spec=pltpu.PrefetchScalarGridSpec(num_scalar_pr...  9.01 us
    pallas_call x5, Pallas kernels, project(): pl.pallas_call(body, in_specs=whole(2 * pieces + 1), out_specs=whole(len(...  8.54 us
    pallas_call x1, Pallas kernels, fetch(): pl.pallas_call(body, grid_spec=pltpu.PrefetchScalarGridSpec(num_scalar_pr...  5.84 us
    ppermute x4, starting transfers between devices, over_y(): return lax.ppermute(a, 'head', [(0, 1), (1, 0)])  4.83 us
  transfers between devices with their start and end apart: 35, of which 12 were waited for; matrix products, arithmetic and copies ran while one was open for 1% of the time, Pallas kernels for 33%

profile of v4, /device:TPU:0, one launch (start us, length us, event | category | flops | bytes accessed | tf_op | source)
XLA Modules:
  0.0 139.1 jit_solution(6288004972513982751)
XLA Ops:
  0.0 3.0 %collective-permute-start.1 = (bf16[256,1536]{1,0:T(8,128)(2,1)}, bf16[256,1536]{1,0:T(8,128)(2,1)S(1)}, u32[]{:S(2)}, u32[]{:S(2)}) collective-permute-start(bf16[256,1536]{1,0:T(8,128)(2,1)} %refs_0_.3), channel_id=1, source_target_pairs={{0,1},{1,0},{2,3},{3,2},{4,5},{5,4},{6,7},{7,6},{8,9},{9,8},{10,11... | collective-permute-start | bytes 2359304 | tf_op jit(solution)/shard_map/ppermute | solution.py:333
  3.0 1.2 fusion
  4.1 2.7 %collective-permute-start = (bf16[128,1536]{1,0:T(8,128)(2,1)S(1)}, bf16[128,1536]{1,0:T(8,128)(2,1)S(1)}, u32[]{:S(2)}, u32[]{:S(2)}) collective-permute-start(bf16[128,1536]{1,0:T(8,128)(2,1)S(1)} %get-tuple-element.94), channel_id=1, source_target_pairs={{0,16},{2,18},{4,20},{6,22},{8,24},{10,26},{12,28},{14,30},{16,0},... | collective-permute-start | bytes 1179656 | tf_op jit(solution)/shard_map/ppermute | solution.py:336
  6.9 0.7 copy-done.1
  7.6 0.7 copy-done.2
  8.2 1.1 shard_map.73.refs_3_.refs_22_.refs_26_
  9.3 5.8 %shard_map.74.refs_2_.refs_4_ = bf16[6,3072,384]{2,1,0:T(8,128)(2,1)S(1)} custom-call(s32[4]{0:T(128)S(1)} %pad_add_fusion.s, bf16[3072,1536]{1,0:T(8,128)(2,1)} %refs_0_.1, bf16[3072,1536]{1,0:T(8,128)(2,1)} %refs_1_.1, bf16[3072,1536]{1,0:T(8,128)(2,1)} %refs_2_.1, f32[8,4096]{1,0:T(8,128)S(1)} %shard_map.73.refs_3_.refs_22_.refs_26_), custom_call_target="tpu_custom_call" | custom-call | flops 1024 | bytes 1024 | tf_op jit(solution)/shard_map/pallas_call | solution.py:69
  15.2 8.9 %collective-permute-done.refs_0_ = bf16[128,1536]{1,0:T(8,128)(2,1)S(1)} collective-permute-done((bf16[128,1536]{1,0:T(8,128)(2,1)S(1)}, bf16[128,1536]{1,0:T(8,128)(2,1)S(1)}, u32[]{:S(2)}, u32[]{:S(2)}) %collective-permute-start) | collective-permute-done | bytes 393248 | tf_op jit(solution)/shard_map/ppermute | solution.py:336
  24.6 2.6 %shard_map.75 = (bf16[6,256,128]{2,1,0:T(8,128)(2,1)S(1)}, bf16[6,256,128]{2,1,0:T(8,128)(2,1)S(1)}) custom-call(bf16[256,1536]{1,0:T(8,128)(2,1)S(1)} %copy-done, bf16[256,1536]{1,0:T(8,128)(2,1)S(1)} %collective-permute-done.1.refs_1_, bf16[6,3072,384]{2,1,0:T(8,128)(2,1)S(1)} %shard_map.74.refs_2_.refs_4_), custom_call_target="tpu_custom_call" | custom-call | flops 1024 | bytes 1024 | tf_op jit(solution)/shard_map/pallas_call | solution.py:112
  27.2 4.2 %collective-permute-start.4 = (bf16[6,256,128]{2,1,0:T(8,128)(2,1)S(1)}, bf16[6,256,128]{2,1,0:T(8,128)(2,1)S(1)}, u32[]{:S(2)}, u32[]{:S(2)}) collective-permute-start(bf16[6,256,128]{2,1,0:T(8,128)(2,1)S(1)} %get-tuple-element.52), channel_id=1, source_target_pairs={{0,8},{2,10},{4,12},{6,14},{8,0},{10,2},{12,4},{14,6},{16,24},{18,... | collective-permute-start | bytes 1179656 | tf_op jit(solution)/shard_map/ppermute | solution.py:336
  31.3 1.5 %collective-permute-start.5 = (bf16[6,256,128]{2,1,0:T(8,128)(2,1)S(1)}, bf16[6,256,128]{2,1,0:T(8,128)(2,1)S(1)}, u32[]{:S(2)}, u32[]{:S(2)}) collective-permute-start(bf16[6,256,128]{2,1,0:T(8,128)(2,1)S(1)} %get-tuple-element.58.refs_6_.refs_14_), channel_id=1, source_target_pairs={{0,4},{2,6},{4,0},{6,2},{8,12},{10,14},{12,8},{14,10},{16,20},{18,... | collective-permute-start | bytes 1179656 | tf_op jit(solution)/shard_map/ppermute | solution.py:336
  32.8 1.4 shard_map.76
  34.2 9.3 %collective-permute-done.3.refs_1_ = bf16[128,1536]{1,0:T(8,128)(2,1)S(1)} collective-permute-done((bf16[128,1536]{1,0:T(8,128)(2,1)S(1)}, bf16[128,1536]{1,0:T(8,128)(2,1)S(1)}, u32[]{:S(2)}, u32[]{:S(2)}) %collective-permute-start.3) | collective-permute-done | bytes 393248 | tf_op jit(solution)/shard_map/ppermute | solution.py:336
  44.0 2.5 %collective-permute-done.4.refs_10_.refs_18_ = bf16[6,256,128]{2,1,0:T(8,128)(2,1)S(1)} collective-permute-done((bf16[6,256,128]{2,1,0:T(8,128)(2,1)S(1)}, bf16[6,256,128]{2,1,0:T(8,128)(2,1)S(1)}, u32[]{:S(2)}, u32[]{:S(2)}) %collective-permute-start.4) | collective-permute-done | bytes 393248 | tf_op jit(solution)/shard_map/ppermute | solution.py:336
  46.5 1.5 %collective-permute-start.14 = (bf16[6,256,128]{2,1,0:T(8,128)(2,1)S(1)}, bf16[6,256,128]{2,1,0:T(8,128)(2,1)S(1)}, u32[]{:S(2)}, u32[]{:S(2)}) collective-permute-start(bf16[6,256,128]{2,1,0:T(8,128)(2,1)S(1)} %collective-permute-done.4.refs_10_.refs_18_), channel_id=1, source_target_pairs={{0,4},{2,6},{4,0},{6,2},{8,12},{10,14},{12,8},{14,10},{16,20},{18,... | collective-permute-start | bytes 1179656 | tf_op jit(solution)/shard_map/ppermute | solution.py:336
  48.5 4.0 %collective-permute-done.7.refs_3_ = bf16[128,1536]{1,0:T(8,128)(2,1)S(1)} collective-permute-done((bf16[128,1536]{1,0:T(8,128)(2,1)S(1)}, bf16[128,1536]{1,0:T(8,128)(2,1)S(1)}, u32[]{:S(2)}, u32[]{:S(2)}) %collective-permute-start.7) | collective-permute-done | bytes 393248 | tf_op jit(solution)/shard_map/ppermute | solution.py:333
  52.5 1.4 shard_map.77
  53.9 1.4 shard_map.78.refs_4_.refs_12_
  55.3 1.8 %shard_map.79 = (bf16[4,256,128]{2,1,0:T(8,128)(2,1)S(1)}, bf16[3,256,128]{2,1,0:T(8,128)(2,1)S(1)}) custom-call(bf16[128,1536]{1,0:T(8,128)(2,1)S(1)} %collective-permute-done.refs_0_, bf16[128,1536]{1,0:T(8,128)(2,1)S(1)} %collective-permute-done.3.refs_1_, bf16[128,1536]{1,0:T(8,128)(2,1)S(1)} %collective-permute-done.6.refs_2_, ...), custom_call_target="tpu_custom_call" | custom-call | flops 1024 | bytes 1024 | tf_op jit(solution)/shard_map/pallas_call | solution.py:112
  57.1 0.6 collective-permute-start.16
  57.7 1.5 %collective-permute-start.9 = (bf16[6,256,128]{2,1,0:T(8,128)(2,1)S(1)}, bf16[6,256,128]{2,1,0:T(8,128)(2,1)S(1)}, u32[]{:S(2)}, u32[]{:S(2)}) collective-permute-start(bf16[6,256,128]{2,1,0:T(8,128)(2,1)S(1)} %shard_map.78.refs_4_.refs_12_), channel_id=1, source_target_pairs={{0,4},{2,6},{4,0},{6,2},{8,12},{10,14},{12,8},{14,10},{16,20},{18,... | collective-permute-start | bytes 1179656 | tf_op jit(solution)/shard_map/ppermute | solution.py:336
  59.5 1.7 %collective-permute-start.11 = (bf16[2,256,128]{2,1,0:T(8,128)(2,1)S(1)}, bf16[2,256,128]{2,1,0:T(8,128)(2,1)S(1)}, u32[]{:S(2)}, u32[]{:S(2)}) collective-permute-start(bf16[2,256,128]{2,1,0:T(8,128)(2,1)S(1)} %get-tuple-element.63), channel_id=1, source_target_pairs={{0,8},{2,10},{4,12},{6,14},{8,0},{10,2},{12,4},{14,6},{16,24},{18,... | collective-permute-start | bytes 393224 | tf_op jit(solution)/shard_map/ppermute | solution.py:336
  61.6 5.5 %shard_map.80 = (f32[3,512,128]{2,1,0:T(8,128)S(1)}, f32[3,512,128]{2,1,0:T(8,128)S(1)}, f32[3,512,128]{2,1,0:T(8,128)S(1)}) custom-call(bf16[3,256,128]{2,1,0:T(8,128)(2,1)S(1)} %get-tuple-element.54.refs_0_.refs_2_.refs_4_, bf16[3,256,128]{2,1,0:T(8,128)(2,1)S(1)} %collective-permute-done.2.refs_1_.refs_3_.refs_5_, ...), custom_call_target="tpu_custom_call" | custom-call | flops 1024 | bytes 1024 | tf_op jit(solution)/shard_map/pallas_call | solution.py:262
  67.0 4.1 %collective-permute-done.11.refs_8_.refs_16_ = bf16[2,256,128]{2,1,0:T(8,128)(2,1)S(1)} collective-permute-done((bf16[2,256,128]{2,1,0:T(8,128)(2,1)S(1)}, bf16[2,256,128]{2,1,0:T(8,128)(2,1)S(1)}, u32[]{:S(2)}, u32[]{:S(2)}) %collective-permute-start.11) | collective-permute-done | bytes 131104 | tf_op jit(solution)/shard_map/ppermute | solution.py:336
  71.2 0.5 collective-permute-start.19
  71.7 1.5 %collective-permute-start.22 = (bf16[4,256,128]{2,1,0:T(8,128)(2,1)S(1)}, bf16[4,256,128]{2,1,0:T(8,128)(2,1)S(1)}, u32[]{:S(2)}, u32[]{:S(2)}) collective-permute-start(bf16[4,256,128]{2,1,0:T(8,128)(2,1)S(1)} %collective-permute-done.10.refs_24_.refs_8_.refs_16_), channel_id=1, source_target_pairs={{0,4},{2,6},{4,0},{6,2},{8,12},{10,14},{12,8},{14,10},{16,20},{18,... | collective-permute-start | bytes 786440 | tf_op jit(solution)/shard_map/ppermute | solution.py:336
  73.2 0.5 collective-permute-start.18
  74.2 5.5 %shard_map.81 = (f32[3,512,128]{2,1,0:T(8,128)S(1)}, f32[3,512,128]{2,1,0:T(8,128)S(1)}, f32[3,512,128]{2,1,0:T(8,128)S(1)}) custom-call(bf16[3,256,128]{2,1,0:T(8,128)(2,1)S(1)} %get-tuple-element.66.refs_0_.refs_2_.refs_4_, bf16[3,256,128]{2,1,0:T(8,128)(2,1)S(1)} %collective-permute-done.8.refs_1_.refs_3_.refs_5_, ...), custom_call_target="tpu_custom_call" | custom-call | flops 1024 | bytes 1024 | tf_op jit(solution)/shard_map/pallas_call | solution.py:262
  80.3 0.8 collective-permute-done.21.refs_11_.refs_19_
  81.6 1.2 collective-permute-done.20.refs_10_.refs_18_
  82.9 4.9 %shard_map.82 = (bf16[256,128]{1,0:T(8,128)(2,1)S(1)}, bf16[256,128]{1,0:T(8,128)(2,1)S(1)}, bf16[256,128]{1,0:T(8,128)(2,1)S(1)}, bf16[256,128]{1,0:T(8,128)(2,1)S(1)}) custom-call(bf16[3,256,128]{2,1,0:T(8,128)(2,1)S(1)} %get-tuple-element.54.refs_0_.refs_2_.refs_4_, bf16[3,256,128]{2,1,0:T(8,128)(2,1)S(1)} %collective-permute-done.2.refs_1_.refs_3_.refs_5_, ...), custom_call_target="tpu_custom_call" | custom-call | flops 1024 | bytes 1024 | tf_op jit(solution)/shard_map/pallas_call | solution.py:262
  88.2 3.4 %collective-permute-start.28 = (bf16[256,128]{1,0:T(8,128)(2,1)S(1)}, bf16[256,128]{1,0:T(8,128)(2,1)S(1)}, u32[]{:S(2)}, u32[]{:S(2)}) collective-permute-start(bf16[256,128]{1,0:T(8,128)(2,1)S(1)} %get-tuple-element.87), channel_id=1, source_target_pairs={{0,16},{2,18},{4,20},{6,22},{8,24},{10,26},{12,28},{14,30},{16,0},... | collective-permute-start | bytes 196616 | tf_op jit(solution)/shard_map/ppermute | solution.py:336
  91.6 0.7 collective-permute-start.31
  92.2 4.9 %shard_map.83 = (bf16[256,128]{1,0:T(8,128)(2,1)S(1)}, bf16[256,128]{1,0:T(8,128)(2,1)S(1)}, bf16[256,128]{1,0:T(8,128)(2,1)S(1)}, bf16[256,128]{1,0:T(8,128)(2,1)S(1)}) custom-call(bf16[3,256,128]{2,1,0:T(8,128)(2,1)S(1)} %get-tuple-element.54.refs_0_.refs_2_.refs_4_, bf16[3,256,128]{2,1,0:T(8,128)(2,1)S(1)} %collective-permute-done.2.refs_1_.refs_3_.refs_5_, ...), custom_call_target="tpu_custom_call" | custom-call | flops 1024 | bytes 1024 | tf_op jit(solution)/shard_map/pallas_call | solution.py:262
  97.2 5.0 %shard_map.84 = (bf16[256,128]{1,0:T(8,128)(2,1)S(1)}, bf16[256,128]{1,0:T(8,128)(2,1)S(1)}, bf16[256,128]{1,0:T(8,128)(2,1)S(1)}, bf16[256,128]{1,0:T(8,128)(2,1)S(1)}) custom-call(bf16[3,256,128]{2,1,0:T(8,128)(2,1)S(1)} %get-tuple-element.54.refs_0_.refs_2_.refs_4_, bf16[3,256,128]{2,1,0:T(8,128)(2,1)S(1)} %collective-permute-done.2.refs_1_.refs_3_.refs_5_, ...), custom_call_target="tpu_custom_call" | custom-call | flops 1024 | bytes 1024 | tf_op jit(solution)/shard_map/pallas_call | solution.py:262
  102.2 2.0 %collective-permute-start.27 = (bf16[256,128]{1,0:T(8,128)(2,1)S(1)}, bf16[256,128]{1,0:T(8,128)(2,1)S(1)}, u32[]{:S(2)}, u32[]{:S(2)}) collective-permute-start(bf16[256,128]{1,0:T(8,128)(2,1)S(1)} %get-tuple-element.86), channel_id=1, source_target_pairs={{0,8},{2,10},{4,12},{6,14},{8,0},{10,2},{12,4},{14,6},{16,24},{18,... | collective-permute-start | bytes 196616 | tf_op jit(solution)/shard_map/ppermute | solution.py:336
  104.2 1.8 %collective-permute-start.29 = (bf16[256,128]{1,0:T(8,128)(2,1)S(1)}, bf16[256,128]{1,0:T(8,128)(2,1)S(1)}, u32[]{:S(2)}, u32[]{:S(2)}) collective-permute-start(bf16[256,128]{1,0:T(8,128)(2,1)S(1)} %get-tuple-element.88), channel_id=1, source_target_pairs={{0,16},{2,18},{4,20},{6,22},{8,24},{10,26},{12,28},{14,30},{16,0},... | collective-permute-start | bytes 196616 | tf_op jit(solution)/shard_map/ppermute | solution.py:336
  106.0 1.1 collective-permute-start.30
  107.1 3.2 %collective-permute-start.32 = (bf16[256,128]{1,0:T(8,128)(2,1)S(1)}, bf16[256,128]{1,0:T(8,128)(2,1)S(1)}, u32[]{:S(2)}, u32[]{:S(2)}) collective-permute-start(bf16[256,128]{1,0:T(8,128)(2,1)S(1)} %get-tuple-element.91), channel_id=1, source_target_pairs={{0,24},{2,26},{4,28},{6,30},{8,16},{10,18},{12,20},{14,22},{16,8},... | collective-permute-start | bytes 196616 | tf_op jit(solution)/shard_map/ppermute | solution.py:336
  110.3 0.7 collective-permute-start.33
  111.0 3.3 %collective-permute-done.29.refs_7_ = bf16[256,128]{1,0:T(8,128)(2,1)S(1)} collective-permute-done((bf16[256,128]{1,0:T(8,128)(2,1)S(1)}, bf16[256,128]{1,0:T(8,128)(2,1)S(1)}, u32[]{:S(2)}, u32[]{:S(2)}) %collective-permute-start.29) | collective-permute-done | bytes 65568 | tf_op jit(solution)/shard_map/ppermute | solution.py:336
  114.3 1.4 %collective-permute-done.30.refs_8_ = bf16[256,128]{1,0:T(8,128)(2,1)S(1)} collective-permute-done((bf16[256,128]{1,0:T(8,128)(2,1)S(1)}, bf16[256,128]{1,0:T(8,128)(2,1)S(1)}, u32[]{:S(2)}, u32[]{:S(2)}) %collective-permute-start.30) | collective-permute-done | bytes 65568 | tf_op jit(solution)/shard_map/ppermute | solution.py:336
  115.7 0.8 collective-permute-done.33.refs_11_
  116.5 4.5 %shard_map.86 = bf16[256,1536]{1,0:T(8,128)(2,1)S(1)} custom-call(s32[4]{0:T(128)S(1)} %pad_add_fusion.s, bf16[256,128]{1,0:T(8,128)(2,1)S(1)} %get-tuple-element.80.refs_27_.refs_0_, bf16[256,128]{1,0:T(8,128)(2,1)S(1)} %get-tuple-element.82.refs_27_.refs_1_, bf16[256,128]{1,0:T(8,128)(2,1)S(1)} %get-tuple-element.83.refs_2_, ...), custom_call_target="tpu_custom_call" | custom-call | flops 1024 | bytes 1024 | tf_op jit(solution)/shard_map/pallas_call | solution.py:305
  121.0 0.9 collective-permute-start.34
  121.9 4.5 %shard_map.85 = bf16[256,1536]{1,0:T(8,128)(2,1)S(1)} custom-call(s32[4]{0:T(128)S(1)} %pad_add_fusion.s, bf16[256,128]{1,0:T(8,128)(2,1)S(1)} %get-tuple-element.80.refs_27_.refs_0_, bf16[256,128]{1,0:T(8,128)(2,1)S(1)} %get-tuple-element.82.refs_27_.refs_1_, bf16[256,128]{1,0:T(8,128)(2,1)S(1)} %get-tuple-element.83.refs_2_, ...), custom_call_target="tpu_custom_call" | custom-call | flops 1024 | bytes 1024 | tf_op jit(solution)/shard_map/pallas_call | solution.py:305
  126.4 11.6 %collective-permute-done.34 = bf16[256,1536]{1,0:T(8,128)(2,1)S(1)} collective-permute-done((bf16[256,1536]{1,0:T(8,128)(2,1)S(1)}, bf16[256,1536]{1,0:T(8,128)(2,1)S(1)}, u32[]{:S(2)}, u32[]{:S(2)}) %collective-permute-start.34) | collective-permute-done | bytes 786464 | tf_op jit(solution)/shard_map/ppermute | solution.py:333
  138.0 1.1 add_convert_fusion
  (45 shorter events, 4.3 us)
Async XLA Ops:
  0.0 24.6 %collective-permute-start.1 = (bf16[256,1536]{1,0:T(8,128)(2,1)}, bf16[256,1536]{1,0:T(8,128)(2,1)S(1)}, u32[]{:S(2)}, u32[]{:S(2)}) collective-permute-start(bf16[256,1536]{1,0:T(8,128)(2,1)} %refs_0_.3), channel_id=1, source_target_pairs={{0,1},{1,0},{2,3},{3,2},{4,5},{5,4},{6,7},{7,6},{8,9},{9,8},{10,11... | collective-permute-start | bytes 2359304 | tf_op jit(solution)/shard_map/ppermute | solution.py:333
  4.1 20.0 %collective-permute-start = (bf16[128,1536]{1,0:T(8,128)(2,1)S(1)}, bf16[128,1536]{1,0:T(8,128)(2,1)S(1)}, u32[]{:S(2)}, u32[]{:S(2)}) collective-permute-start(bf16[128,1536]{1,0:T(8,128)(2,1)S(1)} %get-tuple-element.94), channel_id=1, source_target_pairs={{0,16},{2,18},{4,20},{6,22},{8,24},{10,26},{12,28},{14,30},{16,0},... | collective-permute-start | bytes 1179656 | tf_op jit(solution)/shard_map/ppermute | solution.py:336
  6.9 0.7 copy-start.1
  7.6 0.7 copy-start.2
  9.3 15.3 %copy-start = (bf16[256,1536]{1,0:T(8,128)(2,1)S(1)}, bf16[256,1536]{1,0:T(8,128)(2,1)}, u32[]{:S(2)}) copy-start(bf16[256,1536]{1,0:T(8,128)(2,1)} %refs_0_.3) | copy-start | bytes 2359300
  24.1 19.4 %collective-permute-start.3 = (bf16[128,1536]{1,0:T(8,128)(2,1)S(1)}, bf16[128,1536]{1,0:T(8,128)(2,1)S(1)}, u32[]{:S(2)}, u32[]{:S(2)}) collective-permute-start(bf16[128,1536]{1,0:T(8,128)(2,1)S(1)} %get-tuple-element.56), channel_id=1, source_target_pairs={{0,16},{2,18},{4,20},{6,22},{8,24},{10,26},{12,28},{14,30},{16,0},... | collective-permute-start | bytes 1179656 | tf_op jit(solution)/shard_map/ppermute | solution.py:336
  24.1 19.4 %collective-permute-start.6 = (bf16[128,1536]{1,0:T(8,128)(2,1)S(1)}, bf16[128,1536]{1,0:T(8,128)(2,1)S(1)}, u32[]{:S(2)}, u32[]{:S(2)}) collective-permute-start(bf16[128,1536]{1,0:T(8,128)(2,1)S(1)} %collective-permute-done.refs_0_), channel_id=1, source_target_pairs={{0,1},{1,0},{2,3},{3,2},{4,5},{5,4},{6,7},{7,6},{8,9},{9,8},{10,11... | collective-permute-start | bytes 1179656 | tf_op jit(solution)/shard_map/ppermute | solution.py:333
  27.2 19.3 %collective-permute-start.4 = (bf16[6,256,128]{2,1,0:T(8,128)(2,1)S(1)}, bf16[6,256,128]{2,1,0:T(8,128)(2,1)S(1)}, u32[]{:S(2)}, u32[]{:S(2)}) collective-permute-start(bf16[6,256,128]{2,1,0:T(8,128)(2,1)S(1)} %get-tuple-element.52), channel_id=1, source_target_pairs={{0,8},{2,10},{4,12},{6,14},{8,0},{10,2},{12,4},{14,6},{16,24},{18,... | collective-permute-start | bytes 1179656 | tf_op jit(solution)/shard_map/ppermute | solution.py:336
  31.3 15.1 %collective-permute-start.5 = (bf16[6,256,128]{2,1,0:T(8,128)(2,1)S(1)}, bf16[6,256,128]{2,1,0:T(8,128)(2,1)S(1)}, u32[]{:S(2)}, u32[]{:S(2)}) collective-permute-start(bf16[6,256,128]{2,1,0:T(8,128)(2,1)S(1)} %get-tuple-element.58.refs_6_.refs_14_), channel_id=1, source_target_pairs={{0,4},{2,6},{4,0},{6,2},{8,12},{10,14},{12,8},{14,10},{16,20},{18,... | collective-permute-start | bytes 1179656 | tf_op jit(solution)/shard_map/ppermute | solution.py:336
  43.5 9.0 %collective-permute-start.7 = (bf16[128,1536]{1,0:T(8,128)(2,1)S(1)}, bf16[128,1536]{1,0:T(8,128)(2,1)S(1)}, u32[]{:S(2)}, u32[]{:S(2)}) collective-permute-start(bf16[128,1536]{1,0:T(8,128)(2,1)S(1)} %collective-permute-done.3.refs_1_), channel_id=1, source_target_pairs={{0,1},{1,0},{2,3},{3,2},{4,5},{5,4},{6,7},{7,6},{8,9},{9,8},{10,11... | collective-permute-start | bytes 1179656 | tf_op jit(solution)/shard_map/ppermute | solution.py:333
  46.5 10.6 %collective-permute-start.14 = (bf16[6,256,128]{2,1,0:T(8,128)(2,1)S(1)}, bf16[6,256,128]{2,1,0:T(8,128)(2,1)S(1)}, u32[]{:S(2)}, u32[]{:S(2)}) collective-permute-start(bf16[6,256,128]{2,1,0:T(8,128)(2,1)S(1)} %collective-permute-done.4.refs_10_.refs_18_), channel_id=1, source_target_pairs={{0,4},{2,6},{4,0},{6,2},{8,12},{10,14},{12,8},{14,10},{16,20},{18,... | collective-permute-start | bytes 1179656 | tf_op jit(solution)/shard_map/ppermute | solution.py:336
  48.0 11.2 %collective-permute-start.12 = (bf16[6,256,128]{2,1,0:T(8,128)(2,1)S(1)}, bf16[6,256,128]{2,1,0:T(8,128)(2,1)S(1)}, u32[]{:S(2)}, u32[]{:S(2)}) collective-permute-start(bf16[6,256,128]{2,1,0:T(8,128)(2,1)S(1)} %get-tuple-element.58.refs_6_.refs_14_), channel_id=1, source_target_pairs={{0,2},{2,0},{4,6},{6,4},{8,10},{10,8},{12,14},{14,12},{16,18},{18,... | collective-permute-start | bytes 1179656 | tf_op jit(solution)/shard_map/ppermute | solution.py:336
  48.0 11.6 %collective-permute-start.13 = (bf16[6,256,128]{2,1,0:T(8,128)(2,1)S(1)}, bf16[6,256,128]{2,1,0:T(8,128)(2,1)S(1)}, u32[]{:S(2)}, u32[]{:S(2)}) collective-permute-start(bf16[6,256,128]{2,1,0:T(8,128)(2,1)S(1)} %collective-permute-done.5.refs_7_.refs_15_), channel_id=1, source_target_pairs={{0,2},{2,0},{4,6},{6,4},{8,10},{10,8},{12,14},{14,12},{16,18},{18,... | collective-permute-start | bytes 1179656 | tf_op jit(solution)/shard_map/ppermute | solution.py:336
  48.5 9.2 %collective-permute-start.2 = (bf16[3,256,128]{2,1,0:T(8,128)(2,1)S(1)}, bf16[3,256,128]{2,1,0:T(8,128)(2,1)S(1)}, u32[]{:S(2)}, u32[]{:S(2)}) collective-permute-start(bf16[3,256,128]{2,1,0:T(8,128)(2,1)S(1)} %get-tuple-element.55), channel_id=1, source_target_pairs={{0,8},{2,10},{4,12},{6,14},{8,0},{10,2},{12,4},{14,6},{16,24},{18,... | collective-permute-start | bytes 589832 | tf_op jit(solution)/shard_map/ppermute | solution.py:336
  52.5 8.7 %collective-permute-start.15 = (bf16[6,256,128]{2,1,0:T(8,128)(2,1)S(1)}, bf16[6,256,128]{2,1,0:T(8,128)(2,1)S(1)}, u32[]{:S(2)}, u32[]{:S(2)}) collective-permute-start(bf16[6,256,128]{2,1,0:T(8,128)(2,1)S(1)} %collective-permute-done.4.refs_10_.refs_18_), channel_id=1, source_target_pairs={{0,2},{2,0},{4,6},{6,4},{8,10},{10,8},{12,14},{14,12},{16,18},{18,... | collective-permute-start | bytes 1179656 | tf_op jit(solution)/shard_map/ppermute | solution.py:336
  57.1 4.5 %collective-permute-start.16 = (bf16[6,256,128]{2,1,0:T(8,128)(2,1)S(1)}, bf16[6,256,128]{2,1,0:T(8,128)(2,1)S(1)}, u32[]{:S(2)}, u32[]{:S(2)}) collective-permute-start(bf16[6,256,128]{2,1,0:T(8,128)(2,1)S(1)} %collective-permute-done.14.refs_11_.refs_19_), channel_id=1, source_target_pairs={{0,2},{2,0},{4,6},{6,4},{8,10},{10,8},{12,14},{14,12},{16,18},{18,... | collective-permute-start | bytes 1179656 | tf_op jit(solution)/shard_map/ppermute | solution.py:336
  57.7 15.5 %collective-permute-start.9 = (bf16[6,256,128]{2,1,0:T(8,128)(2,1)S(1)}, bf16[6,256,128]{2,1,0:T(8,128)(2,1)S(1)}, u32[]{:S(2)}, u32[]{:S(2)}) collective-permute-start(bf16[6,256,128]{2,1,0:T(8,128)(2,1)S(1)} %shard_map.78.refs_4_.refs_12_), channel_id=1, source_target_pairs={{0,4},{2,6},{4,0},{6,2},{8,12},{10,14},{12,8},{14,10},{16,20},{18,... | collective-permute-start | bytes 1179656 | tf_op jit(solution)/shard_map/ppermute | solution.py:336
  59.2 12.5 %collective-permute-start.10 = (bf16[4,256,128]{2,1,0:T(8,128)(2,1)S(1)}, bf16[4,256,128]{2,1,0:T(8,128)(2,1)S(1)}, u32[]{:S(2)}, u32[]{:S(2)}) collective-permute-start(bf16[4,256,128]{2,1,0:T(8,128)(2,1)S(1)} %get-tuple-element.68), channel_id=1, source_target_pairs={{0,8},{2,10},{4,12},{6,14},{8,0},{10,2},{12,4},{14,6},{16,24},{18,... | collective-permute-start | bytes 786440 | tf_op jit(solution)/shard_map/ppermute | solution.py:336
  59.5 11.7 %collective-permute-start.11 = (bf16[2,256,128]{2,1,0:T(8,128)(2,1)S(1)}, bf16[2,256,128]{2,1,0:T(8,128)(2,1)S(1)}, u32[]{:S(2)}, u32[]{:S(2)}) collective-permute-start(bf16[2,256,128]{2,1,0:T(8,128)(2,1)S(1)} %get-tuple-element.63), channel_id=1, source_target_pairs={{0,8},{2,10},{4,12},{6,14},{8,0},{10,2},{12,4},{14,6},{16,24},{18,... | collective-permute-start | bytes 393224 | tf_op jit(solution)/shard_map/ppermute | solution.py:336
  61.2 13.0 %collective-permute-start.8 = (bf16[3,256,128]{2,1,0:T(8,128)(2,1)S(1)}, bf16[3,256,128]{2,1,0:T(8,128)(2,1)S(1)}, u32[]{:S(2)}, u32[]{:S(2)}) collective-permute-start(bf16[3,256,128]{2,1,0:T(8,128)(2,1)S(1)} %get-tuple-element.67), channel_id=1, source_target_pairs={{0,8},{2,10},{4,12},{6,14},{8,0},{10,2},{12,4},{14,6},{16,24},{18,... | collective-permute-start | bytes 589832 | tf_op jit(solution)/shard_map/ppermute | solution.py:336
  71.2 8.5 %collective-permute-start.19 = (bf16[2,256,128]{2,1,0:T(8,128)(2,1)S(1)}, bf16[2,256,128]{2,1,0:T(8,128)(2,1)S(1)}, u32[]{:S(2)}, u32[]{:S(2)}) collective-permute-start(bf16[2,256,128]{2,1,0:T(8,128)(2,1)S(1)} %collective-permute-done.11.refs_8_.refs_16_), channel_id=1, source_target_pairs={{0,4},{2,6},{4,0},{6,2},{8,12},{10,14},{12,8},{14,10},{16,20},{18,... | collective-permute-start | bytes 393224 | tf_op jit(solution)/shard_map/ppermute | solution.py:336
  71.7 8.6 %collective-permute-start.22 = (bf16[4,256,128]{2,1,0:T(8,128)(2,1)S(1)}, bf16[4,256,128]{2,1,0:T(8,128)(2,1)S(1)}, u32[]{:S(2)}, u32[]{:S(2)}) collective-permute-start(bf16[4,256,128]{2,1,0:T(8,128)(2,1)S(1)} %collective-permute-done.10.refs_24_.refs_8_.refs_16_), channel_id=1, source_target_pairs={{0,4},{2,6},{4,0},{6,2},{8,12},{10,14},{12,8},{14,10},{16,20},{18,... | collective-permute-start | bytes 786440 | tf_op jit(solution)/shard_map/ppermute | solution.py:336
  73.2 8.4 %collective-permute-start.17 = (bf16[6,256,128]{2,1,0:T(8,128)(2,1)S(1)}, bf16[6,256,128]{2,1,0:T(8,128)(2,1)S(1)}, u32[]{:S(2)}, u32[]{:S(2)}) collective-permute-start(bf16[6,256,128]{2,1,0:T(8,128)(2,1)S(1)} %shard_map.78.refs_4_.refs_12_), channel_id=1, source_target_pairs={{0,2},{2,0},{4,6},{6,4},{8,10},{10,8},{12,14},{14,12},{16,18},{18,... | collective-permute-start | bytes 1179656 | tf_op jit(solution)/shard_map/ppermute | solution.py:336
  73.2 9.6 %collective-permute-start.18 = (bf16[6,256,128]{2,1,0:T(8,128)(2,1)S(1)}, bf16[6,256,128]{2,1,0:T(8,128)(2,1)S(1)}, u32[]{:S(2)}, u32[]{:S(2)}) collective-permute-start(bf16[6,256,128]{2,1,0:T(8,128)(2,1)S(1)} %collective-permute-done.9.refs_23_.refs_5_.refs_13_), channel_id=1, source_target_pairs={{0,2},{2,0},{4,6},{6,4},{8,10},{10,8},{12,14},{14,12},{16,18},{18,... | collective-permute-start | bytes 1179656 | tf_op jit(solution)/shard_map/ppermute | solution.py:336
  79.7 1.4 %collective-permute-start.21 = (bf16[2,256,128]{2,1,0:T(8,128)(2,1)S(1)}, bf16[2,256,128]{2,1,0:T(8,128)(2,1)S(1)}, u32[]{:S(2)}, u32[]{:S(2)}) collective-permute-start(bf16[2,256,128]{2,1,0:T(8,128)(2,1)S(1)} %collective-permute-done.19.refs_9_.refs_17_), channel_id=1, source_target_pairs={{0,2},{2,0},{4,6},{6,4},{8,10},{10,8},{12,14},{14,12},{16,18},{18,... | collective-permute-start | bytes 393224 | tf_op jit(solution)/shard_map/ppermute | solution.py:336
  79.8 12.4 %collective-permute-start.23 = (bf16[4,256,128]{2,1,0:T(8,128)(2,1)S(1)}, bf16[4,256,128]{2,1,0:T(8,128)(2,1)S(1)}, u32[]{:S(2)}, u32[]{:S(2)}) collective-permute-start(bf16[4,256,128]{2,1,0:T(8,128)(2,1)S(1)} %collective-permute-done.10.refs_24_.refs_8_.refs_16_), channel_id=1, source_target_pairs={{0,2},{2,0},{4,6},{6,4},{8,10},{10,8},{12,14},{14,12},{16,18},{18,... | collective-permute-start | bytes 786440 | tf_op jit(solution)/shard_map/ppermute | solution.py:336
  81.1 11.1 %collective-permute-start.24 = (bf16[4,256,128]{2,1,0:T(8,128)(2,1)S(1)}, bf16[4,256,128]{2,1,0:T(8,128)(2,1)S(1)}, u32[]{:S(2)}, u32[]{:S(2)}) collective-permute-start(bf16[4,256,128]{2,1,0:T(8,128)(2,1)S(1)} %collective-permute-done.22.refs_9_.refs_17_), channel_id=1, source_target_pairs={{0,2},{2,0},{4,6},{6,4},{8,10},{10,8},{12,14},{14,12},{16,18},{18,... | collective-permute-start | bytes 786440 | tf_op jit(solution)/shard_map/ppermute | solution.py:336
  81.3 1.6 %collective-permute-start.20 = (bf16[2,256,128]{2,1,0:T(8,128)(2,1)S(1)}, bf16[2,256,128]{2,1,0:T(8,128)(2,1)S(1)}, u32[]{:S(2)}, u32[]{:S(2)}) collective-permute-start(bf16[2,256,128]{2,1,0:T(8,128)(2,1)S(1)} %collective-permute-done.11.refs_8_.refs_16_), channel_id=1, source_target_pairs={{0,2},{2,0},{4,6},{6,4},{8,10},{10,8},{12,14},{14,12},{16,18},{18,... | collective-permute-start | bytes 393224 | tf_op jit(solution)/shard_map/ppermute | solution.py:336
  87.8 16.4 %collective-permute-start.25 = (bf16[256,128]{1,0:T(8,128)(2,1)S(1)}, bf16[256,128]{1,0:T(8,128)(2,1)S(1)}, u32[]{:S(2)}, u32[]{:S(2)}) collective-permute-start(bf16[256,128]{1,0:T(8,128)(2,1)S(1)} %get-tuple-element.84), channel_id=1, source_target_pairs={{0,8},{2,10},{4,12},{6,14},{8,0},{10,2},{12,4},{14,6},{16,24},{18,... | collective-permute-start | bytes 196616 | tf_op jit(solution)/shard_map/ppermute | solution.py:336
  88.2 17.8 %collective-permute-start.28 = (bf16[256,128]{1,0:T(8,128)(2,1)S(1)}, bf16[256,128]{1,0:T(8,128)(2,1)S(1)}, u32[]{:S(2)}, u32[]{:S(2)}) collective-permute-start(bf16[256,128]{1,0:T(8,128)(2,1)S(1)} %get-tuple-element.87), channel_id=1, source_target_pairs={{0,16},{2,18},{4,20},{6,22},{8,24},{10,26},{12,28},{14,30},{16,0},... | collective-permute-start | bytes 196616 | tf_op jit(solution)/shard_map/ppermute | solution.py:336
  91.6 15.6 %collective-permute-start.31 = (bf16[256,128]{1,0:T(8,128)(2,1)S(1)}, bf16[256,128]{1,0:T(8,128)(2,1)S(1)}, u32[]{:S(2)}, u32[]{:S(2)}) collective-permute-start(bf16[256,128]{1,0:T(8,128)(2,1)S(1)} %get-tuple-element.90), channel_id=1, source_target_pairs={{0,24},{2,26},{4,28},{6,30},{8,16},{10,18},{12,20},{14,22},{16,8},... | collective-permute-start | bytes 196616 | tf_op jit(solution)/shard_map/ppermute | solution.py:336
  97.1 13.2 %collective-permute-start.26 = (bf16[256,128]{1,0:T(8,128)(2,1)S(1)}, bf16[256,128]{1,0:T(8,128)(2,1)S(1)}, u32[]{:S(2)}, u32[]{:S(2)}) collective-permute-start(bf16[256,128]{1,0:T(8,128)(2,1)S(1)} %get-tuple-element.85), channel_id=1, source_target_pairs={{0,8},{2,10},{4,12},{6,14},{8,0},{10,2},{12,4},{14,6},{16,24},{18,... | collective-permute-start | bytes 196616 | tf_op jit(solution)/shard_map/ppermute | solution.py:336
  102.2 8.8 %collective-permute-start.27 = (bf16[256,128]{1,0:T(8,128)(2,1)S(1)}, bf16[256,128]{1,0:T(8,128)(2,1)S(1)}, u32[]{:S(2)}, u32[]{:S(2)}) collective-permute-start(bf16[256,128]{1,0:T(8,128)(2,1)S(1)} %get-tuple-element.86), channel_id=1, source_target_pairs={{0,8},{2,10},{4,12},{6,14},{8,0},{10,2},{12,4},{14,6},{16,24},{18,... | collective-permute-start | bytes 196616 | tf_op jit(solution)/shard_map/ppermute | solution.py:336
  104.2 10.1 %collective-permute-start.29 = (bf16[256,128]{1,0:T(8,128)(2,1)S(1)}, bf16[256,128]{1,0:T(8,128)(2,1)S(1)}, u32[]{:S(2)}, u32[]{:S(2)}) collective-permute-start(bf16[256,128]{1,0:T(8,128)(2,1)S(1)} %get-tuple-element.88), channel_id=1, source_target_pairs={{0,16},{2,18},{4,20},{6,22},{8,24},{10,26},{12,28},{14,30},{16,0},... | collective-permute-start | bytes 196616 | tf_op jit(solution)/shard_map/ppermute | solution.py:336
  106.0 9.7 %collective-permute-start.30 = (bf16[256,128]{1,0:T(8,128)(2,1)S(1)}, bf16[256,128]{1,0:T(8,128)(2,1)S(1)}, u32[]{:S(2)}, u32[]{:S(2)}) collective-permute-start(bf16[256,128]{1,0:T(8,128)(2,1)S(1)} %get-tuple-element.89), channel_id=1, source_target_pairs={{0,16},{2,18},{4,20},{6,22},{8,24},{10,26},{12,28},{14,30},{16,0},... | collective-permute-start | bytes 196616 | tf_op jit(solution)/shard_map/ppermute | solution.py:336
  107.1 8.6 %collective-permute-start.32 = (bf16[256,128]{1,0:T(8,128)(2,1)S(1)}, bf16[256,128]{1,0:T(8,128)(2,1)S(1)}, u32[]{:S(2)}, u32[]{:S(2)}) collective-permute-start(bf16[256,128]{1,0:T(8,128)(2,1)S(1)} %get-tuple-element.91), channel_id=1, source_target_pairs={{0,24},{2,26},{4,28},{6,30},{8,16},{10,18},{12,20},{14,22},{16,8},... | collective-permute-start | bytes 196616 | tf_op jit(solution)/shard_map/ppermute | solution.py:336
  110.3 6.2 %collective-permute-start.33 = (bf16[256,128]{1,0:T(8,128)(2,1)S(1)}, bf16[256,128]{1,0:T(8,128)(2,1)S(1)}, u32[]{:S(2)}, u32[]{:S(2)}) collective-permute-start(bf16[256,128]{1,0:T(8,128)(2,1)S(1)} %get-tuple-element.92), channel_id=1, source_target_pairs={{0,24},{2,26},{4,28},{6,30},{8,16},{10,18},{12,20},{14,22},{16,8},... | collective-permute-start | bytes 196616 | tf_op jit(solution)/shard_map/ppermute | solution.py:336
  121.0 17.0 %collective-permute-start.34 = (bf16[256,1536]{1,0:T(8,128)(2,1)S(1)}, bf16[256,1536]{1,0:T(8,128)(2,1)S(1)}, u32[]{:S(2)}, u32[]{:S(2)}) collective-permute-start(bf16[256,1536]{1,0:T(8,128)(2,1)S(1)} %shard_map.86), channel_id=1, source_target_pairs={{0,1},{1,0},{2,3},{3,2},{4,5},{5,4},{6,7},{7,6},{8,9},{9,8},{10,11... | collective-permute-start | bytes 2359304 | tf_op jit(solution)/shard_map/ppermute | solution.py:333

commit v5 on v4

--- a/solution.py
+++ b/solution.py
@@ -41,7 +41,7 @@
     return [pl.BlockSpec(memory_space=pltpu.VMEM)] * count
 
 
-def fetch(where, weights, width, fence):
+def fetch(where, weights, width, groups, fence):
     depth = weights[0].shape[0]
     half = depth // 2
     kinds = len(weights)
@@ -50,7 +50,7 @@
         out, sems = refs[kinds + 1], refs[kinds + 2]
         copies = []
         for g in range(2):
-            columns = pl.ds(pl.multiple_of((s[1] ^ g) * width, width), width)
+            columns = pl.ds(pl.multiple_of((s[1] ^ groups[g]) * width, width), width)
             for k in range(kinds):
                 for part in range(2):
                     rows = pl.ds(pl.multiple_of((s[0] ^ part) * half, half), half)
@@ -81,24 +81,17 @@
     )(where, *weights, fence)
 
 
-def project(own, other, held, outputs):
-    pieces = len(own)
-    rows = sum(a.shape[0] for a in own)
+def project(own, other, held, outputs, start=0):
+    rows = own.shape[0] - start
     kinds = held.shape[0] // 2
     flat = [block for blocks in outputs for block in blocks]
 
     def body(*refs):
-        held_ref, outs = refs[2 * pieces], refs[2 * pieces + 1 :]
-        tokens = jnp.concatenate(
-            [
-                jnp.concatenate([r[...] for r in refs[:pieces]], axis=0),
-                jnp.concatenate([r[...] for r in refs[pieces : 2 * pieces]], axis=0),
-            ],
-            axis=1,
-        )
+        held_ref, outs = refs[2], refs[3:]
+        tokens = jnp.concatenate([refs[0][start:], refs[1][start:]], axis=1)
         at = [(o, i) for o, blocks in enumerate(outputs) for i in range(len(blocks))]
-        for start in range(0, len(flat), 2):
-            pair = flat[start : start + 2]
+        for first in range(0, len(flat), 2):
+            pair = flat[first : first + 2]
             weight = [
                 held_ref[g * kinds + k, :, h * HEAD_DIM : (h + 1) * HEAD_DIM] for g, k, h in pair
             ]
@@ -106,17 +99,66 @@
                 tokens, jnp.concatenate(weight, axis=1), preferred_element_type=F32
             ).astype(BF16)
             for i in range(len(pair)):
-                o, place_in = at[start + i]
+                o, place_in = at[first + i]
                 outs[o][place_in] = total[:, i * HEAD_DIM : (i + 1) * HEAD_DIM]
 
     return pl.pallas_call(
         body,
-        in_specs=whole(2 * pieces + 1),
+        in_specs=whole(3),
         out_specs=whole(len(outputs)),
         out_shape=[jax.ShapeDtypeStruct((len(b), rows, HEAD_DIM), BF16) for b in outputs],
-        compiler_params=params(16),
-        cost_estimate=LIGHT,
-    )(*own, *other, held)
+        compiler_params=params(8),
+        cost_estimate=LIGHT,
+    )(own, other, held)
+
+
+def take(array, ranges):
+    def body(in_ref, *outs):
+        for out, (first, last) in zip(outs, ranges):
+            out[...] = in_ref[first:last]
+
+    return pl.pallas_call(
+        body,
+        in_specs=whole(1),
+        out_specs=whole(len(ranges)),
+        out_shape=[
+            jax.ShapeDtypeStruct((last - first,) + array.shape[1:], array.dtype)
+            for first, last in ranges
+        ],
+        compiler_params=params(4),
+        cost_estimate=LIGHT,
+    )(array)
+
+
+def pack(sides, picks):
+    arrays = [a for side in sides for half in side for a in half]
+    rows = sum(half[0].shape[1] for half in sides[0])
+
+    def body(*refs):
+        ins, outs = list(refs[: len(arrays)]), refs[len(arrays) :]
+        blocks = []
+        for side in sides:
+            for half in side:
+                blocks.append([])
+                for a in half:
+                    ref = ins.pop(0)
+                    blocks[-1] += [(ref, b) for b in range(a.shape[0])]
+        for out, wanted in zip(outs, picks):
+            for n, (side, upper, lower) in enumerate(wanted):
+                ref, b = blocks[2 * side][upper]
+                size = ref.shape[1]
+                out[n, :size] = ref[b]
+                ref, b = blocks[2 * side + 1][lower]
+                out[n, size:] = ref[b]
+
+    return pl.pallas_call(
+        body,
+        in_specs=whole(len(arrays)),
+        out_specs=whole(len(picks)),
+        out_shape=[jax.ShapeDtypeStruct((len(p), rows, HEAD_DIM), BF16) for p in picks],
+        compiler_params=params(4),
+        cost_estimate=LIGHT,
+    )(*arrays)
 
 
 def mask_rows(where, block_order, block_mask, rows):
@@ -154,7 +196,7 @@
     )(where, block_order[None, :], block_mask)
 
 
-def attend(queries, parts, states, bias, query_at, key_at, last, fences):
+def attend(queries, parts, states, bias, query_at, key_at, last, fences, earlier=()):
     rows = queries[0][0][0].shape[1]
     tile = parts[0][0][0].shape[1]
     n = len(parts[0])
@@ -178,6 +220,7 @@
         state_refs = [take(3) for _ in states]
         (bias_ref,) = take(1)
         take(len(fences))
+        earlier_refs = take(len(earlier))
         outs = take(2 * steps if last else 3)
         q_ref = refs[0]
         step = pl.program_id(0)
@@ -232,8 +275,12 @@
 
                 @pl.when(step == i)
                 def _(i=i):
-                    outs[2 * i][...] = result[:rows]
-                    outs[2 * i + 1][...] = result[rows:]
+                    for half in range(2):
+                        out, piece = outs[2 * i + half], result[half * rows : (half + 1) * rows]
+                        if earlier:
+                            before = earlier_refs[2 * i + half][...]
+                            piece = jnp.concatenate([before, piece], axis=1)
+                        out[...] = piece
 
         else:
             outs[0][0] = jnp.broadcast_to(top, (both, HEAD_DIM))
@@ -245,17 +292,18 @@
 
     def part_spec(kind):
         def one(u):
-            base = parts[0][u][kind]
+            base = parts[0][u][2 * kind + 1]
             stride = 0 if same_parts else 1
             return pl.BlockSpec((1, tile, HEAD_DIM), lambda i: (base + i * stride, 0, 0))
 
         return [one(u) for u in range(n)]
 
-    arrays = [p[0] for p in parts[0]]
+    arrays = [p[2 * kind] for kind in range(2) for p in parts[0]]
     state_block = (1, both, HEAD_DIM)
     if last:
-        out_specs = [pl.BlockSpec((rows, HEAD_DIM), lambda i: (0, 0))] * (2 * steps)
-        out_shape = [jax.ShapeDtypeStruct((rows, HEAD_DIM), BF16)] * (2 * steps)
+        out_width = HEAD_DIM + (earlier[0].shape[1] if earlier else 0)
+        out_specs = [pl.BlockSpec((rows, out_width), lambda i: (0, 0))] * (2 * steps)
+        out_shape = [jax.ShapeDtypeStruct((rows, out_width), BF16)] * (2 * steps)
     else:
         out_specs = [pl.BlockSpec(state_block, lambda i: (i, 0, 0))] * 3
         out_shape = [jax.ShapeDtypeStruct((steps, both, HEAD_DIM), F32)] * 3
@@ -263,11 +311,12 @@
         body,
         grid=(steps,),
         in_specs=[fixed((1, rows, HEAD_DIM), at) for row in queries for _, at in row]
+        + part_spec(0)
         + part_spec(1)
-        + part_spec(2)
         + [fixed(state_block, at) for _, at in states for _ in range(3)]
         + [pl.BlockSpec(bias.shape, lambda i: (0, 0))]
-        + [pl.BlockSpec(memory_space=pl.ANY)] * len(fences),
+        + [pl.BlockSpec(memory_space=pl.ANY)] * len(fences)
+        + [pl.BlockSpec(e.shape, lambda i: (0, 0)) for e in earlier],
         out_specs=out_specs,
         out_shape=out_shape,
         scratch_shapes=[pltpu.VMEM((both, HEAD_DIM), BF16)]
@@ -277,50 +326,88 @@
     )(
         *[a for row in queries for a, _ in row],
         *arrays,
-        *arrays,
         *[a for held, _ in states for a in held],
         bias,
         *fences,
-    )
-
-
-def mix(where, attended, w_out, flip, step_width):
-    rows = attended[0].shape[0]
-    depth = w_out.shape[0] // Z
-    half = w_out.shape[1] // 2
-    steps = half // step_width
-    count = len(attended)
-
-    def body(s, *refs):
-        rows_all = jnp.concatenate([r[...] for r in refs[:count]], axis=1)
-        weight = jnp.concatenate([r[...] for r in refs[count : count + Z]], axis=0)
-        refs[-1][...] = jnp.dot(rows_all, weight, preferred_element_type=F32).astype(BF16)
-
-    def weight_spec(dz):
-        return pl.BlockSpec(
-            (depth, step_width),
-            lambda i, s: (s[1] ^ dz, (1 - s[0] if flip else s[0]) * steps + i),
-        )
+        *earlier,
+    )
+
+
+def fetch_out(where, w_out, fence):
+    depth, width = w_out.shape
+    group, half = depth // Z, width // 2
+
+    def body(s, w_ref, fence_ref, out, sems):
+        copies = []
+        for dz in range(Z):
+            rows = pl.ds(pl.multiple_of((s[1] ^ dz) * group, group), group)
+            for part in range(2):
+                columns = pl.ds(pl.multiple_of((1 - s[0] if part == 0 else s[0]) * half, half), half)
+                copies.append(
+                    pltpu.make_async_copy(
+                        w_ref.at[rows, columns],
+                        out.at[pl.ds(dz * group, group), pl.ds(part * half, half)],
+                        sems.at[len(copies)],
+                    )
+                )
+        for copy in copies:
+            copy.start()
+        for copy in copies:
+            copy.wait()
 
     return pl.pallas_call(
         body,
         grid_spec=pltpu.PrefetchScalarGridSpec(
             num_scalar_prefetch=1,
-            grid=(steps,),
-            in_specs=[pl.BlockSpec(a.shape, lambda i, s: (0, 0)) for a in attended]
-            + [weight_spec(dz) for dz in range(Z)],
-            out_specs=pl.BlockSpec((rows, step_width), lambda i, s: (0, i)),
+            grid=(),
+            in_specs=[pl.BlockSpec(memory_space=pl.ANY)] * 2,
+            out_specs=whole(1)[0],
+            scratch_shapes=[pltpu.SemaphoreType.DMA((2 * Z,))],
         ),
-        out_shape=jax.ShapeDtypeStruct((rows, half), BF16),
-        compiler_params=params(24),
-        cost_estimate=LIGHT,
-    )(where, *attended, *([w_out] * Z))
+        out_shape=pltpu.VMEM((depth, width), BF16),
+        compiler_params=params(4),
+        cost_estimate=LIGHT,
+    )(where, w_out, fence)
+
+
+def mix(attended, held, skip, columns, earlier, out_type):
+    rows, width = attended[0].shape
+    depth = held.shape[0] // Z
+    count = len(attended)
+    first, last = columns
+    step = (last - first) // 3
+
+    def body(*refs):
+        rows_all = jnp.concatenate([r[...] for r in refs[:count]], axis=1)
+        for i in range(3):
+            at = slice(first + i * step, first + (i + 1) * step)
+            weight = jnp.concatenate(
+                [
+                    refs[count][g * depth + skip : g * depth + skip + width, at]
+                    for g in range(count)
+                ],
+                axis=0,
+            )
+            total = jnp.dot(rows_all, weight, preferred_element_type=F32)
+            if earlier is not None:
+                total += refs[count + 1][:, at]
+            refs[-1][:, i * step : (i + 1) * step] = total.astype(out_type)
+
+    more = [] if earlier is None else [earlier]
+    return pl.pallas_call(
+        body,
+        in_specs=whole(count + 1 + len(more)),
+        out_specs=whole(1)[0],
+        out_shape=jax.ShapeDtypeStruct((rows, last - first), out_type),
+        compiler_params=params(16),
+        cost_estimate=LIGHT,
+    )(*attended, held, *more)
 
 
 def split_heads(tokens, block_order, block_mask, w_query, w_key, w_value, w_out):
     rows, half = tokens.shape
     group_heads = w_query.shape[1] // HEAD_DIM // Z
-    cut = rows // 2
+    cut = rows * 9 // 16
     ctx = lax.axis_index("ctx")
     y = lax.axis_index("head")
     where = jnp.stack([y, ctx // (X * C), (ctx // C) % X, ctx % C]).astype(jnp.int32)
@@ -342,63 +429,81 @@
         return [(group, 0, h) for h in heads]
 
     other = over_y(tokens)
-    far = [over(tokens[:cut], 2, 0, 0)]
+    far = over(tokens[:cut], 2, 0, 0)
     bias = mask_rows(where, block_order, block_mask, rows)
-    held = fetch(where, weights, span, bias)
-
-    other = after(other, held)
-    far[0] = after(far[0], held)
-    far.append(over(after(tokens[cut:], far[0]), 2, 0, 0))
-    far_other = [over_y(far[0])]
-    own_kv, sent_kv = project(
-        [after(tokens, far[0])], [other], held, [pairs(0, heads), pairs(1, heads)]
-    )
-    came_kv = over(sent_kv, 1, 0, 0)
+    held = fetch(where, weights, span, (0, 1), bias)
+    held_far = fetch(where, weights, span, (2, 3), held)
+
+    other = after(other, held_far)
+    own_kv, sent = project(
+        tokens, other, held, [pairs(0, heads), singles(1) + pairs(1, heads)]
+    )
+    came = over(sent, 1, 0, 0)
     own_across = over(own_kv, 0, 1, 0)
     own_core = over(own_kv, 0, 0, 1)
-    own_q, sent_q = project(
-        [after(tokens, sent_kv)], [other], held, [singles(0), singles(1)]
-    )
-    came_q = over(sent_q, 1, 0, 0)
-    far[1] = after(far[1], sent_q)
-    far_other.append(over_y(after(far[1], far_other[0])))
+    far = after(far, sent)
+    far_other = over_y(far)
+    low2, low3 = project(
+        after(tokens, far),
+        other,
+        held_far,
+        [singles(0) + pairs(0, heads), singles(1) + pairs(1, heads)],
+        cut,
+    )
+    (own_q,) = project(after(tokens, own_core, low2), other, held, [singles(0)])
+    low2 = over(low2, 2, 0, 0)
+    low3 = over(low3, 3, 0, 0)
+    out_held = fetch_out(where, w_out, own_q)
+    own_across = after(own_across, out_held)
     own_across_core = over(own_across, 0, 0, 1)
-    came_kv = after(came_kv, own_across)
-    came_across = over(came_kv, 0, 1, 0)
+
+    far_sent_q, far_sent, far_kept = project(
+        far,
+        after(far_other, out_held),
+        held,
+        [singles(1), pairs(1, heads), singles(0) + pairs(0, heads)],
+    )
+    far_came_q = over(far_sent_q, 1, 0, 0)
+    far_came = over(far_sent, 1, 0, 0)
+    came = after(came, far_sent, own_across)
+    n = group_heads
+    came_kv, came_k, came_v = take(came, [(n, 3 * n), (n, 2 * n), (2 * n, 3 * n)])
+    across_k = over(came_k, 0, 1, 0)
+    across_v = over(came_v, 0, 1, 0)
     came_core = over(came_kv, 0, 0, 1)
-
-    far[1] = after(far[1], came_kv)
-    far_other[1] = after(far_other[1], came_kv)
+    across_core_k = over(across_k, 0, 0, 1)
+    across_core_v = over(across_v, 0, 0, 1)
+
     first, rest = (0,), tuple(heads)[1:]
-    far_sent_kv, far_sent_q = project(far, far_other, held, [pairs(1, first), singles(1)])
-    far_came_kv = over(far_sent_kv, 1, 0, 0)
-    far_came_q = over(far_sent_q, 1, 0, 0)
-    (far_kv,) = project(
-        [far[0], after(far[1], far_sent_kv)], far_other, held, [pairs(0, heads)]
-    )
-    far_across = over(far_kv, 0, 1, 0)
-    far_core = over(far_kv, 0, 0, 1)
-    far_sent_kv2, far_q = project(
-        [far[0], after(far[1], far_kv)], far_other, held, [pairs(1, rest), singles(0)]
-    )
-    far_came_kv2 = over(far_sent_kv2, 1, 0, 0)
-    came_across = after(came_across, far_q)
-    came_across_core = over(came_across, 0, 0, 1)
-
-    near = [own_kv, own_across, own_core, own_across_core]
-    near += [came_kv, came_across, came_core, came_across_core]
-    near_parts = [[(a, 0, group_heads) for a in near], None]
+    far_came = after(far_came, across_k, across_v, low2, low3)
+    sides = [[[far_kept], [low2]], [[far_came], [low3]]]
+
+    def picks(chunk):
+        kept = [(0, k * n + h, k * n + h) for k in (1, 2) for h in chunk]
+        return kept + [(1, (k - 1) * n + h, k * n + h) for k in (1, 2) for h in chunk]
+
+    far_first, far_rest, far_q = pack(
+        sides, [picks(first), picks(rest), [(0, h, h) for h in heads]]
+    )
+    first_across = over(far_first, 0, 1, 0)
+    first_core = over(far_first, 0, 0, 1)
+    rest_across = over(far_rest, 0, 1, 0)
+    rest_core = over(far_rest, 0, 0, 1)
+
+    near = [(a, 0, a, n) for a in (own_kv, own_across, own_core, own_across_core)]
+    near += [
+        (came_kv, 0, came_kv, n),
+        (across_k, 0, across_v, 0),
+        (came_core, 0, came_core, n),
+        (across_core_k, 0, across_core_v, 0),
+    ]
+    near_parts = [near, None]
     state_near = attend(
-        [[(own_q, j), (came_q, j)] for j in heads], near_parts, [], bias, (0, 0), 0, False, []
-    )
-    far_came_kv = after(far_came_kv, state_near[0])
-    first_across = over(far_came_kv, 0, 1, 0)
-    first_core = over(far_came_kv, 0, 0, 1)
-    far_came_kv2 = after(far_came_kv2, far_came_kv)
-    rest_across = over(far_came_kv2, 0, 1, 0)
-    rest_core = over(far_came_kv2, 0, 0, 1)
-    far_across = after(far_across, far_came_kv2)
-    far_across_core = over(far_across, 0, 0, 1)
+        [[(own_q, j), (came, j)] for j in heads], near_parts, [], bias, (0, 0), 0, False, [far_first]
+    )
+    (far_came_q,) = pack(
+        [[[after(far_came_q, state_near[0])], [low3]]], [[(0, h, h) for h in heads]]
+    )
     state_far = attend(
         [[(far_q, j), (far_came_q, j)] for j in heads],
         near_parts,
@@ -407,39 +512,46 @@
         (2, 0),
         0,
         False,
-        [far_across, far_came_kv2],
+        [state_near[0]],
     )
     first_across = after(first_across, state_far[0])
     first_across_core = over(first_across, 0, 0, 1)
-    rest_across = after(rest_across, first_across_core)
-    rest_across_core = over(rest_across, 0, 0, 1)
-    kept = [far_kv, far_across, far_core, far_across_core]
-    far_first = [far_came_kv, first_across, first_core, first_across_core]
-    far_rest = [far_came_kv2, rest_across, rest_core, rest_across_core]
 
     results = []
     for j in heads:
-        parts = [(a, j, group_heads + j) for a in kept]
         if j == 0:
-            parts += [(a, 0, 1) for a in far_first]
+            arrays, size, at = [far_first, first_across, first_core, first_across_core], 1, 0
+            fences = []
         else:
-            parts += [(a, j - 1, group_heads - 1 + j - 1) for a in far_rest]
-        results.append(
-            attend(
-                [[(own_q, j), (came_q, j)], [(far_q, j), (far_came_q, j)]],
-                [parts],
-                [(state_near, j), (state_far, j)],
-                bias,
-                (0, 2),
-                len(near),
-                True,
-                [results[-1][0]] if j else [],
-            )
+            if j == 1:
+                rest_across = after(rest_across, results[0][0])
+                rest_across_core = over(rest_across, 0, 0, 1)
+            arrays, size, at = [far_rest, rest_across, rest_core, rest_across_core], len(rest), j - 1
+            fences = [results[-1][0]]
+        parts = [
+            (a, 2 * i * size + at, a, (2 * i + 1) * size + at) for i in range(2) for a in arrays
+        ]
+        rows_out = attend(
+            [[(own_q, j), (came, j)], [(far_q, j), (far_came_q, j)]],
+            [parts],
+            [(state_near, j), (state_far, j)],
+            bias,
+            (0, 2),
+            len(near),
+            True,
+            fences,
+            results.pop() if j == 1 else (),
         )
+        results.append(rows_out)
     results = [[r[0]] + [over(r[dz], dz, 0, 0) for dz in range(1, Z)] for r in results]
-    attended = [results[j][dz] for dz in range(Z) for j in heads]
-    arrived = over_y(mix(where, attended, w_out, True, 512))
-    home = mix(where, attended, w_out, False, 512)
+    width = w_out.shape[1]
+    skip = results[0][0].shape[1]
+    partial = mix(results[0], out_held, 0, (0, width), None, F32)
+    rest = results[1][:-1] + [after(results[1][-1], partial)]
+    away = mix(rest, out_held, skip, (0, width // 2), partial, BF16)
+    arrived = over_y(away)
+    rest = rest[:-1] + [after(rest[-1], away)]
+    home = mix(rest, out_held, skip, (width // 2, width), partial, BF16)
     return (home.astype(F32) + arrived.astype(F32)).astype(BF16)
 
 

time: 140 us -> 128 us (0.914)
  waiting for transfers between devices: 48.6 us -> 37.2 us
  starting transfers between devices: 36.5 us -> 30.9 us
  Pallas kernels: 50.2 us -> 55.6 us
    ppermute x31 -> x26, waiting for transfers between devices: 32.9 us -> 20.3 us  [over(): return lax.ppermute(a, 'ctx', hop(dz, dx, dc))]
    ppermute x31 -> x26, starting transfers between devices: 31.7 us -> 25 us  [over(): return lax.ppermute(a, 'ctx', hop(dz, dx, dc))]
    pallas_call x1 -> x2, Pallas kernels: 5.84 us -> 11.7 us  [fetch(): pl.pallas_call(body, grid_spec=pltpu.PrefetchScalarGridSpec(num_scalar_pr...]
    ppermute x4 -> x3, waiting for transfers between devices: 15.6 us -> 16.9 us  [over_y(): return lax.ppermute(a, 'head', [(0, 1), (1, 0)])]
    ppermute x4 -> x3, starting transfers between devices: 4.83 us -> 5.94 us  [over_y(): return lax.ppermute(a, 'head', [(0, 1), (1, 0)])]
    pallas_call x7 -> x11, Pallas kernels: 17.6 us -> 16.8 us  [the longest x4 9.28 us: project(): pl.pallas_call(body, in_specs=whole(3), out_specs=whole(len(outputs)), ou...]
  transfers between devices with their start and end apart: 35 -> 29, of which waited for: 12 -> 10; matrix products, arithmetic and copies ran while one was open for 1% -> 1% of each run, Pallas kernels for 33% -> 39%
where the time goes in v5:
time: 128 us
  Pallas kernels  55.6 us (43%)
  waiting for transfers between devices  37.2 us (29%)
  starting transfers between devices  30.9 us (24%)
  local copies, waits for them, and re-layouts  2.45 us (2%)
    pallas_call x5, Pallas kernels, attend(): pl.pallas_call(body, grid=(steps,), in_specs=[fixed((1, rows, HEAD_DIM),...  26 us
    ppermute x26, starting transfers between devices, over(): return lax.ppermute(a, 'ctx', hop(dz, dx, dc))  25 us
    ppermute x26, waiting for transfers between devices, over(): return lax.ppermute(a, 'ctx', hop(dz, dx, dc))  20.3 us
    ppermute x3, waiting for transfers between devices, over_y(): return lax.ppermute(a, 'head', [(0, 1), (1, 0)])  16.9 us
    pallas_call x2, Pallas kernels, fetch(): pl.pallas_call(body, grid_spec=pltpu.PrefetchScalarGridSpec(num_scalar_pr...  11.7 us
    pallas_call x4, Pallas kernels, project(): pl.pallas_call(body, in_specs=whole(3), out_specs=whole(len(outputs)), ou...  9.28 us
    ppermute x3, starting transfers between devices, over_y(): return lax.ppermute(a, 'head', [(0, 1), (1, 0)])  5.94 us
    pallas_call x1, Pallas kernels, fetch_out(): pl.pallas_call(body, grid_spec=pltpu.PrefetchScalarGridSpec(num_scalar_pr...  4.33 us
  transfers between devices with their start and end apart: 29, of which 10 were waited for; matrix products, arithmetic and copies ran while one was open for 1% of the time, Pallas kernels for 39%

profile of v5, /device:TPU:0, one launch (start us, length us, event | category | flops | bytes accessed | tf_op | source)
XLA Modules:
  0.0 127.5 jit_solution(5448801815382475336)
XLA Ops:
  0.0 3.0 %collective-permute-start = (bf16[256,1536]{1,0:T(8,128)(2,1)}, bf16[256,1536]{1,0:T(8,128)(2,1)S(1)}, u32[]{:S(2)}, u32[]{:S(2)}) collective-permute-start(bf16[256,1536]{1,0:T(8,128)(2,1)} %refs_0_.7), channel_id=1, source_target_pairs={{0,1},{1,0},{2,3},{3,2},{4,5},{5,4},{6,7},{7,6},{8,9},{9,8},{10,11... | collective-permute-start | bytes 2359304 | tf_op jit(solution)/shard_map/ppermute | solution.py:420
  3.0 1.1 slice.3
  4.0 2.7 %collective-permute-start.2 = (bf16[144,1536]{1,0:T(8,128)(2,1)S(1)}, bf16[144,1536]{1,0:T(8,128)(2,1)S(1)}, u32[]{:S(2)}, u32[]{:S(2)}) collective-permute-start(bf16[144,1536]{1,0:T(8,128)(2,1)S(1)} %slice.3), channel_id=1, source_target_pairs={{0,16},{2,18},{4,20},{6,22},{8,24},{10,26},{12,28},{14,30},{16,0},... | collective-permute-start | bytes 1327112 | tf_op jit(solution)/shard_map/ppermute | solution.py:423
  6.8 0.7 copy-done.1
  7.5 0.7 copy-done.2
  8.2 1.1 shard_map.73.refs_3_.refs_22_.refs_26_
  9.2 5.8 %shard_map.74.refs_3_.refs_2_ = bf16[6,3072,384]{2,1,0:T(8,128)(2,1)S(1)} custom-call(s32[4]{0:T(128)S(1)} %pad_add_fusion.s, bf16[3072,1536]{1,0:T(8,128)(2,1)} %refs_0_.4, bf16[3072,1536]{1,0:T(8,128)(2,1)} %refs_1_.3, bf16[3072,1536]{1,0:T(8,128)(2,1)} %refs_2_.3, f32[8,4096]{1,0:T(8,128)S(1)} %shard_map.73.refs_3_.refs_22_.refs_26_), custom_call_target="tpu_custom_call" | custom-call | flops 1024 | bytes 1024 | tf_op jit(solution)/shard_map/pallas_call | solution.py:69
  15.1 5.8 %shard_map.75.refs_2_ = bf16[6,3072,384]{2,1,0:T(8,128)(2,1)S(1)} custom-call(s32[4]{0:T(128)S(1)} %pad_add_fusion.s, bf16[3072,1536]{1,0:T(8,128)(2,1)} %refs_0_.4, bf16[3072,1536]{1,0:T(8,128)(2,1)} %refs_1_.3, bf16[3072,1536]{1,0:T(8,128)(2,1)} %refs_2_.3, bf16[6,3072,384]{2,1,0:T(8,128)(2,1)S(1)} %shard_map.74.refs_3_.refs_2_), custom_call_target="tpu_custom_call" | custom-call | flops 1024 | bytes 1024 | tf_op jit(solution)/shard_map/pallas_call | solution.py:69
  20.9 3.5 %shard_map.76 = (bf16[6,256,128]{2,1,0:T(8,128)(2,1)S(1)}, bf16[9,256,128]{2,1,0:T(8,128)(2,1)S(1)}) custom-call(bf16[256,1536]{1,0:T(8,128)(2,1)S(1)} %copy-done, bf16[256,1536]{1,0:T(8,128)(2,1)S(1)} %collective-permute-done.refs_1_, bf16[6,3072,384]{2,1,0:T(8,128)(2,1)S(1)} %shard_map.74.refs_3_.refs_2_), custom_call_target="tpu_custom_call" | custom-call | flops 1024 | bytes 1024 | tf_op jit(solution)/shard_map/pallas_call | solution.py:105
  24.4 1.6 %collective-permute-start.3 = (bf16[9,256,128]{2,1,0:T(8,128)(2,1)S(1)}, bf16[9,256,128]{2,1,0:T(8,128)(2,1)S(1)}, u32[]{:S(2)}, u32[]{:S(2)}) collective-permute-start(bf16[9,256,128]{2,1,0:T(8,128)(2,1)S(1)} %get-tuple-element.51), channel_id=1, source_target_pairs={{0,8},{2,10},{4,12},{6,14},{8,0},{10,2},{12,4},{14,6},{16,24},{18,... | collective-permute-start | bytes 1769480 | tf_op jit(solution)/shard_map/ppermute | solution.py:423
  26.1 1.5 %collective-permute-start.5 = (bf16[6,256,128]{2,1,0:T(8,128)(2,1)S(1)}, bf16[6,256,128]{2,1,0:T(8,128)(2,1)S(1)}, u32[]{:S(2)}, u32[]{:S(2)}) collective-permute-start(bf16[6,256,128]{2,1,0:T(8,128)(2,1)S(1)} %get-tuple-element.50.refs_6_.refs_14_), channel_id=1, source_target_pairs={{0,4},{2,6},{4,0},{6,2},{8,12},{10,14},{12,8},{14,10},{16,20},{18,... | collective-permute-start | bytes 1179656 | tf_op jit(solution)/shard_map/ppermute | solution.py:423
  27.6 1.5 %collective-permute-start.4 = (bf16[144,1536]{1,0:T(8,128)(2,1)S(1)}, bf16[144,1536]{1,0:T(8,128)(2,1)S(1)}, u32[]{:S(2)}, u32[]{:S(2)}) collective-permute-start(bf16[144,1536]{1,0:T(8,128)(2,1)S(1)} %collective-permute-done.2.refs_0_), channel_id=1, source_target_pairs={{0,1},{1,0},{2,3},{3,2},{4,5},{5,4},{6,7},{7,6},{8,9},{9,8},{10,11... | collective-permute-start | bytes 1327112 | tf_op jit(solution)/shard_map/ppermute | solution.py:420
  29.1 2.4 %shard_map.77 = (bf16[9,112,128]{2,1,0:T(8,128)(2,1)S(1)}, bf16[9,112,128]{2,1,0:T(8,128)(2,1)S(1)}) custom-call(bf16[256,1536]{1,0:T(8,128)(2,1)S(1)} %copy-done, bf16[256,1536]{1,0:T(8,128)(2,1)S(1)} %collective-permute-done.refs_1_, bf16[6,3072,384]{2,1,0:T(8,128)(2,1)S(1)} %shard_map.75.refs_2_), custom_call_target="tpu_custom_call" | custom-call | flops 1024 | bytes 1024 | tf_op jit(solution)/shard_map/pallas_call | solution.py:105
  31.5 2.5 %collective-permute-start.10 = (bf16[9,112,128]{2,1,0:T(8,128)(2,1)S(1)}, bf16[9,112,128]{2,1,0:T(8,128)(2,1)S(1)}, u32[]{:S(2)}, u32[]{:S(2)}) collective-permute-start(bf16[9,112,128]{2,1,0:T(8,128)(2,1)S(1)} %get-tuple-element.63), channel_id=1, source_target_pairs={{0,24},{2,26},{4,28},{6,30},{8,16},{10,18},{12,20},{14,22},{16,8},... | collective-permute-start | bytes 774152 | tf_op jit(solution)/shard_map/ppermute | solution.py:423
  34.3 1.0 shard_map.78.fence_ref.refs_0_.refs_2_.refs_4_
  35.3 4.3 %shard_map.79.refs_4_ = bf16[1536,3072]{1,0:T(8,128)(2,1)S(1)} custom-call(s32[4]{0:T(128)S(1)} %pad_add_fusion.s, bf16[1536,3072]{1,0:T(8,128)(2,1)} %w_ref.1, bf16[3,256,128]{2,1,0:T(8,128)(2,1)S(1)} %shard_map.78.fence_ref.refs_0_.refs_2_.refs_4_), custom_call_target="tpu_custom_call" | custom-call | flops 1024 | bytes 1024 | tf_op jit(solution)/shard_map/pallas_call | solution.py:358
  39.9 2.4 %shard_map.80 = (bf16[3,144,128]{2,1,0:T(8,128)(2,1)S(1)}, bf16[6,144,128]{2,1,0:T(8,128)(2,1)S(1)}, bf16[9,144,128]{2,1,0:T(8,128)(2,1)S(1)}) custom-call(bf16[144,1536]{1,0:T(8,128)(2,1)S(1)} %collective-permute-done.2.refs_0_, bf16[144,1536]{1,0:T(8,128)(2,1)S(1)} %collective-permute-done.4.refs_1_, bf16[6,3072,384]{2,1,0:T(8,128)(2,1)S(1)} %shard_map.74.refs_3_.refs_2_), custom_call_target="tpu_custom_call" | custom-call | flops 1024 | bytes 1024 | tf_op jit(solution)/shard_map/pallas_call | solution.py:105
  42.4 0.6 collective-permute-start.8
  43.0 1.5 %collective-permute-start.7 = (bf16[6,144,128]{2,1,0:T(8,128)(2,1)S(1)}, bf16[6,144,128]{2,1,0:T(8,128)(2,1)S(1)}, u32[]{:S(2)}, u32[]{:S(2)}) collective-permute-start(bf16[6,144,128]{2,1,0:T(8,128)(2,1)S(1)} %get-tuple-element.57), channel_id=1, source_target_pairs={{0,8},{2,10},{4,12},{6,14},{8,0},{10,2},{12,4},{14,6},{16,24},{18,... | collective-permute-start | bytes 663560 | tf_op jit(solution)/shard_map/ppermute | solution.py:423
  44.5 3.9 %collective-permute-done.10.refs_3_.refs_1_ = bf16[9,112,128]{2,1,0:T(8,128)(2,1)S(1)} collective-permute-done((bf16[9,112,128]{2,1,0:T(8,128)(2,1)S(1)}, bf16[9,112,128]{2,1,0:T(8,128)(2,1)S(1)}, u32[]{:S(2)}, u32[]{:S(2)}) %collective-permute-start.10) | collective-permute-done | bytes 258080 | tf_op jit(solution)/shard_map/ppermute | solution.py:423
  48.4 1.5 %collective-permute-start.9 = (bf16[3,256,128]{2,1,0:T(8,128)(2,1)S(1)}, bf16[3,256,128]{2,1,0:T(8,128)(2,1)S(1)}, u32[]{:S(2)}, u32[]{:S(2)}) collective-permute-start(bf16[3,256,128]{2,1,0:T(8,128)(2,1)S(1)} %get-tuple-element.62), channel_id=1, source_target_pairs={{0,4},{2,6},{4,0},{6,2},{8,12},{10,14},{12,8},{14,10},{16,20},{18,... | collective-permute-start | bytes 589832 | tf_op jit(solution)/shard_map/ppermute | solution.py:423
  49.9 7.2 %collective-permute-done.6.refs_1_ = bf16[9,112,128]{2,1,0:T(8,128)(2,1)S(1)} collective-permute-done((bf16[9,112,128]{2,1,0:T(8,128)(2,1)S(1)}, bf16[9,112,128]{2,1,0:T(8,128)(2,1)S(1)}, u32[]{:S(2)}, u32[]{:S(2)}) %collective-permute-start.6) | collective-permute-done | bytes 258080 | tf_op jit(solution)/shard_map/ppermute | solution.py:423
  57.1 0.5 collective-permute-start.14
  57.7 0.6 collective-permute-start.17
  58.3 1.5 %collective-permute-start.16 = (bf16[8,256,128]{2,1,0:T(8,128)(2,1)S(1)}, bf16[8,256,128]{2,1,0:T(8,128)(2,1)S(1)}, u32[]{:S(2)}, u32[]{:S(2)}) collective-permute-start(bf16[8,256,128]{2,1,0:T(8,128)(2,1)S(1)} %get-tuple-element.71.refs_4_.refs_8_.refs_12_.refs_16_), channel_id=1, source_target_pairs={{0,4},{2,6},{4,0},{6,2},{8,12},{10,14},{12,8},{14,10},{16,20},{18,... | collective-permute-start | bytes 1572872 | tf_op jit(solution)/shard_map/ppermute | solution.py:423
  59.9 1.4 %collective-permute-done.15.refs_21_ = bf16[3,256,128]{2,1,0:T(8,128)(2,1)S(1)} collective-permute-done((bf16[3,256,128]{2,1,0:T(8,128)(2,1)S(1)}, bf16[3,256,128]{2,1,0:T(8,128)(2,1)S(1)}, u32[]{:S(2)}, u32[]{:S(2)}) %collective-permute-start.15) | collective-permute-done | bytes 196640 | tf_op jit(solution)/shard_map/ppermute | solution.py:423
  61.4 5.5 %shard_map.83 = (f32[3,512,128]{2,1,0:T(8,128)S(1)}, f32[3,512,128]{2,1,0:T(8,128)S(1)}, f32[3,512,128]{2,1,0:T(8,128)S(1)}) custom-call(bf16[3,256,128]{2,1,0:T(8,128)(2,1)S(1)} %shard_map.78.fence_ref.refs_0_.refs_2_.refs_4_, bf16[9,256,128]{2,1,0:T(8,128)(2,1)S(1)} %collective-permute-done.3.in_ref.refs_1_.refs_3_.refs_5_, ...), custom_call_target="tpu_custom_call" | custom-call | flops 1024 | bytes 1024 | tf_op jit(solution)/shard_map/pallas_call | solution.py:310
  66.9 5.6 %shard_map.85 = (f32[3,512,128]{2,1,0:T(8,128)S(1)}, f32[3,512,128]{2,1,0:T(8,128)S(1)}, f32[3,512,128]{2,1,0:T(8,128)S(1)}) custom-call(bf16[3,256,128]{2,1,0:T(8,128)(2,1)S(1)} %get-tuple-element.65.refs_0_.refs_2_.refs_4_, bf16[3,256,128]{2,1,0:T(8,128)(2,1)S(1)} %shard_map.84.refs_1_.refs_3_.refs_5_, ...), custom_call_target="tpu_custom_call" | custom-call | flops 1024 | bytes 1024 | tf_op jit(solution)/shard_map/pallas_call | solution.py:310
  72.5 0.4 collective-permute-start.19
  73.1 1.0 collective-permute-done.19.refs_7_.refs_11_.refs_15_.refs_19_
  74.1 4.9 %shard_map.86 = (bf16[256,128]{1,0:T(8,128)(2,1)S(1)}, bf16[256,128]{1,0:T(8,128)(2,1)S(1)}, bf16[256,128]{1,0:T(8,128)(2,1)S(1)}, bf16[256,128]{1,0:T(8,128)(2,1)S(1)}) custom-call(bf16[3,256,128]{2,1,0:T(8,128)(2,1)S(1)} %shard_map.78.fence_ref.refs_0_.refs_2_.refs_4_, bf16[9,256,128]{2,1,0:T(8,128)(2,1)S(1)} %collective-permute-done.3.in_ref.refs_1_.refs_3_.refs_5_, ...), custom_call_target="tpu_custom_call" | custom-call | flops 1024 | bytes 1024 | tf_op jit(solution)/shard_map/pallas_call | solution.py:310
  79.0 0.4 collective-permute-start.21
  79.5 1.5 %collective-permute-done.21.refs_7_.refs_11_.refs_15_.refs_19_ = bf16[8,256,128]{2,1,0:T(8,128)(2,1)S(1)} collective-permute-done((bf16[8,256,128]{2,1,0:T(8,128)(2,1)S(1)}, bf16[8,256,128]{2,1,0:T(8,128)(2,1)S(1)}, u32[]{:S(2)}, u32[]{:S(2)}) %collective-permute-start.21) | collective-permute-done | bytes 524320 | tf_op jit(solution)/shard_map/ppermute | solution.py:423
  81.0 4.9 %shard_map.87 = (bf16[256,256]{1,0:T(8,128)(2,1)S(1)}, bf16[256,256]{1,0:T(8,128)(2,1)S(1)}, bf16[256,256]{1,0:T(8,128)(2,1)S(1)}, bf16[256,256]{1,0:T(8,128)(2,1)S(1)}) custom-call(bf16[3,256,128]{2,1,0:T(8,128)(2,1)S(1)} %shard_map.78.fence_ref.refs_0_.refs_2_.refs_4_, bf16[9,256,128]{2,1,0:T(8,128)(2,1)S(1)} %collective-permute-done.3.in_ref.refs_1_.refs_3_.refs_5_, ...), custom_call_target="tpu_custom_call" | custom-call | flops 1024 | bytes 1024 | tf_op jit(solution)/shard_map/pallas_call | solution.py:310
  85.9 0.8 collective-permute-start.25
  86.8 2.5 %collective-permute-start.26 = (bf16[256,256]{1,0:T(8,128)(2,1)S(1)}, bf16[256,256]{1,0:T(8,128)(2,1)S(1)}, u32[]{:S(2)}, u32[]{:S(2)}) collective-permute-start(bf16[256,256]{1,0:T(8,128)(2,1)S(1)} %get-tuple-element.89), channel_id=1, source_target_pairs={{0,16},{2,18},{4,20},{6,22},{8,24},{10,26},{12,28},{14,30},{16,0},... | collective-permute-start | bytes 393224 | tf_op jit(solution)/shard_map/ppermute | solution.py:423
  89.3 1.1 collective-permute-start.27
  90.4 5.1 %shard_map.88 = (bf16[256,128]{1,0:T(8,128)(2,1)S(1)}, bf16[256,128]{1,0:T(8,128)(2,1)S(1)}, bf16[256,128]{1,0:T(8,128)(2,1)S(1)}, bf16[256,128]{1,0:T(8,128)(2,1)S(1)}) custom-call(bf16[3,256,128]{2,1,0:T(8,128)(2,1)S(1)} %shard_map.78.fence_ref.refs_0_.refs_2_.refs_4_, bf16[9,256,128]{2,1,0:T(8,128)(2,1)S(1)} %collective-permute-done.3.in_ref.refs_1_.refs_3_.refs_5_, ...), custom_call_target="tpu_custom_call" | custom-call | flops 1024 | bytes 1024 | tf_op jit(solution)/shard_map/pallas_call | solution.py:310
  95.5 2.8 %collective-permute-start.24 = (bf16[256,128]{1,0:T(8,128)(2,1)S(1)}, bf16[256,128]{1,0:T(8,128)(2,1)S(1)}, u32[]{:S(2)}, u32[]{:S(2)}) collective-permute-start(bf16[256,128]{1,0:T(8,128)(2,1)S(1)} %get-tuple-element.87), channel_id=1, source_target_pairs={{0,24},{2,26},{4,28},{6,30},{8,16},{10,18},{12,20},{14,22},{16,8},... | collective-permute-start | bytes 196616 | tf_op jit(solution)/shard_map/ppermute | solution.py:423
  98.4 1.6 %collective-permute-start.23 = (bf16[256,128]{1,0:T(8,128)(2,1)S(1)}, bf16[256,128]{1,0:T(8,128)(2,1)S(1)}, u32[]{:S(2)}, u32[]{:S(2)}) collective-permute-start(bf16[256,128]{1,0:T(8,128)(2,1)S(1)} %get-tuple-element.86), channel_id=1, source_target_pairs={{0,16},{2,18},{4,20},{6,22},{8,24},{10,26},{12,28},{14,30},{16,0},... | collective-permute-start | bytes 196616 | tf_op jit(solution)/shard_map/ppermute | solution.py:423
  100.3 1.8 %shard_map.89.refs_5_ = f32[256,3072]{1,0:T(8,128)S(1)} custom-call(bf16[256,256]{1,0:T(8,128)(2,1)S(1)} %get-tuple-element.83.refs_27_.refs_0_, bf16[256,256]{1,0:T(8,128)(2,1)S(1)} %collective-permute-done.25.refs_1_, bf16[256,256]{1,0:T(8,128)(2,1)S(1)} %collective-permute-done.26.refs_2_, bf16[256,256]{1,0:T(8,128)(2,1)S(1)} %collective-permute-done.27.refs_3_, ...), custom_call_target="tpu_custom_call" | custom-call | flops 1024 | bytes 1024 | tf_op jit(solution)/shard_map/pallas_call | solution.py:397
  102.2 0.4 collective-permute-done.22.refs_1_
  102.6 4.5 %collective-permute-done.23.refs_2_ = bf16[256,128]{1,0:T(8,128)(2,1)S(1)} collective-permute-done((bf16[256,128]{1,0:T(8,128)(2,1)S(1)}, bf16[256,128]{1,0:T(8,128)(2,1)S(1)}, u32[]{:S(2)}, u32[]{:S(2)}) %collective-permute-start.23) | collective-permute-done | bytes 65568 | tf_op jit(solution)/shard_map/ppermute | solution.py:423
  107.2 0.6 shard_map.90
  107.8 1.5 %collective-permute-start.28 = (bf16[256,1536]{1,0:T(8,128)(2,1)S(1)}, bf16[256,1536]{1,0:T(8,128)(2,1)S(1)}, u32[]{:S(2)}, u32[]{:S(2)}) collective-permute-start(bf16[256,1536]{1,0:T(8,128)(2,1)S(1)} %shard_map.90), channel_id=1, source_target_pairs={{0,1},{1,0},{2,3},{3,2},{4,5},{5,4},{6,7},{7,6},{8,9},{9,8},{10,11... | collective-permute-start | bytes 2359304 | tf_op jit(solution)/shard_map/ppermute | solution.py:420
  109.2 0.6 shard_map.91
  109.8 16.7 %collective-permute-done.28 = bf16[256,1536]{1,0:T(8,128)(2,1)S(1)} collective-permute-done((bf16[256,1536]{1,0:T(8,128)(2,1)S(1)}, bf16[256,1536]{1,0:T(8,128)(2,1)S(1)}, u32[]{:S(2)}, u32[]{:S(2)}) %collective-permute-start.28) | collective-permute-done | bytes 786464 | tf_op jit(solution)/shard_map/ppermute | solution.py:420
  126.5 1.1 add_convert_fusion
  (38 shorter events, 1.5 us)
Async XLA Ops:
  0.0 20.9 %collective-permute-start = (bf16[256,1536]{1,0:T(8,128)(2,1)}, bf16[256,1536]{1,0:T(8,128)(2,1)S(1)}, u32[]{:S(2)}, u32[]{:S(2)}) collective-permute-start(bf16[256,1536]{1,0:T(8,128)(2,1)} %refs_0_.7), channel_id=1, source_target_pairs={{0,1},{1,0},{2,3},{3,2},{4,5},{5,4},{6,7},{7,6},{8,9},{9,8},{10,11... | collective-permute-start | bytes 2359304 | tf_op jit(solution)/shard_map/ppermute | solution.py:420
  4.0 23.5 %collective-permute-start.2 = (bf16[144,1536]{1,0:T(8,128)(2,1)S(1)}, bf16[144,1536]{1,0:T(8,128)(2,1)S(1)}, u32[]{:S(2)}, u32[]{:S(2)}) collective-permute-start(bf16[144,1536]{1,0:T(8,128)(2,1)S(1)} %slice.3), channel_id=1, source_target_pairs={{0,16},{2,18},{4,20},{6,22},{8,24},{10,26},{12,28},{14,30},{16,0},... | collective-permute-start | bytes 1327112 | tf_op jit(solution)/shard_map/ppermute | solution.py:423
  6.8 0.7 copy-start.1
  7.5 0.7 copy-start.2
  15.1 5.9 %copy-start = (bf16[256,1536]{1,0:T(8,128)(2,1)S(1)}, bf16[256,1536]{1,0:T(8,128)(2,1)}, u32[]{:S(2)}) copy-start(bf16[256,1536]{1,0:T(8,128)(2,1)} %refs_0_.7) | copy-start | bytes 2359300
  24.4 17.8 %collective-permute-start.3 = (bf16[9,256,128]{2,1,0:T(8,128)(2,1)S(1)}, bf16[9,256,128]{2,1,0:T(8,128)(2,1)S(1)}, u32[]{:S(2)}, u32[]{:S(2)}) collective-permute-start(bf16[9,256,128]{2,1,0:T(8,128)(2,1)S(1)} %get-tuple-element.51), channel_id=1, source_target_pairs={{0,8},{2,10},{4,12},{6,14},{8,0},{10,2},{12,4},{14,6},{16,24},{18,... | collective-permute-start | bytes 1769480 | tf_op jit(solution)/shard_map/ppermute | solution.py:423
  26.1 8.0 %collective-permute-start.1 = (bf16[6,256,128]{2,1,0:T(8,128)(2,1)S(1)}, bf16[6,256,128]{2,1,0:T(8,128)(2,1)S(1)}, u32[]{:S(2)}, u32[]{:S(2)}) collective-permute-start(bf16[6,256,128]{2,1,0:T(8,128)(2,1)S(1)} %get-tuple-element.50.refs_6_.refs_14_), channel_id=1, source_target_pairs={{0,2},{2,0},{4,6},{6,4},{8,10},{10,8},{12,14},{14,12},{16,18},{18,... | collective-permute-start | bytes 1179656 | tf_op jit(solution)/shard_map/ppermute | solution.py:423
  26.1 13.5 %collective-permute-start.5 = (bf16[6,256,128]{2,1,0:T(8,128)(2,1)S(1)}, bf16[6,256,128]{2,1,0:T(8,128)(2,1)S(1)}, u32[]{:S(2)}, u32[]{:S(2)}) collective-permute-start(bf16[6,256,128]{2,1,0:T(8,128)(2,1)S(1)} %get-tuple-element.50.refs_6_.refs_14_), channel_id=1, source_target_pairs={{0,4},{2,6},{4,0},{6,2},{8,12},{10,14},{12,8},{14,10},{16,20},{18,... | collective-permute-start | bytes 1179656 | tf_op jit(solution)/shard_map/ppermute | solution.py:423
  27.6 12.3 %collective-permute-start.4 = (bf16[144,1536]{1,0:T(8,128)(2,1)S(1)}, bf16[144,1536]{1,0:T(8,128)(2,1)S(1)}, u32[]{:S(2)}, u32[]{:S(2)}) collective-permute-start(bf16[144,1536]{1,0:T(8,128)(2,1)S(1)} %collective-permute-done.2.refs_0_), channel_id=1, source_target_pairs={{0,1},{1,0},{2,3},{3,2},{4,5},{5,4},{6,7},{7,6},{8,9},{9,8},{10,11... | collective-permute-start | bytes 1327112 | tf_op jit(solution)/shard_map/ppermute | solution.py:420
  31.5 16.9 %collective-permute-start.10 = (bf16[9,112,128]{2,1,0:T(8,128)(2,1)S(1)}, bf16[9,112,128]{2,1,0:T(8,128)(2,1)S(1)}, u32[]{:S(2)}, u32[]{:S(2)}) collective-permute-start(bf16[9,112,128]{2,1,0:T(8,128)(2,1)S(1)} %get-tuple-element.63), channel_id=1, source_target_pairs={{0,24},{2,26},{4,28},{6,30},{8,16},{10,18},{12,20},{14,22},{16,8},... | collective-permute-start | bytes 774152 | tf_op jit(solution)/shard_map/ppermute | solution.py:423
  34.1 23.0 %collective-permute-start.6 = (bf16[9,112,128]{2,1,0:T(8,128)(2,1)S(1)}, bf16[9,112,128]{2,1,0:T(8,128)(2,1)S(1)}, u32[]{:S(2)}, u32[]{:S(2)}) collective-permute-start(bf16[9,112,128]{2,1,0:T(8,128)(2,1)S(1)} %get-tuple-element.54), channel_id=1, source_target_pairs={{0,16},{2,18},{4,20},{6,22},{8,24},{10,26},{12,28},{14,30},{16,0},... | collective-permute-start | bytes 774152 | tf_op jit(solution)/shard_map/ppermute | solution.py:423
  39.6 20.2 %collective-permute-start.12 = (bf16[6,256,128]{2,1,0:T(8,128)(2,1)S(1)}, bf16[6,256,128]{2,1,0:T(8,128)(2,1)S(1)}, u32[]{:S(2)}, u32[]{:S(2)}) collective-permute-start(bf16[6,256,128]{2,1,0:T(8,128)(2,1)S(1)} %collective-permute-done.5.refs_7_.refs_15_), channel_id=1, source_target_pairs={{0,2},{2,0},{4,6},{6,4},{8,10},{10,8},{12,14},{14,12},{16,18},{18,... | collective-permute-start | bytes 1179656 | tf_op jit(solution)/shard_map/ppermute | solution.py:423
  42.4 14.7 %collective-permute-start.8 = (bf16[3,256,128]{2,1,0:T(8,128)(2,1)S(1)}, bf16[3,256,128]{2,1,0:T(8,128)(2,1)S(1)}, u32[]{:S(2)}, u32[]{:S(2)}) collective-permute-start(bf16[3,256,128]{2,1,0:T(8,128)(2,1)S(1)} %get-tuple-element.61), channel_id=1, source_target_pairs={{0,4},{2,6},{4,0},{6,2},{8,12},{10,14},{12,8},{14,10},{16,20},{18,... | collective-permute-start | bytes 589832 | tf_op jit(solution)/shard_map/ppermute | solution.py:423
  43.0 14.6 %collective-permute-start.7 = (bf16[6,144,128]{2,1,0:T(8,128)(2,1)S(1)}, bf16[6,144,128]{2,1,0:T(8,128)(2,1)S(1)}, u32[]{:S(2)}, u32[]{:S(2)}) collective-permute-start(bf16[6,144,128]{2,1,0:T(8,128)(2,1)S(1)} %get-tuple-element.57), channel_id=1, source_target_pairs={{0,8},{2,10},{4,12},{6,14},{8,0},{10,2},{12,4},{14,6},{16,24},{18,... | collective-permute-start | bytes 663560 | tf_op jit(solution)/shard_map/ppermute | solution.py:423
  48.4 9.2 %collective-permute-start.9 = (bf16[3,256,128]{2,1,0:T(8,128)(2,1)S(1)}, bf16[3,256,128]{2,1,0:T(8,128)(2,1)S(1)}, u32[]{:S(2)}, u32[]{:S(2)}) collective-permute-start(bf16[3,256,128]{2,1,0:T(8,128)(2,1)S(1)} %get-tuple-element.62), channel_id=1, source_target_pairs={{0,4},{2,6},{4,0},{6,2},{8,12},{10,14},{12,8},{14,10},{16,20},{18,... | collective-permute-start | bytes 589832 | tf_op jit(solution)/shard_map/ppermute | solution.py:423
  57.1 4.3 %collective-permute-start.13 = (bf16[6,256,128]{2,1,0:T(8,128)(2,1)S(1)}, bf16[6,256,128]{2,1,0:T(8,128)(2,1)S(1)}, u32[]{:S(2)}, u32[]{:S(2)}) collective-permute-start(bf16[6,256,128]{2,1,0:T(8,128)(2,1)S(1)} %get-tuple-element.67.refs_10_.refs_18_), channel_id=1, source_target_pairs={{0,2},{2,0},{4,6},{6,4},{8,10},{10,8},{12,14},{14,12},{16,18},{18,... | collective-permute-start | bytes 1179656 | tf_op jit(solution)/shard_map/ppermute | solution.py:423
  57.1 2.7 %collective-permute-start.14 = (bf16[3,256,128]{2,1,0:T(8,128)(2,1)S(1)}, bf16[3,256,128]{2,1,0:T(8,128)(2,1)S(1)}, u32[]{:S(2)}, u32[]{:S(2)}) collective-permute-start(bf16[3,256,128]{2,1,0:T(8,128)(2,1)S(1)} %collective-permute-done.8.refs_11_), channel_id=1, source_target_pairs={{0,2},{2,0},{4,6},{6,4},{8,10},{10,8},{12,14},{14,12},{16,18},{18,... | collective-permute-start | bytes 589832 | tf_op jit(solution)/shard_map/ppermute | solution.py:423
  57.7 14.8 %collective-permute-start.17 = (bf16[4,256,128]{2,1,0:T(8,128)(2,1)S(1)}, bf16[4,256,128]{2,1,0:T(8,128)(2,1)S(1)}, u32[]{:S(2)}, u32[]{:S(2)}) collective-permute-start(bf16[4,256,128]{2,1,0:T(8,128)(2,1)S(1)} %get-tuple-element.68.refs_23_.refs_4_.refs_8_.refs_12_.refs_16_), channel_id=1, source_target_pairs={{0,4},{2,6},{4,0},{6,2},{8,12},{10,14},{12,8},{14,10},{16,20},{18,... | collective-permute-start | bytes 786440 | tf_op jit(solution)/shard_map/ppermute | solution.py:423
  58.3 20.7 %collective-permute-start.16 = (bf16[8,256,128]{2,1,0:T(8,128)(2,1)S(1)}, bf16[8,256,128]{2,1,0:T(8,128)(2,1)S(1)}, u32[]{:S(2)}, u32[]{:S(2)}) collective-permute-start(bf16[8,256,128]{2,1,0:T(8,128)(2,1)S(1)} %get-tuple-element.71.refs_4_.refs_8_.refs_12_.refs_16_), channel_id=1, source_target_pairs={{0,4},{2,6},{4,0},{6,2},{8,12},{10,14},{12,8},{14,10},{16,20},{18,... | collective-permute-start | bytes 1572872 | tf_op jit(solution)/shard_map/ppermute | solution.py:423
  59.8 1.4 %collective-permute-start.15 = (bf16[3,256,128]{2,1,0:T(8,128)(2,1)S(1)}, bf16[3,256,128]{2,1,0:T(8,128)(2,1)S(1)}, u32[]{:S(2)}, u32[]{:S(2)}) collective-permute-start(bf16[3,256,128]{2,1,0:T(8,128)(2,1)S(1)} %collective-permute-done.9.refs_19_), channel_id=1, source_target_pairs={{0,2},{2,0},{4,6},{6,4},{8,10},{10,8},{12,14},{14,12},{16,18},{18,... | collective-permute-start | bytes 589832 | tf_op jit(solution)/shard_map/ppermute | solution.py:423
  59.8 7.1 %collective-permute-start.11 = (bf16[3,144,128]{2,1,0:T(8,128)(2,1)S(1)}, bf16[3,144,128]{2,1,0:T(8,128)(2,1)S(1)}, u32[]{:S(2)}, u32[]{:S(2)}) collective-permute-start(bf16[3,144,128]{2,1,0:T(8,128)(2,1)S(1)} %get-tuple-element.66), channel_id=1, source_target_pairs={{0,8},{2,10},{4,12},{6,14},{8,0},{10,2},{12,4},{14,6},{16,24},{18,... | collective-permute-start | bytes 331784 | tf_op jit(solution)/shard_map/ppermute | solution.py:423
  61.2 11.9 %collective-permute-start.18 = (bf16[4,256,128]{2,1,0:T(8,128)(2,1)S(1)}, bf16[4,256,128]{2,1,0:T(8,128)(2,1)S(1)}, u32[]{:S(2)}, u32[]{:S(2)}) collective-permute-start(bf16[4,256,128]{2,1,0:T(8,128)(2,1)S(1)} %get-tuple-element.68.refs_23_.refs_4_.refs_8_.refs_12_.refs_16_), channel_id=1, source_target_pairs={{0,2},{2,0},{4,6},{6,4},{8,10},{10,8},{12,14},{14,12},{16,18},{18,... | collective-permute-start | bytes 786440 | tf_op jit(solution)/shard_map/ppermute | solution.py:423
  72.5 1.6 %collective-permute-start.19 = (bf16[4,256,128]{2,1,0:T(8,128)(2,1)S(1)}, bf16[4,256,128]{2,1,0:T(8,128)(2,1)S(1)}, u32[]{:S(2)}, u32[]{:S(2)}) collective-permute-start(bf16[4,256,128]{2,1,0:T(8,128)(2,1)S(1)} %collective-permute-done.17.refs_5_.refs_9_.refs_13_.refs_17_), channel_id=1, source_target_pairs={{0,2},{2,0},{4,6},{6,4},{8,10},{10,8},{12,14},{14,12},{16,18},{18,... | collective-permute-start | bytes 786440 | tf_op jit(solution)/shard_map/ppermute | solution.py:423
  72.9 6.5 %collective-permute-start.20 = (bf16[8,256,128]{2,1,0:T(8,128)(2,1)S(1)}, bf16[8,256,128]{2,1,0:T(8,128)(2,1)S(1)}, u32[]{:S(2)}, u32[]{:S(2)}) collective-permute-start(bf16[8,256,128]{2,1,0:T(8,128)(2,1)S(1)} %get-tuple-element.71.refs_4_.refs_8_.refs_12_.refs_16_), channel_id=1, source_target_pairs={{0,2},{2,0},{4,6},{6,4},{8,10},{10,8},{12,14},{14,12},{16,18},{18,... | collective-permute-start | bytes 1572872 | tf_op jit(solution)/shard_map/ppermute | solution.py:423
  79.0 2.0 %collective-permute-start.21 = (bf16[8,256,128]{2,1,0:T(8,128)(2,1)S(1)}, bf16[8,256,128]{2,1,0:T(8,128)(2,1)S(1)}, u32[]{:S(2)}, u32[]{:S(2)}) collective-permute-start(bf16[8,256,128]{2,1,0:T(8,128)(2,1)S(1)} %collective-permute-done.16.refs_5_.refs_9_.refs_13_.refs_17_), channel_id=1, source_target_pairs={{0,2},{2,0},{4,6},{6,4},{8,10},{10,8},{12,14},{14,12},{16,18},{18,... | collective-permute-start | bytes 1572872 | tf_op jit(solution)/shard_map/ppermute | solution.py:423
  85.9 12.4 %collective-permute-start.25 = (bf16[256,256]{1,0:T(8,128)(2,1)S(1)}, bf16[256,256]{1,0:T(8,128)(2,1)S(1)}, u32[]{:S(2)}, u32[]{:S(2)}) collective-permute-start(bf16[256,256]{1,0:T(8,128)(2,1)S(1)} %get-tuple-element.88), channel_id=1, source_target_pairs={{0,8},{2,10},{4,12},{6,14},{8,0},{10,2},{12,4},{14,6},{16,24},{18,... | collective-permute-start | bytes 393224 | tf_op jit(solution)/shard_map/ppermute | solution.py:423
  86.8 13.6 %collective-permute-start.26 = (bf16[256,256]{1,0:T(8,128)(2,1)S(1)}, bf16[256,256]{1,0:T(8,128)(2,1)S(1)}, u32[]{:S(2)}, u32[]{:S(2)}) collective-permute-start(bf16[256,256]{1,0:T(8,128)(2,1)S(1)} %get-tuple-element.89), channel_id=1, source_target_pairs={{0,16},{2,18},{4,20},{6,22},{8,24},{10,26},{12,28},{14,30},{16,0},... | collective-permute-start | bytes 393224 | tf_op jit(solution)/shard_map/ppermute | solution.py:423
  89.3 11.0 %collective-permute-start.27 = (bf16[256,256]{1,0:T(8,128)(2,1)S(1)}, bf16[256,256]{1,0:T(8,128)(2,1)S(1)}, u32[]{:S(2)}, u32[]{:S(2)}) collective-permute-start(bf16[256,256]{1,0:T(8,128)(2,1)S(1)} %get-tuple-element.90), channel_id=1, source_target_pairs={{0,24},{2,26},{4,28},{6,30},{8,16},{10,18},{12,20},{14,22},{16,8},... | collective-permute-start | bytes 393224 | tf_op jit(solution)/shard_map/ppermute | solution.py:423
  95.5 6.6 %collective-permute-start.24 = (bf16[256,128]{1,0:T(8,128)(2,1)S(1)}, bf16[256,128]{1,0:T(8,128)(2,1)S(1)}, u32[]{:S(2)}, u32[]{:S(2)}) collective-permute-start(bf16[256,128]{1,0:T(8,128)(2,1)S(1)} %get-tuple-element.87), channel_id=1, source_target_pairs={{0,24},{2,26},{4,28},{6,30},{8,16},{10,18},{12,20},{14,22},{16,8},... | collective-permute-start | bytes 196616 | tf_op jit(solution)/shard_map/ppermute | solution.py:423
  98.3 4.3 %collective-permute-start.22 = (bf16[256,128]{1,0:T(8,128)(2,1)S(1)}, bf16[256,128]{1,0:T(8,128)(2,1)S(1)}, u32[]{:S(2)}, u32[]{:S(2)}) collective-permute-start(bf16[256,128]{1,0:T(8,128)(2,1)S(1)} %get-tuple-element.85), channel_id=1, source_target_pairs={{0,8},{2,10},{4,12},{6,14},{8,0},{10,2},{12,4},{14,6},{16,24},{18,... | collective-permute-start | bytes 196616 | tf_op jit(solution)/shard_map/ppermute | solution.py:423
  98.4 8.8 %collective-permute-start.23 = (bf16[256,128]{1,0:T(8,128)(2,1)S(1)}, bf16[256,128]{1,0:T(8,128)(2,1)S(1)}, u32[]{:S(2)}, u32[]{:S(2)}) collective-permute-start(bf16[256,128]{1,0:T(8,128)(2,1)S(1)} %get-tuple-element.86), channel_id=1, source_target_pairs={{0,16},{2,18},{4,20},{6,22},{8,24},{10,26},{12,28},{14,30},{16,0},... | collective-permute-start | bytes 196616 | tf_op jit(solution)/shard_map/ppermute | solution.py:423
  107.8 18.7 %collective-permute-start.28 = (bf16[256,1536]{1,0:T(8,128)(2,1)S(1)}, bf16[256,1536]{1,0:T(8,128)(2,1)S(1)}, u32[]{:S(2)}, u32[]{:S(2)}) collective-permute-start(bf16[256,1536]{1,0:T(8,128)(2,1)S(1)} %shard_map.90), channel_id=1, source_target_pairs={{0,1},{1,0},{2,3},{3,2},{4,5},{5,4},{6,7},{7,6},{8,9},{9,8},{10,11... | collective-permute-start | bytes 2359304 | tf_op jit(solution)/shard_map/ppermute | solution.py:420

commit v6 on v5

--- a/solution.py
+++ b/solution.py
@@ -14,6 +14,7 @@
 MIB = 1 << 20
 BF16, F32 = jnp.bfloat16, jnp.float32
 LIGHT = pl.CostEstimate(flops=1024, bytes_accessed=1024, transcendentals=0)
+SOME = pl.CostEstimate(flops=1024, bytes_accessed=1 << 20, transcendentals=0)
 
 
 def place(z, x, c):
@@ -196,141 +197,120 @@
     )(where, block_order[None, :], block_mask)
 
 
-def attend(queries, parts, states, bias, query_at, key_at, last, fences, earlier=()):
-    rows = queries[0][0][0].shape[1]
-    tile = parts[0][0][0].shape[1]
-    n = len(parts[0])
-    group = 4
+def attend(steps, parts, stride, bias, mask_at, mask_stride, key_at, outputs, earlier, fences):
+    tile = parts[0][0].shape[1]
+    n, count = len(parts), len(steps)
     scale = math.log2(math.e) / math.sqrt(HEAD_DIM)
-    per = rows // BLOCK
-    both = 2 * rows
-    steps = len(queries)
-    same_parts = len(parts) == 1
+    every = sum(q[3] for q in steps[0][0])
+    width = n * tile
+    carried = bool(steps[0][1])
+    arrays = []
+
+    def index_of(array):
+        for i, known in enumerate(arrays):
+            if known is array:
+                return i
+        arrays.append(array)
+        return len(arrays) - 1
+
+    plan = [
+        (
+            [(index_of(q), *rest) for q, *rest in queries],
+            [([index_of(a) for a in held], *rest) for held, *rest in states],
+            results,
+        )
+        for queries, states, results in steps
+    ]
+    part_plan = [(index_of(p[0]), p[1], index_of(p[2]), p[3]) for p in parts]
+    earlier_plan = [(index_of(a), low, out) for a, low, out in earlier]
+    bias_index = index_of(bias)
+    total_arrays = len(arrays)
 
     def body(*refs):
-        refs = list(refs)
-
-        def take(count):
-            got = refs[:count]
-            del refs[:count]
-            return got
-
-        q_refs = take(2 * steps)
-        k_refs, v_refs = take(n), take(n)
-        state_refs = [take(3) for _ in states]
-        (bias_ref,) = take(1)
-        take(len(fences))
-        earlier_refs = take(len(earlier))
-        outs = take(2 * steps if last else 3)
-        q_ref = refs[0]
+        ins = refs[:total_arrays]
+        outs = refs[total_arrays + len(fences) :]
+        q_ref = outs[-1 - (3 if carried else 0)]
+        held_refs = outs[len(outs) - 3 :]
         step = pl.program_id(0)
-        for i in range(steps):
+        for i, (queries, states, _) in enumerate(plan):
 
             @pl.when(step == i)
-            def _(i=i):
-                q_ref[:rows] = q_refs[2 * i][0]
-                q_ref[rows:] = q_refs[2 * i + 1][0]
-                if states:
-                    for held, ref in zip(refs[1:], state_refs[i]):
-                        held[...] = ref[0]
-
-        query = q_ref[...]
-        if states:
-            top, total, accum = refs[1][:, :1], refs[2][...], refs[3][...]
+            def _(i=i, queries=queries, states=states):
+                at = 0
+                for q, block, low, size in queries:
+                    q_ref[at : at + size] = ins[q][block, low : low + size]
+                    at += size
+                at = 0
+                for held, block, low, size in states:
+                    for k in range(3):
+                        held_refs[k][at : at + size] = ins[held[k]][block, low : low + size]
+                    at += size
+                if i == 0:
+                    for a, low, out in earlier_plan:
+                        outs[out][:, :HEAD_DIM] = ins[a][low : low + outs[out].shape[0]]
+
+        shift = step * stride
+        key = jnp.concatenate([ins[k][at + shift] for k, at, _, _ in part_plan], axis=0)
+        value = jnp.concatenate([ins[v][at + shift] for _, _, v, at in part_plan], axis=0)
+        if carried:
+            top, total, accum = held_refs[0][:, :1], held_refs[1][...], held_refs[2][...]
         else:
-            top = jnp.full((both, 1), -1e30, F32)
-            total = jnp.zeros((both, HEAD_DIM), F32)
-            accum = jnp.zeros((both, HEAD_DIM), F32)
-        first_row = (query_at[0] + step * query_at[1]) * per
-        for t in range(0, n, group):
-            key = jnp.concatenate([k_refs[u][0] for u in range(t, t + group)], axis=0)
-            value = jnp.concatenate([v_refs[u][0] for u in range(t, t + group)], axis=0)
-            width = group * tile
-            at = (key_at + t) * tile
-            score = lax.dot_general(
-                query, key, (((1,), (1,)), ((), ())), preferred_element_type=F32
+            top = jnp.full((every, 1), -1e30, F32)
+            total = jnp.zeros((every, HEAD_DIM), F32)
+            accum = jnp.zeros((every, HEAD_DIM), F32)
+        score = lax.dot_general(
+            q_ref[...], key, (((1,), (1,)), ((), ())), preferred_element_type=F32
+        )
+        columns = slice(key_at * tile, key_at * tile + width)
+        keep = [
+            jnp.broadcast_to(
+                ins[bias_index][pl.ds(row + step * mask_stride, 1), columns], (BLOCK, width)
             )
-            keep = [
-                jnp.broadcast_to(bias_ref[pl.ds(first_row + r, 1), at : at + width], (BLOCK, width))
-                for r in range(2 * per)
-            ]
-            score = score + jnp.concatenate(keep, axis=0)
-            best = score[:, :HEAD_DIM]
-            for u in range(HEAD_DIM, width, HEAD_DIM):
-                best = jnp.maximum(best, score[:, u : u + HEAD_DIM])
-            top_next = jnp.maximum(top, jnp.max(best, axis=1, keepdims=True))
-            factor = jnp.exp2((top - top_next) * scale)
-            top = top_next
-            weight = jnp.exp2(score * scale - top * scale)
-            add = weight[:, :HEAD_DIM]
-            for u in range(HEAD_DIM, width, HEAD_DIM):
-                add = add + weight[:, u : u + HEAD_DIM]
-            total = total * factor + add
-            accum = accum * factor + jnp.dot(
-                weight.astype(BF16), value, preferred_element_type=F32
-            )
-        if last:
-            result = (accum / jnp.sum(total, axis=1, keepdims=True)).astype(BF16)
-            for i in range(steps):
-
-                @pl.when(step == i)
-                def _(i=i):
-                    for half in range(2):
-                        out, piece = outs[2 * i + half], result[half * rows : (half + 1) * rows]
-                        if earlier:
-                            before = earlier_refs[2 * i + half][...]
-                            piece = jnp.concatenate([before, piece], axis=1)
-                        out[...] = piece
-
-        else:
-            outs[0][0] = jnp.broadcast_to(top, (both, HEAD_DIM))
-            outs[1][0] = total
-            outs[2][0] = accum
-
-    def fixed(block, index):
-        return pl.BlockSpec(block, lambda i: (index,) + (0,) * (len(block) - 1))
-
-    def part_spec(kind):
-        def one(u):
-            base = parts[0][u][2 * kind + 1]
-            stride = 0 if same_parts else 1
-            return pl.BlockSpec((1, tile, HEAD_DIM), lambda i: (base + i * stride, 0, 0))
-
-        return [one(u) for u in range(n)]
-
-    arrays = [p[2 * kind] for kind in range(2) for p in parts[0]]
-    state_block = (1, both, HEAD_DIM)
-    if last:
-        out_width = HEAD_DIM + (earlier[0].shape[1] if earlier else 0)
-        out_specs = [pl.BlockSpec((rows, out_width), lambda i: (0, 0))] * (2 * steps)
-        out_shape = [jax.ShapeDtypeStruct((rows, out_width), BF16)] * (2 * steps)
+            for row in mask_at
+        ]
+        score = score + jnp.concatenate(keep, axis=0)
+        best = score[:, :HEAD_DIM]
+        for u in range(HEAD_DIM, width, HEAD_DIM):
+            best = jnp.maximum(best, score[:, u : u + HEAD_DIM])
+        top_next = jnp.maximum(top, jnp.max(best, axis=1, keepdims=True))
+        factor = jnp.exp2((top - top_next) * scale)
+        weight = jnp.exp2(score * scale - top_next * scale)
+        add = weight[:, :HEAD_DIM]
+        for u in range(HEAD_DIM, width, HEAD_DIM):
+            add = add + weight[:, u : u + HEAD_DIM]
+        total = total * factor + add
+        accum = accum * factor + jnp.dot(weight.astype(BF16), value, preferred_element_type=F32)
+        if outputs is None:
+            outs[0][step] = jnp.broadcast_to(top_next, (every, HEAD_DIM))
+            outs[1][step] = total
+            outs[2][step] = accum
+            return
+        result = (accum / jnp.sum(total, axis=1, keepdims=True)).astype(BF16)
+        for i, (queries, _, results) in enumerate(plan):
+
+            @pl.when(step == i)
+            def _(queries=queries, results=results):
+                at = 0
+                for (_, _, _, size), (out, head) in zip(queries, results):
+                    lanes = slice(head * HEAD_DIM, (head + 1) * HEAD_DIM)
+                    outs[out][:, lanes] = result[at : at + size]
+                    at += size
+
+    if outputs is None:
+        out_shape = [jax.ShapeDtypeStruct((count, every, HEAD_DIM), F32)] * 3
     else:
-        out_specs = [pl.BlockSpec(state_block, lambda i: (i, 0, 0))] * 3
-        out_shape = [jax.ShapeDtypeStruct((steps, both, HEAD_DIM), F32)] * 3
-    return pl.pallas_call(
-        body,
-        grid=(steps,),
-        in_specs=[fixed((1, rows, HEAD_DIM), at) for row in queries for _, at in row]
-        + part_spec(0)
-        + part_spec(1)
-        + [fixed(state_block, at) for _, at in states for _ in range(3)]
-        + [pl.BlockSpec(bias.shape, lambda i: (0, 0))]
-        + [pl.BlockSpec(memory_space=pl.ANY)] * len(fences)
-        + [pl.BlockSpec(e.shape, lambda i: (0, 0)) for e in earlier],
-        out_specs=out_specs,
+        out_shape = [jax.ShapeDtypeStruct(shape, BF16) for shape in outputs]
+    return pl.pallas_call(
+        body,
+        grid=(count,),
+        in_specs=whole(total_arrays) + [pl.BlockSpec(memory_space=pl.ANY)] * len(fences),
+        out_specs=whole(len(out_shape)),
         out_shape=out_shape,
-        scratch_shapes=[pltpu.VMEM((both, HEAD_DIM), BF16)]
-        + [pltpu.VMEM((both, HEAD_DIM), F32)] * (3 if states else 0),
+        scratch_shapes=[pltpu.VMEM((every, HEAD_DIM), BF16)]
+        + [pltpu.VMEM((every, HEAD_DIM), F32)] * (3 if carried else 0),
         compiler_params=params(24),
         cost_estimate=LIGHT,
-    )(
-        *[a for row in queries for a, _ in row],
-        *arrays,
-        *[a for held, _ in states for a in held],
-        bias,
-        *fences,
-        *earlier,
-    )
+    )(*arrays, *fences)
 
 
 def fetch_out(where, w_out, fence):
@@ -370,43 +350,55 @@
     )(where, w_out, fence)
 
 
-def mix(attended, held, skip, columns, earlier, out_type):
-    rows, width = attended[0].shape
-    depth = held.shape[0] // Z
+def mix(attended, held, part):
+    rows = attended[0].shape[0]
+    half = held.shape[1] // 2
     count = len(attended)
-    first, last = columns
-    step = (last - first) // 3
+    step = half // 3
 
     def body(*refs):
         rows_all = jnp.concatenate([r[...] for r in refs[:count]], axis=1)
         for i in range(3):
-            at = slice(first + i * step, first + (i + 1) * step)
-            weight = jnp.concatenate(
-                [
-                    refs[count][g * depth + skip : g * depth + skip + width, at]
-                    for g in range(count)
-                ],
-                axis=0,
-            )
-            total = jnp.dot(rows_all, weight, preferred_element_type=F32)
-            if earlier is not None:
-                total += refs[count + 1][:, at]
-            refs[-1][:, i * step : (i + 1) * step] = total.astype(out_type)
-
-    more = [] if earlier is None else [earlier]
-    return pl.pallas_call(
-        body,
-        in_specs=whole(count + 1 + len(more)),
+            weight = refs[count][:, part * half + i * step : part * half + (i + 1) * step]
+            refs[-1][:, i * step : (i + 1) * step] = jnp.dot(
+                rows_all, weight, preferred_element_type=F32
+            ).astype(BF16)
+
+    return pl.pallas_call(
+        body,
+        in_specs=whole(count + 1),
         out_specs=whole(1)[0],
-        out_shape=jax.ShapeDtypeStruct((rows, last - first), out_type),
+        out_shape=jax.ShapeDtypeStruct((rows, half), BF16),
         compiler_params=params(16),
         cost_estimate=LIGHT,
-    )(*attended, held, *more)
+    )(*attended, held)
+
+
+def finish(home, arrived, above, cost):
+    rows, width = home.shape
+    first = 0 if above is None else above.shape[0]
+
+    def body(*refs):
+        total = refs[0][...].astype(F32) + refs[1][...].astype(F32)
+        if above is not None:
+            refs[-1][:first] = refs[2][...]
+        refs[-1][first:] = total.astype(BF16)
+
+    more = [] if above is None else [above]
+    return pl.pallas_call(
+        body,
+        in_specs=whole(2 + len(more)),
+        out_specs=whole(1)[0],
+        out_shape=jax.ShapeDtypeStruct((first + rows, width), BF16),
+        compiler_params=params(8),
+        cost_estimate=cost,
+    )(home, arrived, *more)
 
 
 def split_heads(tokens, block_order, block_mask, w_query, w_key, w_value, w_out):
     rows, half = tokens.shape
     group_heads = w_query.shape[1] // HEAD_DIM // Z
+    per = rows // BLOCK
     cut = rows * 9 // 16
     ctx = lax.axis_index("ctx")
     y = lax.axis_index("head")
@@ -497,62 +489,92 @@
         (came_core, 0, came_core, n),
         (across_core_k, 0, across_core_v, 0),
     ]
-    near_parts = [near, None]
+
+    def whole_rows(arrays, j):
+        return [(a, j, 0, rows) for a in arrays]
+
     state_near = attend(
-        [[(own_q, j), (came, j)] for j in heads], near_parts, [], bias, (0, 0), 0, False, [far_first]
+        [(whole_rows([own_q, came], j), [], []) for j in heads],
+        near,
+        1,
+        bias,
+        range(2 * per),
+        0,
+        0,
+        None,
+        [],
+        [far_first],
     )
     (far_came_q,) = pack(
         [[[after(far_came_q, state_near[0])], [low3]]], [[(0, h, h) for h in heads]]
     )
     state_far = attend(
-        [[(far_q, j), (far_came_q, j)] for j in heads],
-        near_parts,
+        [(whole_rows([far_q, far_came_q], j), [], []) for j in heads],
+        near,
+        1,
+        bias,
+        range(2 * per, 4 * per),
+        0,
+        0,
+        None,
         [],
-        bias,
-        (2, 0),
-        0,
-        False,
         [state_near[0]],
     )
     first_across = after(first_across, state_far[0])
     first_across_core = over(first_across, 0, 0, 1)
 
-    results = []
-    for j in heads:
-        if j == 0:
-            arrays, size, at = [far_first, first_across, first_core, first_across_core], 1, 0
-            fences = []
-        else:
-            if j == 1:
-                rest_across = after(rest_across, results[0][0])
-                rest_across_core = over(rest_across, 0, 0, 1)
-            arrays, size, at = [far_rest, rest_across, rest_core, rest_across_core], len(rest), j - 1
-            fences = [results[-1][0]]
-        parts = [
-            (a, 2 * i * size + at, a, (2 * i + 1) * size + at) for i in range(2) for a in arrays
+    def far_parts(arrays, size):
+        return [(a, 2 * i * size, a, (2 * i + 1) * size) for i in range(2) for a in arrays]
+
+    first_rows = attend(
+        [
+            (whole_rows([own_q, came], 0), [(state_near, 0, 0, 2 * rows)], [(0, 0), (1, 0)]),
+            (whole_rows([far_q, far_came_q], 0), [(state_far, 0, 0, 2 * rows)], [(2, 0), (3, 0)]),
+        ],
+        far_parts([far_first, first_across, first_core, first_across_core], 1),
+        0,
+        bias,
+        range(2 * per),
+        2 * per,
+        len(near),
+        [(rows, HEAD_DIM)] * Z,
+        [],
+        [],
+    )
+    rest_across = after(rest_across, first_rows[0])
+    rest_across_core = over(rest_across, 0, 0, 1)
+    rest_parts = far_parts([far_rest, rest_across, rest_core, rest_across_core], len(rest))
+    homes, arrived, fences = [], [], []
+    for low in range(0, rows, BLOCK):
+        steps = [
+            (
+                [(a, j, low, BLOCK) for a in (own_q, came, far_q, far_came_q)],
+                [(s, j, i * rows + low, BLOCK) for s in (state_near, state_far) for i in range(2)],
+                [(i, j) for i in range(Z)],
+            )
+            for j in rest
         ]
-        rows_out = attend(
-            [[(own_q, j), (came, j)], [(far_q, j), (far_came_q, j)]],
-            [parts],
-            [(state_near, j), (state_far, j)],
+        done = attend(
+            steps,
+            rest_parts,
+            1,
             bias,
-            (0, 2),
+            [i * per + low // BLOCK for i in range(Z)],
+            0,
             len(near),
-            True,
+            [(BLOCK, span)] * Z,
+            [(first_rows[i], low, i) for i in range(Z)],
             fences,
-            results.pop() if j == 1 else (),
         )
-        results.append(rows_out)
-    results = [[r[0]] + [over(r[dz], dz, 0, 0) for dz in range(1, Z)] for r in results]
-    width = w_out.shape[1]
-    skip = results[0][0].shape[1]
-    partial = mix(results[0], out_held, 0, (0, width), None, F32)
-    rest = results[1][:-1] + [after(results[1][-1], partial)]
-    away = mix(rest, out_held, skip, (0, width // 2), partial, BF16)
-    arrived = over_y(away)
-    rest = rest[:-1] + [after(rest[-1], away)]
-    home = mix(rest, out_held, skip, (width // 2, width), partial, BF16)
-    return (home.astype(F32) + arrived.astype(F32)).astype(BF16)
+        fences = [done[0]]
+        back = [done[0]] + [over(done[dz], dz, 0, 0) for dz in range(1, Z)]
+        if arrived:
+            back[-1] = after(back[-1], homes[0])
+        away = mix(back, out_held, 0)
+        arrived.append(over_y(away))
+        homes.append(mix(back[:-1] + [after(back[-1], away)], out_held, 1))
+    upper = finish(homes[0], arrived[0], None, SOME)
+    return finish(homes[1], after(arrived[1], upper), upper, LIGHT)
 
 
 def gather_all(tokens, block_order, block_mask, w_query, w_key, w_value, w_out):

time: 128 us -> 118 us (0.922)
  waiting for transfers between devices: 37.2 us -> 29.2 us
  Pallas kernels: 55.6 us -> 54 us
    ppermute x3 -> x4, waiting for transfers between devices: 16.9 us -> 8.6 us  [over_y(): return lax.ppermute(a, 'head', [(0, 1), (1, 0)])]
    pallas_call x8 -> x11, Pallas kernels: 29 us -> 27.5 us  [the longest x5 23.1 us: attend(): pl.pallas_call(body, grid=(count,), in_specs=whole(total_arrays) + [pl.Bl...]
    ppermute x3 -> x4, starting transfers between devices: 5.94 us -> 6.57 us  [over_y(): return lax.ppermute(a, 'head', [(0, 1), (1, 0)])]
  transfers between devices with their start and end apart: 29 -> 30, of which waited for: 10 -> 10; matrix products, arithmetic and copies ran while one was open for 1% -> 1% of each run, Pallas kernels for 39% -> 42%
where the time goes in v6:
time: 118 us
  Pallas kernels  54 us (46%)
  starting transfers between devices  31.5 us (27%)
  waiting for transfers between devices  29.2 us (25%)
  local copies, waits for them, and re-layouts  2.45 us (2%)
    ppermute x26, starting transfers between devices, over(): return lax.ppermute(a, 'ctx', hop(dz, dx, dc))  25 us
    pallas_call x5, Pallas kernels, attend(): pl.pallas_call(body, grid=(count,), in_specs=whole(total_arrays) + [pl.Bl...  23.1 us
    ppermute x26, waiting for transfers between devices, over(): return lax.ppermute(a, 'ctx', hop(dz, dx, dc))  20.6 us
    pallas_call x2, Pallas kernels, fetch(): pl.pallas_call(body, grid_spec=pltpu.PrefetchScalarGridSpec(num_scalar_pr...  11.7 us
    pallas_call x4, Pallas kernels, project(): pl.pallas_call(body, in_specs=whole(3), out_specs=whole(len(outputs)), ou...  9.28 us
    ppermute x4, waiting for transfers between devices, over_y(): return lax.ppermute(a, 'head', [(0, 1), (1, 0)])  8.6 us
    ppermute x4, starting transfers between devices, over_y(): return lax.ppermute(a, 'head', [(0, 1), (1, 0)])  6.57 us
    pallas_call x1, Pallas kernels, fetch_out(): pl.pallas_call(body, grid_spec=pltpu.PrefetchScalarGridSpec(num_scalar_pr...  4.33 us
  transfers between devices with their start and end apart: 30, of which 10 were waited for; matrix products, arithmetic and copies ran while one was open for 1% of the time, Pallas kernels for 42%

profile of v6, /device:TPU:0, one launch (start us, length us, event | category | flops | bytes accessed | tf_op | source)
XLA Modules:
  0.0 117.6 jit_solution(1458474832597520750)
XLA Ops:
  0.0 3.0 %collective-permute-start = (bf16[256,1536]{1,0:T(8,128)(2,1)}, bf16[256,1536]{1,0:T(8,128)(2,1)S(1)}, u32[]{:S(2)}, u32[]{:S(2)}) collective-permute-start(bf16[256,1536]{1,0:T(8,128)(2,1)} %refs_0_.7), channel_id=1, source_target_pairs={{0,1},{1,0},{2,3},{3,2},{4,5},{5,4},{6,7},{7,6},{8,9},{9,8},{10,11... | collective-permute-start | bytes 2359304 | tf_op jit(solution)/shard_map/ppermute | solution.py:412
  3.0 1.1 slice.3
  4.0 2.7 %collective-permute-start.2 = (bf16[144,1536]{1,0:T(8,128)(2,1)S(1)}, bf16[144,1536]{1,0:T(8,128)(2,1)S(1)}, u32[]{:S(2)}, u32[]{:S(2)}) collective-permute-start(bf16[144,1536]{1,0:T(8,128)(2,1)S(1)} %slice.3), channel_id=1, source_target_pairs={{0,16},{2,18},{4,20},{6,22},{8,24},{10,26},{12,28},{14,30},{16,0},... | collective-permute-start | bytes 1327112 | tf_op jit(solution)/shard_map/ppermute | solution.py:415
  6.8 0.7 copy-done.1
  7.5 0.7 copy-done.2
  8.2 1.1 shard_map.73.refs_3_.refs_12_.refs_14_.refs_18_
  9.2 5.8 %shard_map.74.refs_3_.refs_2_ = bf16[6,3072,384]{2,1,0:T(8,128)(2,1)S(1)} custom-call(s32[4]{0:T(128)S(1)} %pad_add_fusion.s, bf16[3072,1536]{1,0:T(8,128)(2,1)} %refs_0_.4, bf16[3072,1536]{1,0:T(8,128)(2,1)} %refs_1_.3, bf16[3072,1536]{1,0:T(8,128)(2,1)} %refs_2_.3, f32[8,4096]{1,0:T(8,128)S(1)} %shard_map.73.refs_3_.refs_12_.refs_14_.refs_18_), custom_call_target="tpu_custom_call" | custom-call | flops 1024 | bytes 1024 | tf_op jit(solution)/shard_map/pallas_call | solution.py:70
  15.1 5.8 %shard_map.75.refs_2_ = bf16[6,3072,384]{2,1,0:T(8,128)(2,1)S(1)} custom-call(s32[4]{0:T(128)S(1)} %pad_add_fusion.s, bf16[3072,1536]{1,0:T(8,128)(2,1)} %refs_0_.4, bf16[3072,1536]{1,0:T(8,128)(2,1)} %refs_1_.3, bf16[3072,1536]{1,0:T(8,128)(2,1)} %refs_2_.3, bf16[6,3072,384]{2,1,0:T(8,128)(2,1)S(1)} %shard_map.74.refs_3_.refs_2_), custom_call_target="tpu_custom_call" | custom-call | flops 1024 | bytes 1024 | tf_op jit(solution)/shard_map/pallas_call | solution.py:70
  20.9 3.5 %shard_map.76 = (bf16[6,256,128]{2,1,0:T(8,128)(2,1)S(1)}, bf16[9,256,128]{2,1,0:T(8,128)(2,1)S(1)}) custom-call(bf16[256,1536]{1,0:T(8,128)(2,1)S(1)} %copy-done, bf16[256,1536]{1,0:T(8,128)(2,1)S(1)} %collective-permute-done.refs_1_, bf16[6,3072,384]{2,1,0:T(8,128)(2,1)S(1)} %shard_map.74.refs_3_.refs_2_), custom_call_target="tpu_custom_call" | custom-call | flops 1024 | bytes 1024 | tf_op jit(solution)/shard_map/pallas_call | solution.py:106
  24.4 1.6 %collective-permute-start.3 = (bf16[9,256,128]{2,1,0:T(8,128)(2,1)S(1)}, bf16[9,256,128]{2,1,0:T(8,128)(2,1)S(1)}, u32[]{:S(2)}, u32[]{:S(2)}) collective-permute-start(bf16[9,256,128]{2,1,0:T(8,128)(2,1)S(1)} %get-tuple-element.53), channel_id=1, source_target_pairs={{0,8},{2,10},{4,12},{6,14},{8,0},{10,2},{12,4},{14,6},{16,24},{18,... | collective-permute-start | bytes 1769480 | tf_op jit(solution)/shard_map/ppermute | solution.py:415
  26.1 1.5 %collective-permute-start.5 = (bf16[6,256,128]{2,1,0:T(8,128)(2,1)S(1)}, bf16[6,256,128]{2,1,0:T(8,128)(2,1)S(1)}, u32[]{:S(2)}, u32[]{:S(2)}) collective-permute-start(bf16[6,256,128]{2,1,0:T(8,128)(2,1)S(1)} %get-tuple-element.52.refs_2_), channel_id=1, source_target_pairs={{0,4},{2,6},{4,0},{6,2},{8,12},{10,14},{12,8},{14,10},{16,20},{18,... | collective-permute-start | bytes 1179656 | tf_op jit(solution)/shard_map/ppermute | solution.py:415
  27.6 1.5 %collective-permute-start.4 = (bf16[144,1536]{1,0:T(8,128)(2,1)S(1)}, bf16[144,1536]{1,0:T(8,128)(2,1)S(1)}, u32[]{:S(2)}, u32[]{:S(2)}) collective-permute-start(bf16[144,1536]{1,0:T(8,128)(2,1)S(1)} %collective-permute-done.2.refs_0_), channel_id=1, source_target_pairs={{0,1},{1,0},{2,3},{3,2},{4,5},{5,4},{6,7},{7,6},{8,9},{9,8},{10,11... | collective-permute-start | bytes 1327112 | tf_op jit(solution)/shard_map/ppermute | solution.py:412
  29.1 2.4 %shard_map.77 = (bf16[9,112,128]{2,1,0:T(8,128)(2,1)S(1)}, bf16[9,112,128]{2,1,0:T(8,128)(2,1)S(1)}) custom-call(bf16[256,1536]{1,0:T(8,128)(2,1)S(1)} %copy-done, bf16[256,1536]{1,0:T(8,128)(2,1)S(1)} %collective-permute-done.refs_1_, bf16[6,3072,384]{2,1,0:T(8,128)(2,1)S(1)} %shard_map.75.refs_2_), custom_call_target="tpu_custom_call" | custom-call | flops 1024 | bytes 1024 | tf_op jit(solution)/shard_map/pallas_call | solution.py:106
  31.5 2.5 %collective-permute-start.10 = (bf16[9,112,128]{2,1,0:T(8,128)(2,1)S(1)}, bf16[9,112,128]{2,1,0:T(8,128)(2,1)S(1)}, u32[]{:S(2)}, u32[]{:S(2)}) collective-permute-start(bf16[9,112,128]{2,1,0:T(8,128)(2,1)S(1)} %get-tuple-element.65), channel_id=1, source_target_pairs={{0,24},{2,26},{4,28},{6,30},{8,16},{10,18},{12,20},{14,22},{16,8},... | collective-permute-start | bytes 774152 | tf_op jit(solution)/shard_map/ppermute | solution.py:415
  34.3 1.0 shard_map.78.fence_ref.refs_0_
  35.3 4.3 %shard_map.79.refs_4_ = bf16[1536,3072]{1,0:T(8,128)(2,1)S(1)} custom-call(s32[4]{0:T(128)S(1)} %pad_add_fusion.s, bf16[1536,3072]{1,0:T(8,128)(2,1)} %w_ref.1, bf16[3,256,128]{2,1,0:T(8,128)(2,1)S(1)} %shard_map.78.fence_ref.refs_0_), custom_call_target="tpu_custom_call" | custom-call | flops 1024 | bytes 1024 | tf_op jit(solution)/shard_map/pallas_call | solution.py:338
  39.9 2.4 %shard_map.80 = (bf16[3,144,128]{2,1,0:T(8,128)(2,1)S(1)}, bf16[6,144,128]{2,1,0:T(8,128)(2,1)S(1)}, bf16[9,144,128]{2,1,0:T(8,128)(2,1)S(1)}) custom-call(bf16[144,1536]{1,0:T(8,128)(2,1)S(1)} %collective-permute-done.2.refs_0_, bf16[144,1536]{1,0:T(8,128)(2,1)S(1)} %collective-permute-done.4.refs_1_, bf16[6,3072,384]{2,1,0:T(8,128)(2,1)S(1)} %shard_map.74.refs_3_.refs_2_), custom_call_target="tpu_custom_call" | custom-call | flops 1024 | bytes 1024 | tf_op jit(solution)/shard_map/pallas_call | solution.py:106
  42.4 0.6 collective-permute-start.8
  43.0 1.5 %collective-permute-start.7 = (bf16[6,144,128]{2,1,0:T(8,128)(2,1)S(1)}, bf16[6,144,128]{2,1,0:T(8,128)(2,1)S(1)}, u32[]{:S(2)}, u32[]{:S(2)}) collective-permute-start(bf16[6,144,128]{2,1,0:T(8,128)(2,1)S(1)} %get-tuple-element.59), channel_id=1, source_target_pairs={{0,8},{2,10},{4,12},{6,14},{8,0},{10,2},{12,4},{14,6},{16,24},{18,... | collective-permute-start | bytes 663560 | tf_op jit(solution)/shard_map/ppermute | solution.py:415
  44.5 3.9 %collective-permute-done.10.refs_3_.refs_1_ = bf16[9,112,128]{2,1,0:T(8,128)(2,1)S(1)} collective-permute-done((bf16[9,112,128]{2,1,0:T(8,128)(2,1)S(1)}, bf16[9,112,128]{2,1,0:T(8,128)(2,1)S(1)}, u32[]{:S(2)}, u32[]{:S(2)}) %collective-permute-start.10) | collective-permute-done | bytes 258080 | tf_op jit(solution)/shard_map/ppermute | solution.py:415
  48.4 1.5 %collective-permute-start.9 = (bf16[3,256,128]{2,1,0:T(8,128)(2,1)S(1)}, bf16[3,256,128]{2,1,0:T(8,128)(2,1)S(1)}, u32[]{:S(2)}, u32[]{:S(2)}) collective-permute-start(bf16[3,256,128]{2,1,0:T(8,128)(2,1)S(1)} %get-tuple-element.64), channel_id=1, source_target_pairs={{0,4},{2,6},{4,0},{6,2},{8,12},{10,14},{12,8},{14,10},{16,20},{18,... | collective-permute-start | bytes 589832 | tf_op jit(solution)/shard_map/ppermute | solution.py:415
  49.9 7.2 %collective-permute-done.6.refs_1_ = bf16[9,112,128]{2,1,0:T(8,128)(2,1)S(1)} collective-permute-done((bf16[9,112,128]{2,1,0:T(8,128)(2,1)S(1)}, bf16[9,112,128]{2,1,0:T(8,128)(2,1)S(1)}, u32[]{:S(2)}, u32[]{:S(2)}) %collective-permute-start.6) | collective-permute-done | bytes 258080 | tf_op jit(solution)/shard_map/ppermute | solution.py:415
  57.7 0.6 collective-permute-start.17
  58.3 1.5 %collective-permute-start.16 = (bf16[8,256,128]{2,1,0:T(8,128)(2,1)S(1)}, bf16[8,256,128]{2,1,0:T(8,128)(2,1)S(1)}, u32[]{:S(2)}, u32[]{:S(2)}) collective-permute-start(bf16[8,256,128]{2,1,0:T(8,128)(2,1)S(1)} %get-tuple-element.78.refs_10_), channel_id=1, source_target_pairs={{0,4},{2,6},{4,0},{6,2},{8,12},{10,14},{12,8},{14,10},{16,20},{18,... | collective-permute-start | bytes 1572872 | tf_op jit(solution)/shard_map/ppermute | solution.py:415
  59.9 1.4 %collective-permute-done.15.refs_11_ = bf16[3,256,128]{2,1,0:T(8,128)(2,1)S(1)} collective-permute-done((bf16[3,256,128]{2,1,0:T(8,128)(2,1)S(1)}, bf16[3,256,128]{2,1,0:T(8,128)(2,1)S(1)}, u32[]{:S(2)}, u32[]{:S(2)}) %collective-permute-start.15) | collective-permute-done | bytes 196640 | tf_op jit(solution)/shard_map/ppermute | solution.py:415
  61.4 5.2 %shard_map.83 = (f32[3,512,128]{2,1,0:T(8,128)S(1)}, f32[3,512,128]{2,1,0:T(8,128)S(1)}, f32[3,512,128]{2,1,0:T(8,128)S(1)}) custom-call(bf16[3,256,128]{2,1,0:T(8,128)(2,1)S(1)} %shard_map.78.fence_ref.refs_0_, bf16[9,256,128]{2,1,0:T(8,128)(2,1)S(1)} %collective-permute-done.3.in_ref.refs_1_, bf16[6,256,128]{2,1,0:T(8,128)(2,1)S(1)} %get-tuple-element.52.refs_2_, ...), custom_call_target="tpu_custom_call" | custom-call | flops 1024 | bytes 1024 | tf_op jit(solution)/shard_map/pallas_call | solution.py:303
  66.6 5.2 %shard_map.85 = (f32[3,512,128]{2,1,0:T(8,128)S(1)}, f32[3,512,128]{2,1,0:T(8,128)S(1)}, f32[3,512,128]{2,1,0:T(8,128)S(1)}) custom-call(bf16[3,256,128]{2,1,0:T(8,128)(2,1)S(1)} %get-tuple-element.67.refs_0_.refs_5_.refs_2_, bf16[3,256,128]{2,1,0:T(8,128)(2,1)S(1)} %shard_map.84.refs_1_.refs_6_.refs_3_, bf16[6,256,128]{2,1,0:T(8,128)(2,1)S(1)} %get-tuple-element.52.refs_2_, ...), custom_call_target="tpu_custom_call" | custom-call | flops 1024 | bytes 1024 | tf_op jit(solution)/shard_map/pallas_call | solution.py:303
  72.5 1.0 collective-permute-done.19.refs_13_
  73.5 4.2 %shard_map.86 = (bf16[256,128]{1,0:T(8,128)(2,1)S(1)}, bf16[256,128]{1,0:T(8,128)(2,1)S(1)}, bf16[256,128]{1,0:T(8,128)(2,1)S(1)}, bf16[256,128]{1,0:T(8,128)(2,1)S(1)}) custom-call(bf16[3,256,128]{2,1,0:T(8,128)(2,1)S(1)} %shard_map.78.fence_ref.refs_0_, bf16[9,256,128]{2,1,0:T(8,128)(2,1)S(1)} %collective-permute-done.3.in_ref.refs_1_, ...), custom_call_target="tpu_custom_call" | custom-call | flops 1024 | bytes 1024 | tf_op jit(solution)/shard_map/pallas_call | solution.py:303
  78.1 1.5 %collective-permute-done.21.refs_13_ = bf16[8,256,128]{2,1,0:T(8,128)(2,1)S(1)} collective-permute-done((bf16[8,256,128]{2,1,0:T(8,128)(2,1)S(1)}, bf16[8,256,128]{2,1,0:T(8,128)(2,1)S(1)}, u32[]{:S(2)}, u32[]{:S(2)}) %collective-permute-start.21) | collective-permute-done | bytes 524320 | tf_op jit(solution)/shard_map/ppermute | solution.py:415
  79.6 4.2 %shard_map.87 = (bf16[128,384]{1,0:T(8,128)(2,1)S(1)}, bf16[128,384]{1,0:T(8,128)(2,1)S(1)}, bf16[128,384]{1,0:T(8,128)(2,1)S(1)}, bf16[128,384]{1,0:T(8,128)(2,1)S(1)}) custom-call(bf16[3,256,128]{2,1,0:T(8,128)(2,1)S(1)} %shard_map.78.fence_ref.refs_0_, bf16[9,256,128]{2,1,0:T(8,128)(2,1)S(1)} %collective-permute-done.3.in_ref.refs_1_, ...), custom_call_target="tpu_custom_call" | custom-call | flops 1024 | bytes 1024 | tf_op jit(solution)/shard_map/pallas_call | solution.py:303
  83.8 0.8 collective-permute-start.25
  84.6 2.6 %collective-permute-start.26 = (bf16[128,384]{1,0:T(8,128)(2,1)S(1)}, bf16[128,384]{1,0:T(8,128)(2,1)S(1)}, u32[]{:S(2)}, u32[]{:S(2)}) collective-permute-start(bf16[128,384]{1,0:T(8,128)(2,1)S(1)} %get-tuple-element.91), channel_id=1, source_target_pairs={{0,16},{2,18},{4,20},{6,22},{8,24},{10,26},{12,28},{14,30},{16,0},... | collective-permute-start | bytes 294920 | tf_op jit(solution)/shard_map/ppermute | solution.py:415
  87.2 1.1 collective-permute-start.27
  88.3 4.4 %shard_map.88 = (bf16[128,384]{1,0:T(8,128)(2,1)S(1)}, bf16[128,384]{1,0:T(8,128)(2,1)S(1)}, bf16[128,384]{1,0:T(8,128)(2,1)S(1)}, bf16[128,384]{1,0:T(8,128)(2,1)S(1)}) custom-call(bf16[3,256,128]{2,1,0:T(8,128)(2,1)S(1)} %shard_map.78.fence_ref.refs_0_, bf16[9,256,128]{2,1,0:T(8,128)(2,1)S(1)} %collective-permute-done.3.in_ref.refs_1_, ...), custom_call_target="tpu_custom_call" | custom-call | flops 1024 | bytes 1024 | tf_op jit(solution)/shard_map/pallas_call | solution.py:303
  92.6 2.8 %collective-permute-start.24 = (bf16[128,384]{1,0:T(8,128)(2,1)S(1)}, bf16[128,384]{1,0:T(8,128)(2,1)S(1)}, u32[]{:S(2)}, u32[]{:S(2)}) collective-permute-start(bf16[128,384]{1,0:T(8,128)(2,1)S(1)} %get-tuple-element.89), channel_id=1, source_target_pairs={{0,24},{2,26},{4,28},{6,30},{8,16},{10,18},{12,20},{14,22},{16,8},... | collective-permute-start | bytes 294920 | tf_op jit(solution)/shard_map/ppermute | solution.py:415
  95.5 1.6 %collective-permute-start.23 = (bf16[128,384]{1,0:T(8,128)(2,1)S(1)}, bf16[128,384]{1,0:T(8,128)(2,1)S(1)}, u32[]{:S(2)}, u32[]{:S(2)}) collective-permute-start(bf16[128,384]{1,0:T(8,128)(2,1)S(1)} %get-tuple-element.88), channel_id=1, source_target_pairs={{0,16},{2,18},{4,20},{6,22},{8,24},{10,26},{12,28},{14,30},{16,0},... | collective-permute-start | bytes 294920 | tf_op jit(solution)/shard_map/ppermute | solution.py:415
  97.1 0.8 shard_map.89
  97.9 0.7 collective-permute-start.29
  98.6 0.8 shard_map.90.refs_0_
  99.4 0.9 collective-permute-done.24.refs_3_
  100.3 0.6 collective-permute-done.22.refs_1_
  100.9 4.1 %collective-permute-done.23.refs_2_ = bf16[128,384]{1,0:T(8,128)(2,1)S(1)} collective-permute-done((bf16[128,384]{1,0:T(8,128)(2,1)S(1)}, bf16[128,384]{1,0:T(8,128)(2,1)S(1)}, u32[]{:S(2)}, u32[]{:S(2)}) %collective-permute-start.23) | collective-permute-done | bytes 98336 | tf_op jit(solution)/shard_map/ppermute | solution.py:415
  105.0 0.8 shard_map.91
  105.8 1.4 %collective-permute-start.28 = (bf16[128,1536]{1,0:T(8,128)(2,1)S(1)}, bf16[128,1536]{1,0:T(8,128)(2,1)S(1)}, u32[]{:S(2)}, u32[]{:S(2)}) collective-permute-start(bf16[128,1536]{1,0:T(8,128)(2,1)S(1)} %shard_map.91), channel_id=1, source_target_pairs={{0,1},{1,0},{2,3},{3,2},{4,5},{5,4},{6,7},{7,6},{8,9},{9,8},{10,11... | collective-permute-start | bytes 1179656 | tf_op jit(solution)/shard_map/ppermute | solution.py:412
  107.2 0.8 shard_map.92.refs_0_
  108.2 8.4 %collective-permute-done.28.refs_1_ = bf16[128,1536]{1,0:T(8,128)(2,1)S(1)} collective-permute-done((bf16[128,1536]{1,0:T(8,128)(2,1)S(1)}, bf16[128,1536]{1,0:T(8,128)(2,1)S(1)}, u32[]{:S(2)}, u32[]{:S(2)}) %collective-permute-start.28) | collective-permute-done | bytes 393248 | tf_op jit(solution)/shard_map/ppermute | solution.py:412
  116.6 1.0 shard_map.94
  (42 shorter events, 2.6 us)
Async XLA Ops:
  0.0 20.9 %collective-permute-start = (bf16[256,1536]{1,0:T(8,128)(2,1)}, bf16[256,1536]{1,0:T(8,128)(2,1)S(1)}, u32[]{:S(2)}, u32[]{:S(2)}) collective-permute-start(bf16[256,1536]{1,0:T(8,128)(2,1)} %refs_0_.7), channel_id=1, source_target_pairs={{0,1},{1,0},{2,3},{3,2},{4,5},{5,4},{6,7},{7,6},{8,9},{9,8},{10,11... | collective-permute-start | bytes 2359304 | tf_op jit(solution)/shard_map/ppermute | solution.py:412
  4.0 23.5 %collective-permute-start.2 = (bf16[144,1536]{1,0:T(8,128)(2,1)S(1)}, bf16[144,1536]{1,0:T(8,128)(2,1)S(1)}, u32[]{:S(2)}, u32[]{:S(2)}) collective-permute-start(bf16[144,1536]{1,0:T(8,128)(2,1)S(1)} %slice.3), channel_id=1, source_target_pairs={{0,16},{2,18},{4,20},{6,22},{8,24},{10,26},{12,28},{14,30},{16,0},... | collective-permute-start | bytes 1327112 | tf_op jit(solution)/shard_map/ppermute | solution.py:415
  6.8 0.7 copy-start.1
  7.5 0.7 copy-start.2
  15.1 5.9 %copy-start = (bf16[256,1536]{1,0:T(8,128)(2,1)S(1)}, bf16[256,1536]{1,0:T(8,128)(2,1)}, u32[]{:S(2)}) copy-start(bf16[256,1536]{1,0:T(8,128)(2,1)} %refs_0_.7) | copy-start | bytes 2359300
  24.4 17.8 %collective-permute-start.3 = (bf16[9,256,128]{2,1,0:T(8,128)(2,1)S(1)}, bf16[9,256,128]{2,1,0:T(8,128)(2,1)S(1)}, u32[]{:S(2)}, u32[]{:S(2)}) collective-permute-start(bf16[9,256,128]{2,1,0:T(8,128)(2,1)S(1)} %get-tuple-element.53), channel_id=1, source_target_pairs={{0,8},{2,10},{4,12},{6,14},{8,0},{10,2},{12,4},{14,6},{16,24},{18,... | collective-permute-start | bytes 1769480 | tf_op jit(solution)/shard_map/ppermute | solution.py:415
  26.1 8.0 %collective-permute-start.1 = (bf16[6,256,128]{2,1,0:T(8,128)(2,1)S(1)}, bf16[6,256,128]{2,1,0:T(8,128)(2,1)S(1)}, u32[]{:S(2)}, u32[]{:S(2)}) collective-permute-start(bf16[6,256,128]{2,1,0:T(8,128)(2,1)S(1)} %get-tuple-element.52.refs_2_), channel_id=1, source_target_pairs={{0,2},{2,0},{4,6},{6,4},{8,10},{10,8},{12,14},{14,12},{16,18},{18,... | collective-permute-start | bytes 1179656 | tf_op jit(solution)/shard_map/ppermute | solution.py:415
  26.1 13.5 %collective-permute-start.5 = (bf16[6,256,128]{2,1,0:T(8,128)(2,1)S(1)}, bf16[6,256,128]{2,1,0:T(8,128)(2,1)S(1)}, u32[]{:S(2)}, u32[]{:S(2)}) collective-permute-start(bf16[6,256,128]{2,1,0:T(8,128)(2,1)S(1)} %get-tuple-element.52.refs_2_), channel_id=1, source_target_pairs={{0,4},{2,6},{4,0},{6,2},{8,12},{10,14},{12,8},{14,10},{16,20},{18,... | collective-permute-start | bytes 1179656 | tf_op jit(solution)/shard_map/ppermute | solution.py:415
  27.6 12.3 %collective-permute-start.4 = (bf16[144,1536]{1,0:T(8,128)(2,1)S(1)}, bf16[144,1536]{1,0:T(8,128)(2,1)S(1)}, u32[]{:S(2)}, u32[]{:S(2)}) collective-permute-start(bf16[144,1536]{1,0:T(8,128)(2,1)S(1)} %collective-permute-done.2.refs_0_), channel_id=1, source_target_pairs={{0,1},{1,0},{2,3},{3,2},{4,5},{5,4},{6,7},{7,6},{8,9},{9,8},{10,11... | collective-permute-start | bytes 1327112 | tf_op jit(solution)/shard_map/ppermute | solution.py:412
  31.5 16.9 %collective-permute-start.10 = (bf16[9,112,128]{2,1,0:T(8,128)(2,1)S(1)}, bf16[9,112,128]{2,1,0:T(8,128)(2,1)S(1)}, u32[]{:S(2)}, u32[]{:S(2)}) collective-permute-start(bf16[9,112,128]{2,1,0:T(8,128)(2,1)S(1)} %get-tuple-element.65), channel_id=1, source_target_pairs={{0,24},{2,26},{4,28},{6,30},{8,16},{10,18},{12,20},{14,22},{16,8},... | collective-permute-start | bytes 774152 | tf_op jit(solution)/shard_map/ppermute | solution.py:415
  34.1 23.0 %collective-permute-start.6 = (bf16[9,112,128]{2,1,0:T(8,128)(2,1)S(1)}, bf16[9,112,128]{2,1,0:T(8,128)(2,1)S(1)}, u32[]{:S(2)}, u32[]{:S(2)}) collective-permute-start(bf16[9,112,128]{2,1,0:T(8,128)(2,1)S(1)} %get-tuple-element.56), channel_id=1, source_target_pairs={{0,16},{2,18},{4,20},{6,22},{8,24},{10,26},{12,28},{14,30},{16,0},... | collective-permute-start | bytes 774152 | tf_op jit(solution)/shard_map/ppermute | solution.py:415
  39.6 20.2 %collective-permute-start.12 = (bf16[6,256,128]{2,1,0:T(8,128)(2,1)S(1)}, bf16[6,256,128]{2,1,0:T(8,128)(2,1)S(1)}, u32[]{:S(2)}, u32[]{:S(2)}) collective-permute-start(bf16[6,256,128]{2,1,0:T(8,128)(2,1)S(1)} %collective-permute-done.5.refs_3_), channel_id=1, source_target_pairs={{0,2},{2,0},{4,6},{6,4},{8,10},{10,8},{12,14},{14,12},{16,18},{18,... | collective-permute-start | bytes 1179656 | tf_op jit(solution)/shard_map/ppermute | solution.py:415
  42.4 14.7 %collective-permute-start.8 = (bf16[3,256,128]{2,1,0:T(8,128)(2,1)S(1)}, bf16[3,256,128]{2,1,0:T(8,128)(2,1)S(1)}, u32[]{:S(2)}, u32[]{:S(2)}) collective-permute-start(bf16[3,256,128]{2,1,0:T(8,128)(2,1)S(1)} %get-tuple-element.63), channel_id=1, source_target_pairs={{0,4},{2,6},{4,0},{6,2},{8,12},{10,14},{12,8},{14,10},{16,20},{18,... | collective-permute-start | bytes 589832 | tf_op jit(solution)/shard_map/ppermute | solution.py:415
  43.0 14.6 %collective-permute-start.7 = (bf16[6,144,128]{2,1,0:T(8,128)(2,1)S(1)}, bf16[6,144,128]{2,1,0:T(8,128)(2,1)S(1)}, u32[]{:S(2)}, u32[]{:S(2)}) collective-permute-start(bf16[6,144,128]{2,1,0:T(8,128)(2,1)S(1)} %get-tuple-element.59), channel_id=1, source_target_pairs={{0,8},{2,10},{4,12},{6,14},{8,0},{10,2},{12,4},{14,6},{16,24},{18,... | collective-permute-start | bytes 663560 | tf_op jit(solution)/shard_map/ppermute | solution.py:415
  48.4 9.2 %collective-permute-start.9 = (bf16[3,256,128]{2,1,0:T(8,128)(2,1)S(1)}, bf16[3,256,128]{2,1,0:T(8,128)(2,1)S(1)}, u32[]{:S(2)}, u32[]{:S(2)}) collective-permute-start(bf16[3,256,128]{2,1,0:T(8,128)(2,1)S(1)} %get-tuple-element.64), channel_id=1, source_target_pairs={{0,4},{2,6},{4,0},{6,2},{8,12},{10,14},{12,8},{14,10},{16,20},{18,... | collective-permute-start | bytes 589832 | tf_op jit(solution)/shard_map/ppermute | solution.py:415
  57.1 4.3 %collective-permute-start.13 = (bf16[6,256,128]{2,1,0:T(8,128)(2,1)S(1)}, bf16[6,256,128]{2,1,0:T(8,128)(2,1)S(1)}, u32[]{:S(2)}, u32[]{:S(2)}) collective-permute-start(bf16[6,256,128]{2,1,0:T(8,128)(2,1)S(1)} %get-tuple-element.69.refs_6_), channel_id=1, source_target_pairs={{0,2},{2,0},{4,6},{6,4},{8,10},{10,8},{12,14},{14,12},{16,18},{18,... | collective-permute-start | bytes 1179656 | tf_op jit(solution)/shard_map/ppermute | solution.py:415
  57.1 2.7 %collective-permute-start.14 = (bf16[3,256,128]{2,1,0:T(8,128)(2,1)S(1)}, bf16[3,256,128]{2,1,0:T(8,128)(2,1)S(1)}, u32[]{:S(2)}, u32[]{:S(2)}) collective-permute-start(bf16[3,256,128]{2,1,0:T(8,128)(2,1)S(1)} %collective-permute-done.8.refs_7_), channel_id=1, source_target_pairs={{0,2},{2,0},{4,6},{6,4},{8,10},{10,8},{12,14},{14,12},{16,18},{18,... | collective-permute-start | bytes 589832 | tf_op jit(solution)/shard_map/ppermute | solution.py:415
  57.7 14.2 %collective-permute-start.17 = (bf16[4,256,128]{2,1,0:T(8,128)(2,1)S(1)}, bf16[4,256,128]{2,1,0:T(8,128)(2,1)S(1)}, u32[]{:S(2)}, u32[]{:S(2)}) collective-permute-start(bf16[4,256,128]{2,1,0:T(8,128)(2,1)S(1)} %get-tuple-element.70.refs_13_.refs_10_), channel_id=1, source_target_pairs={{0,4},{2,6},{4,0},{6,2},{8,12},{10,14},{12,8},{14,10},{16,20},{18,... | collective-permute-start | bytes 786440 | tf_op jit(solution)/shard_map/ppermute | solution.py:415
  58.3 19.3 %collective-permute-start.16 = (bf16[8,256,128]{2,1,0:T(8,128)(2,1)S(1)}, bf16[8,256,128]{2,1,0:T(8,128)(2,1)S(1)}, u32[]{:S(2)}, u32[]{:S(2)}) collective-permute-start(bf16[8,256,128]{2,1,0:T(8,128)(2,1)S(1)} %get-tuple-element.78.refs_10_), channel_id=1, source_target_pairs={{0,4},{2,6},{4,0},{6,2},{8,12},{10,14},{12,8},{14,10},{16,20},{18,... | collective-permute-start | bytes 1572872 | tf_op jit(solution)/shard_map/ppermute | solution.py:415
  59.8 1.4 %collective-permute-start.15 = (bf16[3,256,128]{2,1,0:T(8,128)(2,1)S(1)}, bf16[3,256,128]{2,1,0:T(8,128)(2,1)S(1)}, u32[]{:S(2)}, u32[]{:S(2)}) collective-permute-start(bf16[3,256,128]{2,1,0:T(8,128)(2,1)S(1)} %collective-permute-done.9.refs_8_), channel_id=1, source_target_pairs={{0,2},{2,0},{4,6},{6,4},{8,10},{10,8},{12,14},{14,12},{16,18},{18,... | collective-permute-start | bytes 589832 | tf_op jit(solution)/shard_map/ppermute | solution.py:415
  59.8 6.8 %collective-permute-start.11 = (bf16[3,144,128]{2,1,0:T(8,128)(2,1)S(1)}, bf16[3,144,128]{2,1,0:T(8,128)(2,1)S(1)}, u32[]{:S(2)}, u32[]{:S(2)}) collective-permute-start(bf16[3,144,128]{2,1,0:T(8,128)(2,1)S(1)} %get-tuple-element.68), channel_id=1, source_target_pairs={{0,8},{2,10},{4,12},{6,14},{8,0},{10,2},{12,4},{14,6},{16,24},{18,... | collective-permute-start | bytes 331784 | tf_op jit(solution)/shard_map/ppermute | solution.py:415
  61.2 11.2 %collective-permute-start.18 = (bf16[4,256,128]{2,1,0:T(8,128)(2,1)S(1)}, bf16[4,256,128]{2,1,0:T(8,128)(2,1)S(1)}, u32[]{:S(2)}, u32[]{:S(2)}) collective-permute-start(bf16[4,256,128]{2,1,0:T(8,128)(2,1)S(1)} %get-tuple-element.70.refs_13_.refs_10_), channel_id=1, source_target_pairs={{0,2},{2,0},{4,6},{6,4},{8,10},{10,8},{12,14},{14,12},{16,18},{18,... | collective-permute-start | bytes 786440 | tf_op jit(solution)/shard_map/ppermute | solution.py:415
  71.9 1.6 %collective-permute-start.19 = (bf16[4,256,128]{2,1,0:T(8,128)(2,1)S(1)}, bf16[4,256,128]{2,1,0:T(8,128)(2,1)S(1)}, u32[]{:S(2)}, u32[]{:S(2)}) collective-permute-start(bf16[4,256,128]{2,1,0:T(8,128)(2,1)S(1)} %collective-permute-done.17.refs_11_), channel_id=1, source_target_pairs={{0,2},{2,0},{4,6},{6,4},{8,10},{10,8},{12,14},{14,12},{16,18},{18,... | collective-permute-start | bytes 786440 | tf_op jit(solution)/shard_map/ppermute | solution.py:415
  72.3 5.8 %collective-permute-start.20 = (bf16[8,256,128]{2,1,0:T(8,128)(2,1)S(1)}, bf16[8,256,128]{2,1,0:T(8,128)(2,1)S(1)}, u32[]{:S(2)}, u32[]{:S(2)}) collective-permute-start(bf16[8,256,128]{2,1,0:T(8,128)(2,1)S(1)} %get-tuple-element.78.refs_10_), channel_id=1, source_target_pairs={{0,2},{2,0},{4,6},{6,4},{8,10},{10,8},{12,14},{14,12},{16,18},{18,... | collective-permute-start | bytes 1572872 | tf_op jit(solution)/shard_map/ppermute | solution.py:415
  77.6 2.0 %collective-permute-start.21 = (bf16[8,256,128]{2,1,0:T(8,128)(2,1)S(1)}, bf16[8,256,128]{2,1,0:T(8,128)(2,1)S(1)}, u32[]{:S(2)}, u32[]{:S(2)}) collective-permute-start(bf16[8,256,128]{2,1,0:T(8,128)(2,1)S(1)} %collective-permute-done.16.refs_11_), channel_id=1, source_target_pairs={{0,2},{2,0},{4,6},{6,4},{8,10},{10,8},{12,14},{14,12},{16,18},{18,... | collective-permute-start | bytes 1572872 | tf_op jit(solution)/shard_map/ppermute | solution.py:415
  83.8 11.7 %collective-permute-start.25 = (bf16[128,384]{1,0:T(8,128)(2,1)S(1)}, bf16[128,384]{1,0:T(8,128)(2,1)S(1)}, u32[]{:S(2)}, u32[]{:S(2)}) collective-permute-start(bf16[128,384]{1,0:T(8,128)(2,1)S(1)} %get-tuple-element.90), channel_id=1, source_target_pairs={{0,8},{2,10},{4,12},{6,14},{8,0},{10,2},{12,4},{14,6},{16,24},{18,... | collective-permute-start | bytes 294920 | tf_op jit(solution)/shard_map/ppermute | solution.py:415
  84.6 12.5 %collective-permute-start.26 = (bf16[128,384]{1,0:T(8,128)(2,1)S(1)}, bf16[128,384]{1,0:T(8,128)(2,1)S(1)}, u32[]{:S(2)}, u32[]{:S(2)}) collective-permute-start(bf16[128,384]{1,0:T(8,128)(2,1)S(1)} %get-tuple-element.91), channel_id=1, source_target_pairs={{0,16},{2,18},{4,20},{6,22},{8,24},{10,26},{12,28},{14,30},{16,0},... | collective-permute-start | bytes 294920 | tf_op jit(solution)/shard_map/ppermute | solution.py:415
  87.2 9.9 %collective-permute-start.27 = (bf16[128,384]{1,0:T(8,128)(2,1)S(1)}, bf16[128,384]{1,0:T(8,128)(2,1)S(1)}, u32[]{:S(2)}, u32[]{:S(2)}) collective-permute-start(bf16[128,384]{1,0:T(8,128)(2,1)S(1)} %get-tuple-element.92), channel_id=1, source_target_pairs={{0,24},{2,26},{4,28},{6,30},{8,16},{10,18},{12,20},{14,22},{16,8},... | collective-permute-start | bytes 294920 | tf_op jit(solution)/shard_map/ppermute | solution.py:415
  92.6 7.6 %collective-permute-start.24 = (bf16[128,384]{1,0:T(8,128)(2,1)S(1)}, bf16[128,384]{1,0:T(8,128)(2,1)S(1)}, u32[]{:S(2)}, u32[]{:S(2)}) collective-permute-start(bf16[128,384]{1,0:T(8,128)(2,1)S(1)} %get-tuple-element.89), channel_id=1, source_target_pairs={{0,24},{2,26},{4,28},{6,30},{8,16},{10,18},{12,20},{14,22},{16,8},... | collective-permute-start | bytes 294920 | tf_op jit(solution)/shard_map/ppermute | solution.py:415
  95.5 5.5 %collective-permute-start.22 = (bf16[128,384]{1,0:T(8,128)(2,1)S(1)}, bf16[128,384]{1,0:T(8,128)(2,1)S(1)}, u32[]{:S(2)}, u32[]{:S(2)}) collective-permute-start(bf16[128,384]{1,0:T(8,128)(2,1)S(1)} %get-tuple-element.87), channel_id=1, source_target_pairs={{0,8},{2,10},{4,12},{6,14},{8,0},{10,2},{12,4},{14,6},{16,24},{18,... | collective-permute-start | bytes 294920 | tf_op jit(solution)/shard_map/ppermute | solution.py:415
  95.5 9.5 %collective-permute-start.23 = (bf16[128,384]{1,0:T(8,128)(2,1)S(1)}, bf16[128,384]{1,0:T(8,128)(2,1)S(1)}, u32[]{:S(2)}, u32[]{:S(2)}) collective-permute-start(bf16[128,384]{1,0:T(8,128)(2,1)S(1)} %get-tuple-element.88), channel_id=1, source_target_pairs={{0,16},{2,18},{4,20},{6,22},{8,24},{10,26},{12,28},{14,30},{16,0},... | collective-permute-start | bytes 294920 | tf_op jit(solution)/shard_map/ppermute | solution.py:415
  97.9 10.2 %collective-permute-start.29 = (bf16[128,1536]{1,0:T(8,128)(2,1)S(1)}, bf16[128,1536]{1,0:T(8,128)(2,1)S(1)}, u32[]{:S(2)}, u32[]{:S(2)}) collective-permute-start(bf16[128,1536]{1,0:T(8,128)(2,1)S(1)} %shard_map.89), channel_id=1, source_target_pairs={{0,1},{1,0},{2,3},{3,2},{4,5},{5,4},{6,7},{7,6},{8,9},{9,8},{10,11... | collective-permute-start | bytes 1179656 | tf_op jit(solution)/shard_map/ppermute | solution.py:412
  105.8 10.7 %collective-permute-start.28 = (bf16[128,1536]{1,0:T(8,128)(2,1)S(1)}, bf16[128,1536]{1,0:T(8,128)(2,1)S(1)}, u32[]{:S(2)}, u32[]{:S(2)}) collective-permute-start(bf16[128,1536]{1,0:T(8,128)(2,1)S(1)} %shard_map.91), channel_id=1, source_target_pairs={{0,1},{1,0},{2,3},{3,2},{4,5},{5,4},{6,7},{7,6},{8,9},{9,8},{10,11... | collective-permute-start | bytes 1179656 | tf_op jit(solution)/shard_map/ppermute | solution.py:412

commit v7 on v6

--- a/solution.py
+++ b/solution.py
@@ -42,13 +42,14 @@
     return [pl.BlockSpec(memory_space=pltpu.VMEM)] * count
 
 
-def fetch(where, weights, width, groups, fence):
+def fetch(where, weights, width, groups, fence, beside=None):
     depth = weights[0].shape[0]
     half = depth // 2
     kinds = len(weights)
+    extra = list(beside or ())
 
     def body(s, *refs):
-        out, sems = refs[kinds + 1], refs[kinds + 2]
+        out, sems = refs[kinds + 1 + len(extra)], refs[-1]
         copies = []
         for g in range(2):
             columns = pl.ds(pl.multiple_of((s[1] ^ groups[g]) * width, width), width)
@@ -64,53 +65,71 @@
                     )
         for copy in copies:
             copy.start()
+        if extra:
+            tokens_ref, held_ref = refs[kinds + 1 : kinds + 3]
+            for i in range(2 * kinds):
+                refs[-2][i] = jnp.dot(
+                    tokens_ref[...], held_ref[i, :half], preferred_element_type=F32
+                )
         for copy in copies:
             copy.wait()
 
+    out_shape = [pltpu.VMEM((2 * kinds, depth, width), BF16)]
+    if extra:
+        out_shape.append(pltpu.VMEM((2 * kinds, extra[0].shape[0], width), F32))
     return pl.pallas_call(
         body,
         grid_spec=pltpu.PrefetchScalarGridSpec(
             num_scalar_prefetch=1,
             grid=(),
-            in_specs=[pl.BlockSpec(memory_space=pl.ANY)] * (kinds + 1),
-            out_specs=pl.BlockSpec(memory_space=pltpu.VMEM),
+            in_specs=[pl.BlockSpec(memory_space=pl.ANY)] * (kinds + 1) + whole(len(extra)),
+            out_specs=whole(len(out_shape)),
             scratch_shapes=[pltpu.SemaphoreType.DMA((4 * kinds,))],
         ),
-        out_shape=pltpu.VMEM((2 * kinds, depth, width), BF16),
+        out_shape=out_shape,
         compiler_params=params(4),
         cost_estimate=LIGHT,
-    )(where, *weights, fence)
-
-
-def project(own, other, held, outputs, start=0):
+    )(where, *weights, fence, *extra)
+
+
+def project(own, other, held, outputs, start=0, partial=None):
     rows = own.shape[0] - start
     kinds = held.shape[0] // 2
     flat = [block for blocks in outputs for block in blocks]
 
     def body(*refs):
         held_ref, outs = refs[2], refs[3:]
-        tokens = jnp.concatenate([refs[0][start:], refs[1][start:]], axis=1)
+        tokens, low = jnp.concatenate([refs[0][start:], refs[1][start:]], axis=1), 0
+        if partial is not None:
+            tokens, low, outs = refs[1][start:], own.shape[1], refs[4:]
         at = [(o, i) for o, blocks in enumerate(outputs) for i in range(len(blocks))]
         for first in range(0, len(flat), 2):
             pair = flat[first : first + 2]
             weight = [
-                held_ref[g * kinds + k, :, h * HEAD_DIM : (h + 1) * HEAD_DIM] for g, k, h in pair
+                held_ref[g * kinds + k, low:, h * HEAD_DIM : (h + 1) * HEAD_DIM] for g, k, h in pair
             ]
             total = jnp.dot(
                 tokens, jnp.concatenate(weight, axis=1), preferred_element_type=F32
-            ).astype(BF16)
+            )
+            if partial is not None:
+                done = [
+                    refs[3][g * kinds + k, :, h * HEAD_DIM : (h + 1) * HEAD_DIM] for g, k, h in pair
+                ]
+                total = total + jnp.concatenate(done, axis=1)
+            total = total.astype(BF16)
             for i in range(len(pair)):
                 o, place_in = at[first + i]
                 outs[o][place_in] = total[:, i * HEAD_DIM : (i + 1) * HEAD_DIM]
 
-    return pl.pallas_call(
-        body,
-        in_specs=whole(3),
+    more = [] if partial is None else [partial]
+    return pl.pallas_call(
+        body,
+        in_specs=whole(3 + len(more)),
         out_specs=whole(len(outputs)),
         out_shape=[jax.ShapeDtypeStruct((len(b), rows, HEAD_DIM), BF16) for b in outputs],
         compiler_params=params(8),
         cost_estimate=LIGHT,
-    )(own, other, held)
+    )(own, other, held, *more)
 
 
 def take(array, ranges):
@@ -422,13 +441,16 @@
 
     other = over_y(tokens)
     far = over(tokens[:cut], 2, 0, 0)
-    bias = mask_rows(where, block_order, block_mask, rows)
-    held = fetch(where, weights, span, (0, 1), bias)
-    held_far = fetch(where, weights, span, (2, 3), held)
+    (held,) = fetch(where, weights, span, (0, 1), where)
+    held_far, partial = fetch(where, weights, span, (2, 3), where, (tokens, held))
 
     other = after(other, held_far)
     own_kv, sent = project(
-        tokens, other, held, [pairs(0, heads), singles(1) + pairs(1, heads)]
+        tokens,
+        other,
+        held,
+        [pairs(0, heads), singles(1) + pairs(1, heads)],
+        partial=partial,
     )
     came = over(sent, 1, 0, 0)
     own_across = over(own_kv, 0, 1, 0)
@@ -442,10 +464,13 @@
         [singles(0) + pairs(0, heads), singles(1) + pairs(1, heads)],
         cut,
     )
-    (own_q,) = project(after(tokens, own_core, low2), other, held, [singles(0)])
+    (own_q,) = project(
+        after(tokens, own_core, low2), other, held, [singles(0)], partial=partial
+    )
     low2 = over(low2, 2, 0, 0)
     low3 = over(low3, 3, 0, 0)
-    out_held = fetch_out(where, w_out, own_q)
+    bias = mask_rows(after(where, own_q), block_order, block_mask, rows)
+    out_held = fetch_out(where, w_out, bias)
     own_across = after(own_across, out_held)
     own_across_core = over(own_across, 0, 0, 1)
 
@@ -463,11 +488,12 @@
     across_k = over(came_k, 0, 1, 0)
     across_v = over(came_v, 0, 1, 0)
     came_core = over(came_kv, 0, 0, 1)
+    far_came = after(far_came, low2, low3)
+    across_k, across_v = after(across_k, far_came), after(across_v, far_came)
     across_core_k = over(across_k, 0, 0, 1)
     across_core_v = over(across_v, 0, 0, 1)
 
     first, rest = (0,), tuple(heads)[1:]
-    far_came = after(far_came, across_k, across_v, low2, low3)
     sides = [[[far_kept], [low2]], [[far_came], [low3]]]
 
     def picks(chunk):

time: 118 us -> 116 us (0.983)
  waiting for transfers between devices: 29.2 us -> 26.3 us
  starting transfers between devices: 31.5 us -> 33.4 us
  local copies, waits for them, and re-layouts: 2.45 us -> 1.09 us
    ppermute x26, waiting for transfers between devices: 20.6 us -> 17.4 us  [over(): return lax.ppermute(a, 'ctx', hop(dz, dx, dc))]
    ppermute x26, starting transfers between devices: 25 us -> 28 us  [over(): return lax.ppermute(a, 'ctx', hop(dz, dx, dc))]
    pallas_call x2, Pallas kernels: 11.7 us -> 14.2 us  [fetch(): pl.pallas_call(body, grid_spec=pltpu.PrefetchScalarGridSpec(num_scalar_pr...]
    pallas_call x4, Pallas kernels: 9.28 us -> 7.08 us  [project(): pl.pallas_call(body, in_specs=whole(3 + len(more)), out_specs=whole(len(o...]
    unnamed x6, local copies, waits for them, and re-layouts: 1.38 us -> 0.02 us
    ppermute x4, starting transfers between devices: 6.57 us -> 5.35 us  [over_y(): return lax.ppermute(a, 'head', [(0, 1), (1, 0)])]
  transfers between devices with their start and end apart: 30 -> 30, of which waited for: 10 -> 12; matrix products, arithmetic and copies ran while one was open for 1% -> 1% of each run, Pallas kernels for 42% -> 43%
where the time goes in v7:
time: 116 us
  Pallas kernels  54.4 us (47%)
  starting transfers between devices  33.4 us (29%)
  waiting for transfers between devices  26.3 us (23%)
    ppermute x26, starting transfers between devices, over(): return lax.ppermute(a, 'ctx', hop(dz, dx, dc))  28 us
    pallas_call x5, Pallas kernels, attend(): pl.pallas_call(body, grid=(count,), in_specs=whole(total_arrays) + [pl.Bl...  23.1 us
    ppermute x26, waiting for transfers between devices, over(): return lax.ppermute(a, 'ctx', hop(dz, dx, dc))  17.4 us
    pallas_call x2, Pallas kernels, fetch(): pl.pallas_call(body, grid_spec=pltpu.PrefetchScalarGridSpec(num_scalar_pr...  14.2 us
    ppermute x4, waiting for transfers between devices, over_y(): return lax.ppermute(a, 'head', [(0, 1), (1, 0)])  9 us
    pallas_call x4, Pallas kernels, project(): pl.pallas_call(body, in_specs=whole(3 + len(more)), out_specs=whole(len(o...  7.08 us
    ppermute x4, starting transfers between devices, over_y(): return lax.ppermute(a, 'head', [(0, 1), (1, 0)])  5.35 us
    pallas_call x1, Pallas kernels, fetch_out(): pl.pallas_call(body, grid_spec=pltpu.PrefetchScalarGridSpec(num_scalar_pr...  4.33 us
  transfers between devices with their start and end apart: 30, of which 12 were waited for; matrix products, arithmetic and copies ran while one was open for 1% of the time, Pallas kernels for 43%

profile of v7, /device:TPU:0, one launch (start us, length us, event | category | flops | bytes accessed | tf_op | source)
XLA Modules:
  0.0 115.6 jit_solution(2561843755730750636)
XLA Ops:
  0.0 3.0 %collective-permute-start = (bf16[256,1536]{1,0:T(8,128)(2,1)}, bf16[256,1536]{1,0:T(8,128)(2,1)S(1)}, u32[]{:S(2)}, u32[]{:S(2)}) collective-permute-start(bf16[256,1536]{1,0:T(8,128)(2,1)} %refs_0_.7), channel_id=1, source_target_pairs={{0,1},{1,0},{2,3},{3,2},{4,5},{5,4},{6,7},{7,6},{8,9},{9,8},{10,11... | collective-permute-start | bytes 2359304 | tf_op jit(solution)/shard_map/ppermute | solution.py:431
  3.0 1.1 slice.3
  4.0 2.7 %collective-permute-start.2 = (bf16[144,1536]{1,0:T(8,128)(2,1)S(1)}, bf16[144,1536]{1,0:T(8,128)(2,1)S(1)}, u32[]{:S(2)}, u32[]{:S(2)}) collective-permute-start(bf16[144,1536]{1,0:T(8,128)(2,1)S(1)} %slice.3), channel_id=1, source_target_pairs={{0,16},{2,18},{4,20},{6,22},{8,24},{10,26},{12,28},{14,30},{16,0},... | collective-permute-start | bytes 1327112 | tf_op jit(solution)/shard_map/ppermute | solution.py:434
  6.8 5.8 %shard_map.73.refs_5_.refs_2_ = bf16[6,3072,384]{2,1,0:T(8,128)(2,1)S(1)} custom-call(s32[4]{0:T(128)S(1)} %pad_add_fusion.s.refs_3_, bf16[3072,1536]{1,0:T(8,128)(2,1)} %refs_0_.4, bf16[3072,1536]{1,0:T(8,128)(2,1)} %refs_1_.3, bf16[3072,1536]{1,0:T(8,128)(2,1)} %refs_2_.3, s32[4]{0:T(128)S(1)} %pad_add_fusion.s.refs_3_), custom_call_target="tpu_custom_call" | custom-call | flops 1024 | bytes 1024 | tf_op jit(solution)/shard_map/pallas_call | solution.py:80
  12.6 8.3 %shard_map.74 = (bf16[6,3072,384]{2,1,0:T(8,128)(2,1)S(1)}, f32[6,256,384]{2,1,0:T(8,128)S(1)}) custom-call(s32[4]{0:T(128)S(1)} %pad_add_fusion.s.refs_3_, bf16[3072,1536]{1,0:T(8,128)(2,1)} %refs_0_.4, bf16[3072,1536]{1,0:T(8,128)(2,1)} %refs_1_.3, bf16[3072,1536]{1,0:T(8,128)(2,1)} %refs_2_.3, s32[4]{0:T(128)S(1)} %pad_add_fusion.s.refs_3_, ...), custom_call_target="tpu_custom_call" | custom-call | flops 1024 | bytes 1024 | tf_op jit(solution)/shard_map/pallas_call | solution.py:80
  21.0 1.9 %shard_map.75 = (bf16[6,256,128]{2,1,0:T(8,128)(2,1)S(1)}, bf16[9,256,128]{2,1,0:T(8,128)(2,1)S(1)}) custom-call(bf16[256,1536]{1,0:T(8,128)(2,1)S(1)} %copy-done, bf16[256,1536]{1,0:T(8,128)(2,1)S(1)} %collective-permute-done.refs_1_, bf16[6,3072,384]{2,1,0:T(8,128)(2,1)S(1)} %shard_map.73.refs_5_.refs_2_, f32[6,256,384]{2,1,0:T(8,128)S(1)} %get-tuple-element.58.refs_3_), custom_call_target="tpu_custom_call" | custom-call | flops 1024 | bytes 1024 | tf_op jit(solution)/shard_map/pallas_call | solution.py:125
  22.9 1.6 %collective-permute-start.3 = (bf16[9,256,128]{2,1,0:T(8,128)(2,1)S(1)}, bf16[9,256,128]{2,1,0:T(8,128)(2,1)S(1)}, u32[]{:S(2)}, u32[]{:S(2)}) collective-permute-start(bf16[9,256,128]{2,1,0:T(8,128)(2,1)S(1)} %get-tuple-element.60), channel_id=1, source_target_pairs={{0,8},{2,10},{4,12},{6,14},{8,0},{10,2},{12,4},{14,6},{16,24},{18,... | collective-permute-start | bytes 1769480 | tf_op jit(solution)/shard_map/ppermute | solution.py:434
  24.5 1.5 %collective-permute-start.5 = (bf16[6,256,128]{2,1,0:T(8,128)(2,1)S(1)}, bf16[6,256,128]{2,1,0:T(8,128)(2,1)S(1)}, u32[]{:S(2)}, u32[]{:S(2)}) collective-permute-start(bf16[6,256,128]{2,1,0:T(8,128)(2,1)S(1)} %get-tuple-element.59.refs_2_), channel_id=1, source_target_pairs={{0,4},{2,6},{4,0},{6,2},{8,12},{10,14},{12,8},{14,10},{16,20},{18,... | collective-permute-start | bytes 1179656 | tf_op jit(solution)/shard_map/ppermute | solution.py:434
  26.2 1.2 %collective-permute-start.4 = (bf16[144,1536]{1,0:T(8,128)(2,1)S(1)}, bf16[144,1536]{1,0:T(8,128)(2,1)S(1)}, u32[]{:S(2)}, u32[]{:S(2)}) collective-permute-start(bf16[144,1536]{1,0:T(8,128)(2,1)S(1)} %collective-permute-done.2.refs_0_), channel_id=1, source_target_pairs={{0,1},{1,0},{2,3},{3,2},{4,5},{5,4},{6,7},{7,6},{8,9},{9,8},{10,11... | collective-permute-start | bytes 1327112 | tf_op jit(solution)/shard_map/ppermute | solution.py:431
  27.5 2.3 %shard_map.76 = (bf16[9,112,128]{2,1,0:T(8,128)(2,1)S(1)}, bf16[9,112,128]{2,1,0:T(8,128)(2,1)S(1)}) custom-call(bf16[256,1536]{1,0:T(8,128)(2,1)S(1)} %copy-done, bf16[256,1536]{1,0:T(8,128)(2,1)S(1)} %collective-permute-done.refs_1_, bf16[6,3072,384]{2,1,0:T(8,128)(2,1)S(1)} %get-tuple-element.56.refs_2_), custom_call_target="tpu_custom_call" | custom-call | flops 1024 | bytes 1024 | tf_op jit(solution)/shard_map/pallas_call | solution.py:125
  29.8 2.8 %collective-permute-start.8 = (bf16[9,112,128]{2,1,0:T(8,128)(2,1)S(1)}, bf16[9,112,128]{2,1,0:T(8,128)(2,1)S(1)}, u32[]{:S(2)}, u32[]{:S(2)}) collective-permute-start(bf16[9,112,128]{2,1,0:T(8,128)(2,1)S(1)} %get-tuple-element.71), channel_id=1, source_target_pairs={{0,24},{2,26},{4,28},{6,30},{8,16},{10,18},{12,20},{14,22},{16,8},... | collective-permute-start | bytes 774152 | tf_op jit(solution)/shard_map/ppermute | solution.py:434
  32.6 0.6 shard_map.77.refs_0_
  33.2 1.1 shard_map.78.fence_ref.refs_12_.refs_14_.refs_18_
  34.2 4.3 %shard_map.79.refs_4_ = bf16[1536,3072]{1,0:T(8,128)(2,1)S(1)} custom-call(s32[4]{0:T(128)S(1)} %pad_add_fusion.s.refs_3_, bf16[1536,3072]{1,0:T(8,128)(2,1)} %w_ref.1, f32[8,4096]{1,0:T(8,128)S(1)} %shard_map.78.fence_ref.refs_12_.refs_14_.refs_18_), custom_call_target="tpu_custom_call" | custom-call | flops 1024 | bytes 1024 | tf_op jit(solution)/shard_map/pallas_call | solution.py:357
  38.7 2.4 %shard_map.80 = (bf16[3,144,128]{2,1,0:T(8,128)(2,1)S(1)}, bf16[6,144,128]{2,1,0:T(8,128)(2,1)S(1)}, bf16[9,144,128]{2,1,0:T(8,128)(2,1)S(1)}) custom-call(bf16[144,1536]{1,0:T(8,128)(2,1)S(1)} %collective-permute-done.2.refs_0_, bf16[144,1536]{1,0:T(8,128)(2,1)S(1)} %collective-permute-done.4.refs_1_, bf16[6,3072,384]{2,1,0:T(8,128)(2,1)S(1)} %shard_map.73.refs_5_.refs_2_), custom_call_target="tpu_custom_call" | custom-call | flops 1024 | bytes 1024 | tf_op jit(solution)/shard_map/pallas_call | solution.py:125
  41.0 1.7 %collective-permute-start.7 = (bf16[6,144,128]{2,1,0:T(8,128)(2,1)S(1)}, bf16[6,144,128]{2,1,0:T(8,128)(2,1)S(1)}, u32[]{:S(2)}, u32[]{:S(2)}) collective-permute-start(bf16[6,144,128]{2,1,0:T(8,128)(2,1)S(1)} %get-tuple-element.67), channel_id=1, source_target_pairs={{0,8},{2,10},{4,12},{6,14},{8,0},{10,2},{12,4},{14,6},{16,24},{18,... | collective-permute-start | bytes 663560 | tf_op jit(solution)/shard_map/ppermute | solution.py:434
  43.0 3.4 %collective-permute-start.11 = (bf16[3,256,128]{2,1,0:T(8,128)(2,1)S(1)}, bf16[3,256,128]{2,1,0:T(8,128)(2,1)S(1)}, u32[]{:S(2)}, u32[]{:S(2)}) collective-permute-start(bf16[3,256,128]{2,1,0:T(8,128)(2,1)S(1)} %get-tuple-element.76), channel_id=1, source_target_pairs={{0,4},{2,6},{4,0},{6,2},{8,12},{10,14},{12,8},{14,10},{16,20},{18,... | collective-permute-start | bytes 589832 | tf_op jit(solution)/shard_map/ppermute | solution.py:434
  46.8 1.5 %collective-permute-start.12 = (bf16[3,256,128]{2,1,0:T(8,128)(2,1)S(1)}, bf16[3,256,128]{2,1,0:T(8,128)(2,1)S(1)}, u32[]{:S(2)}, u32[]{:S(2)}) collective-permute-start(bf16[3,256,128]{2,1,0:T(8,128)(2,1)S(1)} %get-tuple-element.78), channel_id=1, source_target_pairs={{0,4},{2,6},{4,0},{6,2},{8,12},{10,14},{12,8},{14,10},{16,20},{18,... | collective-permute-start | bytes 589832 | tf_op jit(solution)/shard_map/ppermute | solution.py:434
  48.3 7.1 %collective-permute-done.6.refs_1_ = bf16[9,112,128]{2,1,0:T(8,128)(2,1)S(1)} collective-permute-done((bf16[9,112,128]{2,1,0:T(8,128)(2,1)S(1)}, bf16[9,112,128]{2,1,0:T(8,128)(2,1)S(1)}, u32[]{:S(2)}, u32[]{:S(2)}) %collective-permute-start.6) | collective-permute-done | bytes 258080 | tf_op jit(solution)/shard_map/ppermute | solution.py:434
  55.4 0.5 collective-permute-start.14
  55.9 0.7 collective-permute-start.17
  56.6 1.4 %collective-permute-start.16 = (bf16[8,256,128]{2,1,0:T(8,128)(2,1)S(1)}, bf16[8,256,128]{2,1,0:T(8,128)(2,1)S(1)}, u32[]{:S(2)}, u32[]{:S(2)}) collective-permute-start(bf16[8,256,128]{2,1,0:T(8,128)(2,1)S(1)} %get-tuple-element.88.refs_10_), channel_id=1, source_target_pairs={{0,4},{2,6},{4,0},{6,2},{8,12},{10,14},{12,8},{14,10},{16,20},{18,... | collective-permute-start | bytes 1572872 | tf_op jit(solution)/shard_map/ppermute | solution.py:434
  58.1 1.4 %collective-permute-done.15.refs_11_ = bf16[3,256,128]{2,1,0:T(8,128)(2,1)S(1)} collective-permute-done((bf16[3,256,128]{2,1,0:T(8,128)(2,1)S(1)}, bf16[3,256,128]{2,1,0:T(8,128)(2,1)S(1)}, u32[]{:S(2)}, u32[]{:S(2)}) %collective-permute-start.15) | collective-permute-done | bytes 196640 | tf_op jit(solution)/shard_map/ppermute | solution.py:434
  59.6 5.2 %shard_map.83 = (f32[3,512,128]{2,1,0:T(8,128)S(1)}, f32[3,512,128]{2,1,0:T(8,128)S(1)}, f32[3,512,128]{2,1,0:T(8,128)S(1)}) custom-call(bf16[3,256,128]{2,1,0:T(8,128)(2,1)S(1)} %shard_map.77.refs_0_, bf16[9,256,128]{2,1,0:T(8,128)(2,1)S(1)} %collective-permute-done.3.in_ref.refs_1_, bf16[6,256,128]{2,1,0:T(8,128)(2,1)S(1)} %get-tuple-element.59.refs_2_, ...), custom_call_target="tpu_custom_call" | custom-call | flops 1024 | bytes 1024 | tf_op jit(solution)/shard_map/pallas_call | solution.py:322
  64.8 5.2 %shard_map.85 = (f32[3,512,128]{2,1,0:T(8,128)S(1)}, f32[3,512,128]{2,1,0:T(8,128)S(1)}, f32[3,512,128]{2,1,0:T(8,128)S(1)}) custom-call(bf16[3,256,128]{2,1,0:T(8,128)(2,1)S(1)} %get-tuple-element.73.refs_0_.refs_5_.refs_2_, bf16[3,256,128]{2,1,0:T(8,128)(2,1)S(1)} %shard_map.84.refs_1_.refs_6_.refs_3_, bf16[6,256,128]{2,1,0:T(8,128)(2,1)S(1)} %get-tuple-element.59.refs_2_, ...), custom_call_target="tpu_custom_call" | custom-call | flops 1024 | bytes 1024 | tf_op jit(solution)/shard_map/pallas_call | solution.py:322
  70.7 1.0 collective-permute-done.19.refs_13_
  71.7 4.1 %shard_map.86 = (bf16[256,128]{1,0:T(8,128)(2,1)S(1)}, bf16[256,128]{1,0:T(8,128)(2,1)S(1)}, bf16[256,128]{1,0:T(8,128)(2,1)S(1)}, bf16[256,128]{1,0:T(8,128)(2,1)S(1)}) custom-call(bf16[3,256,128]{2,1,0:T(8,128)(2,1)S(1)} %shard_map.77.refs_0_, bf16[9,256,128]{2,1,0:T(8,128)(2,1)S(1)} %collective-permute-done.3.in_ref.refs_1_, ...), custom_call_target="tpu_custom_call" | custom-call | flops 1024 | bytes 1024 | tf_op jit(solution)/shard_map/pallas_call | solution.py:322
  75.8 0.4 collective-permute-start.21
  76.3 1.5 %collective-permute-done.21.refs_13_ = bf16[8,256,128]{2,1,0:T(8,128)(2,1)S(1)} collective-permute-done((bf16[8,256,128]{2,1,0:T(8,128)(2,1)S(1)}, bf16[8,256,128]{2,1,0:T(8,128)(2,1)S(1)}, u32[]{:S(2)}, u32[]{:S(2)}) %collective-permute-start.21) | collective-permute-done | bytes 524320 | tf_op jit(solution)/shard_map/ppermute | solution.py:434
  77.8 4.2 %shard_map.87 = (bf16[128,384]{1,0:T(8,128)(2,1)S(1)}, bf16[128,384]{1,0:T(8,128)(2,1)S(1)}, bf16[128,384]{1,0:T(8,128)(2,1)S(1)}, bf16[128,384]{1,0:T(8,128)(2,1)S(1)}) custom-call(bf16[3,256,128]{2,1,0:T(8,128)(2,1)S(1)} %shard_map.77.refs_0_, bf16[9,256,128]{2,1,0:T(8,128)(2,1)S(1)} %collective-permute-done.3.in_ref.refs_1_, ...), custom_call_target="tpu_custom_call" | custom-call | flops 1024 | bytes 1024 | tf_op jit(solution)/shard_map/pallas_call | solution.py:322
  82.0 0.8 collective-permute-start.25
  82.8 2.6 %collective-permute-start.26 = (bf16[128,384]{1,0:T(8,128)(2,1)S(1)}, bf16[128,384]{1,0:T(8,128)(2,1)S(1)}, u32[]{:S(2)}, u32[]{:S(2)}) collective-permute-start(bf16[128,384]{1,0:T(8,128)(2,1)S(1)} %get-tuple-element.101), channel_id=1, source_target_pairs={{0,16},{2,18},{4,20},{6,22},{8,24},{10,26},{12,28},{14,30},{16,0},... | collective-permute-start | bytes 294920 | tf_op jit(solution)/shard_map/ppermute | solution.py:434
  85.3 1.1 collective-permute-start.27
  86.5 4.4 %shard_map.88 = (bf16[128,384]{1,0:T(8,128)(2,1)S(1)}, bf16[128,384]{1,0:T(8,128)(2,1)S(1)}, bf16[128,384]{1,0:T(8,128)(2,1)S(1)}, bf16[128,384]{1,0:T(8,128)(2,1)S(1)}) custom-call(bf16[3,256,128]{2,1,0:T(8,128)(2,1)S(1)} %shard_map.77.refs_0_, bf16[9,256,128]{2,1,0:T(8,128)(2,1)S(1)} %collective-permute-done.3.in_ref.refs_1_, ...), custom_call_target="tpu_custom_call" | custom-call | flops 1024 | bytes 1024 | tf_op jit(solution)/shard_map/pallas_call | solution.py:322
  90.8 2.8 %collective-permute-start.24 = (bf16[128,384]{1,0:T(8,128)(2,1)S(1)}, bf16[128,384]{1,0:T(8,128)(2,1)S(1)}, u32[]{:S(2)}, u32[]{:S(2)}) collective-permute-start(bf16[128,384]{1,0:T(8,128)(2,1)S(1)} %get-tuple-element.99), channel_id=1, source_target_pairs={{0,24},{2,26},{4,28},{6,30},{8,16},{10,18},{12,20},{14,22},{16,8},... | collective-permute-start | bytes 294920 | tf_op jit(solution)/shard_map/ppermute | solution.py:434
  93.6 1.7 %collective-permute-start.23 = (bf16[128,384]{1,0:T(8,128)(2,1)S(1)}, bf16[128,384]{1,0:T(8,128)(2,1)S(1)}, u32[]{:S(2)}, u32[]{:S(2)}) collective-permute-start(bf16[128,384]{1,0:T(8,128)(2,1)S(1)} %get-tuple-element.98), channel_id=1, source_target_pairs={{0,16},{2,18},{4,20},{6,22},{8,24},{10,26},{12,28},{14,30},{16,0},... | collective-permute-start | bytes 294920 | tf_op jit(solution)/shard_map/ppermute | solution.py:434
  95.3 0.9 shard_map.89
  96.2 0.6 collective-permute-start.29
  96.7 0.8 shard_map.90.refs_0_
  97.6 0.9 collective-permute-done.24.refs_3_
  98.5 0.7 collective-permute-done.22.refs_1_
  99.2 4.0 %collective-permute-done.23.refs_2_ = bf16[128,384]{1,0:T(8,128)(2,1)S(1)} collective-permute-done((bf16[128,384]{1,0:T(8,128)(2,1)S(1)}, bf16[128,384]{1,0:T(8,128)(2,1)S(1)}, u32[]{:S(2)}, u32[]{:S(2)}) %collective-permute-start.23) | collective-permute-done | bytes 98336 | tf_op jit(solution)/shard_map/ppermute | solution.py:434
  103.2 0.8 shard_map.91
  104.0 0.6 collective-permute-start.28
  104.6 0.8 shard_map.92.refs_0_
  105.5 0.5 collective-permute-done.29.refs_1_
  106.0 8.5 %collective-permute-done.28.refs_1_ = bf16[128,1536]{1,0:T(8,128)(2,1)S(1)} collective-permute-done((bf16[128,1536]{1,0:T(8,128)(2,1)S(1)}, bf16[128,1536]{1,0:T(8,128)(2,1)S(1)}, u32[]{:S(2)}, u32[]{:S(2)}) %collective-permute-start.28) | collective-permute-done | bytes 393248 | tf_op jit(solution)/shard_map/ppermute | solution.py:431
  114.6 1.0 shard_map.94
  (42 shorter events, 2.0 us)
Async XLA Ops:
  0.0 21.0 %collective-permute-start = (bf16[256,1536]{1,0:T(8,128)(2,1)}, bf16[256,1536]{1,0:T(8,128)(2,1)S(1)}, u32[]{:S(2)}, u32[]{:S(2)}) collective-permute-start(bf16[256,1536]{1,0:T(8,128)(2,1)} %refs_0_.7), channel_id=1, source_target_pairs={{0,1},{1,0},{2,3},{3,2},{4,5},{5,4},{6,7},{7,6},{8,9},{9,8},{10,11... | collective-permute-start | bytes 2359304 | tf_op jit(solution)/shard_map/ppermute | solution.py:431
  4.0 22.2 %collective-permute-start.2 = (bf16[144,1536]{1,0:T(8,128)(2,1)S(1)}, bf16[144,1536]{1,0:T(8,128)(2,1)S(1)}, u32[]{:S(2)}, u32[]{:S(2)}) collective-permute-start(bf16[144,1536]{1,0:T(8,128)(2,1)S(1)} %slice.3), channel_id=1, source_target_pairs={{0,16},{2,18},{4,20},{6,22},{8,24},{10,26},{12,28},{14,30},{16,0},... | collective-permute-start | bytes 1327112 | tf_op jit(solution)/shard_map/ppermute | solution.py:434
  6.8 5.9 %copy-start = (bf16[256,1536]{1,0:T(8,128)(2,1)S(1)}, bf16[256,1536]{1,0:T(8,128)(2,1)}, u32[]{:S(2)}) copy-start(bf16[256,1536]{1,0:T(8,128)(2,1)} %refs_0_.7) | copy-start | bytes 2359300
  22.9 20.1 %collective-permute-start.3 = (bf16[9,256,128]{2,1,0:T(8,128)(2,1)S(1)}, bf16[9,256,128]{2,1,0:T(8,128)(2,1)S(1)}, u32[]{:S(2)}, u32[]{:S(2)}) collective-permute-start(bf16[9,256,128]{2,1,0:T(8,128)(2,1)S(1)} %get-tuple-element.60), channel_id=1, source_target_pairs={{0,8},{2,10},{4,12},{6,14},{8,0},{10,2},{12,4},{14,6},{16,24},{18,... | collective-permute-start | bytes 1769480 | tf_op jit(solution)/shard_map/ppermute | solution.py:434
  24.5 8.1 %collective-permute-start.1 = (bf16[6,256,128]{2,1,0:T(8,128)(2,1)S(1)}, bf16[6,256,128]{2,1,0:T(8,128)(2,1)S(1)}, u32[]{:S(2)}, u32[]{:S(2)}) collective-permute-start(bf16[6,256,128]{2,1,0:T(8,128)(2,1)S(1)} %get-tuple-element.59.refs_2_), channel_id=1, source_target_pairs={{0,2},{2,0},{4,6},{6,4},{8,10},{10,8},{12,14},{14,12},{16,18},{18,... | collective-permute-start | bytes 1179656 | tf_op jit(solution)/shard_map/ppermute | solution.py:434
  24.5 14.1 %collective-permute-start.5 = (bf16[6,256,128]{2,1,0:T(8,128)(2,1)S(1)}, bf16[6,256,128]{2,1,0:T(8,128)(2,1)S(1)}, u32[]{:S(2)}, u32[]{:S(2)}) collective-permute-start(bf16[6,256,128]{2,1,0:T(8,128)(2,1)S(1)} %get-tuple-element.59.refs_2_), channel_id=1, source_target_pairs={{0,4},{2,6},{4,0},{6,2},{8,12},{10,14},{12,8},{14,10},{16,20},{18,... | collective-permute-start | bytes 1179656 | tf_op jit(solution)/shard_map/ppermute | solution.py:434
  26.2 12.4 %collective-permute-start.4 = (bf16[144,1536]{1,0:T(8,128)(2,1)S(1)}, bf16[144,1536]{1,0:T(8,128)(2,1)S(1)}, u32[]{:S(2)}, u32[]{:S(2)}) collective-permute-start(bf16[144,1536]{1,0:T(8,128)(2,1)S(1)} %collective-permute-done.2.refs_0_), channel_id=1, source_target_pairs={{0,1},{1,0},{2,3},{3,2},{4,5},{5,4},{6,7},{7,6},{8,9},{9,8},{10,11... | collective-permute-start | bytes 1327112 | tf_op jit(solution)/shard_map/ppermute | solution.py:431
  29.7 3.4 %copy-start.1 = (s32[32,32]{1,0:T(8,128)S(1)}, s32[32,32]{1,0:T(8,128)}, u32[]{:S(2)}) copy-start(s32[32,32]{1,0:T(8,128)} %mask_ref.1) | copy-start | bytes 12292
  29.8 3.4 %copy-start.2 = (s32[32]{0:T(128)S(1)}, s32[32]{0:T(128)}, u32[]{:S(2)}) copy-start(s32[32]{0:T(128)} %param.8) | copy-start | bytes 388
  29.8 17.0 %collective-permute-start.8 = (bf16[9,112,128]{2,1,0:T(8,128)(2,1)S(1)}, bf16[9,112,128]{2,1,0:T(8,128)(2,1)S(1)}, u32[]{:S(2)}, u32[]{:S(2)}) collective-permute-start(bf16[9,112,128]{2,1,0:T(8,128)(2,1)S(1)} %get-tuple-element.71), channel_id=1, source_target_pairs={{0,24},{2,26},{4,28},{6,30},{8,16},{10,18},{12,20},{14,22},{16,8},... | collective-permute-start | bytes 774152 | tf_op jit(solution)/shard_map/ppermute | solution.py:434
  32.6 22.8 %collective-permute-start.6 = (bf16[9,112,128]{2,1,0:T(8,128)(2,1)S(1)}, bf16[9,112,128]{2,1,0:T(8,128)(2,1)S(1)}, u32[]{:S(2)}, u32[]{:S(2)}) collective-permute-start(bf16[9,112,128]{2,1,0:T(8,128)(2,1)S(1)} %get-tuple-element.63), channel_id=1, source_target_pairs={{0,16},{2,18},{4,20},{6,22},{8,24},{10,26},{12,28},{14,30},{16,0},... | collective-permute-start | bytes 774152 | tf_op jit(solution)/shard_map/ppermute | solution.py:434
  38.6 19.5 %collective-permute-start.10 = (bf16[6,256,128]{2,1,0:T(8,128)(2,1)S(1)}, bf16[6,256,128]{2,1,0:T(8,128)(2,1)S(1)}, u32[]{:S(2)}, u32[]{:S(2)}) collective-permute-start(bf16[6,256,128]{2,1,0:T(8,128)(2,1)S(1)} %collective-permute-done.5.refs_3_), channel_id=1, source_target_pairs={{0,2},{2,0},{4,6},{6,4},{8,10},{10,8},{12,14},{14,12},{16,18},{18,... | collective-permute-start | bytes 1179656 | tf_op jit(solution)/shard_map/ppermute | solution.py:434
  41.0 14.3 %collective-permute-start.7 = (bf16[6,144,128]{2,1,0:T(8,128)(2,1)S(1)}, bf16[6,144,128]{2,1,0:T(8,128)(2,1)S(1)}, u32[]{:S(2)}, u32[]{:S(2)}) collective-permute-start(bf16[6,144,128]{2,1,0:T(8,128)(2,1)S(1)} %get-tuple-element.67), channel_id=1, source_target_pairs={{0,8},{2,10},{4,12},{6,14},{8,0},{10,2},{12,4},{14,6},{16,24},{18,... | collective-permute-start | bytes 663560 | tf_op jit(solution)/shard_map/ppermute | solution.py:434
  43.0 12.3 %collective-permute-start.11 = (bf16[3,256,128]{2,1,0:T(8,128)(2,1)S(1)}, bf16[3,256,128]{2,1,0:T(8,128)(2,1)S(1)}, u32[]{:S(2)}, u32[]{:S(2)}) collective-permute-start(bf16[3,256,128]{2,1,0:T(8,128)(2,1)S(1)} %get-tuple-element.76), channel_id=1, source_target_pairs={{0,4},{2,6},{4,0},{6,2},{8,12},{10,14},{12,8},{14,10},{16,20},{18,... | collective-permute-start | bytes 589832 | tf_op jit(solution)/shard_map/ppermute | solution.py:434
  46.8 9.9 %collective-permute-start.12 = (bf16[3,256,128]{2,1,0:T(8,128)(2,1)S(1)}, bf16[3,256,128]{2,1,0:T(8,128)(2,1)S(1)}, u32[]{:S(2)}, u32[]{:S(2)}) collective-permute-start(bf16[3,256,128]{2,1,0:T(8,128)(2,1)S(1)} %get-tuple-element.78), channel_id=1, source_target_pairs={{0,4},{2,6},{4,0},{6,2},{8,12},{10,14},{12,8},{14,10},{16,20},{18,... | collective-permute-start | bytes 589832 | tf_op jit(solution)/shard_map/ppermute | solution.py:434
  55.3 4.3 %collective-permute-start.13 = (bf16[6,256,128]{2,1,0:T(8,128)(2,1)S(1)}, bf16[6,256,128]{2,1,0:T(8,128)(2,1)S(1)}, u32[]{:S(2)}, u32[]{:S(2)}) collective-permute-start(bf16[6,256,128]{2,1,0:T(8,128)(2,1)S(1)} %get-tuple-element.75.refs_6_), channel_id=1, source_target_pairs={{0,2},{2,0},{4,6},{6,4},{8,10},{10,8},{12,14},{14,12},{16,18},{18,... | collective-permute-start | bytes 1179656 | tf_op jit(solution)/shard_map/ppermute | solution.py:434
  55.4 2.7 %collective-permute-start.14 = (bf16[3,256,128]{2,1,0:T(8,128)(2,1)S(1)}, bf16[3,256,128]{2,1,0:T(8,128)(2,1)S(1)}, u32[]{:S(2)}, u32[]{:S(2)}) collective-permute-start(bf16[3,256,128]{2,1,0:T(8,128)(2,1)S(1)} %collective-permute-done.11.refs_7_), channel_id=1, source_target_pairs={{0,2},{2,0},{4,6},{6,4},{8,10},{10,8},{12,14},{14,12},{16,18},{18,... | collective-permute-start | bytes 589832 | tf_op jit(solution)/shard_map/ppermute | solution.py:434
  55.9 14.1 %collective-permute-start.17 = (bf16[4,256,128]{2,1,0:T(8,128)(2,1)S(1)}, bf16[4,256,128]{2,1,0:T(8,128)(2,1)S(1)}, u32[]{:S(2)}, u32[]{:S(2)}) collective-permute-start(bf16[4,256,128]{2,1,0:T(8,128)(2,1)S(1)} %get-tuple-element.80.refs_13_.refs_10_), channel_id=1, source_target_pairs={{0,4},{2,6},{4,0},{6,2},{8,12},{10,14},{12,8},{14,10},{16,20},{18,... | collective-permute-start | bytes 786440 | tf_op jit(solution)/shard_map/ppermute | solution.py:434
  56.6 19.2 %collective-permute-start.16 = (bf16[8,256,128]{2,1,0:T(8,128)(2,1)S(1)}, bf16[8,256,128]{2,1,0:T(8,128)(2,1)S(1)}, u32[]{:S(2)}, u32[]{:S(2)}) collective-permute-start(bf16[8,256,128]{2,1,0:T(8,128)(2,1)S(1)} %get-tuple-element.88.refs_10_), channel_id=1, source_target_pairs={{0,4},{2,6},{4,0},{6,2},{8,12},{10,14},{12,8},{14,10},{16,20},{18,... | collective-permute-start | bytes 1572872 | tf_op jit(solution)/shard_map/ppermute | solution.py:434
  58.0 1.4 %collective-permute-start.15 = (bf16[3,256,128]{2,1,0:T(8,128)(2,1)S(1)}, bf16[3,256,128]{2,1,0:T(8,128)(2,1)S(1)}, u32[]{:S(2)}, u32[]{:S(2)}) collective-permute-start(bf16[3,256,128]{2,1,0:T(8,128)(2,1)S(1)} %collective-permute-done.12.refs_8_), channel_id=1, source_target_pairs={{0,2},{2,0},{4,6},{6,4},{8,10},{10,8},{12,14},{14,12},{16,18},{18,... | collective-permute-start | bytes 589832 | tf_op jit(solution)/shard_map/ppermute | solution.py:434
  58.0 6.8 %collective-permute-start.9 = (bf16[3,144,128]{2,1,0:T(8,128)(2,1)S(1)}, bf16[3,144,128]{2,1,0:T(8,128)(2,1)S(1)}, u32[]{:S(2)}, u32[]{:S(2)}) collective-permute-start(bf16[3,144,128]{2,1,0:T(8,128)(2,1)S(1)} %get-tuple-element.74), channel_id=1, source_target_pairs={{0,8},{2,10},{4,12},{6,14},{8,0},{10,2},{12,4},{14,6},{16,24},{18,... | collective-permute-start | bytes 331784 | tf_op jit(solution)/shard_map/ppermute | solution.py:434
  59.5 11.2 %collective-permute-start.18 = (bf16[4,256,128]{2,1,0:T(8,128)(2,1)S(1)}, bf16[4,256,128]{2,1,0:T(8,128)(2,1)S(1)}, u32[]{:S(2)}, u32[]{:S(2)}) collective-permute-start(bf16[4,256,128]{2,1,0:T(8,128)(2,1)S(1)} %get-tuple-element.80.refs_13_.refs_10_), channel_id=1, source_target_pairs={{0,2},{2,0},{4,6},{6,4},{8,10},{10,8},{12,14},{14,12},{16,18},{18,... | collective-permute-start | bytes 786440 | tf_op jit(solution)/shard_map/ppermute | solution.py:434
  70.1 1.6 %collective-permute-start.19 = (bf16[4,256,128]{2,1,0:T(8,128)(2,1)S(1)}, bf16[4,256,128]{2,1,0:T(8,128)(2,1)S(1)}, u32[]{:S(2)}, u32[]{:S(2)}) collective-permute-start(bf16[4,256,128]{2,1,0:T(8,128)(2,1)S(1)} %collective-permute-done.17.refs_11_), channel_id=1, source_target_pairs={{0,2},{2,0},{4,6},{6,4},{8,10},{10,8},{12,14},{14,12},{16,18},{18,... | collective-permute-start | bytes 786440 | tf_op jit(solution)/shard_map/ppermute | solution.py:434
  70.5 5.8 %collective-permute-start.20 = (bf16[8,256,128]{2,1,0:T(8,128)(2,1)S(1)}, bf16[8,256,128]{2,1,0:T(8,128)(2,1)S(1)}, u32[]{:S(2)}, u32[]{:S(2)}) collective-permute-start(bf16[8,256,128]{2,1,0:T(8,128)(2,1)S(1)} %get-tuple-element.88.refs_10_), channel_id=1, source_target_pairs={{0,2},{2,0},{4,6},{6,4},{8,10},{10,8},{12,14},{14,12},{16,18},{18,... | collective-permute-start | bytes 1572872 | tf_op jit(solution)/shard_map/ppermute | solution.py:434
  75.8 2.0 %collective-permute-start.21 = (bf16[8,256,128]{2,1,0:T(8,128)(2,1)S(1)}, bf16[8,256,128]{2,1,0:T(8,128)(2,1)S(1)}, u32[]{:S(2)}, u32[]{:S(2)}) collective-permute-start(bf16[8,256,128]{2,1,0:T(8,128)(2,1)S(1)} %collective-permute-done.16.refs_11_), channel_id=1, source_target_pairs={{0,2},{2,0},{4,6},{6,4},{8,10},{10,8},{12,14},{14,12},{16,18},{18,... | collective-permute-start | bytes 1572872 | tf_op jit(solution)/shard_map/ppermute | solution.py:434
  82.0 11.6 %collective-permute-start.25 = (bf16[128,384]{1,0:T(8,128)(2,1)S(1)}, bf16[128,384]{1,0:T(8,128)(2,1)S(1)}, u32[]{:S(2)}, u32[]{:S(2)}) collective-permute-start(bf16[128,384]{1,0:T(8,128)(2,1)S(1)} %get-tuple-element.100), channel_id=1, source_target_pairs={{0,8},{2,10},{4,12},{6,14},{8,0},{10,2},{12,4},{14,6},{16,24},{18,... | collective-permute-start | bytes 294920 | tf_op jit(solution)/shard_map/ppermute | solution.py:434
  82.8 12.5 %collective-permute-start.26 = (bf16[128,384]{1,0:T(8,128)(2,1)S(1)}, bf16[128,384]{1,0:T(8,128)(2,1)S(1)}, u32[]{:S(2)}, u32[]{:S(2)}) collective-permute-start(bf16[128,384]{1,0:T(8,128)(2,1)S(1)} %get-tuple-element.101), channel_id=1, source_target_pairs={{0,16},{2,18},{4,20},{6,22},{8,24},{10,26},{12,28},{14,30},{16,0},... | collective-permute-start | bytes 294920 | tf_op jit(solution)/shard_map/ppermute | solution.py:434
  85.3 10.0 %collective-permute-start.27 = (bf16[128,384]{1,0:T(8,128)(2,1)S(1)}, bf16[128,384]{1,0:T(8,128)(2,1)S(1)}, u32[]{:S(2)}, u32[]{:S(2)}) collective-permute-start(bf16[128,384]{1,0:T(8,128)(2,1)S(1)} %get-tuple-element.102), channel_id=1, source_target_pairs={{0,24},{2,26},{4,28},{6,30},{8,16},{10,18},{12,20},{14,22},{16,8},... | collective-permute-start | bytes 294920 | tf_op jit(solution)/shard_map/ppermute | solution.py:434
  90.8 7.6 %collective-permute-start.24 = (bf16[128,384]{1,0:T(8,128)(2,1)S(1)}, bf16[128,384]{1,0:T(8,128)(2,1)S(1)}, u32[]{:S(2)}, u32[]{:S(2)}) collective-permute-start(bf16[128,384]{1,0:T(8,128)(2,1)S(1)} %get-tuple-element.99), channel_id=1, source_target_pairs={{0,24},{2,26},{4,28},{6,30},{8,16},{10,18},{12,20},{14,22},{16,8},... | collective-permute-start | bytes 294920 | tf_op jit(solution)/shard_map/ppermute | solution.py:434
  93.6 5.6 %collective-permute-start.22 = (bf16[128,384]{1,0:T(8,128)(2,1)S(1)}, bf16[128,384]{1,0:T(8,128)(2,1)S(1)}, u32[]{:S(2)}, u32[]{:S(2)}) collective-permute-start(bf16[128,384]{1,0:T(8,128)(2,1)S(1)} %get-tuple-element.97), channel_id=1, source_target_pairs={{0,8},{2,10},{4,12},{6,14},{8,0},{10,2},{12,4},{14,6},{16,24},{18,... | collective-permute-start | bytes 294920 | tf_op jit(solution)/shard_map/ppermute | solution.py:434
  93.6 9.6 %collective-permute-start.23 = (bf16[128,384]{1,0:T(8,128)(2,1)S(1)}, bf16[128,384]{1,0:T(8,128)(2,1)S(1)}, u32[]{:S(2)}, u32[]{:S(2)}) collective-permute-start(bf16[128,384]{1,0:T(8,128)(2,1)S(1)} %get-tuple-element.98), channel_id=1, source_target_pairs={{0,16},{2,18},{4,20},{6,22},{8,24},{10,26},{12,28},{14,30},{16,0},... | collective-permute-start | bytes 294920 | tf_op jit(solution)/shard_map/ppermute | solution.py:434
  96.2 9.7 %collective-permute-start.29 = (bf16[128,1536]{1,0:T(8,128)(2,1)S(1)}, bf16[128,1536]{1,0:T(8,128)(2,1)S(1)}, u32[]{:S(2)}, u32[]{:S(2)}) collective-permute-start(bf16[128,1536]{1,0:T(8,128)(2,1)S(1)} %shard_map.89), channel_id=1, source_target_pairs={{0,1},{1,0},{2,3},{3,2},{4,5},{5,4},{6,7},{7,6},{8,9},{9,8},{10,11... | collective-permute-start | bytes 1179656 | tf_op jit(solution)/shard_map/ppermute | solution.py:431
  104.0 10.5 %collective-permute-start.28 = (bf16[128,1536]{1,0:T(8,128)(2,1)S(1)}, bf16[128,1536]{1,0:T(8,128)(2,1)S(1)}, u32[]{:S(2)}, u32[]{:S(2)}) collective-permute-start(bf16[128,1536]{1,0:T(8,128)(2,1)S(1)} %shard_map.91), channel_id=1, source_target_pairs={{0,1},{1,0},{2,3},{3,2},{4,5},{5,4},{6,7},{7,6},{8,9},{9,8},{10,11... | collective-permute-start | bytes 1179656 | tf_op jit(solution)/shard_map/ppermute | solution.py:431

commit v8 on v7

--- a/solution.py
+++ b/solution.py
@@ -293,7 +293,7 @@
             best = jnp.maximum(best, score[:, u : u + HEAD_DIM])
         top_next = jnp.maximum(top, jnp.max(best, axis=1, keepdims=True))
         factor = jnp.exp2((top - top_next) * scale)
-        weight = jnp.exp2(score * scale - top_next * scale)
+        weight = jnp.exp2((score - top_next) * scale)
         add = weight[:, :HEAD_DIM]
         for u in range(HEAD_DIM, width, HEAD_DIM):
             add = add + weight[:, u : u + HEAD_DIM]

time: 116 us -> 115 us (level)
  transfers between devices with their start and end apart: 30 -> 30, of which waited for: 12 -> 13; matrix products, arithmetic and copies ran while one was open for 1% -> 1% of each run, Pallas kernels for 43% -> 42%
where the time goes in v8:
time: 115 us
  Pallas kernels  54.3 us (47%)
  starting transfers between devices  33.1 us (29%)
  waiting for transfers between devices  26.4 us (23%)
    ppermute x26, starting transfers between devices, over(): return lax.ppermute(a, 'ctx', hop(dz, dx, dc))  27.8 us
    pallas_call x5, Pallas kernels, attend(): pl.pallas_call(body, grid=(count,), in_specs=whole(total_arrays) + [pl.Bl...  23 us
    ppermute x26, waiting for transfers between devices, over(): return lax.ppermute(a, 'ctx', hop(dz, dx, dc))  17.4 us
    pallas_call x2, Pallas kernels, fetch(): pl.pallas_call(body, grid_spec=pltpu.PrefetchScalarGridSpec(num_scalar_pr...  14.2 us
    ppermute x4, waiting for transfers between devices, over_y(): return lax.ppermute(a, 'head', [(0, 1), (1, 0)])  9.02 us
    pallas_call x4, Pallas kernels, project(): pl.pallas_call(body, in_specs=whole(3 + len(more)), out_specs=whole(len(o...  7.08 us
    ppermute x4, starting transfers between devices, over_y(): return lax.ppermute(a, 'head', [(0, 1), (1, 0)])  5.37 us
    pallas_call x1, Pallas kernels, fetch_out(): pl.pallas_call(body, grid_spec=pltpu.PrefetchScalarGridSpec(num_scalar_pr...  4.33 us
  transfers between devices with their start and end apart: 30, of which 13 were waited for; matrix products, arithmetic and copies ran while one was open for 1% of the time, Pallas kernels for 42%

profile of v8, /device:TPU:0, one launch (start us, length us, event | category | flops | bytes accessed | tf_op | source)
XLA Modules:
  0.0 115.3 jit_solution(14235967892154405373)
XLA Ops:
  0.0 3.0 %collective-permute-start = (bf16[256,1536]{1,0:T(8,128)(2,1)}, bf16[256,1536]{1,0:T(8,128)(2,1)S(1)}, u32[]{:S(2)}, u32[]{:S(2)}) collective-permute-start(bf16[256,1536]{1,0:T(8,128)(2,1)} %refs_0_.7), channel_id=1, source_target_pairs={{0,1},{1,0},{2,3},{3,2},{4,5},{5,4},{6,7},{7,6},{8,9},{9,8},{10,11... | collective-permute-start | bytes 2359304 | tf_op jit(solution)/shard_map/ppermute | solution.py:431
  3.0 1.1 slice.3
  4.0 2.7 %collective-permute-start.2 = (bf16[144,1536]{1,0:T(8,128)(2,1)S(1)}, bf16[144,1536]{1,0:T(8,128)(2,1)S(1)}, u32[]{:S(2)}, u32[]{:S(2)}) collective-permute-start(bf16[144,1536]{1,0:T(8,128)(2,1)S(1)} %slice.3), channel_id=1, source_target_pairs={{0,16},{2,18},{4,20},{6,22},{8,24},{10,26},{12,28},{14,30},{16,0},... | collective-permute-start | bytes 1327112 | tf_op jit(solution)/shard_map/ppermute | solution.py:434
  6.8 5.8 %shard_map.73.refs_5_.refs_2_ = bf16[6,3072,384]{2,1,0:T(8,128)(2,1)S(1)} custom-call(s32[4]{0:T(128)S(1)} %pad_add_fusion.s.refs_3_, bf16[3072,1536]{1,0:T(8,128)(2,1)} %refs_0_.4, bf16[3072,1536]{1,0:T(8,128)(2,1)} %refs_1_.3, bf16[3072,1536]{1,0:T(8,128)(2,1)} %refs_2_.3, s32[4]{0:T(128)S(1)} %pad_add_fusion.s.refs_3_), custom_call_target="tpu_custom_call" | custom-call | flops 1024 | bytes 1024 | tf_op jit(solution)/shard_map/pallas_call | solution.py:80
  12.6 8.3 %shard_map.74 = (bf16[6,3072,384]{2,1,0:T(8,128)(2,1)S(1)}, f32[6,256,384]{2,1,0:T(8,128)S(1)}) custom-call(s32[4]{0:T(128)S(1)} %pad_add_fusion.s.refs_3_, bf16[3072,1536]{1,0:T(8,128)(2,1)} %refs_0_.4, bf16[3072,1536]{1,0:T(8,128)(2,1)} %refs_1_.3, bf16[3072,1536]{1,0:T(8,128)(2,1)} %refs_2_.3, s32[4]{0:T(128)S(1)} %pad_add_fusion.s.refs_3_, ...), custom_call_target="tpu_custom_call" | custom-call | flops 1024 | bytes 1024 | tf_op jit(solution)/shard_map/pallas_call | solution.py:80
  21.0 1.9 %shard_map.75 = (bf16[6,256,128]{2,1,0:T(8,128)(2,1)S(1)}, bf16[9,256,128]{2,1,0:T(8,128)(2,1)S(1)}) custom-call(bf16[256,1536]{1,0:T(8,128)(2,1)S(1)} %copy-done, bf16[256,1536]{1,0:T(8,128)(2,1)S(1)} %collective-permute-done.refs_1_, bf16[6,3072,384]{2,1,0:T(8,128)(2,1)S(1)} %shard_map.73.refs_5_.refs_2_, f32[6,256,384]{2,1,0:T(8,128)S(1)} %get-tuple-element.58.refs_3_), custom_call_target="tpu_custom_call" | custom-call | flops 1024 | bytes 1024 | tf_op jit(solution)/shard_map/pallas_call | solution.py:125
  22.9 1.6 %collective-permute-start.3 = (bf16[9,256,128]{2,1,0:T(8,128)(2,1)S(1)}, bf16[9,256,128]{2,1,0:T(8,128)(2,1)S(1)}, u32[]{:S(2)}, u32[]{:S(2)}) collective-permute-start(bf16[9,256,128]{2,1,0:T(8,128)(2,1)S(1)} %get-tuple-element.60), channel_id=1, source_target_pairs={{0,8},{2,10},{4,12},{6,14},{8,0},{10,2},{12,4},{14,6},{16,24},{18,... | collective-permute-start | bytes 1769480 | tf_op jit(solution)/shard_map/ppermute | solution.py:434
  24.5 1.5 %collective-permute-start.5 = (bf16[6,256,128]{2,1,0:T(8,128)(2,1)S(1)}, bf16[6,256,128]{2,1,0:T(8,128)(2,1)S(1)}, u32[]{:S(2)}, u32[]{:S(2)}) collective-permute-start(bf16[6,256,128]{2,1,0:T(8,128)(2,1)S(1)} %get-tuple-element.59.refs_2_), channel_id=1, source_target_pairs={{0,4},{2,6},{4,0},{6,2},{8,12},{10,14},{12,8},{14,10},{16,20},{18,... | collective-permute-start | bytes 1179656 | tf_op jit(solution)/shard_map/ppermute | solution.py:434
  26.2 1.2 %collective-permute-start.4 = (bf16[144,1536]{1,0:T(8,128)(2,1)S(1)}, bf16[144,1536]{1,0:T(8,128)(2,1)S(1)}, u32[]{:S(2)}, u32[]{:S(2)}) collective-permute-start(bf16[144,1536]{1,0:T(8,128)(2,1)S(1)} %collective-permute-done.2.refs_0_), channel_id=1, source_target_pairs={{0,1},{1,0},{2,3},{3,2},{4,5},{5,4},{6,7},{7,6},{8,9},{9,8},{10,11... | collective-permute-start | bytes 1327112 | tf_op jit(solution)/shard_map/ppermute | solution.py:431
  27.5 2.3 %shard_map.76 = (bf16[9,112,128]{2,1,0:T(8,128)(2,1)S(1)}, bf16[9,112,128]{2,1,0:T(8,128)(2,1)S(1)}) custom-call(bf16[256,1536]{1,0:T(8,128)(2,1)S(1)} %copy-done, bf16[256,1536]{1,0:T(8,128)(2,1)S(1)} %collective-permute-done.refs_1_, bf16[6,3072,384]{2,1,0:T(8,128)(2,1)S(1)} %get-tuple-element.56.refs_2_), custom_call_target="tpu_custom_call" | custom-call | flops 1024 | bytes 1024 | tf_op jit(solution)/shard_map/pallas_call | solution.py:125
  29.8 2.8 %collective-permute-start.8 = (bf16[9,112,128]{2,1,0:T(8,128)(2,1)S(1)}, bf16[9,112,128]{2,1,0:T(8,128)(2,1)S(1)}, u32[]{:S(2)}, u32[]{:S(2)}) collective-permute-start(bf16[9,112,128]{2,1,0:T(8,128)(2,1)S(1)} %get-tuple-element.71), channel_id=1, source_target_pairs={{0,24},{2,26},{4,28},{6,30},{8,16},{10,18},{12,20},{14,22},{16,8},... | collective-permute-start | bytes 774152 | tf_op jit(solution)/shard_map/ppermute | solution.py:434
  32.6 0.6 shard_map.77.refs_0_
  33.2 1.1 shard_map.78.fence_ref.refs_12_.refs_14_.refs_18_
  34.2 4.3 %shard_map.79.refs_4_ = bf16[1536,3072]{1,0:T(8,128)(2,1)S(1)} custom-call(s32[4]{0:T(128)S(1)} %pad_add_fusion.s.refs_3_, bf16[1536,3072]{1,0:T(8,128)(2,1)} %w_ref.1, f32[8,4096]{1,0:T(8,128)S(1)} %shard_map.78.fence_ref.refs_12_.refs_14_.refs_18_), custom_call_target="tpu_custom_call" | custom-call | flops 1024 | bytes 1024 | tf_op jit(solution)/shard_map/pallas_call | solution.py:357
  38.7 2.4 %shard_map.80 = (bf16[3,144,128]{2,1,0:T(8,128)(2,1)S(1)}, bf16[6,144,128]{2,1,0:T(8,128)(2,1)S(1)}, bf16[9,144,128]{2,1,0:T(8,128)(2,1)S(1)}) custom-call(bf16[144,1536]{1,0:T(8,128)(2,1)S(1)} %collective-permute-done.2.refs_0_, bf16[144,1536]{1,0:T(8,128)(2,1)S(1)} %collective-permute-done.4.refs_1_, bf16[6,3072,384]{2,1,0:T(8,128)(2,1)S(1)} %shard_map.73.refs_5_.refs_2_), custom_call_target="tpu_custom_call" | custom-call | flops 1024 | bytes 1024 | tf_op jit(solution)/shard_map/pallas_call | solution.py:125
  41.0 1.7 %collective-permute-start.7 = (bf16[6,144,128]{2,1,0:T(8,128)(2,1)S(1)}, bf16[6,144,128]{2,1,0:T(8,128)(2,1)S(1)}, u32[]{:S(2)}, u32[]{:S(2)}) collective-permute-start(bf16[6,144,128]{2,1,0:T(8,128)(2,1)S(1)} %get-tuple-element.67), channel_id=1, source_target_pairs={{0,8},{2,10},{4,12},{6,14},{8,0},{10,2},{12,4},{14,6},{16,24},{18,... | collective-permute-start | bytes 663560 | tf_op jit(solution)/shard_map/ppermute | solution.py:434
  43.0 3.4 %collective-permute-start.11 = (bf16[3,256,128]{2,1,0:T(8,128)(2,1)S(1)}, bf16[3,256,128]{2,1,0:T(8,128)(2,1)S(1)}, u32[]{:S(2)}, u32[]{:S(2)}) collective-permute-start(bf16[3,256,128]{2,1,0:T(8,128)(2,1)S(1)} %get-tuple-element.76), channel_id=1, source_target_pairs={{0,4},{2,6},{4,0},{6,2},{8,12},{10,14},{12,8},{14,10},{16,20},{18,... | collective-permute-start | bytes 589832 | tf_op jit(solution)/shard_map/ppermute | solution.py:434
  46.8 1.5 %collective-permute-start.12 = (bf16[3,256,128]{2,1,0:T(8,128)(2,1)S(1)}, bf16[3,256,128]{2,1,0:T(8,128)(2,1)S(1)}, u32[]{:S(2)}, u32[]{:S(2)}) collective-permute-start(bf16[3,256,128]{2,1,0:T(8,128)(2,1)S(1)} %get-tuple-element.78), channel_id=1, source_target_pairs={{0,4},{2,6},{4,0},{6,2},{8,12},{10,14},{12,8},{14,10},{16,20},{18,... | collective-permute-start | bytes 589832 | tf_op jit(solution)/shard_map/ppermute | solution.py:434
  48.3 7.1 %collective-permute-done.6.refs_1_ = bf16[9,112,128]{2,1,0:T(8,128)(2,1)S(1)} collective-permute-done((bf16[9,112,128]{2,1,0:T(8,128)(2,1)S(1)}, bf16[9,112,128]{2,1,0:T(8,128)(2,1)S(1)}, u32[]{:S(2)}, u32[]{:S(2)}) %collective-permute-start.6) | collective-permute-done | bytes 258080 | tf_op jit(solution)/shard_map/ppermute | solution.py:434
  55.4 0.5 collective-permute-start.14
  55.9 0.7 collective-permute-start.17
  56.6 1.4 %collective-permute-start.16 = (bf16[8,256,128]{2,1,0:T(8,128)(2,1)S(1)}, bf16[8,256,128]{2,1,0:T(8,128)(2,1)S(1)}, u32[]{:S(2)}, u32[]{:S(2)}) collective-permute-start(bf16[8,256,128]{2,1,0:T(8,128)(2,1)S(1)} %get-tuple-element.88.refs_10_), channel_id=1, source_target_pairs={{0,4},{2,6},{4,0},{6,2},{8,12},{10,14},{12,8},{14,10},{16,20},{18,... | collective-permute-start | bytes 1572872 | tf_op jit(solution)/shard_map/ppermute | solution.py:434
  58.1 1.4 %collective-permute-done.15.refs_11_ = bf16[3,256,128]{2,1,0:T(8,128)(2,1)S(1)} collective-permute-done((bf16[3,256,128]{2,1,0:T(8,128)(2,1)S(1)}, bf16[3,256,128]{2,1,0:T(8,128)(2,1)S(1)}, u32[]{:S(2)}, u32[]{:S(2)}) %collective-permute-start.15) | collective-permute-done | bytes 196640 | tf_op jit(solution)/shard_map/ppermute | solution.py:434
  59.6 4.8 %shard_map.83 = (f32[3,512,128]{2,1,0:T(8,128)S(1)}, f32[3,512,128]{2,1,0:T(8,128)S(1)}, f32[3,512,128]{2,1,0:T(8,128)S(1)}) custom-call(bf16[3,256,128]{2,1,0:T(8,128)(2,1)S(1)} %shard_map.77.refs_0_, bf16[9,256,128]{2,1,0:T(8,128)(2,1)S(1)} %collective-permute-done.3.in_ref.refs_1_, bf16[6,256,128]{2,1,0:T(8,128)(2,1)S(1)} %get-tuple-element.59.refs_2_, ...), custom_call_target="tpu_custom_call" | custom-call | flops 1024 | bytes 1024 | tf_op jit(solution)/shard_map/pallas_call | solution.py:322
  64.4 4.8 %shard_map.85 = (f32[3,512,128]{2,1,0:T(8,128)S(1)}, f32[3,512,128]{2,1,0:T(8,128)S(1)}, f32[3,512,128]{2,1,0:T(8,128)S(1)}) custom-call(bf16[3,256,128]{2,1,0:T(8,128)(2,1)S(1)} %get-tuple-element.73.refs_0_.refs_5_.refs_2_, bf16[3,256,128]{2,1,0:T(8,128)(2,1)S(1)} %shard_map.84.refs_1_.refs_6_.refs_3_, bf16[6,256,128]{2,1,0:T(8,128)(2,1)S(1)} %get-tuple-element.59.refs_2_, ...), custom_call_target="tpu_custom_call" | custom-call | flops 1024 | bytes 1024 | tf_op jit(solution)/shard_map/pallas_call | solution.py:322
  69.3 0.4 collective-permute-start.19
  69.8 1.0 collective-permute-done.19.refs_13_
  70.9 4.4 %shard_map.86 = (bf16[256,128]{1,0:T(8,128)(2,1)S(1)}, bf16[256,128]{1,0:T(8,128)(2,1)S(1)}, bf16[256,128]{1,0:T(8,128)(2,1)S(1)}, bf16[256,128]{1,0:T(8,128)(2,1)S(1)}) custom-call(bf16[3,256,128]{2,1,0:T(8,128)(2,1)S(1)} %shard_map.77.refs_0_, bf16[9,256,128]{2,1,0:T(8,128)(2,1)S(1)} %collective-permute-done.3.in_ref.refs_1_, ...), custom_call_target="tpu_custom_call" | custom-call | flops 1024 | bytes 1024 | tf_op jit(solution)/shard_map/pallas_call | solution.py:322
  75.7 1.7 %collective-permute-done.21.refs_13_ = bf16[8,256,128]{2,1,0:T(8,128)(2,1)S(1)} collective-permute-done((bf16[8,256,128]{2,1,0:T(8,128)(2,1)S(1)}, bf16[8,256,128]{2,1,0:T(8,128)(2,1)S(1)}, u32[]{:S(2)}, u32[]{:S(2)}) %collective-permute-start.21) | collective-permute-done | bytes 524320 | tf_op jit(solution)/shard_map/ppermute | solution.py:434
  77.4 4.4 %shard_map.87 = (bf16[128,384]{1,0:T(8,128)(2,1)S(1)}, bf16[128,384]{1,0:T(8,128)(2,1)S(1)}, bf16[128,384]{1,0:T(8,128)(2,1)S(1)}, bf16[128,384]{1,0:T(8,128)(2,1)S(1)}) custom-call(bf16[3,256,128]{2,1,0:T(8,128)(2,1)S(1)} %shard_map.77.refs_0_, bf16[9,256,128]{2,1,0:T(8,128)(2,1)S(1)} %collective-permute-done.3.in_ref.refs_1_, ...), custom_call_target="tpu_custom_call" | custom-call | flops 1024 | bytes 1024 | tf_op jit(solution)/shard_map/pallas_call | solution.py:322
  81.8 0.6 collective-permute-start.25
  82.5 2.7 %collective-permute-start.26 = (bf16[128,384]{1,0:T(8,128)(2,1)S(1)}, bf16[128,384]{1,0:T(8,128)(2,1)S(1)}, u32[]{:S(2)}, u32[]{:S(2)}) collective-permute-start(bf16[128,384]{1,0:T(8,128)(2,1)S(1)} %get-tuple-element.101), channel_id=1, source_target_pairs={{0,16},{2,18},{4,20},{6,22},{8,24},{10,26},{12,28},{14,30},{16,0},... | collective-permute-start | bytes 294920 | tf_op jit(solution)/shard_map/ppermute | solution.py:434
  85.2 1.1 collective-permute-start.27
  86.3 4.6 %shard_map.88 = (bf16[128,384]{1,0:T(8,128)(2,1)S(1)}, bf16[128,384]{1,0:T(8,128)(2,1)S(1)}, bf16[128,384]{1,0:T(8,128)(2,1)S(1)}, bf16[128,384]{1,0:T(8,128)(2,1)S(1)}) custom-call(bf16[3,256,128]{2,1,0:T(8,128)(2,1)S(1)} %shard_map.77.refs_0_, bf16[9,256,128]{2,1,0:T(8,128)(2,1)S(1)} %collective-permute-done.3.in_ref.refs_1_, ...), custom_call_target="tpu_custom_call" | custom-call | flops 1024 | bytes 1024 | tf_op jit(solution)/shard_map/pallas_call | solution.py:322
  90.9 2.8 %collective-permute-start.24 = (bf16[128,384]{1,0:T(8,128)(2,1)S(1)}, bf16[128,384]{1,0:T(8,128)(2,1)S(1)}, u32[]{:S(2)}, u32[]{:S(2)}) collective-permute-start(bf16[128,384]{1,0:T(8,128)(2,1)S(1)} %get-tuple-element.99), channel_id=1, source_target_pairs={{0,24},{2,26},{4,28},{6,30},{8,16},{10,18},{12,20},{14,22},{16,8},... | collective-permute-start | bytes 294920 | tf_op jit(solution)/shard_map/ppermute | solution.py:434
  93.7 1.7 %collective-permute-start.23 = (bf16[128,384]{1,0:T(8,128)(2,1)S(1)}, bf16[128,384]{1,0:T(8,128)(2,1)S(1)}, u32[]{:S(2)}, u32[]{:S(2)}) collective-permute-start(bf16[128,384]{1,0:T(8,128)(2,1)S(1)} %get-tuple-element.98), channel_id=1, source_target_pairs={{0,16},{2,18},{4,20},{6,22},{8,24},{10,26},{12,28},{14,30},{16,0},... | collective-permute-start | bytes 294920 | tf_op jit(solution)/shard_map/ppermute | solution.py:434
  95.4 0.8 shard_map.89
  96.2 0.6 collective-permute-start.29
  96.8 0.8 shard_map.90.refs_0_
  97.7 0.9 collective-permute-done.24.refs_3_
  98.5 0.7 collective-permute-done.22.refs_1_
  99.3 3.6 %collective-permute-done.23.refs_2_ = bf16[128,384]{1,0:T(8,128)(2,1)S(1)} collective-permute-done((bf16[128,384]{1,0:T(8,128)(2,1)S(1)}, bf16[128,384]{1,0:T(8,128)(2,1)S(1)}, u32[]{:S(2)}, u32[]{:S(2)}) %collective-permute-start.23) | collective-permute-done | bytes 98336 | tf_op jit(solution)/shard_map/ppermute | solution.py:434
  102.9 0.8 shard_map.91
  103.7 0.6 collective-permute-start.28
  104.3 0.8 shard_map.92.refs_0_
  105.1 0.7 collective-permute-done.29.refs_1_
  105.9 8.3 %collective-permute-done.28.refs_1_ = bf16[128,1536]{1,0:T(8,128)(2,1)S(1)} collective-permute-done((bf16[128,1536]{1,0:T(8,128)(2,1)S(1)}, bf16[128,1536]{1,0:T(8,128)(2,1)S(1)}, u32[]{:S(2)}, u32[]{:S(2)}) %collective-permute-start.28) | collective-permute-done | bytes 393248 | tf_op jit(solution)/shard_map/ppermute | solution.py:431
  114.3 1.0 shard_map.94
  (42 shorter events, 2.0 us)
Async XLA Ops:
  0.0 21.0 %collective-permute-start = (bf16[256,1536]{1,0:T(8,128)(2,1)}, bf16[256,1536]{1,0:T(8,128)(2,1)S(1)}, u32[]{:S(2)}, u32[]{:S(2)}) collective-permute-start(bf16[256,1536]{1,0:T(8,128)(2,1)} %refs_0_.7), channel_id=1, source_target_pairs={{0,1},{1,0},{2,3},{3,2},{4,5},{5,4},{6,7},{7,6},{8,9},{9,8},{10,11... | collective-permute-start | bytes 2359304 | tf_op jit(solution)/shard_map/ppermute | solution.py:431
  4.0 22.2 %collective-permute-start.2 = (bf16[144,1536]{1,0:T(8,128)(2,1)S(1)}, bf16[144,1536]{1,0:T(8,128)(2,1)S(1)}, u32[]{:S(2)}, u32[]{:S(2)}) collective-permute-start(bf16[144,1536]{1,0:T(8,128)(2,1)S(1)} %slice.3), channel_id=1, source_target_pairs={{0,16},{2,18},{4,20},{6,22},{8,24},{10,26},{12,28},{14,30},{16,0},... | collective-permute-start | bytes 1327112 | tf_op jit(solution)/shard_map/ppermute | solution.py:434
  6.8 5.9 %copy-start = (bf16[256,1536]{1,0:T(8,128)(2,1)S(1)}, bf16[256,1536]{1,0:T(8,128)(2,1)}, u32[]{:S(2)}) copy-start(bf16[256,1536]{1,0:T(8,128)(2,1)} %refs_0_.7) | copy-start | bytes 2359300
  22.9 20.1 %collective-permute-start.3 = (bf16[9,256,128]{2,1,0:T(8,128)(2,1)S(1)}, bf16[9,256,128]{2,1,0:T(8,128)(2,1)S(1)}, u32[]{:S(2)}, u32[]{:S(2)}) collective-permute-start(bf16[9,256,128]{2,1,0:T(8,128)(2,1)S(1)} %get-tuple-element.60), channel_id=1, source_target_pairs={{0,8},{2,10},{4,12},{6,14},{8,0},{10,2},{12,4},{14,6},{16,24},{18,... | collective-permute-start | bytes 1769480 | tf_op jit(solution)/shard_map/ppermute | solution.py:434
  24.5 8.1 %collective-permute-start.1 = (bf16[6,256,128]{2,1,0:T(8,128)(2,1)S(1)}, bf16[6,256,128]{2,1,0:T(8,128)(2,1)S(1)}, u32[]{:S(2)}, u32[]{:S(2)}) collective-permute-start(bf16[6,256,128]{2,1,0:T(8,128)(2,1)S(1)} %get-tuple-element.59.refs_2_), channel_id=1, source_target_pairs={{0,2},{2,0},{4,6},{6,4},{8,10},{10,8},{12,14},{14,12},{16,18},{18,... | collective-permute-start | bytes 1179656 | tf_op jit(solution)/shard_map/ppermute | solution.py:434
  24.5 14.1 %collective-permute-start.5 = (bf16[6,256,128]{2,1,0:T(8,128)(2,1)S(1)}, bf16[6,256,128]{2,1,0:T(8,128)(2,1)S(1)}, u32[]{:S(2)}, u32[]{:S(2)}) collective-permute-start(bf16[6,256,128]{2,1,0:T(8,128)(2,1)S(1)} %get-tuple-element.59.refs_2_), channel_id=1, source_target_pairs={{0,4},{2,6},{4,0},{6,2},{8,12},{10,14},{12,8},{14,10},{16,20},{18,... | collective-permute-start | bytes 1179656 | tf_op jit(solution)/shard_map/ppermute | solution.py:434
  26.2 12.4 %collective-permute-start.4 = (bf16[144,1536]{1,0:T(8,128)(2,1)S(1)}, bf16[144,1536]{1,0:T(8,128)(2,1)S(1)}, u32[]{:S(2)}, u32[]{:S(2)}) collective-permute-start(bf16[144,1536]{1,0:T(8,128)(2,1)S(1)} %collective-permute-done.2.refs_0_), channel_id=1, source_target_pairs={{0,1},{1,0},{2,3},{3,2},{4,5},{5,4},{6,7},{7,6},{8,9},{9,8},{10,11... | collective-permute-start | bytes 1327112 | tf_op jit(solution)/shard_map/ppermute | solution.py:431
  29.7 3.4 %copy-start.1 = (s32[32,32]{1,0:T(8,128)S(1)}, s32[32,32]{1,0:T(8,128)}, u32[]{:S(2)}) copy-start(s32[32,32]{1,0:T(8,128)} %mask_ref.1) | copy-start | bytes 12292
  29.8 3.4 %copy-start.2 = (s32[32]{0:T(128)S(1)}, s32[32]{0:T(128)}, u32[]{:S(2)}) copy-start(s32[32]{0:T(128)} %param.8) | copy-start | bytes 388
  29.8 17.0 %collective-permute-start.8 = (bf16[9,112,128]{2,1,0:T(8,128)(2,1)S(1)}, bf16[9,112,128]{2,1,0:T(8,128)(2,1)S(1)}, u32[]{:S(2)}, u32[]{:S(2)}) collective-permute-start(bf16[9,112,128]{2,1,0:T(8,128)(2,1)S(1)} %get-tuple-element.71), channel_id=1, source_target_pairs={{0,24},{2,26},{4,28},{6,30},{8,16},{10,18},{12,20},{14,22},{16,8},... | collective-permute-start | bytes 774152 | tf_op jit(solution)/shard_map/ppermute | solution.py:434
  32.6 22.8 %collective-permute-start.6 = (bf16[9,112,128]{2,1,0:T(8,128)(2,1)S(1)}, bf16[9,112,128]{2,1,0:T(8,128)(2,1)S(1)}, u32[]{:S(2)}, u32[]{:S(2)}) collective-permute-start(bf16[9,112,128]{2,1,0:T(8,128)(2,1)S(1)} %get-tuple-element.63), channel_id=1, source_target_pairs={{0,16},{2,18},{4,20},{6,22},{8,24},{10,26},{12,28},{14,30},{16,0},... | collective-permute-start | bytes 774152 | tf_op jit(solution)/shard_map/ppermute | solution.py:434
  38.6 19.5 %collective-permute-start.10 = (bf16[6,256,128]{2,1,0:T(8,128)(2,1)S(1)}, bf16[6,256,128]{2,1,0:T(8,128)(2,1)S(1)}, u32[]{:S(2)}, u32[]{:S(2)}) collective-permute-start(bf16[6,256,128]{2,1,0:T(8,128)(2,1)S(1)} %collective-permute-done.5.refs_3_), channel_id=1, source_target_pairs={{0,2},{2,0},{4,6},{6,4},{8,10},{10,8},{12,14},{14,12},{16,18},{18,... | collective-permute-start | bytes 1179656 | tf_op jit(solution)/shard_map/ppermute | solution.py:434
  41.0 14.3 %collective-permute-start.7 = (bf16[6,144,128]{2,1,0:T(8,128)(2,1)S(1)}, bf16[6,144,128]{2,1,0:T(8,128)(2,1)S(1)}, u32[]{:S(2)}, u32[]{:S(2)}) collective-permute-start(bf16[6,144,128]{2,1,0:T(8,128)(2,1)S(1)} %get-tuple-element.67), channel_id=1, source_target_pairs={{0,8},{2,10},{4,12},{6,14},{8,0},{10,2},{12,4},{14,6},{16,24},{18,... | collective-permute-start | bytes 663560 | tf_op jit(solution)/shard_map/ppermute | solution.py:434
  43.0 12.3 %collective-permute-start.11 = (bf16[3,256,128]{2,1,0:T(8,128)(2,1)S(1)}, bf16[3,256,128]{2,1,0:T(8,128)(2,1)S(1)}, u32[]{:S(2)}, u32[]{:S(2)}) collective-permute-start(bf16[3,256,128]{2,1,0:T(8,128)(2,1)S(1)} %get-tuple-element.76), channel_id=1, source_target_pairs={{0,4},{2,6},{4,0},{6,2},{8,12},{10,14},{12,8},{14,10},{16,20},{18,... | collective-permute-start | bytes 589832 | tf_op jit(solution)/shard_map/ppermute | solution.py:434
  46.8 9.9 %collective-permute-start.12 = (bf16[3,256,128]{2,1,0:T(8,128)(2,1)S(1)}, bf16[3,256,128]{2,1,0:T(8,128)(2,1)S(1)}, u32[]{:S(2)}, u32[]{:S(2)}) collective-permute-start(bf16[3,256,128]{2,1,0:T(8,128)(2,1)S(1)} %get-tuple-element.78), channel_id=1, source_target_pairs={{0,4},{2,6},{4,0},{6,2},{8,12},{10,14},{12,8},{14,10},{16,20},{18,... | collective-permute-start | bytes 589832 | tf_op jit(solution)/shard_map/ppermute | solution.py:434
  55.3 4.3 %collective-permute-start.13 = (bf16[6,256,128]{2,1,0:T(8,128)(2,1)S(1)}, bf16[6,256,128]{2,1,0:T(8,128)(2,1)S(1)}, u32[]{:S(2)}, u32[]{:S(2)}) collective-permute-start(bf16[6,256,128]{2,1,0:T(8,128)(2,1)S(1)} %get-tuple-element.75.refs_6_), channel_id=1, source_target_pairs={{0,2},{2,0},{4,6},{6,4},{8,10},{10,8},{12,14},{14,12},{16,18},{18,... | collective-permute-start | bytes 1179656 | tf_op jit(solution)/shard_map/ppermute | solution.py:434
  55.4 2.7 %collective-permute-start.14 = (bf16[3,256,128]{2,1,0:T(8,128)(2,1)S(1)}, bf16[3,256,128]{2,1,0:T(8,128)(2,1)S(1)}, u32[]{:S(2)}, u32[]{:S(2)}) collective-permute-start(bf16[3,256,128]{2,1,0:T(8,128)(2,1)S(1)} %collective-permute-done.11.refs_7_), channel_id=1, source_target_pairs={{0,2},{2,0},{4,6},{6,4},{8,10},{10,8},{12,14},{14,12},{16,18},{18,... | collective-permute-start | bytes 589832 | tf_op jit(solution)/shard_map/ppermute | solution.py:434
  55.9 13.3 %collective-permute-start.17 = (bf16[4,256,128]{2,1,0:T(8,128)(2,1)S(1)}, bf16[4,256,128]{2,1,0:T(8,128)(2,1)S(1)}, u32[]{:S(2)}, u32[]{:S(2)}) collective-permute-start(bf16[4,256,128]{2,1,0:T(8,128)(2,1)S(1)} %get-tuple-element.80.refs_13_.refs_10_), channel_id=1, source_target_pairs={{0,4},{2,6},{4,0},{6,2},{8,12},{10,14},{12,8},{14,10},{16,20},{18,... | collective-permute-start | bytes 786440 | tf_op jit(solution)/shard_map/ppermute | solution.py:434
  56.6 18.9 %collective-permute-start.16 = (bf16[8,256,128]{2,1,0:T(8,128)(2,1)S(1)}, bf16[8,256,128]{2,1,0:T(8,128)(2,1)S(1)}, u32[]{:S(2)}, u32[]{:S(2)}) collective-permute-start(bf16[8,256,128]{2,1,0:T(8,128)(2,1)S(1)} %get-tuple-element.88.refs_10_), channel_id=1, source_target_pairs={{0,4},{2,6},{4,0},{6,2},{8,12},{10,14},{12,8},{14,10},{16,20},{18,... | collective-permute-start | bytes 1572872 | tf_op jit(solution)/shard_map/ppermute | solution.py:434
  58.0 1.4 %collective-permute-start.15 = (bf16[3,256,128]{2,1,0:T(8,128)(2,1)S(1)}, bf16[3,256,128]{2,1,0:T(8,128)(2,1)S(1)}, u32[]{:S(2)}, u32[]{:S(2)}) collective-permute-start(bf16[3,256,128]{2,1,0:T(8,128)(2,1)S(1)} %collective-permute-done.12.refs_8_), channel_id=1, source_target_pairs={{0,2},{2,0},{4,6},{6,4},{8,10},{10,8},{12,14},{14,12},{16,18},{18,... | collective-permute-start | bytes 589832 | tf_op jit(solution)/shard_map/ppermute | solution.py:434
  58.0 6.4 %collective-permute-start.9 = (bf16[3,144,128]{2,1,0:T(8,128)(2,1)S(1)}, bf16[3,144,128]{2,1,0:T(8,128)(2,1)S(1)}, u32[]{:S(2)}, u32[]{:S(2)}) collective-permute-start(bf16[3,144,128]{2,1,0:T(8,128)(2,1)S(1)} %get-tuple-element.74), channel_id=1, source_target_pairs={{0,8},{2,10},{4,12},{6,14},{8,0},{10,2},{12,4},{14,6},{16,24},{18,... | collective-permute-start | bytes 331784 | tf_op jit(solution)/shard_map/ppermute | solution.py:434
  59.5 10.4 %collective-permute-start.18 = (bf16[4,256,128]{2,1,0:T(8,128)(2,1)S(1)}, bf16[4,256,128]{2,1,0:T(8,128)(2,1)S(1)}, u32[]{:S(2)}, u32[]{:S(2)}) collective-permute-start(bf16[4,256,128]{2,1,0:T(8,128)(2,1)S(1)} %get-tuple-element.80.refs_13_.refs_10_), channel_id=1, source_target_pairs={{0,2},{2,0},{4,6},{6,4},{8,10},{10,8},{12,14},{14,12},{16,18},{18,... | collective-permute-start | bytes 786440 | tf_op jit(solution)/shard_map/ppermute | solution.py:434
  69.3 1.6 %collective-permute-start.19 = (bf16[4,256,128]{2,1,0:T(8,128)(2,1)S(1)}, bf16[4,256,128]{2,1,0:T(8,128)(2,1)S(1)}, u32[]{:S(2)}, u32[]{:S(2)}) collective-permute-start(bf16[4,256,128]{2,1,0:T(8,128)(2,1)S(1)} %collective-permute-done.17.refs_11_), channel_id=1, source_target_pairs={{0,2},{2,0},{4,6},{6,4},{8,10},{10,8},{12,14},{14,12},{16,18},{18,... | collective-permute-start | bytes 786440 | tf_op jit(solution)/shard_map/ppermute | solution.py:434
  69.7 6.0 %collective-permute-start.20 = (bf16[8,256,128]{2,1,0:T(8,128)(2,1)S(1)}, bf16[8,256,128]{2,1,0:T(8,128)(2,1)S(1)}, u32[]{:S(2)}, u32[]{:S(2)}) collective-permute-start(bf16[8,256,128]{2,1,0:T(8,128)(2,1)S(1)} %get-tuple-element.88.refs_10_), channel_id=1, source_target_pairs={{0,2},{2,0},{4,6},{6,4},{8,10},{10,8},{12,14},{14,12},{16,18},{18,... | collective-permute-start | bytes 1572872 | tf_op jit(solution)/shard_map/ppermute | solution.py:434
  75.5 1.9 %collective-permute-start.21 = (bf16[8,256,128]{2,1,0:T(8,128)(2,1)S(1)}, bf16[8,256,128]{2,1,0:T(8,128)(2,1)S(1)}, u32[]{:S(2)}, u32[]{:S(2)}) collective-permute-start(bf16[8,256,128]{2,1,0:T(8,128)(2,1)S(1)} %collective-permute-done.16.refs_11_), channel_id=1, source_target_pairs={{0,2},{2,0},{4,6},{6,4},{8,10},{10,8},{12,14},{14,12},{16,18},{18,... | collective-permute-start | bytes 1572872 | tf_op jit(solution)/shard_map/ppermute | solution.py:434
  81.8 11.9 %collective-permute-start.25 = (bf16[128,384]{1,0:T(8,128)(2,1)S(1)}, bf16[128,384]{1,0:T(8,128)(2,1)S(1)}, u32[]{:S(2)}, u32[]{:S(2)}) collective-permute-start(bf16[128,384]{1,0:T(8,128)(2,1)S(1)} %get-tuple-element.100), channel_id=1, source_target_pairs={{0,8},{2,10},{4,12},{6,14},{8,0},{10,2},{12,4},{14,6},{16,24},{18,... | collective-permute-start | bytes 294920 | tf_op jit(solution)/shard_map/ppermute | solution.py:434
  82.5 12.9 %collective-permute-start.26 = (bf16[128,384]{1,0:T(8,128)(2,1)S(1)}, bf16[128,384]{1,0:T(8,128)(2,1)S(1)}, u32[]{:S(2)}, u32[]{:S(2)}) collective-permute-start(bf16[128,384]{1,0:T(8,128)(2,1)S(1)} %get-tuple-element.101), channel_id=1, source_target_pairs={{0,16},{2,18},{4,20},{6,22},{8,24},{10,26},{12,28},{14,30},{16,0},... | collective-permute-start | bytes 294920 | tf_op jit(solution)/shard_map/ppermute | solution.py:434
  85.2 10.2 %collective-permute-start.27 = (bf16[128,384]{1,0:T(8,128)(2,1)S(1)}, bf16[128,384]{1,0:T(8,128)(2,1)S(1)}, u32[]{:S(2)}, u32[]{:S(2)}) collective-permute-start(bf16[128,384]{1,0:T(8,128)(2,1)S(1)} %get-tuple-element.102), channel_id=1, source_target_pairs={{0,24},{2,26},{4,28},{6,30},{8,16},{10,18},{12,20},{14,22},{16,8},... | collective-permute-start | bytes 294920 | tf_op jit(solution)/shard_map/ppermute | solution.py:434
  90.9 7.6 %collective-permute-start.24 = (bf16[128,384]{1,0:T(8,128)(2,1)S(1)}, bf16[128,384]{1,0:T(8,128)(2,1)S(1)}, u32[]{:S(2)}, u32[]{:S(2)}) collective-permute-start(bf16[128,384]{1,0:T(8,128)(2,1)S(1)} %get-tuple-element.99), channel_id=1, source_target_pairs={{0,24},{2,26},{4,28},{6,30},{8,16},{10,18},{12,20},{14,22},{16,8},... | collective-permute-start | bytes 294920 | tf_op jit(solution)/shard_map/ppermute | solution.py:434
  93.7 5.6 %collective-permute-start.22 = (bf16[128,384]{1,0:T(8,128)(2,1)S(1)}, bf16[128,384]{1,0:T(8,128)(2,1)S(1)}, u32[]{:S(2)}, u32[]{:S(2)}) collective-permute-start(bf16[128,384]{1,0:T(8,128)(2,1)S(1)} %get-tuple-element.97), channel_id=1, source_target_pairs={{0,8},{2,10},{4,12},{6,14},{8,0},{10,2},{12,4},{14,6},{16,24},{18,... | collective-permute-start | bytes 294920 | tf_op jit(solution)/shard_map/ppermute | solution.py:434
  93.7 9.2 %collective-permute-start.23 = (bf16[128,384]{1,0:T(8,128)(2,1)S(1)}, bf16[128,384]{1,0:T(8,128)(2,1)S(1)}, u32[]{:S(2)}, u32[]{:S(2)}) collective-permute-start(bf16[128,384]{1,0:T(8,128)(2,1)S(1)} %get-tuple-element.98), channel_id=1, source_target_pairs={{0,16},{2,18},{4,20},{6,22},{8,24},{10,26},{12,28},{14,30},{16,0},... | collective-permute-start | bytes 294920 | tf_op jit(solution)/shard_map/ppermute | solution.py:434
  96.2 9.6 %collective-permute-start.29 = (bf16[128,1536]{1,0:T(8,128)(2,1)S(1)}, bf16[128,1536]{1,0:T(8,128)(2,1)S(1)}, u32[]{:S(2)}, u32[]{:S(2)}) collective-permute-start(bf16[128,1536]{1,0:T(8,128)(2,1)S(1)} %shard_map.89), channel_id=1, source_target_pairs={{0,1},{1,0},{2,3},{3,2},{4,5},{5,4},{6,7},{7,6},{8,9},{9,8},{10,11... | collective-permute-start | bytes 1179656 | tf_op jit(solution)/shard_map/ppermute | solution.py:431
  103.7 10.6 %collective-permute-start.28 = (bf16[128,1536]{1,0:T(8,128)(2,1)S(1)}, bf16[128,1536]{1,0:T(8,128)(2,1)S(1)}, u32[]{:S(2)}, u32[]{:S(2)}) collective-permute-start(bf16[128,1536]{1,0:T(8,128)(2,1)S(1)} %shard_map.91), channel_id=1, source_target_pairs={{0,1},{1,0},{2,3},{3,2},{4,5},{5,4},{6,7},{7,6},{8,9},{9,8},{10,11... | collective-permute-start | bytes 1179656 | tf_op jit(solution)/shard_map/ppermute | solution.py:431

commit v9 on v8

--- a/solution.py
+++ b/solution.py
@@ -11,6 +11,7 @@
 HEAD_DIM = 128
 BLOCK = 128
 Z, X, C = 4, 2, 2
+RETURN_ORDER = (0, 3, 2, 1)
 MIB = 1 << 20
 BF16, F32 = jnp.bfloat16, jnp.float32
 LIGHT = pl.CostEstimate(flops=1024, bytes_accessed=1024, transcendentals=0)
@@ -338,14 +339,14 @@
 
     def body(s, w_ref, fence_ref, out, sems):
         copies = []
-        for dz in range(Z):
+        for row, dz in enumerate(RETURN_ORDER):
             rows = pl.ds(pl.multiple_of((s[1] ^ dz) * group, group), group)
             for part in range(2):
                 columns = pl.ds(pl.multiple_of((1 - s[0] if part == 0 else s[0]) * half, half), half)
                 copies.append(
                     pltpu.make_async_copy(
                         w_ref.at[rows, columns],
-                        out.at[pl.ds(dz * group, group), pl.ds(part * half, half)],
+                        out.at[pl.ds(row * group, group), pl.ds(part * half, half)],
                         sems.at[len(copies)],
                     )
                 )
@@ -593,7 +594,7 @@
             fences,
         )
         fences = [done[0]]
-        back = [done[0]] + [over(done[dz], dz, 0, 0) for dz in range(1, Z)]
+        back = [done[0]] + [over(done[dz], dz, 0, 0) for dz in RETURN_ORDER[1:]]
         if arrived:
             back[-1] = after(back[-1], homes[0])
         away = mix(back, out_held, 0)

time: 115 us -> 115 us (level)
  transfers between devices with their start and end apart: 30 -> 30, of which waited for: 13 -> 11; matrix products, arithmetic and copies ran while one was open for 1% -> 1% of each run, Pallas kernels for 42% -> 43%
where the time goes in v9:
time: 115 us
  Pallas kernels  54.3 us (47%)
  starting transfers between devices  32.2 us (28%)
  waiting for transfers between devices  27 us (23%)
    ppermute x26, starting transfers between devices, over(): return lax.ppermute(a, 'ctx', hop(dz, dx, dc))  26.9 us
    pallas_call x5, Pallas kernels, attend(): pl.pallas_call(body, grid=(count,), in_specs=whole(total_arrays) + [pl.Bl...  23 us
    ppermute x26, waiting for transfers between devices, over(): return lax.ppermute(a, 'ctx', hop(dz, dx, dc))  18.2 us
    pallas_call x2, Pallas kernels, fetch(): pl.pallas_call(body, grid_spec=pltpu.PrefetchScalarGridSpec(num_scalar_pr...  14.2 us
    ppermute x4, waiting for transfers between devices, over_y(): return lax.ppermute(a, 'head', [(0, 1), (1, 0)])  8.77 us
    pallas_call x4, Pallas kernels, project(): pl.pallas_call(body, in_specs=whole(3 + len(more)), out_specs=whole(len(o...  7.08 us
    ppermute x4, starting transfers between devices, over_y(): return lax.ppermute(a, 'head', [(0, 1), (1, 0)])  5.35 us
    pallas_call x1, Pallas kernels, fetch_out(): pl.pallas_call(body, grid_spec=pltpu.PrefetchScalarGridSpec(num_scalar_pr...  4.33 us
  transfers between devices with their start and end apart: 30, of which 11 were waited for; matrix products, arithmetic and copies ran while one was open for 1% of the time, Pallas kernels for 43%

profile of v9, /device:TPU:0, one launch (start us, length us, event | category | flops | bytes accessed | tf_op | source)
XLA Modules:
  0.0 115.0 jit_solution(10292511622270053644)
XLA Ops:
  0.0 3.0 %collective-permute-start = (bf16[256,1536]{1,0:T(8,128)(2,1)}, bf16[256,1536]{1,0:T(8,128)(2,1)S(1)}, u32[]{:S(2)}, u32[]{:S(2)}) collective-permute-start(bf16[256,1536]{1,0:T(8,128)(2,1)} %refs_0_.7), channel_id=1, source_target_pairs={{0,1},{1,0},{2,3},{3,2},{4,5},{5,4},{6,7},{7,6},{8,9},{9,8},{10,11... | collective-permute-start | bytes 2359304 | tf_op jit(solution)/shard_map/ppermute | solution.py:432
  3.0 1.1 slice.3
  4.0 2.7 %collective-permute-start.2 = (bf16[144,1536]{1,0:T(8,128)(2,1)S(1)}, bf16[144,1536]{1,0:T(8,128)(2,1)S(1)}, u32[]{:S(2)}, u32[]{:S(2)}) collective-permute-start(bf16[144,1536]{1,0:T(8,128)(2,1)S(1)} %slice.3), channel_id=1, source_target_pairs={{0,16},{2,18},{4,20},{6,22},{8,24},{10,26},{12,28},{14,30},{16,0},... | collective-permute-start | bytes 1327112 | tf_op jit(solution)/shard_map/ppermute | solution.py:435
  6.8 5.8 %shard_map.73.refs_5_.refs_2_ = bf16[6,3072,384]{2,1,0:T(8,128)(2,1)S(1)} custom-call(s32[4]{0:T(128)S(1)} %pad_add_fusion.s.refs_3_, bf16[3072,1536]{1,0:T(8,128)(2,1)} %refs_0_.4, bf16[3072,1536]{1,0:T(8,128)(2,1)} %refs_1_.3, bf16[3072,1536]{1,0:T(8,128)(2,1)} %refs_2_.3, s32[4]{0:T(128)S(1)} %pad_add_fusion.s.refs_3_), custom_call_target="tpu_custom_call" | custom-call | flops 1024 | bytes 1024 | tf_op jit(solution)/shard_map/pallas_call | solution.py:81
  12.6 8.3 %shard_map.74 = (bf16[6,3072,384]{2,1,0:T(8,128)(2,1)S(1)}, f32[6,256,384]{2,1,0:T(8,128)S(1)}) custom-call(s32[4]{0:T(128)S(1)} %pad_add_fusion.s.refs_3_, bf16[3072,1536]{1,0:T(8,128)(2,1)} %refs_0_.4, bf16[3072,1536]{1,0:T(8,128)(2,1)} %refs_1_.3, bf16[3072,1536]{1,0:T(8,128)(2,1)} %refs_2_.3, s32[4]{0:T(128)S(1)} %pad_add_fusion.s.refs_3_, ...), custom_call_target="tpu_custom_call" | custom-call | flops 1024 | bytes 1024 | tf_op jit(solution)/shard_map/pallas_call | solution.py:81
  21.0 1.9 %shard_map.75 = (bf16[6,256,128]{2,1,0:T(8,128)(2,1)S(1)}, bf16[9,256,128]{2,1,0:T(8,128)(2,1)S(1)}) custom-call(bf16[256,1536]{1,0:T(8,128)(2,1)S(1)} %copy-done, bf16[256,1536]{1,0:T(8,128)(2,1)S(1)} %collective-permute-done.refs_1_, bf16[6,3072,384]{2,1,0:T(8,128)(2,1)S(1)} %shard_map.73.refs_5_.refs_2_, f32[6,256,384]{2,1,0:T(8,128)S(1)} %get-tuple-element.58.refs_3_), custom_call_target="tpu_custom_call" | custom-call | flops 1024 | bytes 1024 | tf_op jit(solution)/shard_map/pallas_call | solution.py:126
  22.9 1.6 %collective-permute-start.3 = (bf16[9,256,128]{2,1,0:T(8,128)(2,1)S(1)}, bf16[9,256,128]{2,1,0:T(8,128)(2,1)S(1)}, u32[]{:S(2)}, u32[]{:S(2)}) collective-permute-start(bf16[9,256,128]{2,1,0:T(8,128)(2,1)S(1)} %get-tuple-element.60), channel_id=1, source_target_pairs={{0,8},{2,10},{4,12},{6,14},{8,0},{10,2},{12,4},{14,6},{16,24},{18,... | collective-permute-start | bytes 1769480 | tf_op jit(solution)/shard_map/ppermute | solution.py:435
  24.5 1.5 %collective-permute-start.5 = (bf16[6,256,128]{2,1,0:T(8,128)(2,1)S(1)}, bf16[6,256,128]{2,1,0:T(8,128)(2,1)S(1)}, u32[]{:S(2)}, u32[]{:S(2)}) collective-permute-start(bf16[6,256,128]{2,1,0:T(8,128)(2,1)S(1)} %get-tuple-element.59.refs_2_), channel_id=1, source_target_pairs={{0,4},{2,6},{4,0},{6,2},{8,12},{10,14},{12,8},{14,10},{16,20},{18,... | collective-permute-start | bytes 1179656 | tf_op jit(solution)/shard_map/ppermute | solution.py:435
  26.2 1.2 %collective-permute-start.4 = (bf16[144,1536]{1,0:T(8,128)(2,1)S(1)}, bf16[144,1536]{1,0:T(8,128)(2,1)S(1)}, u32[]{:S(2)}, u32[]{:S(2)}) collective-permute-start(bf16[144,1536]{1,0:T(8,128)(2,1)S(1)} %collective-permute-done.2.refs_0_), channel_id=1, source_target_pairs={{0,1},{1,0},{2,3},{3,2},{4,5},{5,4},{6,7},{7,6},{8,9},{9,8},{10,11... | collective-permute-start | bytes 1327112 | tf_op jit(solution)/shard_map/ppermute | solution.py:432
  27.5 2.3 %shard_map.76 = (bf16[9,112,128]{2,1,0:T(8,128)(2,1)S(1)}, bf16[9,112,128]{2,1,0:T(8,128)(2,1)S(1)}) custom-call(bf16[256,1536]{1,0:T(8,128)(2,1)S(1)} %copy-done, bf16[256,1536]{1,0:T(8,128)(2,1)S(1)} %collective-permute-done.refs_1_, bf16[6,3072,384]{2,1,0:T(8,128)(2,1)S(1)} %get-tuple-element.56.refs_2_), custom_call_target="tpu_custom_call" | custom-call | flops 1024 | bytes 1024 | tf_op jit(solution)/shard_map/pallas_call | solution.py:126
  29.8 2.8 %collective-permute-start.8 = (bf16[9,112,128]{2,1,0:T(8,128)(2,1)S(1)}, bf16[9,112,128]{2,1,0:T(8,128)(2,1)S(1)}, u32[]{:S(2)}, u32[]{:S(2)}) collective-permute-start(bf16[9,112,128]{2,1,0:T(8,128)(2,1)S(1)} %get-tuple-element.71), channel_id=1, source_target_pairs={{0,24},{2,26},{4,28},{6,30},{8,16},{10,18},{12,20},{14,22},{16,8},... | collective-permute-start | bytes 774152 | tf_op jit(solution)/shard_map/ppermute | solution.py:435
  32.6 0.6 shard_map.77.refs_0_
  33.2 1.1 shard_map.78.fence_ref.refs_12_.refs_14_.refs_18_
  34.2 4.3 %shard_map.79.refs_4_ = bf16[1536,3072]{1,0:T(8,128)(2,1)S(1)} custom-call(s32[4]{0:T(128)S(1)} %pad_add_fusion.s.refs_3_, bf16[1536,3072]{1,0:T(8,128)(2,1)} %w_ref.1, f32[8,4096]{1,0:T(8,128)S(1)} %shard_map.78.fence_ref.refs_12_.refs_14_.refs_18_), custom_call_target="tpu_custom_call" | custom-call | flops 1024 | bytes 1024 | tf_op jit(solution)/shard_map/pallas_call | solution.py:358
  38.7 2.4 %shard_map.80 = (bf16[3,144,128]{2,1,0:T(8,128)(2,1)S(1)}, bf16[6,144,128]{2,1,0:T(8,128)(2,1)S(1)}, bf16[9,144,128]{2,1,0:T(8,128)(2,1)S(1)}) custom-call(bf16[144,1536]{1,0:T(8,128)(2,1)S(1)} %collective-permute-done.2.refs_0_, bf16[144,1536]{1,0:T(8,128)(2,1)S(1)} %collective-permute-done.4.refs_1_, bf16[6,3072,384]{2,1,0:T(8,128)(2,1)S(1)} %shard_map.73.refs_5_.refs_2_), custom_call_target="tpu_custom_call" | custom-call | flops 1024 | bytes 1024 | tf_op jit(solution)/shard_map/pallas_call | solution.py:126
  41.0 1.7 %collective-permute-start.7 = (bf16[6,144,128]{2,1,0:T(8,128)(2,1)S(1)}, bf16[6,144,128]{2,1,0:T(8,128)(2,1)S(1)}, u32[]{:S(2)}, u32[]{:S(2)}) collective-permute-start(bf16[6,144,128]{2,1,0:T(8,128)(2,1)S(1)} %get-tuple-element.67), channel_id=1, source_target_pairs={{0,8},{2,10},{4,12},{6,14},{8,0},{10,2},{12,4},{14,6},{16,24},{18,... | collective-permute-start | bytes 663560 | tf_op jit(solution)/shard_map/ppermute | solution.py:435
  43.0 3.4 %collective-permute-start.11 = (bf16[3,256,128]{2,1,0:T(8,128)(2,1)S(1)}, bf16[3,256,128]{2,1,0:T(8,128)(2,1)S(1)}, u32[]{:S(2)}, u32[]{:S(2)}) collective-permute-start(bf16[3,256,128]{2,1,0:T(8,128)(2,1)S(1)} %get-tuple-element.76), channel_id=1, source_target_pairs={{0,4},{2,6},{4,0},{6,2},{8,12},{10,14},{12,8},{14,10},{16,20},{18,... | collective-permute-start | bytes 589832 | tf_op jit(solution)/shard_map/ppermute | solution.py:435
  46.5 0.3 collective-permute-done.8.refs_3_.refs_1_
  46.8 1.5 %collective-permute-start.12 = (bf16[3,256,128]{2,1,0:T(8,128)(2,1)S(1)}, bf16[3,256,128]{2,1,0:T(8,128)(2,1)S(1)}, u32[]{:S(2)}, u32[]{:S(2)}) collective-permute-start(bf16[3,256,128]{2,1,0:T(8,128)(2,1)S(1)} %get-tuple-element.78), channel_id=1, source_target_pairs={{0,4},{2,6},{4,0},{6,2},{8,12},{10,14},{12,8},{14,10},{16,20},{18,... | collective-permute-start | bytes 589832 | tf_op jit(solution)/shard_map/ppermute | solution.py:435
  48.3 7.1 %collective-permute-done.6.refs_1_ = bf16[9,112,128]{2,1,0:T(8,128)(2,1)S(1)} collective-permute-done((bf16[9,112,128]{2,1,0:T(8,128)(2,1)S(1)}, bf16[9,112,128]{2,1,0:T(8,128)(2,1)S(1)}, u32[]{:S(2)}, u32[]{:S(2)}) %collective-permute-start.6) | collective-permute-done | bytes 258080 | tf_op jit(solution)/shard_map/ppermute | solution.py:435
  55.4 0.5 collective-permute-start.14
  55.9 0.7 collective-permute-start.17
  56.6 1.4 %collective-permute-start.16 = (bf16[8,256,128]{2,1,0:T(8,128)(2,1)S(1)}, bf16[8,256,128]{2,1,0:T(8,128)(2,1)S(1)}, u32[]{:S(2)}, u32[]{:S(2)}) collective-permute-start(bf16[8,256,128]{2,1,0:T(8,128)(2,1)S(1)} %get-tuple-element.88.refs_10_), channel_id=1, source_target_pairs={{0,4},{2,6},{4,0},{6,2},{8,12},{10,14},{12,8},{14,10},{16,20},{18,... | collective-permute-start | bytes 1572872 | tf_op jit(solution)/shard_map/ppermute | solution.py:435
  58.1 1.4 %collective-permute-done.15.refs_11_ = bf16[3,256,128]{2,1,0:T(8,128)(2,1)S(1)} collective-permute-done((bf16[3,256,128]{2,1,0:T(8,128)(2,1)S(1)}, bf16[3,256,128]{2,1,0:T(8,128)(2,1)S(1)}, u32[]{:S(2)}, u32[]{:S(2)}) %collective-permute-start.15) | collective-permute-done | bytes 196640 | tf_op jit(solution)/shard_map/ppermute | solution.py:435
  59.6 4.8 %shard_map.83 = (f32[3,512,128]{2,1,0:T(8,128)S(1)}, f32[3,512,128]{2,1,0:T(8,128)S(1)}, f32[3,512,128]{2,1,0:T(8,128)S(1)}) custom-call(bf16[3,256,128]{2,1,0:T(8,128)(2,1)S(1)} %shard_map.77.refs_0_, bf16[9,256,128]{2,1,0:T(8,128)(2,1)S(1)} %collective-permute-done.3.in_ref.refs_1_, bf16[6,256,128]{2,1,0:T(8,128)(2,1)S(1)} %get-tuple-element.59.refs_2_, ...), custom_call_target="tpu_custom_call" | custom-call | flops 1024 | bytes 1024 | tf_op jit(solution)/shard_map/pallas_call | solution.py:323
  64.4 4.8 %shard_map.85 = (f32[3,512,128]{2,1,0:T(8,128)S(1)}, f32[3,512,128]{2,1,0:T(8,128)S(1)}, f32[3,512,128]{2,1,0:T(8,128)S(1)}) custom-call(bf16[3,256,128]{2,1,0:T(8,128)(2,1)S(1)} %get-tuple-element.73.refs_0_.refs_5_.refs_2_, bf16[3,256,128]{2,1,0:T(8,128)(2,1)S(1)} %shard_map.84.refs_1_.refs_6_.refs_3_, bf16[6,256,128]{2,1,0:T(8,128)(2,1)S(1)} %get-tuple-element.59.refs_2_, ...), custom_call_target="tpu_custom_call" | custom-call | flops 1024 | bytes 1024 | tf_op jit(solution)/shard_map/pallas_call | solution.py:323
  69.3 0.4 collective-permute-start.19
  69.8 1.0 collective-permute-done.19.refs_13_
  70.9 4.4 %shard_map.86 = (bf16[256,128]{1,0:T(8,128)(2,1)S(1)}, bf16[256,128]{1,0:T(8,128)(2,1)S(1)}, bf16[256,128]{1,0:T(8,128)(2,1)S(1)}, bf16[256,128]{1,0:T(8,128)(2,1)S(1)}) custom-call(bf16[3,256,128]{2,1,0:T(8,128)(2,1)S(1)} %shard_map.77.refs_0_, bf16[9,256,128]{2,1,0:T(8,128)(2,1)S(1)} %collective-permute-done.3.in_ref.refs_1_, ...), custom_call_target="tpu_custom_call" | custom-call | flops 1024 | bytes 1024 | tf_op jit(solution)/shard_map/pallas_call | solution.py:323
  75.3 0.2 collective-permute-done.16.refs_11_
  75.7 1.7 %collective-permute-done.21.refs_13_ = bf16[8,256,128]{2,1,0:T(8,128)(2,1)S(1)} collective-permute-done((bf16[8,256,128]{2,1,0:T(8,128)(2,1)S(1)}, bf16[8,256,128]{2,1,0:T(8,128)(2,1)S(1)}, u32[]{:S(2)}, u32[]{:S(2)}) %collective-permute-start.21) | collective-permute-done | bytes 524320 | tf_op jit(solution)/shard_map/ppermute | solution.py:435
  77.4 4.4 %shard_map.87 = (bf16[128,384]{1,0:T(8,128)(2,1)S(1)}, bf16[128,384]{1,0:T(8,128)(2,1)S(1)}, bf16[128,384]{1,0:T(8,128)(2,1)S(1)}, bf16[128,384]{1,0:T(8,128)(2,1)S(1)}) custom-call(bf16[3,256,128]{2,1,0:T(8,128)(2,1)S(1)} %shard_map.77.refs_0_, bf16[9,256,128]{2,1,0:T(8,128)(2,1)S(1)} %collective-permute-done.3.in_ref.refs_1_, ...), custom_call_target="tpu_custom_call" | custom-call | flops 1024 | bytes 1024 | tf_op jit(solution)/shard_map/pallas_call | solution.py:323
  81.8 2.8 %collective-permute-start.25 = (bf16[128,384]{1,0:T(8,128)(2,1)S(1)}, bf16[128,384]{1,0:T(8,128)(2,1)S(1)}, u32[]{:S(2)}, u32[]{:S(2)}) collective-permute-start(bf16[128,384]{1,0:T(8,128)(2,1)S(1)} %get-tuple-element.100), channel_id=1, source_target_pairs={{0,24},{2,26},{4,28},{6,30},{8,16},{10,18},{12,20},{14,22},{16,8},... | collective-permute-start | bytes 294920 | tf_op jit(solution)/shard_map/ppermute | solution.py:435
  84.6 1.7 %collective-permute-start.27 = (bf16[128,384]{1,0:T(8,128)(2,1)S(1)}, bf16[128,384]{1,0:T(8,128)(2,1)S(1)}, u32[]{:S(2)}, u32[]{:S(2)}) collective-permute-start(bf16[128,384]{1,0:T(8,128)(2,1)S(1)} %get-tuple-element.102), channel_id=1, source_target_pairs={{0,8},{2,10},{4,12},{6,14},{8,0},{10,2},{12,4},{14,6},{16,24},{18,... | collective-permute-start | bytes 294920 | tf_op jit(solution)/shard_map/ppermute | solution.py:435
  86.3 4.6 %shard_map.88 = (bf16[128,384]{1,0:T(8,128)(2,1)S(1)}, bf16[128,384]{1,0:T(8,128)(2,1)S(1)}, bf16[128,384]{1,0:T(8,128)(2,1)S(1)}, bf16[128,384]{1,0:T(8,128)(2,1)S(1)}) custom-call(bf16[3,256,128]{2,1,0:T(8,128)(2,1)S(1)} %shard_map.77.refs_0_, bf16[9,256,128]{2,1,0:T(8,128)(2,1)S(1)} %collective-permute-done.3.in_ref.refs_1_, ...), custom_call_target="tpu_custom_call" | custom-call | flops 1024 | bytes 1024 | tf_op jit(solution)/shard_map/pallas_call | solution.py:323
  90.9 0.4 collective-permute-start.24
  91.3 2.4 %collective-permute-start.22 = (bf16[128,384]{1,0:T(8,128)(2,1)S(1)}, bf16[128,384]{1,0:T(8,128)(2,1)S(1)}, u32[]{:S(2)}, u32[]{:S(2)}) collective-permute-start(bf16[128,384]{1,0:T(8,128)(2,1)S(1)} %get-tuple-element.97), channel_id=1, source_target_pairs={{0,24},{2,26},{4,28},{6,30},{8,16},{10,18},{12,20},{14,22},{16,8},... | collective-permute-start | bytes 294920 | tf_op jit(solution)/shard_map/ppermute | solution.py:435
  93.8 0.7 collective-permute-start.23
  94.5 0.8 shard_map.89
  95.3 0.6 collective-permute-start.29
  95.9 0.8 shard_map.90.refs_0_
  96.8 2.5 %collective-permute-done.22.refs_1_ = bf16[128,384]{1,0:T(8,128)(2,1)S(1)} collective-permute-done((bf16[128,384]{1,0:T(8,128)(2,1)S(1)}, bf16[128,384]{1,0:T(8,128)(2,1)S(1)}, u32[]{:S(2)}, u32[]{:S(2)}) %collective-permute-start.22) | collective-permute-done | bytes 98336 | tf_op jit(solution)/shard_map/ppermute | solution.py:435
  99.3 3.5 %collective-permute-done.23.refs_2_ = bf16[128,384]{1,0:T(8,128)(2,1)S(1)} collective-permute-done((bf16[128,384]{1,0:T(8,128)(2,1)S(1)}, bf16[128,384]{1,0:T(8,128)(2,1)S(1)}, u32[]{:S(2)}, u32[]{:S(2)}) %collective-permute-start.23) | collective-permute-done | bytes 98336 | tf_op jit(solution)/shard_map/ppermute | solution.py:435
  102.8 0.9 shard_map.91
  103.7 0.6 collective-permute-start.28
  104.3 0.8 shard_map.92.refs_0_
  105.2 8.8 %collective-permute-done.28.refs_1_ = bf16[128,1536]{1,0:T(8,128)(2,1)S(1)} collective-permute-done((bf16[128,1536]{1,0:T(8,128)(2,1)S(1)}, bf16[128,1536]{1,0:T(8,128)(2,1)S(1)}, u32[]{:S(2)}, u32[]{:S(2)}) %collective-permute-start.28) | collective-permute-done | bytes 393248 | tf_op jit(solution)/shard_map/ppermute | solution.py:432
  114.0 1.0 shard_map.94
  (42 shorter events, 1.4 us)
Async XLA Ops:
  0.0 21.0 %collective-permute-start = (bf16[256,1536]{1,0:T(8,128)(2,1)}, bf16[256,1536]{1,0:T(8,128)(2,1)S(1)}, u32[]{:S(2)}, u32[]{:S(2)}) collective-permute-start(bf16[256,1536]{1,0:T(8,128)(2,1)} %refs_0_.7), channel_id=1, source_target_pairs={{0,1},{1,0},{2,3},{3,2},{4,5},{5,4},{6,7},{7,6},{8,9},{9,8},{10,11... | collective-permute-start | bytes 2359304 | tf_op jit(solution)/shard_map/ppermute | solution.py:432
  4.0 22.2 %collective-permute-start.2 = (bf16[144,1536]{1,0:T(8,128)(2,1)S(1)}, bf16[144,1536]{1,0:T(8,128)(2,1)S(1)}, u32[]{:S(2)}, u32[]{:S(2)}) collective-permute-start(bf16[144,1536]{1,0:T(8,128)(2,1)S(1)} %slice.3), channel_id=1, source_target_pairs={{0,16},{2,18},{4,20},{6,22},{8,24},{10,26},{12,28},{14,30},{16,0},... | collective-permute-start | bytes 1327112 | tf_op jit(solution)/shard_map/ppermute | solution.py:435
  6.8 5.9 %copy-start = (bf16[256,1536]{1,0:T(8,128)(2,1)S(1)}, bf16[256,1536]{1,0:T(8,128)(2,1)}, u32[]{:S(2)}) copy-start(bf16[256,1536]{1,0:T(8,128)(2,1)} %refs_0_.7) | copy-start | bytes 2359300
  22.9 20.1 %collective-permute-start.3 = (bf16[9,256,128]{2,1,0:T(8,128)(2,1)S(1)}, bf16[9,256,128]{2,1,0:T(8,128)(2,1)S(1)}, u32[]{:S(2)}, u32[]{:S(2)}) collective-permute-start(bf16[9,256,128]{2,1,0:T(8,128)(2,1)S(1)} %get-tuple-element.60), channel_id=1, source_target_pairs={{0,8},{2,10},{4,12},{6,14},{8,0},{10,2},{12,4},{14,6},{16,24},{18,... | collective-permute-start | bytes 1769480 | tf_op jit(solution)/shard_map/ppermute | solution.py:435
  24.5 8.1 %collective-permute-start.1 = (bf16[6,256,128]{2,1,0:T(8,128)(2,1)S(1)}, bf16[6,256,128]{2,1,0:T(8,128)(2,1)S(1)}, u32[]{:S(2)}, u32[]{:S(2)}) collective-permute-start(bf16[6,256,128]{2,1,0:T(8,128)(2,1)S(1)} %get-tuple-element.59.refs_2_), channel_id=1, source_target_pairs={{0,2},{2,0},{4,6},{6,4},{8,10},{10,8},{12,14},{14,12},{16,18},{18,... | collective-permute-start | bytes 1179656 | tf_op jit(solution)/shard_map/ppermute | solution.py:435
  24.5 14.1 %collective-permute-start.5 = (bf16[6,256,128]{2,1,0:T(8,128)(2,1)S(1)}, bf16[6,256,128]{2,1,0:T(8,128)(2,1)S(1)}, u32[]{:S(2)}, u32[]{:S(2)}) collective-permute-start(bf16[6,256,128]{2,1,0:T(8,128)(2,1)S(1)} %get-tuple-element.59.refs_2_), channel_id=1, source_target_pairs={{0,4},{2,6},{4,0},{6,2},{8,12},{10,14},{12,8},{14,10},{16,20},{18,... | collective-permute-start | bytes 1179656 | tf_op jit(solution)/shard_map/ppermute | solution.py:435
  26.2 12.4 %collective-permute-start.4 = (bf16[144,1536]{1,0:T(8,128)(2,1)S(1)}, bf16[144,1536]{1,0:T(8,128)(2,1)S(1)}, u32[]{:S(2)}, u32[]{:S(2)}) collective-permute-start(bf16[144,1536]{1,0:T(8,128)(2,1)S(1)} %collective-permute-done.2.refs_0_), channel_id=1, source_target_pairs={{0,1},{1,0},{2,3},{3,2},{4,5},{5,4},{6,7},{7,6},{8,9},{9,8},{10,11... | collective-permute-start | bytes 1327112 | tf_op jit(solution)/shard_map/ppermute | solution.py:432
  29.7 3.4 %copy-start.1 = (s32[32,32]{1,0:T(8,128)S(1)}, s32[32,32]{1,0:T(8,128)}, u32[]{:S(2)}) copy-start(s32[32,32]{1,0:T(8,128)} %mask_ref.1) | copy-start | bytes 12292
  29.8 3.4 %copy-start.2 = (s32[32]{0:T(128)S(1)}, s32[32]{0:T(128)}, u32[]{:S(2)}) copy-start(s32[32]{0:T(128)} %param.8) | copy-start | bytes 388
  29.8 17.0 %collective-permute-start.8 = (bf16[9,112,128]{2,1,0:T(8,128)(2,1)S(1)}, bf16[9,112,128]{2,1,0:T(8,128)(2,1)S(1)}, u32[]{:S(2)}, u32[]{:S(2)}) collective-permute-start(bf16[9,112,128]{2,1,0:T(8,128)(2,1)S(1)} %get-tuple-element.71), channel_id=1, source_target_pairs={{0,24},{2,26},{4,28},{6,30},{8,16},{10,18},{12,20},{14,22},{16,8},... | collective-permute-start | bytes 774152 | tf_op jit(solution)/shard_map/ppermute | solution.py:435
  32.6 22.8 %collective-permute-start.6 = (bf16[9,112,128]{2,1,0:T(8,128)(2,1)S(1)}, bf16[9,112,128]{2,1,0:T(8,128)(2,1)S(1)}, u32[]{:S(2)}, u32[]{:S(2)}) collective-permute-start(bf16[9,112,128]{2,1,0:T(8,128)(2,1)S(1)} %get-tuple-element.63), channel_id=1, source_target_pairs={{0,16},{2,18},{4,20},{6,22},{8,24},{10,26},{12,28},{14,30},{16,0},... | collective-permute-start | bytes 774152 | tf_op jit(solution)/shard_map/ppermute | solution.py:435
  38.6 19.5 %collective-permute-start.10 = (bf16[6,256,128]{2,1,0:T(8,128)(2,1)S(1)}, bf16[6,256,128]{2,1,0:T(8,128)(2,1)S(1)}, u32[]{:S(2)}, u32[]{:S(2)}) collective-permute-start(bf16[6,256,128]{2,1,0:T(8,128)(2,1)S(1)} %collective-permute-done.5.refs_3_), channel_id=1, source_target_pairs={{0,2},{2,0},{4,6},{6,4},{8,10},{10,8},{12,14},{14,12},{16,18},{18,... | collective-permute-start | bytes 1179656 | tf_op jit(solution)/shard_map/ppermute | solution.py:435
  41.0 14.3 %collective-permute-start.7 = (bf16[6,144,128]{2,1,0:T(8,128)(2,1)S(1)}, bf16[6,144,128]{2,1,0:T(8,128)(2,1)S(1)}, u32[]{:S(2)}, u32[]{:S(2)}) collective-permute-start(bf16[6,144,128]{2,1,0:T(8,128)(2,1)S(1)} %get-tuple-element.67), channel_id=1, source_target_pairs={{0,8},{2,10},{4,12},{6,14},{8,0},{10,2},{12,4},{14,6},{16,24},{18,... | collective-permute-start | bytes 663560 | tf_op jit(solution)/shard_map/ppermute | solution.py:435
  43.0 12.3 %collective-permute-start.11 = (bf16[3,256,128]{2,1,0:T(8,128)(2,1)S(1)}, bf16[3,256,128]{2,1,0:T(8,128)(2,1)S(1)}, u32[]{:S(2)}, u32[]{:S(2)}) collective-permute-start(bf16[3,256,128]{2,1,0:T(8,128)(2,1)S(1)} %get-tuple-element.76), channel_id=1, source_target_pairs={{0,4},{2,6},{4,0},{6,2},{8,12},{10,14},{12,8},{14,10},{16,20},{18,... | collective-permute-start | bytes 589832 | tf_op jit(solution)/shard_map/ppermute | solution.py:435
  46.8 9.9 %collective-permute-start.12 = (bf16[3,256,128]{2,1,0:T(8,128)(2,1)S(1)}, bf16[3,256,128]{2,1,0:T(8,128)(2,1)S(1)}, u32[]{:S(2)}, u32[]{:S(2)}) collective-permute-start(bf16[3,256,128]{2,1,0:T(8,128)(2,1)S(1)} %get-tuple-element.78), channel_id=1, source_target_pairs={{0,4},{2,6},{4,0},{6,2},{8,12},{10,14},{12,8},{14,10},{16,20},{18,... | collective-permute-start | bytes 589832 | tf_op jit(solution)/shard_map/ppermute | solution.py:435
  55.3 4.3 %collective-permute-start.13 = (bf16[6,256,128]{2,1,0:T(8,128)(2,1)S(1)}, bf16[6,256,128]{2,1,0:T(8,128)(2,1)S(1)}, u32[]{:S(2)}, u32[]{:S(2)}) collective-permute-start(bf16[6,256,128]{2,1,0:T(8,128)(2,1)S(1)} %get-tuple-element.75.refs_6_), channel_id=1, source_target_pairs={{0,2},{2,0},{4,6},{6,4},{8,10},{10,8},{12,14},{14,12},{16,18},{18,... | collective-permute-start | bytes 1179656 | tf_op jit(solution)/shard_map/ppermute | solution.py:435
  55.4 2.7 %collective-permute-start.14 = (bf16[3,256,128]{2,1,0:T(8,128)(2,1)S(1)}, bf16[3,256,128]{2,1,0:T(8,128)(2,1)S(1)}, u32[]{:S(2)}, u32[]{:S(2)}) collective-permute-start(bf16[3,256,128]{2,1,0:T(8,128)(2,1)S(1)} %collective-permute-done.11.refs_7_), channel_id=1, source_target_pairs={{0,2},{2,0},{4,6},{6,4},{8,10},{10,8},{12,14},{14,12},{16,18},{18,... | collective-permute-start | bytes 589832 | tf_op jit(solution)/shard_map/ppermute | solution.py:435
  55.9 13.3 %collective-permute-start.17 = (bf16[4,256,128]{2,1,0:T(8,128)(2,1)S(1)}, bf16[4,256,128]{2,1,0:T(8,128)(2,1)S(1)}, u32[]{:S(2)}, u32[]{:S(2)}) collective-permute-start(bf16[4,256,128]{2,1,0:T(8,128)(2,1)S(1)} %get-tuple-element.80.refs_13_.refs_10_), channel_id=1, source_target_pairs={{0,4},{2,6},{4,0},{6,2},{8,12},{10,14},{12,8},{14,10},{16,20},{18,... | collective-permute-start | bytes 786440 | tf_op jit(solution)/shard_map/ppermute | solution.py:435
  56.6 18.9 %collective-permute-start.16 = (bf16[8,256,128]{2,1,0:T(8,128)(2,1)S(1)}, bf16[8,256,128]{2,1,0:T(8,128)(2,1)S(1)}, u32[]{:S(2)}, u32[]{:S(2)}) collective-permute-start(bf16[8,256,128]{2,1,0:T(8,128)(2,1)S(1)} %get-tuple-element.88.refs_10_), channel_id=1, source_target_pairs={{0,4},{2,6},{4,0},{6,2},{8,12},{10,14},{12,8},{14,10},{16,20},{18,... | collective-permute-start | bytes 1572872 | tf_op jit(solution)/shard_map/ppermute | solution.py:435
  58.0 1.4 %collective-permute-start.15 = (bf16[3,256,128]{2,1,0:T(8,128)(2,1)S(1)}, bf16[3,256,128]{2,1,0:T(8,128)(2,1)S(1)}, u32[]{:S(2)}, u32[]{:S(2)}) collective-permute-start(bf16[3,256,128]{2,1,0:T(8,128)(2,1)S(1)} %collective-permute-done.12.refs_8_), channel_id=1, source_target_pairs={{0,2},{2,0},{4,6},{6,4},{8,10},{10,8},{12,14},{14,12},{16,18},{18,... | collective-permute-start | bytes 589832 | tf_op jit(solution)/shard_map/ppermute | solution.py:435
  58.0 6.4 %collective-permute-start.9 = (bf16[3,144,128]{2,1,0:T(8,128)(2,1)S(1)}, bf16[3,144,128]{2,1,0:T(8,128)(2,1)S(1)}, u32[]{:S(2)}, u32[]{:S(2)}) collective-permute-start(bf16[3,144,128]{2,1,0:T(8,128)(2,1)S(1)} %get-tuple-element.74), channel_id=1, source_target_pairs={{0,8},{2,10},{4,12},{6,14},{8,0},{10,2},{12,4},{14,6},{16,24},{18,... | collective-permute-start | bytes 331784 | tf_op jit(solution)/shard_map/ppermute | solution.py:435
  59.5 10.4 %collective-permute-start.18 = (bf16[4,256,128]{2,1,0:T(8,128)(2,1)S(1)}, bf16[4,256,128]{2,1,0:T(8,128)(2,1)S(1)}, u32[]{:S(2)}, u32[]{:S(2)}) collective-permute-start(bf16[4,256,128]{2,1,0:T(8,128)(2,1)S(1)} %get-tuple-element.80.refs_13_.refs_10_), channel_id=1, source_target_pairs={{0,2},{2,0},{4,6},{6,4},{8,10},{10,8},{12,14},{14,12},{16,18},{18,... | collective-permute-start | bytes 786440 | tf_op jit(solution)/shard_map/ppermute | solution.py:435
  69.3 1.6 %collective-permute-start.19 = (bf16[4,256,128]{2,1,0:T(8,128)(2,1)S(1)}, bf16[4,256,128]{2,1,0:T(8,128)(2,1)S(1)}, u32[]{:S(2)}, u32[]{:S(2)}) collective-permute-start(bf16[4,256,128]{2,1,0:T(8,128)(2,1)S(1)} %collective-permute-done.17.refs_11_), channel_id=1, source_target_pairs={{0,2},{2,0},{4,6},{6,4},{8,10},{10,8},{12,14},{14,12},{16,18},{18,... | collective-permute-start | bytes 786440 | tf_op jit(solution)/shard_map/ppermute | solution.py:435
  69.7 6.0 %collective-permute-start.20 = (bf16[8,256,128]{2,1,0:T(8,128)(2,1)S(1)}, bf16[8,256,128]{2,1,0:T(8,128)(2,1)S(1)}, u32[]{:S(2)}, u32[]{:S(2)}) collective-permute-start(bf16[8,256,128]{2,1,0:T(8,128)(2,1)S(1)} %get-tuple-element.88.refs_10_), channel_id=1, source_target_pairs={{0,2},{2,0},{4,6},{6,4},{8,10},{10,8},{12,14},{14,12},{16,18},{18,... | collective-permute-start | bytes 1572872 | tf_op jit(solution)/shard_map/ppermute | solution.py:435
  75.5 1.9 %collective-permute-start.21 = (bf16[8,256,128]{2,1,0:T(8,128)(2,1)S(1)}, bf16[8,256,128]{2,1,0:T(8,128)(2,1)S(1)}, u32[]{:S(2)}, u32[]{:S(2)}) collective-permute-start(bf16[8,256,128]{2,1,0:T(8,128)(2,1)S(1)} %collective-permute-done.16.refs_11_), channel_id=1, source_target_pairs={{0,2},{2,0},{4,6},{6,4},{8,10},{10,8},{12,14},{14,12},{16,18},{18,... | collective-permute-start | bytes 1572872 | tf_op jit(solution)/shard_map/ppermute | solution.py:435
  81.8 11.9 %collective-permute-start.25 = (bf16[128,384]{1,0:T(8,128)(2,1)S(1)}, bf16[128,384]{1,0:T(8,128)(2,1)S(1)}, u32[]{:S(2)}, u32[]{:S(2)}) collective-permute-start(bf16[128,384]{1,0:T(8,128)(2,1)S(1)} %get-tuple-element.100), channel_id=1, source_target_pairs={{0,24},{2,26},{4,28},{6,30},{8,16},{10,18},{12,20},{14,22},{16,8},... | collective-permute-start | bytes 294920 | tf_op jit(solution)/shard_map/ppermute | solution.py:435
  84.6 9.9 %collective-permute-start.26 = (bf16[128,384]{1,0:T(8,128)(2,1)S(1)}, bf16[128,384]{1,0:T(8,128)(2,1)S(1)}, u32[]{:S(2)}, u32[]{:S(2)}) collective-permute-start(bf16[128,384]{1,0:T(8,128)(2,1)S(1)} %get-tuple-element.101), channel_id=1, source_target_pairs={{0,16},{2,18},{4,20},{6,22},{8,24},{10,26},{12,28},{14,30},{16,0},... | collective-permute-start | bytes 294920 | tf_op jit(solution)/shard_map/ppermute | solution.py:435
  84.6 9.9 %collective-permute-start.27 = (bf16[128,384]{1,0:T(8,128)(2,1)S(1)}, bf16[128,384]{1,0:T(8,128)(2,1)S(1)}, u32[]{:S(2)}, u32[]{:S(2)}) collective-permute-start(bf16[128,384]{1,0:T(8,128)(2,1)S(1)} %get-tuple-element.102), channel_id=1, source_target_pairs={{0,8},{2,10},{4,12},{6,14},{8,0},{10,2},{12,4},{14,6},{16,24},{18,... | collective-permute-start | bytes 294920 | tf_op jit(solution)/shard_map/ppermute | solution.py:435
  90.9 5.8 %collective-permute-start.24 = (bf16[128,384]{1,0:T(8,128)(2,1)S(1)}, bf16[128,384]{1,0:T(8,128)(2,1)S(1)}, u32[]{:S(2)}, u32[]{:S(2)}) collective-permute-start(bf16[128,384]{1,0:T(8,128)(2,1)S(1)} %get-tuple-element.99), channel_id=1, source_target_pairs={{0,8},{2,10},{4,12},{6,14},{8,0},{10,2},{12,4},{14,6},{16,24},{18,... | collective-permute-start | bytes 294920 | tf_op jit(solution)/shard_map/ppermute | solution.py:435
  91.3 8.0 %collective-permute-start.22 = (bf16[128,384]{1,0:T(8,128)(2,1)S(1)}, bf16[128,384]{1,0:T(8,128)(2,1)S(1)}, u32[]{:S(2)}, u32[]{:S(2)}) collective-permute-start(bf16[128,384]{1,0:T(8,128)(2,1)S(1)} %get-tuple-element.97), channel_id=1, source_target_pairs={{0,24},{2,26},{4,28},{6,30},{8,16},{10,18},{12,20},{14,22},{16,8},... | collective-permute-start | bytes 294920 | tf_op jit(solution)/shard_map/ppermute | solution.py:435
  93.8 9.1 %collective-permute-start.23 = (bf16[128,384]{1,0:T(8,128)(2,1)S(1)}, bf16[128,384]{1,0:T(8,128)(2,1)S(1)}, u32[]{:S(2)}, u32[]{:S(2)}) collective-permute-start(bf16[128,384]{1,0:T(8,128)(2,1)S(1)} %get-tuple-element.98), channel_id=1, source_target_pairs={{0,16},{2,18},{4,20},{6,22},{8,24},{10,26},{12,28},{14,30},{16,0},... | collective-permute-start | bytes 294920 | tf_op jit(solution)/shard_map/ppermute | solution.py:435
  95.3 9.8 %collective-permute-start.29 = (bf16[128,1536]{1,0:T(8,128)(2,1)S(1)}, bf16[128,1536]{1,0:T(8,128)(2,1)S(1)}, u32[]{:S(2)}, u32[]{:S(2)}) collective-permute-start(bf16[128,1536]{1,0:T(8,128)(2,1)S(1)} %shard_map.89), channel_id=1, source_target_pairs={{0,1},{1,0},{2,3},{3,2},{4,5},{5,4},{6,7},{7,6},{8,9},{9,8},{10,11... | collective-permute-start | bytes 1179656 | tf_op jit(solution)/shard_map/ppermute | solution.py:432
  103.7 10.3 %collective-permute-start.28 = (bf16[128,1536]{1,0:T(8,128)(2,1)S(1)}, bf16[128,1536]{1,0:T(8,128)(2,1)S(1)}, u32[]{:S(2)}, u32[]{:S(2)}) collective-permute-start(bf16[128,1536]{1,0:T(8,128)(2,1)S(1)} %shard_map.91), channel_id=1, source_target_pairs={{0,1},{1,0},{2,3},{3,2},{4,5},{5,4},{6,7},{7,6},{8,9},{9,8},{10,11... | collective-permute-start | bytes 1179656 | tf_op jit(solution)/shard_map/ppermute | solution.py:432

commit v10 on v8

--- a/solution.py
+++ b/solution.py
@@ -395,20 +395,24 @@
 
 def finish(home, arrived, above, cost):
     rows, width = home.shape
-    first = 0 if above is None else above.shape[0]
+    low = 0 if above is None else rows
+    more = [] if above is None else [above]
 
     def body(*refs):
+        total_ref, sem = refs[-2:]
         total = refs[0][...].astype(F32) + refs[1][...].astype(F32)
-        if above is not None:
-            refs[-1][:first] = refs[2][...]
-        refs[-1][first:] = total.astype(BF16)
-
-    more = [] if above is None else [above]
-    return pl.pallas_call(
-        body,
-        in_specs=whole(2 + len(more)),
-        out_specs=whole(1)[0],
-        out_shape=jax.ShapeDtypeStruct((first + rows, width), BF16),
+        total_ref[...] = total.astype(BF16)
+        copy = pltpu.make_async_copy(total_ref, refs[-3].at[pl.ds(low, rows)], sem)
+        copy.start()
+        copy.wait()
+
+    return pl.pallas_call(
+        body,
+        in_specs=whole(2) + [pl.BlockSpec(memory_space=pl.ANY)] * len(more),
+        out_specs=pl.BlockSpec(memory_space=pl.ANY),
+        out_shape=jax.ShapeDtypeStruct((2 * rows, width), BF16),
+        scratch_shapes=[pltpu.VMEM((rows, width), BF16), pltpu.SemaphoreType.DMA(())],
+        input_output_aliases={} if above is None else {2: 0},
         compiler_params=params(8),
         cost_estimate=cost,
     )(home, arrived, *more)

time: 115 us -> 115 us (level)
  transfers between devices with their start and end apart: 30 -> 30, of which waited for: 13 -> 13; matrix products, arithmetic and copies ran while one was open for 1% -> 1% of each run, Pallas kernels for 42% -> 43%
where the time goes in v10:
time: 115 us
  Pallas kernels  54.9 us (48%)
  starting transfers between devices  33.1 us (29%)
  waiting for transfers between devices  25.6 us (22%)
    ppermute x26, starting transfers between devices, over(): return lax.ppermute(a, 'ctx', hop(dz, dx, dc))  27.8 us
    pallas_call x5, Pallas kernels, attend(): pl.pallas_call(body, grid=(count,), in_specs=whole(total_arrays) + [pl.Bl...  23 us
    ppermute x26, waiting for transfers between devices, over(): return lax.ppermute(a, 'ctx', hop(dz, dx, dc))  17.4 us
    pallas_call x2, Pallas kernels, fetch(): pl.pallas_call(body, grid_spec=pltpu.PrefetchScalarGridSpec(num_scalar_pr...  14.2 us
    ppermute x4, waiting for transfers between devices, over_y(): return lax.ppermute(a, 'head', [(0, 1), (1, 0)])  8.26 us
    pallas_call x4, Pallas kernels, project(): pl.pallas_call(body, in_specs=whole(3 + len(more)), out_specs=whole(len(o...  7.08 us
    ppermute x4, starting transfers between devices, over_y(): return lax.ppermute(a, 'head', [(0, 1), (1, 0)])  5.37 us
    pallas_call x1, Pallas kernels, fetch_out(): pl.pallas_call(body, grid_spec=pltpu.PrefetchScalarGridSpec(num_scalar_pr...  4.33 us
  transfers between devices with their start and end apart: 30, of which 13 were waited for; matrix products, arithmetic and copies ran while one was open for 1% of the time, Pallas kernels for 43%

profile of v10, /device:TPU:0, one launch (start us, length us, event | category | flops | bytes accessed | tf_op | source)
XLA Modules:
  0.0 115.3 jit_solution(9512988241924956954)
XLA Ops:
  0.0 3.0 %collective-permute-start = (bf16[256,1536]{1,0:T(8,128)(2,1)}, bf16[256,1536]{1,0:T(8,128)(2,1)S(1)}, u32[]{:S(2)}, u32[]{:S(2)}) collective-permute-start(bf16[256,1536]{1,0:T(8,128)(2,1)} %refs_0_.7), channel_id=1, source_target_pairs={{0,1},{1,0},{2,3},{3,2},{4,5},{5,4},{6,7},{7,6},{8,9},{9,8},{10,11... | collective-permute-start | bytes 2359304 | tf_op jit(solution)/shard_map/ppermute | solution.py:435
  3.0 1.1 slice.3
  4.0 2.7 %collective-permute-start.2 = (bf16[144,1536]{1,0:T(8,128)(2,1)S(1)}, bf16[144,1536]{1,0:T(8,128)(2,1)S(1)}, u32[]{:S(2)}, u32[]{:S(2)}) collective-permute-start(bf16[144,1536]{1,0:T(8,128)(2,1)S(1)} %slice.3), channel_id=1, source_target_pairs={{0,16},{2,18},{4,20},{6,22},{8,24},{10,26},{12,28},{14,30},{16,0},... | collective-permute-start | bytes 1327112 | tf_op jit(solution)/shard_map/ppermute | solution.py:438
  6.8 5.8 %shard_map.73.refs_5_.refs_2_ = bf16[6,3072,384]{2,1,0:T(8,128)(2,1)S(1)} custom-call(s32[4]{0:T(128)S(1)} %pad_add_fusion.s.refs_3_, bf16[3072,1536]{1,0:T(8,128)(2,1)} %refs_0_.4, bf16[3072,1536]{1,0:T(8,128)(2,1)} %refs_1_.3, bf16[3072,1536]{1,0:T(8,128)(2,1)} %refs_2_.3, s32[4]{0:T(128)S(1)} %pad_add_fusion.s.refs_3_), custom_call_target="tpu_custom_call" | custom-call | flops 1024 | bytes 1024 | tf_op jit(solution)/shard_map/pallas_call | solution.py:80
  12.6 8.3 %shard_map.74 = (bf16[6,3072,384]{2,1,0:T(8,128)(2,1)S(1)}, f32[6,256,384]{2,1,0:T(8,128)S(1)}) custom-call(s32[4]{0:T(128)S(1)} %pad_add_fusion.s.refs_3_, bf16[3072,1536]{1,0:T(8,128)(2,1)} %refs_0_.4, bf16[3072,1536]{1,0:T(8,128)(2,1)} %refs_1_.3, bf16[3072,1536]{1,0:T(8,128)(2,1)} %refs_2_.3, s32[4]{0:T(128)S(1)} %pad_add_fusion.s.refs_3_, ...), custom_call_target="tpu_custom_call" | custom-call | flops 1024 | bytes 1024 | tf_op jit(solution)/shard_map/pallas_call | solution.py:80
  21.0 1.9 %shard_map.75 = (bf16[6,256,128]{2,1,0:T(8,128)(2,1)S(1)}, bf16[9,256,128]{2,1,0:T(8,128)(2,1)S(1)}) custom-call(bf16[256,1536]{1,0:T(8,128)(2,1)S(1)} %copy-done, bf16[256,1536]{1,0:T(8,128)(2,1)S(1)} %collective-permute-done.refs_1_, bf16[6,3072,384]{2,1,0:T(8,128)(2,1)S(1)} %shard_map.73.refs_5_.refs_2_, f32[6,256,384]{2,1,0:T(8,128)S(1)} %get-tuple-element.58.refs_3_), custom_call_target="tpu_custom_call" | custom-call | flops 1024 | bytes 1024 | tf_op jit(solution)/shard_map/pallas_call | solution.py:125
  22.9 1.6 %collective-permute-start.3 = (bf16[9,256,128]{2,1,0:T(8,128)(2,1)S(1)}, bf16[9,256,128]{2,1,0:T(8,128)(2,1)S(1)}, u32[]{:S(2)}, u32[]{:S(2)}) collective-permute-start(bf16[9,256,128]{2,1,0:T(8,128)(2,1)S(1)} %get-tuple-element.60), channel_id=1, source_target_pairs={{0,8},{2,10},{4,12},{6,14},{8,0},{10,2},{12,4},{14,6},{16,24},{18,... | collective-permute-start | bytes 1769480 | tf_op jit(solution)/shard_map/ppermute | solution.py:438
  24.5 1.5 %collective-permute-start.5 = (bf16[6,256,128]{2,1,0:T(8,128)(2,1)S(1)}, bf16[6,256,128]{2,1,0:T(8,128)(2,1)S(1)}, u32[]{:S(2)}, u32[]{:S(2)}) collective-permute-start(bf16[6,256,128]{2,1,0:T(8,128)(2,1)S(1)} %get-tuple-element.59.refs_2_), channel_id=1, source_target_pairs={{0,4},{2,6},{4,0},{6,2},{8,12},{10,14},{12,8},{14,10},{16,20},{18,... | collective-permute-start | bytes 1179656 | tf_op jit(solution)/shard_map/ppermute | solution.py:438
  26.2 1.2 %collective-permute-start.4 = (bf16[144,1536]{1,0:T(8,128)(2,1)S(1)}, bf16[144,1536]{1,0:T(8,128)(2,1)S(1)}, u32[]{:S(2)}, u32[]{:S(2)}) collective-permute-start(bf16[144,1536]{1,0:T(8,128)(2,1)S(1)} %collective-permute-done.2.refs_0_), channel_id=1, source_target_pairs={{0,1},{1,0},{2,3},{3,2},{4,5},{5,4},{6,7},{7,6},{8,9},{9,8},{10,11... | collective-permute-start | bytes 1327112 | tf_op jit(solution)/shard_map/ppermute | solution.py:435
  27.5 2.3 %shard_map.76 = (bf16[9,112,128]{2,1,0:T(8,128)(2,1)S(1)}, bf16[9,112,128]{2,1,0:T(8,128)(2,1)S(1)}) custom-call(bf16[256,1536]{1,0:T(8,128)(2,1)S(1)} %copy-done, bf16[256,1536]{1,0:T(8,128)(2,1)S(1)} %collective-permute-done.refs_1_, bf16[6,3072,384]{2,1,0:T(8,128)(2,1)S(1)} %get-tuple-element.56.refs_2_), custom_call_target="tpu_custom_call" | custom-call | flops 1024 | bytes 1024 | tf_op jit(solution)/shard_map/pallas_call | solution.py:125
  29.8 2.8 %collective-permute-start.8 = (bf16[9,112,128]{2,1,0:T(8,128)(2,1)S(1)}, bf16[9,112,128]{2,1,0:T(8,128)(2,1)S(1)}, u32[]{:S(2)}, u32[]{:S(2)}) collective-permute-start(bf16[9,112,128]{2,1,0:T(8,128)(2,1)S(1)} %get-tuple-element.71), channel_id=1, source_target_pairs={{0,24},{2,26},{4,28},{6,30},{8,16},{10,18},{12,20},{14,22},{16,8},... | collective-permute-start | bytes 774152 | tf_op jit(solution)/shard_map/ppermute | solution.py:438
  32.6 0.6 shard_map.77.refs_0_
  33.2 1.1 shard_map.78.fence_ref.refs_12_.refs_14_.refs_18_
  34.2 4.3 %shard_map.79.refs_4_ = bf16[1536,3072]{1,0:T(8,128)(2,1)S(1)} custom-call(s32[4]{0:T(128)S(1)} %pad_add_fusion.s.refs_3_, bf16[1536,3072]{1,0:T(8,128)(2,1)} %w_ref.1, f32[8,4096]{1,0:T(8,128)S(1)} %shard_map.78.fence_ref.refs_12_.refs_14_.refs_18_), custom_call_target="tpu_custom_call" | custom-call | flops 1024 | bytes 1024 | tf_op jit(solution)/shard_map/pallas_call | solution.py:357
  38.7 2.4 %shard_map.80 = (bf16[3,144,128]{2,1,0:T(8,128)(2,1)S(1)}, bf16[6,144,128]{2,1,0:T(8,128)(2,1)S(1)}, bf16[9,144,128]{2,1,0:T(8,128)(2,1)S(1)}) custom-call(bf16[144,1536]{1,0:T(8,128)(2,1)S(1)} %collective-permute-done.2.refs_0_, bf16[144,1536]{1,0:T(8,128)(2,1)S(1)} %collective-permute-done.4.refs_1_, bf16[6,3072,384]{2,1,0:T(8,128)(2,1)S(1)} %shard_map.73.refs_5_.refs_2_), custom_call_target="tpu_custom_call" | custom-call | flops 1024 | bytes 1024 | tf_op jit(solution)/shard_map/pallas_call | solution.py:125
  41.0 1.7 %collective-permute-start.7 = (bf16[6,144,128]{2,1,0:T(8,128)(2,1)S(1)}, bf16[6,144,128]{2,1,0:T(8,128)(2,1)S(1)}, u32[]{:S(2)}, u32[]{:S(2)}) collective-permute-start(bf16[6,144,128]{2,1,0:T(8,128)(2,1)S(1)} %get-tuple-element.67), channel_id=1, source_target_pairs={{0,8},{2,10},{4,12},{6,14},{8,0},{10,2},{12,4},{14,6},{16,24},{18,... | collective-permute-start | bytes 663560 | tf_op jit(solution)/shard_map/ppermute | solution.py:438
  43.0 3.4 %collective-permute-start.11 = (bf16[3,256,128]{2,1,0:T(8,128)(2,1)S(1)}, bf16[3,256,128]{2,1,0:T(8,128)(2,1)S(1)}, u32[]{:S(2)}, u32[]{:S(2)}) collective-permute-start(bf16[3,256,128]{2,1,0:T(8,128)(2,1)S(1)} %get-tuple-element.76), channel_id=1, source_target_pairs={{0,4},{2,6},{4,0},{6,2},{8,12},{10,14},{12,8},{14,10},{16,20},{18,... | collective-permute-start | bytes 589832 | tf_op jit(solution)/shard_map/ppermute | solution.py:438
  46.8 1.5 %collective-permute-start.12 = (bf16[3,256,128]{2,1,0:T(8,128)(2,1)S(1)}, bf16[3,256,128]{2,1,0:T(8,128)(2,1)S(1)}, u32[]{:S(2)}, u32[]{:S(2)}) collective-permute-start(bf16[3,256,128]{2,1,0:T(8,128)(2,1)S(1)} %get-tuple-element.78), channel_id=1, source_target_pairs={{0,4},{2,6},{4,0},{6,2},{8,12},{10,14},{12,8},{14,10},{16,20},{18,... | collective-permute-start | bytes 589832 | tf_op jit(solution)/shard_map/ppermute | solution.py:438
  48.3 7.1 %collective-permute-done.6.refs_1_ = bf16[9,112,128]{2,1,0:T(8,128)(2,1)S(1)} collective-permute-done((bf16[9,112,128]{2,1,0:T(8,128)(2,1)S(1)}, bf16[9,112,128]{2,1,0:T(8,128)(2,1)S(1)}, u32[]{:S(2)}, u32[]{:S(2)}) %collective-permute-start.6) | collective-permute-done | bytes 258080 | tf_op jit(solution)/shard_map/ppermute | solution.py:438
  55.4 0.5 collective-permute-start.14
  55.9 0.7 collective-permute-start.17
  56.6 1.4 %collective-permute-start.16 = (bf16[8,256,128]{2,1,0:T(8,128)(2,1)S(1)}, bf16[8,256,128]{2,1,0:T(8,128)(2,1)S(1)}, u32[]{:S(2)}, u32[]{:S(2)}) collective-permute-start(bf16[8,256,128]{2,1,0:T(8,128)(2,1)S(1)} %get-tuple-element.88.refs_10_), channel_id=1, source_target_pairs={{0,4},{2,6},{4,0},{6,2},{8,12},{10,14},{12,8},{14,10},{16,20},{18,... | collective-permute-start | bytes 1572872 | tf_op jit(solution)/shard_map/ppermute | solution.py:438
  58.1 1.4 %collective-permute-done.15.refs_11_ = bf16[3,256,128]{2,1,0:T(8,128)(2,1)S(1)} collective-permute-done((bf16[3,256,128]{2,1,0:T(8,128)(2,1)S(1)}, bf16[3,256,128]{2,1,0:T(8,128)(2,1)S(1)}, u32[]{:S(2)}, u32[]{:S(2)}) %collective-permute-start.15) | collective-permute-done | bytes 196640 | tf_op jit(solution)/shard_map/ppermute | solution.py:438
  59.6 4.8 %shard_map.83 = (f32[3,512,128]{2,1,0:T(8,128)S(1)}, f32[3,512,128]{2,1,0:T(8,128)S(1)}, f32[3,512,128]{2,1,0:T(8,128)S(1)}) custom-call(bf16[3,256,128]{2,1,0:T(8,128)(2,1)S(1)} %shard_map.77.refs_0_, bf16[9,256,128]{2,1,0:T(8,128)(2,1)S(1)} %collective-permute-done.3.in_ref.refs_1_, bf16[6,256,128]{2,1,0:T(8,128)(2,1)S(1)} %get-tuple-element.59.refs_2_, ...), custom_call_target="tpu_custom_call" | custom-call | flops 1024 | bytes 1024 | tf_op jit(solution)/shard_map/pallas_call | solution.py:322
  64.4 4.8 %shard_map.85 = (f32[3,512,128]{2,1,0:T(8,128)S(1)}, f32[3,512,128]{2,1,0:T(8,128)S(1)}, f32[3,512,128]{2,1,0:T(8,128)S(1)}) custom-call(bf16[3,256,128]{2,1,0:T(8,128)(2,1)S(1)} %get-tuple-element.73.refs_0_.refs_5_.refs_2_, bf16[3,256,128]{2,1,0:T(8,128)(2,1)S(1)} %shard_map.84.refs_1_.refs_6_.refs_3_, bf16[6,256,128]{2,1,0:T(8,128)(2,1)S(1)} %get-tuple-element.59.refs_2_, ...), custom_call_target="tpu_custom_call" | custom-call | flops 1024 | bytes 1024 | tf_op jit(solution)/shard_map/pallas_call | solution.py:322
  69.8 1.0 collective-permute-done.19.refs_13_
  70.9 4.4 %shard_map.86 = (bf16[256,128]{1,0:T(8,128)(2,1)S(1)}, bf16[256,128]{1,0:T(8,128)(2,1)S(1)}, bf16[256,128]{1,0:T(8,128)(2,1)S(1)}, bf16[256,128]{1,0:T(8,128)(2,1)S(1)}) custom-call(bf16[3,256,128]{2,1,0:T(8,128)(2,1)S(1)} %shard_map.77.refs_0_, bf16[9,256,128]{2,1,0:T(8,128)(2,1)S(1)} %collective-permute-done.3.in_ref.refs_1_, ...), custom_call_target="tpu_custom_call" | custom-call | flops 1024 | bytes 1024 | tf_op jit(solution)/shard_map/pallas_call | solution.py:322
  75.7 1.7 %collective-permute-done.21.refs_13_ = bf16[8,256,128]{2,1,0:T(8,128)(2,1)S(1)} collective-permute-done((bf16[8,256,128]{2,1,0:T(8,128)(2,1)S(1)}, bf16[8,256,128]{2,1,0:T(8,128)(2,1)S(1)}, u32[]{:S(2)}, u32[]{:S(2)}) %collective-permute-start.21) | collective-permute-done | bytes 524320 | tf_op jit(solution)/shard_map/ppermute | solution.py:438
  77.4 4.4 %shard_map.87 = (bf16[128,384]{1,0:T(8,128)(2,1)S(1)}, bf16[128,384]{1,0:T(8,128)(2,1)S(1)}, bf16[128,384]{1,0:T(8,128)(2,1)S(1)}, bf16[128,384]{1,0:T(8,128)(2,1)S(1)}) custom-call(bf16[3,256,128]{2,1,0:T(8,128)(2,1)S(1)} %shard_map.77.refs_0_, bf16[9,256,128]{2,1,0:T(8,128)(2,1)S(1)} %collective-permute-done.3.in_ref.refs_1_, ...), custom_call_target="tpu_custom_call" | custom-call | flops 1024 | bytes 1024 | tf_op jit(solution)/shard_map/pallas_call | solution.py:322
  81.8 0.6 collective-permute-start.25
  82.5 2.7 %collective-permute-start.26 = (bf16[128,384]{1,0:T(8,128)(2,1)S(1)}, bf16[128,384]{1,0:T(8,128)(2,1)S(1)}, u32[]{:S(2)}, u32[]{:S(2)}) collective-permute-start(bf16[128,384]{1,0:T(8,128)(2,1)S(1)} %get-tuple-element.101), channel_id=1, source_target_pairs={{0,16},{2,18},{4,20},{6,22},{8,24},{10,26},{12,28},{14,30},{16,0},... | collective-permute-start | bytes 294920 | tf_op jit(solution)/shard_map/ppermute | solution.py:438
  85.2 1.1 collective-permute-start.27
  86.3 4.6 %shard_map.88 = (bf16[128,384]{1,0:T(8,128)(2,1)S(1)}, bf16[128,384]{1,0:T(8,128)(2,1)S(1)}, bf16[128,384]{1,0:T(8,128)(2,1)S(1)}, bf16[128,384]{1,0:T(8,128)(2,1)S(1)}) custom-call(bf16[3,256,128]{2,1,0:T(8,128)(2,1)S(1)} %shard_map.77.refs_0_, bf16[9,256,128]{2,1,0:T(8,128)(2,1)S(1)} %collective-permute-done.3.in_ref.refs_1_, ...), custom_call_target="tpu_custom_call" | custom-call | flops 1024 | bytes 1024 | tf_op jit(solution)/shard_map/pallas_call | solution.py:322
  90.9 2.8 %collective-permute-start.24 = (bf16[128,384]{1,0:T(8,128)(2,1)S(1)}, bf16[128,384]{1,0:T(8,128)(2,1)S(1)}, u32[]{:S(2)}, u32[]{:S(2)}) collective-permute-start(bf16[128,384]{1,0:T(8,128)(2,1)S(1)} %get-tuple-element.99), channel_id=1, source_target_pairs={{0,24},{2,26},{4,28},{6,30},{8,16},{10,18},{12,20},{14,22},{16,8},... | collective-permute-start | bytes 294920 | tf_op jit(solution)/shard_map/ppermute | solution.py:438
  93.7 1.7 %collective-permute-start.23 = (bf16[128,384]{1,0:T(8,128)(2,1)S(1)}, bf16[128,384]{1,0:T(8,128)(2,1)S(1)}, u32[]{:S(2)}, u32[]{:S(2)}) collective-permute-start(bf16[128,384]{1,0:T(8,128)(2,1)S(1)} %get-tuple-element.98), channel_id=1, source_target_pairs={{0,16},{2,18},{4,20},{6,22},{8,24},{10,26},{12,28},{14,30},{16,0},... | collective-permute-start | bytes 294920 | tf_op jit(solution)/shard_map/ppermute | solution.py:438
  95.4 0.8 shard_map.89
  96.2 0.6 collective-permute-start.29
  96.8 0.8 shard_map.90.refs_0_
  97.7 0.9 collective-permute-done.24.refs_3_
  98.5 0.7 collective-permute-done.22.refs_1_
  99.3 3.6 %collective-permute-done.23.refs_2_ = bf16[128,384]{1,0:T(8,128)(2,1)S(1)} collective-permute-done((bf16[128,384]{1,0:T(8,128)(2,1)S(1)}, bf16[128,384]{1,0:T(8,128)(2,1)S(1)}, u32[]{:S(2)}, u32[]{:S(2)}) %collective-permute-start.23) | collective-permute-done | bytes 98336 | tf_op jit(solution)/shard_map/ppermute | solution.py:438
  102.9 0.8 shard_map.91
  103.7 0.6 collective-permute-start.28
  104.3 0.8 shard_map.92.refs_0_
  105.1 0.7 collective-permute-done.29.refs_1_
  105.8 0.8 shard_map.93.refs_2_
  106.7 7.6 %collective-permute-done.28.refs_1_ = bf16[128,1536]{1,0:T(8,128)(2,1)S(1)} collective-permute-done((bf16[128,1536]{1,0:T(8,128)(2,1)S(1)}, bf16[128,1536]{1,0:T(8,128)(2,1)S(1)}, u32[]{:S(2)}, u32[]{:S(2)}) %collective-permute-start.28) | collective-permute-done | bytes 393248 | tf_op jit(solution)/shard_map/ppermute | solution.py:435
  114.3 0.8 shard_map.94
  (42 shorter events, 2.4 us)
Async XLA Ops:
  0.0 21.0 %collective-permute-start = (bf16[256,1536]{1,0:T(8,128)(2,1)}, bf16[256,1536]{1,0:T(8,128)(2,1)S(1)}, u32[]{:S(2)}, u32[]{:S(2)}) collective-permute-start(bf16[256,1536]{1,0:T(8,128)(2,1)} %refs_0_.7), channel_id=1, source_target_pairs={{0,1},{1,0},{2,3},{3,2},{4,5},{5,4},{6,7},{7,6},{8,9},{9,8},{10,11... | collective-permute-start | bytes 2359304 | tf_op jit(solution)/shard_map/ppermute | solution.py:435
  4.0 22.2 %collective-permute-start.2 = (bf16[144,1536]{1,0:T(8,128)(2,1)S(1)}, bf16[144,1536]{1,0:T(8,128)(2,1)S(1)}, u32[]{:S(2)}, u32[]{:S(2)}) collective-permute-start(bf16[144,1536]{1,0:T(8,128)(2,1)S(1)} %slice.3), channel_id=1, source_target_pairs={{0,16},{2,18},{4,20},{6,22},{8,24},{10,26},{12,28},{14,30},{16,0},... | collective-permute-start | bytes 1327112 | tf_op jit(solution)/shard_map/ppermute | solution.py:438
  6.8 5.9 %copy-start = (bf16[256,1536]{1,0:T(8,128)(2,1)S(1)}, bf16[256,1536]{1,0:T(8,128)(2,1)}, u32[]{:S(2)}) copy-start(bf16[256,1536]{1,0:T(8,128)(2,1)} %refs_0_.7) | copy-start | bytes 2359300
  22.9 20.1 %collective-permute-start.3 = (bf16[9,256,128]{2,1,0:T(8,128)(2,1)S(1)}, bf16[9,256,128]{2,1,0:T(8,128)(2,1)S(1)}, u32[]{:S(2)}, u32[]{:S(2)}) collective-permute-start(bf16[9,256,128]{2,1,0:T(8,128)(2,1)S(1)} %get-tuple-element.60), channel_id=1, source_target_pairs={{0,8},{2,10},{4,12},{6,14},{8,0},{10,2},{12,4},{14,6},{16,24},{18,... | collective-permute-start | bytes 1769480 | tf_op jit(solution)/shard_map/ppermute | solution.py:438
  24.5 8.1 %collective-permute-start.1 = (bf16[6,256,128]{2,1,0:T(8,128)(2,1)S(1)}, bf16[6,256,128]{2,1,0:T(8,128)(2,1)S(1)}, u32[]{:S(2)}, u32[]{:S(2)}) collective-permute-start(bf16[6,256,128]{2,1,0:T(8,128)(2,1)S(1)} %get-tuple-element.59.refs_2_), channel_id=1, source_target_pairs={{0,2},{2,0},{4,6},{6,4},{8,10},{10,8},{12,14},{14,12},{16,18},{18,... | collective-permute-start | bytes 1179656 | tf_op jit(solution)/shard_map/ppermute | solution.py:438
  24.5 14.1 %collective-permute-start.5 = (bf16[6,256,128]{2,1,0:T(8,128)(2,1)S(1)}, bf16[6,256,128]{2,1,0:T(8,128)(2,1)S(1)}, u32[]{:S(2)}, u32[]{:S(2)}) collective-permute-start(bf16[6,256,128]{2,1,0:T(8,128)(2,1)S(1)} %get-tuple-element.59.refs_2_), channel_id=1, source_target_pairs={{0,4},{2,6},{4,0},{6,2},{8,12},{10,14},{12,8},{14,10},{16,20},{18,... | collective-permute-start | bytes 1179656 | tf_op jit(solution)/shard_map/ppermute | solution.py:438
  26.2 12.4 %collective-permute-start.4 = (bf16[144,1536]{1,0:T(8,128)(2,1)S(1)}, bf16[144,1536]{1,0:T(8,128)(2,1)S(1)}, u32[]{:S(2)}, u32[]{:S(2)}) collective-permute-start(bf16[144,1536]{1,0:T(8,128)(2,1)S(1)} %collective-permute-done.2.refs_0_), channel_id=1, source_target_pairs={{0,1},{1,0},{2,3},{3,2},{4,5},{5,4},{6,7},{7,6},{8,9},{9,8},{10,11... | collective-permute-start | bytes 1327112 | tf_op jit(solution)/shard_map/ppermute | solution.py:435
  29.7 3.4 %copy-start.1 = (s32[32,32]{1,0:T(8,128)S(1)}, s32[32,32]{1,0:T(8,128)}, u32[]{:S(2)}) copy-start(s32[32,32]{1,0:T(8,128)} %mask_ref.1) | copy-start | bytes 12292
  29.8 3.4 %copy-start.2 = (s32[32]{0:T(128)S(1)}, s32[32]{0:T(128)}, u32[]{:S(2)}) copy-start(s32[32]{0:T(128)} %param.8) | copy-start | bytes 388
  29.8 17.0 %collective-permute-start.8 = (bf16[9,112,128]{2,1,0:T(8,128)(2,1)S(1)}, bf16[9,112,128]{2,1,0:T(8,128)(2,1)S(1)}, u32[]{:S(2)}, u32[]{:S(2)}) collective-permute-start(bf16[9,112,128]{2,1,0:T(8,128)(2,1)S(1)} %get-tuple-element.71), channel_id=1, source_target_pairs={{0,24},{2,26},{4,28},{6,30},{8,16},{10,18},{12,20},{14,22},{16,8},... | collective-permute-start | bytes 774152 | tf_op jit(solution)/shard_map/ppermute | solution.py:438
  32.6 22.8 %collective-permute-start.6 = (bf16[9,112,128]{2,1,0:T(8,128)(2,1)S(1)}, bf16[9,112,128]{2,1,0:T(8,128)(2,1)S(1)}, u32[]{:S(2)}, u32[]{:S(2)}) collective-permute-start(bf16[9,112,128]{2,1,0:T(8,128)(2,1)S(1)} %get-tuple-element.63), channel_id=1, source_target_pairs={{0,16},{2,18},{4,20},{6,22},{8,24},{10,26},{12,28},{14,30},{16,0},... | collective-permute-start | bytes 774152 | tf_op jit(solution)/shard_map/ppermute | solution.py:438
  38.6 19.5 %collective-permute-start.10 = (bf16[6,256,128]{2,1,0:T(8,128)(2,1)S(1)}, bf16[6,256,128]{2,1,0:T(8,128)(2,1)S(1)}, u32[]{:S(2)}, u32[]{:S(2)}) collective-permute-start(bf16[6,256,128]{2,1,0:T(8,128)(2,1)S(1)} %collective-permute-done.5.refs_3_), channel_id=1, source_target_pairs={{0,2},{2,0},{4,6},{6,4},{8,10},{10,8},{12,14},{14,12},{16,18},{18,... | collective-permute-start | bytes 1179656 | tf_op jit(solution)/shard_map/ppermute | solution.py:438
  41.0 14.3 %collective-permute-start.7 = (bf16[6,144,128]{2,1,0:T(8,128)(2,1)S(1)}, bf16[6,144,128]{2,1,0:T(8,128)(2,1)S(1)}, u32[]{:S(2)}, u32[]{:S(2)}) collective-permute-start(bf16[6,144,128]{2,1,0:T(8,128)(2,1)S(1)} %get-tuple-element.67), channel_id=1, source_target_pairs={{0,8},{2,10},{4,12},{6,14},{8,0},{10,2},{12,4},{14,6},{16,24},{18,... | collective-permute-start | bytes 663560 | tf_op jit(solution)/shard_map/ppermute | solution.py:438
  43.0 12.3 %collective-permute-start.11 = (bf16[3,256,128]{2,1,0:T(8,128)(2,1)S(1)}, bf16[3,256,128]{2,1,0:T(8,128)(2,1)S(1)}, u32[]{:S(2)}, u32[]{:S(2)}) collective-permute-start(bf16[3,256,128]{2,1,0:T(8,128)(2,1)S(1)} %get-tuple-element.76), channel_id=1, source_target_pairs={{0,4},{2,6},{4,0},{6,2},{8,12},{10,14},{12,8},{14,10},{16,20},{18,... | collective-permute-start | bytes 589832 | tf_op jit(solution)/shard_map/ppermute | solution.py:438
  46.8 9.9 %collective-permute-start.12 = (bf16[3,256,128]{2,1,0:T(8,128)(2,1)S(1)}, bf16[3,256,128]{2,1,0:T(8,128)(2,1)S(1)}, u32[]{:S(2)}, u32[]{:S(2)}) collective-permute-start(bf16[3,256,128]{2,1,0:T(8,128)(2,1)S(1)} %get-tuple-element.78), channel_id=1, source_target_pairs={{0,4},{2,6},{4,0},{6,2},{8,12},{10,14},{12,8},{14,10},{16,20},{18,... | collective-permute-start | bytes 589832 | tf_op jit(solution)/shard_map/ppermute | solution.py:438
  55.3 4.3 %collective-permute-start.13 = (bf16[6,256,128]{2,1,0:T(8,128)(2,1)S(1)}, bf16[6,256,128]{2,1,0:T(8,128)(2,1)S(1)}, u32[]{:S(2)}, u32[]{:S(2)}) collective-permute-start(bf16[6,256,128]{2,1,0:T(8,128)(2,1)S(1)} %get-tuple-element.75.refs_6_), channel_id=1, source_target_pairs={{0,2},{2,0},{4,6},{6,4},{8,10},{10,8},{12,14},{14,12},{16,18},{18,... | collective-permute-start | bytes 1179656 | tf_op jit(solution)/shard_map/ppermute | solution.py:438
  55.4 2.7 %collective-permute-start.14 = (bf16[3,256,128]{2,1,0:T(8,128)(2,1)S(1)}, bf16[3,256,128]{2,1,0:T(8,128)(2,1)S(1)}, u32[]{:S(2)}, u32[]{:S(2)}) collective-permute-start(bf16[3,256,128]{2,1,0:T(8,128)(2,1)S(1)} %collective-permute-done.11.refs_7_), channel_id=1, source_target_pairs={{0,2},{2,0},{4,6},{6,4},{8,10},{10,8},{12,14},{14,12},{16,18},{18,... | collective-permute-start | bytes 589832 | tf_op jit(solution)/shard_map/ppermute | solution.py:438
  55.9 13.3 %collective-permute-start.17 = (bf16[4,256,128]{2,1,0:T(8,128)(2,1)S(1)}, bf16[4,256,128]{2,1,0:T(8,128)(2,1)S(1)}, u32[]{:S(2)}, u32[]{:S(2)}) collective-permute-start(bf16[4,256,128]{2,1,0:T(8,128)(2,1)S(1)} %get-tuple-element.80.refs_13_.refs_10_), channel_id=1, source_target_pairs={{0,4},{2,6},{4,0},{6,2},{8,12},{10,14},{12,8},{14,10},{16,20},{18,... | collective-permute-start | bytes 786440 | tf_op jit(solution)/shard_map/ppermute | solution.py:438
  56.6 18.9 %collective-permute-start.16 = (bf16[8,256,128]{2,1,0:T(8,128)(2,1)S(1)}, bf16[8,256,128]{2,1,0:T(8,128)(2,1)S(1)}, u32[]{:S(2)}, u32[]{:S(2)}) collective-permute-start(bf16[8,256,128]{2,1,0:T(8,128)(2,1)S(1)} %get-tuple-element.88.refs_10_), channel_id=1, source_target_pairs={{0,4},{2,6},{4,0},{6,2},{8,12},{10,14},{12,8},{14,10},{16,20},{18,... | collective-permute-start | bytes 1572872 | tf_op jit(solution)/shard_map/ppermute | solution.py:438
  58.0 1.4 %collective-permute-start.15 = (bf16[3,256,128]{2,1,0:T(8,128)(2,1)S(1)}, bf16[3,256,128]{2,1,0:T(8,128)(2,1)S(1)}, u32[]{:S(2)}, u32[]{:S(2)}) collective-permute-start(bf16[3,256,128]{2,1,0:T(8,128)(2,1)S(1)} %collective-permute-done.12.refs_8_), channel_id=1, source_target_pairs={{0,2},{2,0},{4,6},{6,4},{8,10},{10,8},{12,14},{14,12},{16,18},{18,... | collective-permute-start | bytes 589832 | tf_op jit(solution)/shard_map/ppermute | solution.py:438
  58.0 6.4 %collective-permute-start.9 = (bf16[3,144,128]{2,1,0:T(8,128)(2,1)S(1)}, bf16[3,144,128]{2,1,0:T(8,128)(2,1)S(1)}, u32[]{:S(2)}, u32[]{:S(2)}) collective-permute-start(bf16[3,144,128]{2,1,0:T(8,128)(2,1)S(1)} %get-tuple-element.74), channel_id=1, source_target_pairs={{0,8},{2,10},{4,12},{6,14},{8,0},{10,2},{12,4},{14,6},{16,24},{18,... | collective-permute-start | bytes 331784 | tf_op jit(solution)/shard_map/ppermute | solution.py:438
  59.5 10.4 %collective-permute-start.18 = (bf16[4,256,128]{2,1,0:T(8,128)(2,1)S(1)}, bf16[4,256,128]{2,1,0:T(8,128)(2,1)S(1)}, u32[]{:S(2)}, u32[]{:S(2)}) collective-permute-start(bf16[4,256,128]{2,1,0:T(8,128)(2,1)S(1)} %get-tuple-element.80.refs_13_.refs_10_), channel_id=1, source_target_pairs={{0,2},{2,0},{4,6},{6,4},{8,10},{10,8},{12,14},{14,12},{16,18},{18,... | collective-permute-start | bytes 786440 | tf_op jit(solution)/shard_map/ppermute | solution.py:438
  69.3 1.6 %collective-permute-start.19 = (bf16[4,256,128]{2,1,0:T(8,128)(2,1)S(1)}, bf16[4,256,128]{2,1,0:T(8,128)(2,1)S(1)}, u32[]{:S(2)}, u32[]{:S(2)}) collective-permute-start(bf16[4,256,128]{2,1,0:T(8,128)(2,1)S(1)} %collective-permute-done.17.refs_11_), channel_id=1, source_target_pairs={{0,2},{2,0},{4,6},{6,4},{8,10},{10,8},{12,14},{14,12},{16,18},{18,... | collective-permute-start | bytes 786440 | tf_op jit(solution)/shard_map/ppermute | solution.py:438
  69.7 6.0 %collective-permute-start.20 = (bf16[8,256,128]{2,1,0:T(8,128)(2,1)S(1)}, bf16[8,256,128]{2,1,0:T(8,128)(2,1)S(1)}, u32[]{:S(2)}, u32[]{:S(2)}) collective-permute-start(bf16[8,256,128]{2,1,0:T(8,128)(2,1)S(1)} %get-tuple-element.88.refs_10_), channel_id=1, source_target_pairs={{0,2},{2,0},{4,6},{6,4},{8,10},{10,8},{12,14},{14,12},{16,18},{18,... | collective-permute-start | bytes 1572872 | tf_op jit(solution)/shard_map/ppermute | solution.py:438
  75.5 1.9 %collective-permute-start.21 = (bf16[8,256,128]{2,1,0:T(8,128)(2,1)S(1)}, bf16[8,256,128]{2,1,0:T(8,128)(2,1)S(1)}, u32[]{:S(2)}, u32[]{:S(2)}) collective-permute-start(bf16[8,256,128]{2,1,0:T(8,128)(2,1)S(1)} %collective-permute-done.16.refs_11_), channel_id=1, source_target_pairs={{0,2},{2,0},{4,6},{6,4},{8,10},{10,8},{12,14},{14,12},{16,18},{18,... | collective-permute-start | bytes 1572872 | tf_op jit(solution)/shard_map/ppermute | solution.py:438
  81.8 11.9 %collective-permute-start.25 = (bf16[128,384]{1,0:T(8,128)(2,1)S(1)}, bf16[128,384]{1,0:T(8,128)(2,1)S(1)}, u32[]{:S(2)}, u32[]{:S(2)}) collective-permute-start(bf16[128,384]{1,0:T(8,128)(2,1)S(1)} %get-tuple-element.100), channel_id=1, source_target_pairs={{0,8},{2,10},{4,12},{6,14},{8,0},{10,2},{12,4},{14,6},{16,24},{18,... | collective-permute-start | bytes 294920 | tf_op jit(solution)/shard_map/ppermute | solution.py:438
  82.5 12.9 %collective-permute-start.26 = (bf16[128,384]{1,0:T(8,128)(2,1)S(1)}, bf16[128,384]{1,0:T(8,128)(2,1)S(1)}, u32[]{:S(2)}, u32[]{:S(2)}) collective-permute-start(bf16[128,384]{1,0:T(8,128)(2,1)S(1)} %get-tuple-element.101), channel_id=1, source_target_pairs={{0,16},{2,18},{4,20},{6,22},{8,24},{10,26},{12,28},{14,30},{16,0},... | collective-permute-start | bytes 294920 | tf_op jit(solution)/shard_map/ppermute | solution.py:438
  85.2 10.2 %collective-permute-start.27 = (bf16[128,384]{1,0:T(8,128)(2,1)S(1)}, bf16[128,384]{1,0:T(8,128)(2,1)S(1)}, u32[]{:S(2)}, u32[]{:S(2)}) collective-permute-start(bf16[128,384]{1,0:T(8,128)(2,1)S(1)} %get-tuple-element.102), channel_id=1, source_target_pairs={{0,24},{2,26},{4,28},{6,30},{8,16},{10,18},{12,20},{14,22},{16,8},... | collective-permute-start | bytes 294920 | tf_op jit(solution)/shard_map/ppermute | solution.py:438
  90.9 7.6 %collective-permute-start.24 = (bf16[128,384]{1,0:T(8,128)(2,1)S(1)}, bf16[128,384]{1,0:T(8,128)(2,1)S(1)}, u32[]{:S(2)}, u32[]{:S(2)}) collective-permute-start(bf16[128,384]{1,0:T(8,128)(2,1)S(1)} %get-tuple-element.99), channel_id=1, source_target_pairs={{0,24},{2,26},{4,28},{6,30},{8,16},{10,18},{12,20},{14,22},{16,8},... | collective-permute-start | bytes 294920 | tf_op jit(solution)/shard_map/ppermute | solution.py:438
  93.7 5.6 %collective-permute-start.22 = (bf16[128,384]{1,0:T(8,128)(2,1)S(1)}, bf16[128,384]{1,0:T(8,128)(2,1)S(1)}, u32[]{:S(2)}, u32[]{:S(2)}) collective-permute-start(bf16[128,384]{1,0:T(8,128)(2,1)S(1)} %get-tuple-element.97), channel_id=1, source_target_pairs={{0,8},{2,10},{4,12},{6,14},{8,0},{10,2},{12,4},{14,6},{16,24},{18,... | collective-permute-start | bytes 294920 | tf_op jit(solution)/shard_map/ppermute | solution.py:438
  93.7 9.2 %collective-permute-start.23 = (bf16[128,384]{1,0:T(8,128)(2,1)S(1)}, bf16[128,384]{1,0:T(8,128)(2,1)S(1)}, u32[]{:S(2)}, u32[]{:S(2)}) collective-permute-start(bf16[128,384]{1,0:T(8,128)(2,1)S(1)} %get-tuple-element.98), channel_id=1, source_target_pairs={{0,16},{2,18},{4,20},{6,22},{8,24},{10,26},{12,28},{14,30},{16,0},... | collective-permute-start | bytes 294920 | tf_op jit(solution)/shard_map/ppermute | solution.py:438
  96.2 9.6 %collective-permute-start.29 = (bf16[128,1536]{1,0:T(8,128)(2,1)S(1)}, bf16[128,1536]{1,0:T(8,128)(2,1)S(1)}, u32[]{:S(2)}, u32[]{:S(2)}) collective-permute-start(bf16[128,1536]{1,0:T(8,128)(2,1)S(1)} %shard_map.89), channel_id=1, source_target_pairs={{0,1},{1,0},{2,3},{3,2},{4,5},{5,4},{6,7},{7,6},{8,9},{9,8},{10,11... | collective-permute-start | bytes 1179656 | tf_op jit(solution)/shard_map/ppermute | solution.py:435
  103.7 10.6 %collective-permute-start.28 = (bf16[128,1536]{1,0:T(8,128)(2,1)S(1)}, bf16[128,1536]{1,0:T(8,128)(2,1)S(1)}, u32[]{:S(2)}, u32[]{:S(2)}) collective-permute-start(bf16[128,1536]{1,0:T(8,128)(2,1)S(1)} %shard_map.91), channel_id=1, source_target_pairs={{0,1},{1,0},{2,3},{3,2},{4,5},{5,4},{6,7},{7,6},{8,9},{9,8},{10,11... | collective-permute-start | bytes 1179656 | tf_op jit(solution)/shard_map/ppermute | solution.py:435
